TPU v7x, 32 devices: a whole 2x2x4 slice. The times are simulated.
32 devices in a mesh: row: 8 (over y, x, core), col: 4 (over z).
Axes of the slice: x: 2, y: 2, z: 4, core: 2. Of those that a mesh axis runs over, the one named last changes fastest.
Arguments:
- hidden: bfloat16 [4096, 2048], P('col', 'row'), may hold values from -6 to 6
- lengths: int32 [32], replicated, may hold values from 16 to 128, as said below
- square_matrix_shards: float32 [7, 2048, 2048], P(None, ('row', 'col')), may hold values from -0.125 to 0.125
- channel_mix_shards: float32 [2, 2048, 8192], P(None, ('row', 'col')), may hold values from -0.09375 to 0.09375
- lowrank_down: bfloat16 [2, 2048, 96], replicated, may hold values from -0.125 to 0.125
- lowrank_up: bfloat16 [2, 96, 2048], replicated, may hold values from -0.625 to 0.625
- token_shift_weights: float32 [9, 2048], replicated, may hold values from 0 to 1
- attention_coefficients: float32 [6, 2048], replicated, may hold values from -8 to 2, as said below
- norm_parameters: float32 [6, 2048], P(None, 'row'), may hold values from 0.25 to 1.75
Outputs:
- out_hidden: bfloat16 [4096, 2048], P('col', 'row')
- next_rkv: bfloat16 [3, 4096, 2048], P(None, 'row', 'col')
- final_state: float32 [32, 32, 4096], P('row', 'col')
Inputs may be any that keep to these rules, and one draw needn't show every extreme that they name: `lengths`: every prompt length lies between 16 and 128; in every draw at least one prompt has length 128, most are under 41. `attention_coefficients`: row 0 lies in -8 to -1, row 1 in -2 to 2, row 2 in 0.5 to 1.5, row 3 in -1 to 1, row 4 in 0.5 to 1.5, row 5 in -0.5 to 0.5.
All inputs are finite; a program needn't handle non-finite values.
Results may differ from a plain program's by a relative error of at most 0.034.
Values may be sent and summed in bfloat16 or wider, within the bound.
No kernel may reach another device: no remote copies, remote signals or barrier semaphores. Data moves between devices by JAX's collectives and lax.ppermute only.
A program may use at most 128 MiB of HBM per device.

v0:
```python
import jax
import jax.numpy as jnp
from jax import lax
from jax.sharding import PartitionSpec as P

MODEL_WIDTH = 2048
ATTENTION_DIM = 64
LMAX = 128
SPAN = 16


def shifted(source):
    grid = source.reshape(-1, LMAX, source.shape[-1])
    before = jnp.concatenate([jnp.zeros_like(grid[:, :1]), grid[:, :-1]], axis=1)
    return before.reshape(source.shape)


def mixed(source, weight):
    wide = source.astype(jnp.float32)
    return (wide + (shifted(wide) - wide) * weight).astype(jnp.bfloat16)


def normed(source, gain, bias):
    totals, squares = lax.psum((jnp.sum(source, axis=-1), jnp.sum(source * source, axis=-1)), "row")
    center = (totals / MODEL_WIDTH)[:, None]
    second = (squares / MODEL_WIDTH)[:, None]
    scaled = (source - center) * lax.rsqrt(second - center * center + 1e-05)
    return (scaled * gain + bias).astype(jnp.bfloat16)


def gather_cols(source):
    return lax.all_gather(source, "col", axis=0, tiled=True)


def row_sums(term_fn, rows):
    return lax.psum_scatter(
        term_fn(jnp.int32(0), rows * lax.axis_size("row")).astype(jnp.bfloat16),
        "row",
        scatter_dimension=0,
        tiled=True,
    ).astype(jnp.float32)


def span_step(
    state, acceptance_gate_entries, key_vecs, value_vecs, decay_logarithm, remove_dir, write_dir
):
    highest = lax.Precision.HIGHEST
    cumul = jnp.cumsum(decay_logarithm, axis=1)
    before = cumul - decay_logarithm
    last = cumul[:, -1]
    pull_t = remove_dir * jnp.exp(before)
    read_t = acceptance_gate_entries * jnp.exp(cumul)
    back = jnp.exp(-cumul)
    write_back = write_dir * back
    key_back = key_vecs * back
    order = jnp.arange(SPAN)
    strict = (order[:, None] > order[None, :]).astype(jnp.float32)
    upto = (order[:, None] >= order[None, :]).astype(jnp.float32)
    mix_write = jnp.einsum("sthk,suhk->shtu", pull_t, write_back, precision=highest) * strict
    mix_key = jnp.einsum("sthk,suhk->shtu", pull_t, key_back, precision=highest) * strict
    rhs_side = jnp.einsum("sthk,shvk->shtv", pull_t, state, precision=highest) + jnp.einsum(
        "shtu,suhv->shtv", mix_key, value_vecs, precision=highest
    )
    system = jnp.eye(SPAN, dtype=jnp.float32) - mix_write
    pulled = jax.scipy.linalg.solve_triangular(system, rhs_side, lower=True, unit_diagonal=True)
    read_write = jnp.einsum("sthk,suhk->shtu", read_t, write_back, precision=highest) * upto
    read_key = jnp.einsum("sthk,suhk->shtu", read_t, key_back, precision=highest) * upto
    output = jnp.einsum("sthk,shvk->sthv", read_t, state, precision=highest)
    output = output + jnp.einsum("shtu,shuv->sthv", read_write, pulled, precision=highest)
    output = output + jnp.einsum("shtu,suhv->sthv", read_key, value_vecs, precision=highest)
    tail = jnp.exp(last[:, None] - cumul)
    new_state = state * jnp.exp(last)[:, :, None, :]
    new_state = new_state + jnp.einsum(
        "shtv,sthk->shvk", pulled, write_dir * tail, precision=highest
    )
    new_state = new_state + jnp.einsum(
        "sthv,sthk->shvk", value_vecs, key_vecs * tail, precision=highest
    )
    return (new_state, output)


def time_core(
    acceptance_gate_entries,
    key_vecs,
    value_vecs,
    decay_lowrank,
    rate_lowrank,
    head_local,
    up_shard_local,
    prompt_lengths,
):
    rows_here, shard_width = acceptance_gate_entries.shape
    decay_input = jnp.tanh(decay_lowrank).astype(jnp.bfloat16)
    decay_logarithm = -0.606531 * jax.nn.sigmoid(
        head_local[0] + jnp.dot(decay_input, up_shard_local[0], preferred_element_type=jnp.float32)
    )
    incontext_rate = jax.nn.sigmoid(
        head_local[1]
        + jnp.dot(
            rate_lowrank.astype(jnp.bfloat16), up_shard_local[1], preferred_element_type=jnp.float32
        )
    )
    prompt_count = rows_here // LMAX
    head_count = shard_width // ATTENTION_DIM

    def split_heads(source):
        return source.reshape(prompt_count, LMAX, head_count, ATTENTION_DIM)

    acceptance_gate_entries = split_heads(acceptance_gate_entries)
    key_vecs = split_heads(key_vecs)
    value_vecs = split_heads(value_vecs)
    decay_logarithm = split_heads(decay_logarithm)
    incontext_rate = split_heads(incontext_rate)
    kappa = key_vecs * head_local[2].reshape(head_count, ATTENTION_DIM)
    kappa_hat = kappa * lax.rsqrt(jnp.sum(kappa * kappa, axis=-1, keepdims=True) + 1e-05)
    present_entries = (jnp.arange(LMAX)[None, :] < prompt_lengths[:, None]).astype(jnp.float32)[
        :, :, None, None
    ]
    remove_dir = -kappa_hat * present_entries
    write_dir = kappa_hat * incontext_rate * present_entries
    present_address_vector = key_vecs * present_entries
    present_payload_vector = value_vecs * present_entries
    block_total = LMAX // SPAN
    stacked = jnp.stack(
        [
            acceptance_gate_entries,
            present_address_vector,
            present_payload_vector,
            decay_logarithm * present_entries,
            remove_dir,
            write_dir,
        ]
    )
    stacked = stacked.reshape(6, prompt_count, block_total, SPAN, head_count, ATTENTION_DIM)

    def advance(block_index, carry):
        state, result_entries = carry
        weight_slices = lax.dynamic_index_in_dim(stacked, block_index, 2, keepdims=False)
        new_state, output = span_step(
            state,
            weight_slices[0],
            weight_slices[1],
            weight_slices[2],
            weight_slices[3],
            weight_slices[4],
            weight_slices[5],
        )
        result_entries = lax.dynamic_update_index_in_dim(result_entries, output, block_index, 1)
        return (new_state, result_entries)

    start_state = jnp.zeros((prompt_count, head_count, ATTENTION_DIM, ATTENTION_DIM), jnp.float32)
    start_out = jnp.zeros((prompt_count, block_total, SPAN, head_count, ATTENTION_DIM), jnp.float32)
    final, result_entries = lax.fori_loop(0, block_total, advance, (start_state, start_out))
    result_entries = result_entries.reshape(prompt_count, LMAX, head_count, ATTENTION_DIM)
    extra_reward_factor = (
        jnp.sum(
            acceptance_gate_entries
            * present_address_vector
            * head_local[3].reshape(head_count, ATTENTION_DIM),
            axis=-1,
            keepdims=True,
        )
        * present_payload_vector
    )
    attention_results = (result_entries + extra_reward_factor) * present_entries
    center = jnp.mean(attention_results, axis=-1, keepdims=True)
    spread = jnp.mean(jnp.square(attention_results - center), axis=-1, keepdims=True)
    grouped = ((attention_results - center) * lax.rsqrt(spread + 0.00064)).reshape(
        rows_here, shard_width
    )
    att = (grouped * head_local[4] + head_local[5]).astype(jnp.bfloat16)
    return (att, final.reshape(prompt_count, head_count, ATTENTION_DIM * ATTENTION_DIM))


def block_products(sources, weights, n_row):
    feat_width = sources[0].shape[1] // n_row

    def add_block(block_index, totals):
        start = block_index * feat_width
        result = []
        for source, weight, total in zip(sources, weights, totals):
            piece = lax.dynamic_slice_in_dim(source, start, feat_width, 1)
            weight_piece = lax.dynamic_slice_in_dim(weight, start, feat_width, 0)
            partial_sum = jnp.dot(piece, weight_piece, preferred_element_type=jnp.float32)
            result.append(
                total
                + lax.optimization_barrier(partial_sum.astype(jnp.bfloat16)).astype(jnp.float32)
            )
        return tuple(result)

    starts = tuple(
        (
            jnp.zeros((source.shape[0], weight.shape[1]), jnp.float32)
            for source, weight in zip(sources, weights)
        )
    )
    return lax.fori_loop(0, n_row, add_block, starts)


def per_device(
    hidden,
    lengths,
    square_matrix_shards,
    channel_mix_shards,
    lowrank_down,
    lowrank_up,
    token_shift_weights,
    attention_coefficients,
    norm_parameters,
):
    n_row = lax.axis_size("row")
    n_col = lax.axis_size("col")
    row_lookup = lax.axis_index("row")
    column_lookup = lax.axis_index("col")
    square_low = square_matrix_shards.astype(jnp.bfloat16)
    mlp_low = channel_mix_shards.astype(jnp.bfloat16)
    relay_part = square_low[4:7]
    next_base = 0
    square = lax.all_to_all(relay_part, "col", split_axis=2, concat_axis=1, tiled=True)
    mlp_group = lax.all_gather(mlp_low, "col", axis=1, tiled=True)
    mlp_weights = lax.all_to_all(mlp_group, "row", split_axis=2, concat_axis=1, tiled=True)
    feature_row = hidden.shape[1]
    row_mix = lax.dynamic_slice_in_dim(
        token_shift_weights, row_lookup * feature_row, feature_row, 1
    )
    resid = hidden.astype(jnp.float32)
    first = normed(resid, norm_parameters[0], norm_parameters[1])
    time_group = lax.all_gather(square_low[0:4], "col", axis=1, tiled=True)
    time_weights = lax.all_to_all(time_group, "row", split_axis=2, concat_axis=1, tiled=True)
    full_features = lax.all_gather(first, "row", axis=1, tiled=True)
    shift_blends = [
        mixed(full_features, token_shift_weights[column_step]) for column_step in range(5)
    ]
    rows_mine = full_features.shape[0]
    shard_width = time_weights.shape[2]
    acceptance_gate_entries, key_vecs, value_vecs, decay_lowrank, rate_lowrank = block_products(
        shift_blends,
        [time_weights[0], time_weights[1], time_weights[2], lowrank_down[0], lowrank_down[1]],
        n_row,
    )
    head_local = lax.dynamic_slice_in_dim(
        attention_coefficients, row_lookup * shard_width, shard_width, 1
    )
    up_shard_local = lax.dynamic_slice_in_dim(lowrank_up, row_lookup * shard_width, shard_width, 2)
    prompt_count = rows_mine // LMAX
    prompt_lengths = lax.dynamic_slice_in_dim(
        lengths, column_lookup * prompt_count, prompt_count, 0
    )
    att, final_local = time_core(
        acceptance_gate_entries,
        key_vecs,
        value_vecs,
        decay_lowrank,
        rate_lowrank,
        head_local,
        up_shard_local,
        prompt_lengths,
    )
    partial_out = lax.dot_general(
        att, time_weights[3], (((1,), (1,)), ((), ())), preferred_element_type=jnp.float32
    )
    attn_out = lax.psum_scatter(
        partial_out.astype(jnp.bfloat16), "row", scatter_dimension=1, tiled=True
    ).astype(jnp.float32)
    states_all = lax.all_gather(final_local.astype(jnp.bfloat16), "col", axis=0, tiled=True).astype(
        final_local.dtype
    )
    states_mine = lax.all_to_all(
        states_all.astype(jnp.bfloat16), "row", split_axis=0, concat_axis=1, tiled=True
    ).astype(states_all.dtype)
    head_share = states_mine.shape[1] // n_col
    final_state = lax.dynamic_slice_in_dim(states_mine, column_lookup * head_share, head_share, 1)
    mid = (resid + attn_out).astype(jnp.bfloat16)
    mid_wide = mid.astype(jnp.float32)
    channel_in = mixed(normed(mid_wide, norm_parameters[2], norm_parameters[3]), row_mix[5])
    rows_next = channel_in.shape[0] * n_col // n_row
    full_rows = lax.all_gather(channel_in, "row", axis=1, tiled=True)
    pre_act = jnp.dot(full_rows, mlp_weights[0], preferred_element_type=jnp.float32)
    act = jnp.square(jax.nn.relu(pre_act)).astype(jnp.bfloat16)
    partial_mlp = lax.dot_general(
        act, mlp_weights[1], (((1,), (1,)), ((), ())), preferred_element_type=jnp.float32
    )
    channel_out = lax.psum_scatter(
        partial_mlp.astype(jnp.bfloat16), "row", scatter_dimension=1, tiled=True
    ).astype(jnp.float32)
    out_hidden = (mid_wide + channel_out).astype(jnp.bfloat16)
    third = normed(out_hidden.astype(jnp.float32), norm_parameters[4], norm_parameters[5])
    third_all = gather_cols(third)
    next_mixes = [mixed(third_all, row_mix[6 + column_step]) for column_step in range(3)]
    next_width = square.shape[2]

    def next_terms(start, count):
        parts = [
            jnp.dot(
                next_mixes[column_step],
                square[next_base + column_step],
                preferred_element_type=jnp.float32,
            )
            for column_step in range(3)
        ]
        return jnp.concatenate(parts, axis=1)

    next_summed = row_sums(next_terms, rows_next)
    next_rkv = jnp.stack(
        [
            next_summed[:, column_step * next_width : (column_step + 1) * next_width]
            for column_step in range(3)
        ]
    ).astype(jnp.bfloat16)
    return (out_hidden, next_rkv, final_state)


def solution(mesh):
    return jax.shard_map(
        per_device,
        mesh=mesh,
        in_specs=(
            P("col", "row"),
            P(),
            P(None, ("row", "col"), None),
            P(None, ("row", "col"), None),
            P(),
            P(),
            P(),
            P(),
            P(None, "row"),
        ),
        out_specs=(P("col", "row"), P(None, "row", "col"), P("row", "col", None)),
        check_vma=False,
    )
```

profile of v0, /device:TPU:12, one launch (start us, length us, event | category | flops | bytes accessed | tf_op | source)
XLA Modules:
  0.0 1280.8 jit_solution(6694006173465902055)
XLA Ops:
  11.3 13.0 %all-reduce.5 = (f32[1024]{0:T(1024)S(1)}, f32[1024]{0:T(1024)S(1)}) all-reduce(f32[1024]{0:T(1024)S(1)} %get-tuple-element.485, f32[1024]{0:T(1024)S(1)} %get-tuple-element.484), channel_id=1, replica_groups=mesh['row'=8,'col'=4] {'row'}, use_global_device_ids=true, to_apply=%region_3.0 | all-reduce | flops 2048 | bytes 16384 | tf_op jit(solution)/shard_map/psum | solution.py:24
  26.0 64.4 %all-gather.9.cloned.1.call-done = bf16[4,256,2048]{2,0,1:T(4,128)(2,1)} async-done(((bf16[4,64,2048]{2,0,1:T(4,128)(2,1)}), bf16[4,256,2048]{2,0,1:T(4,128)(2,1)}) %all-gather.9.cloned.1.call-update) | async-done | bytes 4194320 | tf_op jit(solution)/shard_map/all_gather | solution.py:228
  90.5 10.2 copy.281
  100.7 4.8 all-to-all-start
  105.5 6.8 copy.418
  120.4 36.2 %all-gather.7.cloned.1.call-done = bf16[1024,2048]{1,0:T(8,128)(2,1)} async-done(((bf16[1024,256]{1,0:T(8,128)(2,1)}), bf16[1024,2048]{1,0:T(8,128)(2,1)}) %all-gather.7.cloned.1.call-update) | async-done | bytes 4194320 | tf_op jit(solution)/shard_map/all_gather | solution.py:230
  156.6 3.2 slice.259
  159.8 4.3 concatenate.20
  164.2 12.8 fusion.64
  176.9 3.3 copy.282
  189.3 113.1 %while.38 = (s32[]{:T(128)}, f32[1024,256]{1,0:T(8,128)}, f32[1024,256]{1,0:T(8,128)}, f32[1024,256]{1,0:T(8,128)S(1)}, f32[1024,96]{0,1:T(8,128)}, /*index=5*/f...) while((s32[]{:T(128)}, f32[1024,256]{1,0:T(8,128)}, ...), condition=%wide.region_5.0_spmd.clone, body=%wide.region_4.0_spmd.clone.sunk | while | flops 507248640 | bytes 21239136 | solution.py:197
  192.8 2.9 select_add_fusion.9
  205.6 3.2 select_add_fusion.9
  219.9 3.2 select_add_fusion.9
  234.3 3.2 select_add_fusion.9
  248.6 3.2 select_add_fusion.9
  262.9 3.2 select_add_fusion.9
  277.3 3.2 select_add_fusion.9
  291.6 3.2 select_add_fusion.9
  302.3 2.9 copy.292
  305.3 3.1 stack.26
  308.4 2.6 copy.288
  310.9 3.1 reshape.355
  318.7 3.2 constant_dynamic-update-slice_fusion
  325.5 3.3 reshape.357
  331.6 3.6 multiply_dynamic-update-slice_fusion.4
  339.7 3.5 multiply_dynamic-update-slice_fusion.1
  343.2 3.5 multiply_dynamic-update-slice_fusion
  346.7 430.7 %while.39 = (s32[]{:T(128)}, f32[8,4,64,64]{3,2,1,0:T(8,128)S(1)}, f32[8,8,16,4,64]{4,3,2,1,0:T(4,128)}, f32[6,8,8,16,4,64]{5,4,3,2,1,0:T(4,128)}, s32[]{:T(128)...) while((s32[]{:T(128)}, f32[8,4,64,64]{3,2,1,0:T(8,128)S(1)}, ...), condition=%wide.region_9.10_spmd.clone, body=%wide.region_7.9_spmd.clone.sunk | while | flops 153119008 | bytes 10718541 | solution.py:153
  352.0 39.6 %custom-call.19 = f32[8,4,1,16,16]{3,4,2,1,0:T(8,128)S(1)} custom-call(f32[8,4,1,16,16]{4,3,2,1,0:T(8,128)S(1)} %fusion.209), custom_call_target="InvertDiagBlocksLowerTriangular" | custom-call | tf_op jit(solution)/shard_map/while/body/eval_jaxpr/jit(_solve_triangular)/vmap(vmap())/triangular_solve | solution.py:65
  405.8 39.6 %custom-call.19 = f32[8,4,1,16,16]{3,4,2,1,0:T(8,128)S(1)} custom-call(f32[8,4,1,16,16]{4,3,2,1,0:T(8,128)S(1)} %fusion.209), custom_call_target="InvertDiagBlocksLowerTriangular" | custom-call | tf_op jit(solution)/shard_map/while/body/eval_jaxpr/jit(_solve_triangular)/vmap(vmap())/triangular_solve | solution.py:65
  459.6 39.6 %custom-call.19 = f32[8,4,1,16,16]{3,4,2,1,0:T(8,128)S(1)} custom-call(f32[8,4,1,16,16]{4,3,2,1,0:T(8,128)S(1)} %fusion.209), custom_call_target="InvertDiagBlocksLowerTriangular" | custom-call | tf_op jit(solution)/shard_map/while/body/eval_jaxpr/jit(_solve_triangular)/vmap(vmap())/triangular_solve | solution.py:65
  513.5 39.6 %custom-call.19 = f32[8,4,1,16,16]{3,4,2,1,0:T(8,128)S(1)} custom-call(f32[8,4,1,16,16]{4,3,2,1,0:T(8,128)S(1)} %fusion.209), custom_call_target="InvertDiagBlocksLowerTriangular" | custom-call | tf_op jit(solution)/shard_map/while/body/eval_jaxpr/jit(_solve_triangular)/vmap(vmap())/triangular_solve | solution.py:65
  567.3 39.6 %custom-call.19 = f32[8,4,1,16,16]{3,4,2,1,0:T(8,128)S(1)} custom-call(f32[8,4,1,16,16]{4,3,2,1,0:T(8,128)S(1)} %fusion.209), custom_call_target="InvertDiagBlocksLowerTriangular" | custom-call | tf_op jit(solution)/shard_map/while/body/eval_jaxpr/jit(_solve_triangular)/vmap(vmap())/triangular_solve | solution.py:65
  621.1 39.6 %custom-call.19 = f32[8,4,1,16,16]{3,4,2,1,0:T(8,128)S(1)} custom-call(f32[8,4,1,16,16]{4,3,2,1,0:T(8,128)S(1)} %fusion.209), custom_call_target="InvertDiagBlocksLowerTriangular" | custom-call | tf_op jit(solution)/shard_map/while/body/eval_jaxpr/jit(_solve_triangular)/vmap(vmap())/triangular_solve | solution.py:65
  675.0 39.6 %custom-call.19 = f32[8,4,1,16,16]{3,4,2,1,0:T(8,128)S(1)} custom-call(f32[8,4,1,16,16]{4,3,2,1,0:T(8,128)S(1)} %fusion.209), custom_call_target="InvertDiagBlocksLowerTriangular" | custom-call | tf_op jit(solution)/shard_map/while/body/eval_jaxpr/jit(_solve_triangular)/vmap(vmap())/triangular_solve | solution.py:65
  728.8 39.6 %custom-call.19 = f32[8,4,1,16,16]{3,4,2,1,0:T(8,128)S(1)} custom-call(f32[8,4,1,16,16]{4,3,2,1,0:T(8,128)S(1)} %fusion.209), custom_call_target="InvertDiagBlocksLowerTriangular" | custom-call | tf_op jit(solution)/shard_map/while/body/eval_jaxpr/jit(_solve_triangular)/vmap(vmap())/triangular_solve | solution.py:65
  777.4 3.1 reshape.362
  780.7 5.5 fusion.104
  787.2 3.2 reshape.360
  790.4 7.5 multiply_reduce_fusion
  803.0 2.5 copy.293
  807.8 5.8 convolution_convert_fusion.8
  813.7 29.0 %copy.305 = bf16[2,256,8192]{1,0,2:T(2,128)(2,1)} copy(bf16[2,256,8192]{2,0,1:T(2,128)(2,1)} %all-gather.13.cloned.1.call-done) | data formatting | bytes 16777216 | tf_op jit(solution)/shard_map/all_gather | solution.py:220
  842.7 14.2 %all-to-all-start.1 = ((bf16[2,256,8192]{1,0,2:T(2,128)(2,1)}), bf16[2,256,8192]{1,0,2:T(2,128)(2,1)}, u32[]{:S(2)}, u32[]{:S(2)}) async-start(bf16[2,256,8192]{1,0,2:T(2,128)(2,1)} %copy.305), calls=%async_computation.2 | async-start | bytes 16777216 | tf_op jit(solution)/shard_map/all_to_all | solution.py:221
  856.9 61.9 %reduce-scatter.4.cloned.1.call-done = bf16[1024,256]{1,0:T(8,128)(2,1)} async-done(((bf16[1024,2048]{1,0:T(8,128)(2,1)}), bf16[1024,256]{1,0:T(8,128)(2,1)}) %reduce-scatter.4.cloned.1.call-update) | async-done | bytes 524304 | tf_op jit(solution)/shard_map/reduce_scatter | solution.py:262
  920.2 43.1 %all-reduce.4 = (f32[1024]{0:T(1024)S(1)}, f32[1024]{0:T(1024)S(1)}) all-reduce(f32[1024]{0:T(1024)S(1)} %get-tuple-element.483, f32[1024]{0:T(1024)S(1)} %get-tuple-element.482), channel_id=1, replica_groups=mesh['row'=8,'col'=4] {'row'}, use_global_device_ids=true, to_apply=%region_17.18 | all-reduce | flops 2048 | bytes 16384 | tf_op jit(solution)/shard_map/psum | solution.py:24
  965.0 7.7 copy.306
  972.7 6.4 fusion.107
  979.1 6.4 copy.307
  985.5 6.5 copy.308
  992.0 9.9 all-gather.11.cloned.1.call-done
  1001.9 14.5 %convolution_convert_fusion.9 = bf16[1024,2048]{1,0:T(8,128)(2,1)} fusion(bf16[2048,1024]{1,0:T(8,128)(2,1)} %bitcast.305, bf16[1024,2048]{1,0:T(8,128)(2,1)} %all-gather.11.cloned.1.call-done, bf16[2048,1024]{1,0:T(8,128)(2,1)} %bitcast.304), kind=kOutput, calls=%fused_computation.118 | convolution fusion | flops 8595177472 | bytes 16777216 | tf_op jit(solution)/shard_map/dot_general | solution.py:280
  1016.4 52.1 %reduce-scatter.6.cloned.1.call-done = bf16[1024,256]{1,0:T(8,128)(2,1)} async-done(((bf16[1024,2048]{1,0:T(8,128)(2,1)}), bf16[1024,256]{1,0:T(8,128)(2,1)}) %reduce-scatter.6.cloned.1.call-update) | async-done | bytes 524304 | tf_op jit(solution)/shard_map/reduce_scatter | solution.py:283
  1069.9 13.0 %all-reduce.3 = (f32[1024]{0:T(1024)S(1)}, f32[1024]{0:T(1024)S(1)}) all-reduce(f32[1024]{0:T(1024)S(1)} %get-tuple-element.481, f32[1024]{0:T(1024)S(1)} %get-tuple-element.480), channel_id=1, replica_groups=mesh['row'=8,'col'=4] {'row'}, use_global_device_ids=true, to_apply=%region_22.23 | all-reduce | flops 2048 | bytes 16384 | tf_op jit(solution)/shard_map/psum | solution.py:24
  1086.3 2.7 copy.309
  1089.1 3.3 reshape.384
  1092.3 42.9 %all_to_all.54 = bf16[4,2,49152]{2,1,0:T(2,128)(2,1)S(1)} all-to-all(bf16[4,2,49152]{2,1,0:T(2,128)(2,1)S(1)} %reshape.384), channel_id=1, replica_groups=mesh['row'=8,'col'=4] {'col'}, dimensions={0} | all-to-all | bytes 1572864 | tf_op jit(solution)/shard_map/all_to_all | solution.py:219
  1135.3 2.5 reshape.385
  1137.8 3.2 copy.322
  1152.8 17.8 %pad_maximum_fusion = bf16[4096,1536]{0,1:T(8,128)(2,1)} fusion(bf16[4096,512]{0,1:T(8,128)(2,1)S(1)} %convolution_convert_fusion.5, bf16[4096,512]{0,1:T(8,128)(2,1)S(1)} %convolution_convert_fusion.6, bf16[4096,512]{0,1:T(8,128)(2,1)S(1)} %convolution_convert_fusion.7), kind=kLoop, calls=%fused_computation.95 | loop fusion | flops 37748736 | bytes 25165824 | tf_op jit(solution)/shard_map/concatenate | solution.py:301
  1170.6 5.0 all-gather.17.cloned.1.call-done
  1175.6 18.1 %all_to_all.55 = bf16[32,4,4096]{2,1,0:T(4,128)(2,1)S(1)} all-to-all(bf16[32,4,4096]{2,1,0:T(4,128)(2,1)} %all-gather.17.cloned.1.call-done), channel_id=1, replica_groups=mesh['row'=8,'col'=4] {'row'}, dimensions={0} | all-to-all | bytes 2097152 | tf_op jit(solution)/shard_map/all_to_all | solution.py:268
  1196.6 74.3 %reduce-scatter.8.cloned.1.call-done = bf16[512,1536]{0,1:T(8,128)(2,1)} async-done(((bf16[4096,1536]{0,1:T(8,128)(2,1)}), bf16[512,1536]{0,1:T(8,128)(2,1)}) %reduce-scatter.8.cloned.1.call-update) | async-done | bytes 1572880 | tf_op jit(solution)/shard_map/reduce_scatter | solution.py:36
  (459 shorter events, 272.6 us)
Async XLA Ops:
  7.2 316.9 %copy-start = (bf16[2,96,2048]{2,1,0:T(8,128)(2,1)S(1)}, bf16[2,96,2048]{2,1,0:T(8,128)(2,1)}, u32[]{:S(2)}) copy-start(bf16[2,96,2048]{2,1,0:T(8,128)(2,1)} %param.18) | copy-start | bytes 2359300
  7.2 3.8 copy-start.17
  7.2 17.1 %copy-start.20 = (f32[6,256]{1,0:T(8,128)S(1)}, f32[6,256]{1,0:T(8,128)}, u32[]{:S(2)}) copy-start(f32[6,256]{1,0:T(8,128)} %param.21) | copy-start | bytes 18436
  7.2 83.3 %all-gather.9.cloned.1.call-start = ((), (), s32[]{:S(2)}) async-start(), calls=%async_computation.8 | async-start | bytes 5242880 | tf_op jit(solution)/shard_map/all_gather | solution.py:228
  10.9 145.7 %all-gather.7.cloned.1.call-start = ((), (), s32[]{:S(2)}) async-start(), calls=%async_computation.7 | async-start | bytes 4718592 | tf_op jit(solution)/shard_map/all_gather | solution.py:230
  100.7 76.2 %all-to-all-start = ((bf16[4,256,2048]{1,0,2:T(4,128)(2,1)}), bf16[4,256,2048]{1,0,2:T(4,128)(2,1)}, u32[]{:S(2)}, u32[]{:S(2)}) async-start(bf16[4,256,2048]{1,0,2:T(4,128)(2,1)} %copy.281), calls=%async_computation | async-start | bytes 8388608 | tf_op jit(solution)/shard_map/all_to_all | solution.py:229
  105.5 708.2 %all-gather.13.cloned.1.call-start = ((), (), s32[]{:S(2)}) async-start(), calls=%async_computation.11 | async-start | bytes 10485760 | tf_op jit(solution)/shard_map/all_gather | solution.py:220
  112.3 6.8 copy-start.26
  112.3 806.5 %reduce-scatter.4.cloned.1.call-start = ((), (), s32[]{:S(2)}) async-start(), calls=%async_computation.9 | async-start | bytes 4718592 | tf_op jit(solution)/shard_map/reduce_scatter | solution.py:262
  159.8 4.3 copy-start.4
  192.8 5.6 copy-start.7
  192.8 5.6 copy-start.10
  198.6 0.8 copy-start.8
  198.6 0.9 copy-start.11
  205.6 5.9 copy-start.7
  205.6 5.9 copy-start.10
  211.7 0.8 copy-start.8
  211.8 0.9 copy-start.11
  219.9 5.9 copy-start.7
  219.9 5.9 copy-start.10
  226.1 0.8 copy-start.8
  226.1 0.9 copy-start.11
  234.3 5.9 copy-start.7
  234.3 5.9 copy-start.10
  240.4 0.8 copy-start.8
  240.4 0.9 copy-start.11
  248.6 5.9 copy-start.7
  248.6 5.9 copy-start.10
  254.8 0.8 copy-start.8
  254.8 0.9 copy-start.11
  262.9 5.9 copy-start.7
  262.9 5.9 copy-start.10
  269.1 0.8 copy-start.8
  269.1 0.9 copy-start.11
  277.3 5.9 copy-start.7
  277.3 5.9 copy-start.10
  283.4 0.9 copy-start.11
  291.6 5.9 copy-start.7
  291.6 5.9 copy-start.10
  297.7 0.9 copy-start.11
  302.3 19.5 %copy-start.2 = (f32[1024,256]{1,0:T(8,128)}, f32[1024,256]{1,0:T(8,128)S(1)}, u32[]{:S(2)}) copy-start(f32[1024,256]{1,0:T(8,128)S(1)} %get-tuple-element.348) | copy-start | bytes 3145732
  317.6 6.5 copy-start.9
  324.1 4.7 copy-start.12
  331.6 3.6 copy-start.13
  331.6 5.8 copy-start.14
  335.2 4.6 copy-start.5
  335.2 4.6 copy-start.16
  337.4 5.8 copy-start.15
  801.8 6.0 copy-start.3
  842.7 76.1 %copy-start.18 = (bf16[1024,256]{1,0:T(8,128)(2,1)S(1)}, bf16[1024,256]{1,0:T(8,128)(2,1)}, u32[]{:S(2)}) copy-start(bf16[1024,256]{1,0:T(8,128)(2,1)} %param.13) | copy-start | bytes 1572868
  842.7 122.3 %all-to-all-start.1 = ((bf16[2,256,8192]{1,0,2:T(2,128)(2,1)}), bf16[2,256,8192]{1,0,2:T(2,128)(2,1)}, u32[]{:S(2)}, u32[]{:S(2)}) async-start(bf16[2,256,8192]{1,0,2:T(2,128)(2,1)} %copy.305), calls=%async_computation.2 | async-start | bytes 16777216 | tf_op jit(solution)/shard_map/all_to_all | solution.py:221
  856.9 145.0 %all-gather.11.cloned.1.call-start = ((), (), s32[]{:S(2)}) async-start(), calls=%async_computation.10 | async-start | bytes 4718592 | tf_op jit(solution)/shard_map/all_gather | solution.py:277
  964.9 103.5 %reduce-scatter.6.cloned.1.call-start = ((), (), s32[]{:S(2)}) async-start(), calls=%async_computation.12 | async-start | bytes 4718592 | tf_op jit(solution)/shard_map/reduce_scatter | solution.py:283
  1016.3 66.6 %copy-start.24 = (f32[1,256]{1,0:T(1,128)S(1)}, f32[1,256]{1,0:T(1,128)}, u32[]{:S(2)}) copy-start(f32[1,256]{1,0:T(1,128)} %get-tuple-element.585) | copy-start | bytes 3076
  1016.3 66.6 %copy-start.25 = (f32[1,256]{1,0:T(1,128)S(1)}, f32[1,256]{1,0:T(1,128)}, u32[]{:S(2)}) copy-start(f32[1,256]{1,0:T(1,128)} %get-tuple-element.590) | copy-start | bytes 3076
  1016.3 127.1 %all-gather.15.cloned.1.call-start = ((), (), s32[]{:S(2)}) async-start(), calls=%async_computation.13 | async-start | bytes 2621440 | tf_op jit(solution)/shard_map/all_gather | solution.py:32
  1069.9 14.3 %copy-start.19 = (bf16[1024,256]{1,0:T(8,128)(2,1)}, bf16[1024,256]{1,0:T(8,128)(2,1)S(1)}, u32[]{:S(2)}) copy-start(bf16[1024,256]{1,0:T(8,128)(2,1)S(1)} %get-tuple-element.534) | copy-start | bytes 1572868
  1084.1 91.5 %all-gather.17.cloned.1.call-start = ((), (), s32[]{:S(2)}) async-start(), calls=%async_computation.15 | async-start | bytes 1310720 | tf_op jit(solution)/shard_map/all_gather | solution.py:265
  1142.6 128.2 %reduce-scatter.8.cloned.1.call-start = ((), (), s32[]{:S(2)}) async-start(), calls=%async_computation.14 | async-start | bytes 14155776 | tf_op jit(solution)/shard_map/reduce_scatter | solution.py:36
  1145.5 1.6 copy-start.6
  1145.5 1.6 copy-start.21
  1145.5 1.6 copy-start.22
  1145.5 1.6 copy-start.23
  1195.5 78.6 %copy-start.1 = (bf16[2,96,2048]{2,1,0:T(8,128)(2,1)S(1)}, bf16[2,96,2048]{2,1,0:T(8,128)(2,1)}, u32[]{:S(2)}) copy-start(bf16[2,96,2048]{2,1,0:T(8,128)(2,1)} %param.18) | copy-start | bytes 2359300
  (2 other events, 1.5 us)
Sparse Core Ops, SparseCore 0:
  11.0 79.4 all-gather.8
  92.9 63.6 all-gather.6
  158.2 157.6 all-gather.12
  813.8 104.9 reduce-scatter.3
  965.1 36.7 all-gather.10
  1016.5 51.9 reduce-scatter.5
  1084.2 59.1 all-gather.14
  1145.5 30.0 all-gather.16
  1179.1 91.7 reduce-scatter.7
where the time goes:
time: 1290 us; the launch traced here: 1280 us
  other arithmetic  433 us (34%)
  waiting for transfers between devices  305 us (24%)
  local copies, waits for them, and re-layouts  199 us (15%)
  matrix products  178 us (14%)
  blocking collectives  130 us (10%)
  starting transfers between devices  19.3 us (1%)
  between operations  14.6 us (1%)
    another operation x24, other arithmetic, span_step(): jax.scipy.linalg.solve_triangular(system, rhs_side, lower=True, unit_diag...  317 us
    reduce_scatter x1, waiting for transfers between devices, row_sums(): lax.psum_scatter(term_fn(jnp.int32(0), rows * lax.axis_size('row')).astyp...  74.3 us
    psum x3, blocking collectives, normed(): lax.psum((jnp.sum(source, axis=-1), jnp.sum(source * source, axis=-1)), '...  69 us
    all_gather x1, waiting for transfers between devices, per_device(): time_group = lax.all_gather(square_low[0:4], 'col', axis=1, tiled=True)  64.4 us
    reduce_scatter x1, waiting for transfers between devices, per_device(): lax.psum_scatter(partial_out.astype(jnp.bfloat16), 'row', scatter_dimensi...  61.9 us
    dot_general x40, matrix products, add_block(): jnp.dot(piece, weight_piece, preferred_element_type=jnp.float32)  60.7 us
    reduce_scatter x1, waiting for transfers between devices, per_device(): lax.psum_scatter(partial_mlp.astype(jnp.bfloat16), 'row', scatter_dimensi...  52.1 us
    add x24, other arithmetic, add_block(): total + lax.optimization_barrier(partial_sum.astype(jnp.bfloat16)).astype...  44.7 us
  transfers between devices with their start and end apart: 11, of which 8 were waited for; matrix products, arithmetic and copies ran while one was open for 61% of the time, Pallas kernels for 0%

commit v1 on v0

v1 whole, which is shorter than its diff:
```python
import functools

import jax
import jax.numpy as jnp
from jax import lax
from jax.experimental import pallas as pl
from jax.experimental.pallas import tpu as pltpu
from jax.sharding import PartitionSpec as P

LMAX = 128
HEAD = 64
F32 = jnp.float32
BF16 = jnp.bfloat16


def bdot(a, b, ca=1, cb=0):
    return lax.dot_general(
        a.astype(BF16), b.astype(BF16), (((ca,), (cb,)), ((), ())), preferred_element_type=F32
    )


def halves(x):
    top = x.astype(BF16)
    return top, (x - top.astype(F32)).astype(BF16)


def dot3(a, b, ca=1, cb=0):
    ah, al = halves(a)
    bh, bl = halves(b)
    return bdot(ah, bh, ca, cb) + (bdot(ah, bl, ca, cb) + bdot(al, bh, ca, cb))


def head_sums(x, same):
    top, low = halves(x)
    return bdot(top, same) + bdot(low, same)


def time_kernel(nb, per, lens, *refs):
    xg = refs[:nb]
    gb, shift, w, ld, lu, co, wo, out_ref, state_ref, mixes = refs[nb:]
    rows = per * LMAX
    fw = xg[0].shape[1]
    width = nb * fw
    hc = w.shape[2]
    blocks = [x[...].astype(F32) for x in xg]
    total = sum(jnp.sum(b, axis=1, keepdims=True) for b in blocks)
    square = sum(jnp.sum(b * b, axis=1, keepdims=True) for b in blocks)
    center = total / width
    scale = lax.rsqrt(square / width - center * center + 1e-05)
    first_row = lax.broadcasted_iota(jnp.int32, (rows, fw), 0) % LMAX == 0
    for i in range(nb):
        z = (xg[i][...].astype(F32) - center) * scale * gb[i : i + 1] + gb[nb + i : nb + i + 1]
        z = z.astype(BF16).astype(F32)
        step = jnp.where(first_row, 0.0, pltpu.roll(z, 1, 0)) - z
        for j in range(5):
            mixes[j, :, i * fw : (i + 1) * fw] = (z + step * shift[j * nb + i : j * nb + i + 1]).astype(BF16)
    r = bdot(mixes[0], w[0])
    k = bdot(mixes[1], w[1])
    v = bdot(mixes[2], w[2])
    dl = bdot(mixes[3], ld[0])
    al = bdot(mixes[4], ld[1])
    logd = -0.606531 * jax.nn.sigmoid(co[0:1] + bdot(jnp.tanh(dl), lu[0]))
    rate = jax.nn.sigmoid(co[1:2] + bdot(al, lu[1]))
    lane_a = lax.broadcasted_iota(jnp.int32, (hc, hc), 0) // HEAD
    lane_b = lax.broadcasted_iota(jnp.int32, (hc, hc), 1) // HEAD
    same = (lane_a == lane_b).astype(BF16)
    kappa = k * co[2:3]
    kappa = kappa * lax.rsqrt(head_sums(kappa * kappa, same) + 1e-05)
    t_of = lax.broadcasted_iota(jnp.int32, (LMAX, LMAX), 0)
    u_of = lax.broadcasted_iota(jnp.int32, (LMAX, LMAX), 1)
    upto = u_of <= t_of
    before = u_of < t_of
    lower = upto.astype(BF16)
    low_lane = u_of < HEAD
    side = jnp.concatenate([low_lane, low_lane], axis=0)
    levels = [((t_of >> n) == (u_of >> n) + 1) & (((t_of >> n) & 1) == 1) for n in range(7)]
    eye = (t_of == u_of).astype(F32)
    place = lax.broadcasted_iota(jnp.int32, (LMAX, hc), 0)
    chains = []
    keep = []
    for p in range(per):
        at = slice(p * LMAX, (p + 1) * LMAX)
        live = (place < lens[pl.program_id(0) * per + p]).astype(F32)
        rp, kp, vp = r[at], k[at] * live, v[at] * live
        dp = logd[at] * live
        kh = kappa[at] * live
        wr = kh * rate[at]
        d1 = dp.astype(BF16)
        d2, d3 = halves(dp - d1.astype(F32))
        cum = bdot(lower, d1) + (bdot(lower, d2) + bdot(lower, d3))
        last = cum[LMAX - 1 : LMAX]
        mid = 0.5 * last
        grow = jnp.exp(mid - cum)
        tail = jnp.exp(last - mid)
        pull = -kh * jnp.exp(cum - dp - mid)
        read = rp * jnp.exp(cum - mid)
        wb = wr * grow
        kb = kp * grow
        keep.append((live, head_sums(rp * kp * co[3:4], same) * vp))
        for q in range(hc // 128):
            ln = slice(q * 128, (q + 1) * 128)
            right = jnp.concatenate([wb[:, ln], kb[:, ln]], axis=0)
            left = jnp.concatenate([pull[:, ln], read[:, ln]], axis=0)
            pair = []
            for h in range(2):
                g = bdot(jnp.where(side == (h == 0), left, 0.0), right, 1, 1)
                pair.append(
                    (
                        jnp.where(before, g[:LMAX, :LMAX], 0.0),
                        jnp.where(before, g[:LMAX, LMAX:], 0.0),
                        jnp.where(upto, g[LMAX:, :LMAX], 0.0),
                        jnp.where(upto, g[LMAX:, LMAX:], 0.0),
                    )
                )
            chains.append((p, q, pair, vp[:, ln], wb[:, ln] * tail[:, ln], kb[:, ln] * tail[:, ln]))
    strict = [c[2][h][0] for c in chains for h in range(2)]
    inverse = [eye + jnp.where(levels[0], a, 0.0) for a in strict]
    for n in range(1, 7):
        inner = [dot3(jnp.where(levels[n], a, 0.0), t) for a, t in zip(strict, inverse)]
        inverse = [t + dot3(t, m) for t, m in zip(inverse, inner)]
    outs = {}
    for i, (p, q, pair, vq, wt, kt) in enumerate(chains):
        us, ys = [], []
        for h in range(2):
            _, b, rw, rk = pair[h]
            u = dot3(inverse[2 * i + h], bdot(b, vq))
            us.append(u)
            ys.append(bdot(jnp.concatenate([rw, rk], axis=1), jnp.concatenate([u, vq], axis=0)))
        u = jnp.where(low_lane, us[0], us[1])
        outs[p, q] = jnp.where(low_lane, ys[0], ys[1])
        final = bdot(jnp.concatenate([u, vq], axis=0), jnp.concatenate([wt, kt], axis=0), 0, 0)
        state_ref[p, 2 * q] = final[:HEAD, :HEAD].astype(BF16)
        state_ref[p, 2 * q + 1] = final[HEAD:, HEAD:].astype(BF16)
    atts = []
    for p in range(per):
        live, extra = keep[p]
        y = jnp.concatenate([outs[p, q] for q in range(hc // 128)], axis=1)
        y = (y + extra) * live
        y = y - head_sums(y, same) / HEAD
        spread = head_sums(y * y, same) / HEAD
        atts.append((y * lax.rsqrt(spread + 0.00064) * co[4:5] + co[5:6]).astype(BF16))
    out_ref[...] = bdot(jnp.concatenate(atts, axis=0), wo[...], 1, 1).astype(BF16)


def time_mix(lens, xg, gb, shift, w, ld, lu, co, wo, per):
    nb = len(xg)
    tokens, fw = xg[0].shape
    prompts = tokens // LMAX
    hc = w.shape[2]

    def full(a):
        return pl.BlockSpec(a.shape, lambda i: (0,) * a.ndim)

    rest = (gb, shift, w, ld, lu, co, wo)
    return pl.pallas_call(
        functools.partial(time_kernel, nb, per),
        grid=(prompts // per,),
        in_specs=[pl.BlockSpec(memory_space=pltpu.SMEM)]
        + [pl.BlockSpec((per * LMAX, fw), lambda i: (i, 0))] * nb
        + [full(a) for a in rest],
        out_specs=[
            pl.BlockSpec((per * LMAX, wo.shape[0]), lambda i: (i, 0)),
            pl.BlockSpec((per, hc // HEAD, HEAD, HEAD), lambda i: (i, 0, 0, 0)),
        ],
        out_shape=[
            jax.ShapeDtypeStruct((tokens, wo.shape[0]), BF16),
            jax.ShapeDtypeStruct((prompts, hc // HEAD, HEAD, HEAD), BF16),
        ],
        scratch_shapes=[pltpu.VMEM((5, per * LMAX, nb * fw), BF16)],
        compiler_params=pltpu.CompilerParams(vmem_limit_bytes=50 * 2**20),
        cost_estimate=pl.CostEstimate(flops=40 * 10**9, bytes_accessed=2**24, transcendentals=0),
    )(lens, *xg, *rest)


def norm_of(z, gain, bias):
    width = z.shape[1]
    center = jnp.sum(z, axis=1, keepdims=True) / width
    second = jnp.sum(z * z, axis=1, keepdims=True) / width
    return ((z - center) * lax.rsqrt(second - center * center + 1e-05) * gain + bias).astype(BF16)


def next_kernel(nb, x, gate, w, out):
    z = x[...].astype(F32)
    rows = z.shape[0]
    first_row = lax.broadcasted_iota(jnp.int32, z.shape, 0) % LMAX == 0
    step = jnp.where(first_row, 0.0, pltpu.roll(z, 1, 0)) - z
    for m in range(3):
        mixed = (z + step * gate[m : m + 1]).astype(BF16)
        fw = w.shape[2]
        total = jnp.zeros((rows, w.shape[3]), F32)
        for i in range(nb):
            total += bdot(mixed[:, i * fw : (i + 1) * fw], w[i, m])
        out[m] = total.astype(BF16)


def next_products(x, gate, w):
    tokens, width = x.shape
    nb, _, fw, cols = w.shape
    return pl.pallas_call(
        functools.partial(next_kernel, nb),
        grid=(tokens // LMAX,),
        in_specs=[
            pl.BlockSpec((LMAX, width), lambda i: (i, 0)),
            pl.BlockSpec(gate.shape, lambda i: (0, 0)),
            pl.BlockSpec(w.shape, lambda i: (0, 0, 0, 0)),
        ],
        out_specs=pl.BlockSpec((3, LMAX, cols), lambda i: (0, i, 0)),
        out_shape=jax.ShapeDtypeStruct((3, tokens, cols), BF16),
        compiler_params=pltpu.CompilerParams(vmem_limit_bytes=50 * 2**20),
        cost_estimate=pl.CostEstimate(flops=6 * 10**9, bytes_accessed=2**24, transcendentals=0),
    )(x, gate, w)


def per_device(
    hidden,
    lengths,
    square_matrix_shards,
    channel_mix_shards,
    lowrank_down,
    lowrank_up,
    token_shift_weights,
    attention_coefficients,
    norm_parameters,
):
    n_row = lax.axis_size("row")
    n_col = lax.axis_size("col")
    row = lax.axis_index("row")
    col = lax.axis_index("col")
    chips = n_row // 2
    tokens, fw = hidden.shape
    width = token_shift_weights.shape[1]
    chunk = tokens // n_row
    deep = square_matrix_shards.shape[1]
    hc = width // n_row
    by_row = row ^ jnp.arange(n_row)

    def to_row(x, k):
        return lax.ppermute(x, "row", [(i, i ^ k) for i in range(n_row)])

    def chunk_of(r):
        return (r % 2) * chips + r // 2

    def row_of(n):
        return (n % chips) * 2 + n // chips

    def gather_row(x):
        mine = [x] + [to_row(x, 2 * k) for k in range(1, chips)]
        return [piece for m in mine for piece in (m, to_row(m, 1))]

    def spread_row(blocks):
        return [lax.dynamic_index_in_dim(blocks, row ^ k, 0, keepdims=False) for k in range(n_row)]

    def exchange_row(blocks):
        sent = spread_row(blocks)
        return [sent[0]] + [to_row(sent[k], k) for k in range(1, n_row)]

    def sum_row(blocks):
        other = to_row(blocks[1::2], 1)
        near = (blocks[0::2].astype(F32) + other.astype(F32)).astype(BF16)
        total = near[0].astype(F32)
        for k in range(1, chips):
            total = total + to_row(near[k], 2 * k).astype(F32)
        return total

    xg = gather_row(hidden)
    norms = lax.all_gather(norm_parameters, "row", axis=0, tiled=False)
    square_low = square_matrix_shards.astype(BF16)
    early = square_low[0:4].reshape(4, deep, n_row, hc).transpose(2, 0, 1, 3).reshape(n_row, 4 * deep, hc)
    early = jnp.concatenate(exchange_row(early), axis=0)
    early = lax.all_gather(early, "col", axis=0, tiled=True)
    early = early.reshape(n_col, n_row, 4, deep, hc)
    w_in = early[:, :, 0:3].transpose(2, 1, 0, 3, 4).reshape(3, width, hc)
    w_out = jnp.take(early[:, :, 3], by_row, axis=1).transpose(1, 0, 2, 3).reshape(width, hc)
    ff = channel_mix_shards.shape[2] // n_row
    late = channel_mix_shards.astype(BF16).reshape(2, deep, n_row, ff).transpose(2, 0, 1, 3)
    late = jnp.stack(exchange_row(late))
    late = jnp.take(late, by_row, axis=0).reshape(n_row * 2 * deep, ff)
    late = lax.all_gather(late, "col", axis=0, tiled=True).reshape(n_col, n_row, 2, deep, ff)
    late = late.transpose(2, 1, 0, 3, 4).reshape(2, width, ff)
    cols = width // n_col
    last = square_low[4:7].reshape(3, deep, n_col, cols).transpose(2, 0, 1, 3)
    sent = [lax.dynamic_index_in_dim(last, col ^ k, 0, keepdims=False) for k in range(n_col)]
    got = [sent[0]] + [
        lax.ppermute(sent[k], "col", [(i, i ^ k) for i in range(n_col)]) for k in range(1, n_col)
    ]
    last = jnp.take(jnp.stack(got), col ^ jnp.arange(n_col), axis=0)
    last = last.transpose(1, 0, 2, 3).reshape(3 * n_col * deep, cols)
    last = lax.all_gather(last, "row", axis=0, tiled=True).reshape(n_row, 3, n_col * deep, cols)

    prompts = tokens // LMAX
    lens = lax.dynamic_slice_in_dim(lengths, col * prompts, prompts, 0)
    gb = jnp.take(norms[:, 0:2], by_row, axis=0).transpose(1, 0, 2).reshape(2 * n_row, fw)
    shift = jnp.take(token_shift_weights[0:5].reshape(5, n_row, fw), by_row, axis=1).reshape(5 * n_row, fw)
    down = jnp.take(lowrank_down.reshape(2, n_row, fw, -1), by_row, axis=1).reshape(lowrank_down.shape)
    up = lax.dynamic_slice_in_dim(lowrank_up, row * hc, hc, 2)
    co = lax.dynamic_slice_in_dim(attention_coefficients, row * hc, hc, 1)
    partial, states = time_mix(lens, xg, gb, shift, w_in, down, up, co, w_out, 2)

    half = prompts // 2
    share = n_row // n_col
    states = states.reshape(2, half, states.shape[1], HEAD, HEAD)
    moved = []
    for j in range(2):
        pairs = []
        for r in range(n_row):
            for c in range(n_col):
                h = (r % 2) ^ j
                pairs.append((r * n_col + c, (2 * c + h) * n_col + r // share))
        piece = lax.dynamic_index_in_dim(states, (row % 2) ^ j, 0, keepdims=False)
        moved.append(lax.ppermute(piece, ("row", "col"), pairs))
    moved = jnp.take(jnp.stack(moved), (row % 2) ^ jnp.arange(2), axis=0)
    final_state = moved.transpose(1, 0, 2, 3, 4).reshape(half, -1, HEAD * HEAD).astype(F32)

    here = chunk_of(row) * chunk
    parts = jnp.take(partial.reshape(n_row, chunk, width), chunk_of(by_row), axis=0)
    attn = sum_row(parts)
    own = jnp.stack([lax.dynamic_slice_in_dim(x, here, chunk, 0) for x in xg])
    own = jnp.take(own, by_row, axis=0).transpose(1, 0, 2).reshape(chunk, width)
    mid = (own.astype(F32) + attn).astype(BF16).astype(F32)
    gains = norms.transpose(1, 0, 2).reshape(-1, width)
    second = norm_of(mid, gains[2], gains[3]).astype(F32)
    edge = jnp.zeros_like(second[:1])
    if chunk % LMAX:
        pairs = [(row_of(n), row_of(n + 1)) for n in range(n_row - 1)]
        edge = lax.ppermute(second[-1:].astype(BF16), "row", pairs).astype(F32)
        edge = jnp.where(here % LMAX == 0, 0.0, edge)
    moved_on = jnp.concatenate([edge, second[:-1]], axis=0)
    channel_in = (second + (moved_on - second) * token_shift_weights[5]).astype(BF16)
    rows_in = jnp.concatenate(gather_row(channel_in), axis=0)
    pre = jnp.dot(rows_in, late[0], preferred_element_type=F32)
    act = jnp.square(jax.nn.relu(pre)).astype(BF16)
    mlp = lax.dot_general(act, late[1], (((1,), (1,)), ((), ())), preferred_element_type=F32)
    channel_out = sum_row(mlp.astype(BF16).reshape(n_row, chunk, width))
    out_own = (mid + channel_out).astype(BF16)
    pieces = exchange_row(out_own.reshape(chunk, n_row, fw).transpose(1, 0, 2))
    out_hidden = jnp.take(jnp.stack(pieces), row ^ row_of(jnp.arange(n_row)), axis=0).reshape(tokens, fw)

    third = norm_of(out_own.astype(F32), gains[4], gains[5])
    arrived = []
    for j in range(n_col):
        pairs = []
        for r in range(n_row):
            for c in range(n_col):
                pairs.append((r * n_col + c, (2 * c + r % 2) * n_col + ((r // 2) ^ j)))
        arrived.append(lax.ppermute(third, ("row", "col"), pairs))
    third_all = jnp.take(jnp.stack(arrived), col ^ jnp.arange(n_col), axis=0).reshape(-1, width)
    next_rkv = next_products(third_all, token_shift_weights[6:9], last)
    return (out_hidden, next_rkv, final_state)


def solution(mesh):
    return jax.shard_map(
        per_device,
        mesh=mesh,
        in_specs=(
            P("col", "row"),
            P(),
            P(None, ("row", "col"), None),
            P(None, ("row", "col"), None),
            P(),
            P(),
            P(),
            P(),
            P(None, "row"),
        ),
        out_specs=(P("col", "row"), P(None, "row", "col"), P("row", "col", None)),
        check_vma=False,
    )
```

time: 1290 us -> 484 us (0.38)
  the two profiles are of different devices: /device:TPU:12 before, /device:TPU:0 now
where the time goes in v1:
time: 484 us; the launch traced here: 475 us
  waiting for transfers between devices  133 us (27%)
  local copies, waits for them, and re-layouts  125 us (26%)
  starting transfers between devices  94.5 us (20%)
  Pallas kernels  48.5 us (10%)
  other arithmetic  35.8 us (7%)
  between operations  15.1 us (3%)
  matrix products  14.4 us (3%)
  blocking collectives  9.29 us (2%)
    ppermute x43, waiting for transfers between devices, to_row(): return lax.ppermute(x, 'row', [(i, i ^ k) for i in range(n_row)])  111 us
    ppermute x43, starting transfers between devices, to_row(): return lax.ppermute(x, 'row', [(i, i ^ k) for i in range(n_row)])  62.4 us
    unnamed x88, local copies, waits for them, and re-layouts  45.1 us
    pallas_call x1, Pallas kernels, time_mix(): pl.pallas_call(functools.partial(time_kernel, nb, per), grid=(prompts //...  40.9 us
    ppermute x4, starting transfers between devices, per_device(): arrived.append(lax.ppermute(third, ('row', 'col'), pairs))  26.3 us
    ppermute x3, waiting for transfers between devices, per_device(): lax.ppermute(sent[k], 'col', [(i, i ^ k) for i in range(n_col)])  22.1 us
    dot_general x1, matrix products, per_device(): lax.dot_general(act, late[1], (((1,), (1,)), ((), ())), preferred_element...  14.4 us
    another operation x3, local copies, waits for them, and re-layouts  11.4 us
  transfers between devices with their start and end apart: 55, of which 21 were waited for; matrix products, arithmetic and copies ran while one was open for 35% of the time, Pallas kernels for 9%

profile of v1, /device:TPU:0, one launch (start us, length us, event | category | flops | bytes accessed | tf_op | source)
XLA Modules:
  0.0 475.2 jit_solution(2241810476869331949)
XLA Ops:
  7.3 2.4 convert_element_type.105
  12.4 2.5 collective-permute-start.8
  16.8 2.6 collective-permute-start.12
  24.1 4.5 collective-permute-done.11
  34.3 2.4 convert_element_type.119
  38.1 5.5 %constant_dynamic-slice_fusion.12 = (bf16[2,64,1,1024]{3,2,1,0:T(2,128)(2,1)S(1)}, bf16[2,64,1,1024]{3,2,1,0:T(2,128)(2,1)S(1)}, bf16[2,64,1,1024]{3,2,1,0:T(2,1...) fusion(bf16[2,64,8,1024]{3,2,1,0:T(8,128)(2,1)S(1)} %bitcast.24, ...), kind=kLoop, calls=%fused_computation.150 | loop fusion | bytes 4194336 | tf_op jit(solution)/shard_map/dynamic-slice.7
  56.5 6.0 %collective-permute-done.26 = bf16[2,64,1024]{2,1,0:T(8,128)(2,1)} collective-permute-done((bf16[2,64,1024]{2,1,0:T(8,128)(2,1)}, bf16[2,64,1024]{2,1,0:T(8,128)(2,1)}, u32[]{:S(2)}, u32[]{:S(2)}) %collective-permute-start.26) | collective-permute-done | bytes 262176 | tf_op jit(solution)/shard_map/ppermute | solution.py:238
  67.4 1.9 collective-permute-start.29
  70.4 2.5 collective-permute-start.30
  73.6 7.6 %collective-permute-done.29 = bf16[2,64,1024]{2,1,0:T(8,128)(2,1)S(1)} collective-permute-done((bf16[2,64,1024]{2,1,0:T(8,128)(2,1)S(1)}, bf16[2,64,1024]{2,1,0:T(8,128)(2,1)S(1)}, u32[]{:S(2)}, u32[]{:S(2)}) %collective-permute-start.29) | collective-permute-done | bytes 262176 | tf_op jit(solution)/shard_map/ppermute | solution.py:238
  81.2 2.7 collective-permute-start.31
  85.4 4.6 collective-permute-done.31
  90.8 3.6 gather_fusion.5
  94.4 3.2 bitcast_select_fusion.1
  97.8 9.3 %all-gather.1 = f32[8,6,256]{2,1,0:T(8,128)S(1)} all-gather(f32[1,6,256]{2,1,0:T(8,128)S(1)} %bitcast.296), channel_id=2, replica_groups=mesh['row'=8,'col'=4] {'row'}, dimensions={0}, use_global_device_ids=true | all-gather | bytes 55296 | tf_op jit(solution)/shard_map/all_gather | solution.py:266
  108.6 2.1 copy.120
  110.7 2.6 gather_fusion.2
  113.3 2.4 copy.55
  115.8 2.3 bitcast_select_fusion.2.refs_11_
  118.9 2.7 slice_bitcast_fusion
  121.6 2.0 copy.53
  123.6 2.3 slice_bitcast_fusion.1
  126.0 2.9 gather_fusion.3
  128.9 2.4 broadcast_select_fusion.1
  133.1 40.9 %shard_map.112 = (bf16[1024,2048]{1,0:T(8,128)(2,1)}, bf16[8,4,64,64]{3,2,1,0:T(8,128)(2,1)S(1)}) custom-call(s32[8]{0:T(128)S(1)} %dynamic_slice.102.lens, bf16[1024,256]{1,0:T(8,128)(2,1)S(1)} %copy-done.2, bf16[1024,256]{1,0:T(8,128)(2,1)S(1)} %collective-permute-done.refs_1_, bf16[1024,256]{1,0:T(8,128)(2,1)S(1)} %collective-permute-done.1.refs_2_, ...), custom_call_target="tpu_custom_call" | custom-call | flops 40000000000 | bytes 16777216 | tf_op jit(solution)/shard_map/pallas_call | solution.py:155
  174.0 5.0 %gather_fusion.4 = bf16[8,128,2048]{2,1,0:T(8,128)(2,1)} fusion(bf16[8,128,2048]{2,1,0:T(8,128)(2,1)} %bitcast.254, s32[1024]{0:T(1024)S(1)} %pad_clamp_fusion.3), kind=kCustom, calls=%fused_computation.6 | custom fusion | bytes 8388640 | tf_op jit(solution)/shard_map/jit(_take)/gather | solution.py:315
  179.0 2.7 broadcast_select_fusion
  181.7 2.1 copy-done.5
  185.4 2.1 slice.155
  187.5 3.2 reshape.333
  190.7 4.8 %constant_dynamic-slice_fusion.3 = (bf16[3,64,1,512]{3,2,1,0:T(2,128)(2,1)}, bf16[3,64,1,512]{3,2,1,0:T(2,128)(2,1)}, bf16[3,64,1,512]{3,2,1,0:T(2,128)(2,1)}, bf16[3,64,1,512]{3,2,1,0:T(2,128)(2,1)S(1)}) fusion(bf16[3,64,4,512]{3,2,1,0:T(4,128)(2,1)} %reshape.333, s32[]{:T(128)S(6)} %select_n.303, s32[]{:T(128)S(6)} %select_n.306, s32[]{:T(128)S(6)} %select_n.305, ...), kind=kLoop, calls=%fused_computation.141 | loop fusion | bytes 1572880 | tf_op jit(solution)/shard_map/dynamic-slice.16
  201.9 3.0 add_convert_fusion.1
  215.9 2.5 copy.49
  218.5 2.5 copy.56
  221.2 10.9 %collective-permute-done.16 = bf16[128,2048]{1,0:T(8,128)(2,1)} collective-permute-done((bf16[128,2048]{1,0:T(8,128)(2,1)}, bf16[128,2048]{1,0:T(8,128)(2,1)}, u32[]{:S(2)}, u32[]{:S(2)}) %collective-permute-start.16) | collective-permute-done | bytes 524320 | tf_op jit(solution)/shard_map/ppermute | solution.py:238
  232.2 2.1 convert_reduce_fusion
  237.2 2.6 collective-permute-start.48
  241.3 22.1 %collective-permute-done.48 = bf16[3,64,512]{2,1,0:T(8,128)(2,1)S(1)} collective-permute-done((bf16[3,64,512]{2,1,0:T(8,128)(2,1)S(1)}, bf16[3,64,512]{2,1,0:T(8,128)(2,1)S(1)}, u32[]{:S(2)}, u32[]{:S(2)}) %collective-permute-start.48) | collective-permute-done | bytes 196640 | tf_op jit(solution)/shard_map/ppermute | solution.py:284
  268.2 1.9 constant_dynamic-update-slice_fusion.21
  272.0 5.9 %collective-permute-done.23 = bf16[128,2048]{1,0:T(8,128)(2,1)} collective-permute-done((bf16[128,2048]{1,0:T(8,128)(2,1)S(1)}, bf16[128,2048]{1,0:T(8,128)(2,1)}, u32[]{:S(2)}, u32[]{:S(2)}) %collective-permute-start.23) | collective-permute-done | bytes 524320 | tf_op jit(solution)/shard_map/ppermute | solution.py:238
  279.8 1.9 constant_dynamic-update-slice_fusion.18
  282.5 1.9 constant_dynamic-update-slice_fusion.16
  285.3 4.7 fusion.32
  290.0 2.4 copy.57
  292.4 2.5 copy.58
  294.9 14.4 %convolution_convert_fusion = bf16[1024,2048]{1,0:T(8,128)(2,1)} fusion(bf16[2048,1024]{1,0:T(8,128)(2,1)} %bitcast.256, bf16[1024,2048]{1,0:T(8,128)(2,1)} %constant_dynamic-update-slice_fusion.15, bf16[2048,1024]{1,0:T(8,128)(2,1)} %bitcast.255), kind=kOutput, calls=%fused_computation.15 | convolution fusion | flops 8595177472 | bytes 16777216 | tf_op jit(solution)/shard_map/dot_general | solution.py:332
  312.8 3.1 collective-permute-done.32
  315.9 3.1 add_convert_fusion
  320.2 15.1 %collective-permute-start.33 = (bf16[128,2048]{1,0:T(8,128)(2,1)}, bf16[128,2048]{1,0:T(8,128)(2,1)}, u32[]{:S(2)}, u32[]{:S(2)}) collective-permute-start(bf16[128,2048]{1,0:T(8,128)(2,1)} %get-tuple-element.18), channel_id=1, source_target_pairs={{0,8},{4,12},{8,0},{12,4},{16,24},{20,28},{24,16},{28,20},{1,9},{5... | collective-permute-start | bytes 1572872 | tf_op jit(solution)/shard_map/ppermute | solution.py:238
  340.6 2.4 reshape.340
  343.0 16.0 %collective-permute-done.33 = bf16[128,2048]{1,0:T(8,128)(2,1)} collective-permute-done((bf16[128,2048]{1,0:T(8,128)(2,1)}, bf16[128,2048]{1,0:T(8,128)(2,1)}, u32[]{:S(2)}, u32[]{:S(2)}) %collective-permute-start.33) | collective-permute-done | bytes 524320 | tf_op jit(solution)/shard_map/ppermute | solution.py:238
  359.0 5.2 %collective-permute-done.34 = bf16[128,2048]{1,0:T(8,128)(2,1)} collective-permute-done((bf16[128,2048]{1,0:T(8,128)(2,1)}, bf16[128,2048]{1,0:T(8,128)(2,1)}, u32[]{:S(2)}, u32[]{:S(2)}) %collective-permute-start.34) | collective-permute-done | bytes 524320 | tf_op jit(solution)/shard_map/ppermute | solution.py:238
  364.3 5.2 %collective-permute-done.35 = bf16[128,2048]{1,0:T(8,128)(2,1)} collective-permute-done((bf16[128,2048]{1,0:T(8,128)(2,1)}, bf16[128,2048]{1,0:T(8,128)(2,1)}, u32[]{:S(2)}, u32[]{:S(2)}) %collective-permute-start.35) | collective-permute-done | bytes 524320 | tf_op jit(solution)/shard_map/ppermute | solution.py:238
  372.5 25.5 %collective-permute-start.45 = (bf16[128,2048]{1,0:T(8,128)(2,1)S(1)}, bf16[128,2048]{1,0:T(8,128)(2,1)S(1)}, u32[]{:S(2)}, u32[]{:S(2)}) collective-permute-start(bf16[128,2048]{1,0:T(8,128)(2,1)S(1)} %fusion.3), channel_id=1, source_target_pairs={{0,2},{1,10},{2,18},{3,26},{4,6},{5,14},{6,22},{7,30},{8,3},{9,11}... | collective-permute-start | bytes 1572872 | tf_op jit(solution)/shard_map/ppermute | solution.py:345
  402.0 2.8 collective-permute-done.37
  406.3 2.5 collective-permute-done.38
  408.8 8.9 %collective-permute-start.39 = (bf16[128,256]{1,0:T(8,128)(2,1)S(1)}, bf16[128,256]{1,0:T(8,128)(2,1)S(1)}, u32[]{:S(2)}, u32[]{:S(2)}) collective-permute-start(bf16[128,256]{1,0:T(8,128)(2,1)S(1)} %bitcast.289), channel_id=1, source_target_pairs={{0,16},{4,20},{8,24},{12,28},{16,0},{20,4},{24,8},{28,12},{1,17},{... | collective-permute-start | bytes 196616 | tf_op jit(solution)/shard_map/ppermute | solution.py:238
  417.7 11.1 %collective-permute-done.39 = bf16[128,256]{1,0:T(8,128)(2,1)S(1)} collective-permute-done((bf16[128,256]{1,0:T(8,128)(2,1)S(1)}, bf16[128,256]{1,0:T(8,128)(2,1)S(1)}, u32[]{:S(2)}, u32[]{:S(2)}) %collective-permute-start.39) | collective-permute-done | bytes 65568 | tf_op jit(solution)/shard_map/ppermute | solution.py:238
  428.8 2.0 collective-permute-start.40
  430.7 2.4 collective-permute-done.40
  433.2 14.4 %collective-permute-done.41 = bf16[128,256]{1,0:T(8,128)(2,1)S(1)} collective-permute-done((bf16[128,256]{1,0:T(8,128)(2,1)S(1)}, bf16[128,256]{1,0:T(8,128)(2,1)S(1)}, u32[]{:S(2)}, u32[]{:S(2)}) %collective-permute-start.41) | collective-permute-done | bytes 65568 | tf_op jit(solution)/shard_map/ppermute | solution.py:238
  447.6 5.1 %collective-permute-done.42 = bf16[128,256]{1,0:T(8,128)(2,1)S(1)} collective-permute-done((bf16[128,256]{1,0:T(8,128)(2,1)S(1)}, bf16[128,256]{1,0:T(8,128)(2,1)S(1)}, u32[]{:S(2)}, u32[]{:S(2)}) %collective-permute-start.42) | collective-permute-done | bytes 65568 | tf_op jit(solution)/shard_map/ppermute | solution.py:238
  456.7 2.0 gather_fusion.6
  460.6 7.7 %shard_map.113 = bf16[3,512,512]{2,1,0:T(8,128)(2,1)} custom-call(bf16[512,2048]{1,0:T(8,128)(2,1)S(1)} %bitcast_select_fusion.x, f32[3,2048]{1,0:T(4,128)S(1)} %slice.112.gate, bf16[8,3,256,512]{3,2,1,0:T(8,128)(2,1)} %bitcast.297), custom_call_target="tpu_custom_call" | custom-call | flops 6000000000 | bytes 16777216 | tf_op jit(solution)/shard_map/pallas_call | solution.py:199
  (242 shorter events, 100.4 us)
Async XLA Ops:
  7.2 42.1 %copy-start = (bf16[2,96,2048]{2,1,0:T(8,128)(2,1)S(1)}, bf16[2,96,2048]{2,1,0:T(8,128)(2,1)}, u32[]{:S(2)}) copy-start(bf16[2,96,2048]{2,1,0:T(8,128)(2,1)} %param.16) | copy-start | bytes 2359300
  7.2 111.7 %all-gather.6.cloned.1.call-start = ((), (), s32[]{:S(2)}) async-start(), calls=%async_computation | async-start | bytes 5242880 | tf_op jit(solution)/shard_map/all_gather | solution.py:270
  10.9 19.9 %copy-start.2 = (bf16[1024,256]{1,0:T(8,128)(2,1)S(1)}, bf16[1024,256]{1,0:T(8,128)(2,1)}, u32[]{:S(2)}) copy-start(bf16[1024,256]{1,0:T(8,128)(2,1)} %refs_0_.1) | copy-start | bytes 1572868
  11.9 4.8 %collective-permute-start.7 = (bf16[256,256]{1,0:T(8,128)(2,1)}, bf16[256,256]{1,0:T(8,128)(2,1)}, u32[]{:S(2)}, u32[]{:S(2)}) collective-permute-start(bf16[256,256]{1,0:T(8,128)(2,1)} %get-tuple-element.38), channel_id=1, source_target_pairs={{0,4},{4,0},{8,12},{12,8},{16,20},{20,16},{24,28},{28,24},{1,5},{5... | collective-permute-start | bytes 393224 | tf_op jit(solution)/shard_map/ppermute | solution.py:238
  12.4 7.9 %collective-permute-start.8 = (bf16[256,256]{1,0:T(8,128)(2,1)}, bf16[256,256]{1,0:T(8,128)(2,1)}, u32[]{:S(2)}, u32[]{:S(2)}) collective-permute-start(bf16[256,256]{1,0:T(8,128)(2,1)} %get-tuple-element.37), channel_id=1, source_target_pairs={{0,8},{4,12},{8,0},{12,4},{16,24},{20,28},{24,16},{28,20},{1,9},{5... | collective-permute-start | bytes 393224 | tf_op jit(solution)/shard_map/ppermute | solution.py:238
  14.9 7.4 %collective-permute-start.9 = (bf16[256,256]{1,0:T(8,128)(2,1)}, bf16[256,256]{1,0:T(8,128)(2,1)}, u32[]{:S(2)}, u32[]{:S(2)}) collective-permute-start(bf16[256,256]{1,0:T(8,128)(2,1)} %get-tuple-element.36), channel_id=1, source_target_pairs={{0,12},{4,8},{8,4},{12,0},{16,28},{20,24},{24,20},{28,16},{1,13},{... | collective-permute-start | bytes 393224 | tf_op jit(solution)/shard_map/ppermute | solution.py:238
  15.0 8.2 %collective-permute-start.10 = (bf16[256,256]{1,0:T(8,128)(2,1)}, bf16[256,256]{1,0:T(8,128)(2,1)}, u32[]{:S(2)}, u32[]{:S(2)}) collective-permute-start(bf16[256,256]{1,0:T(8,128)(2,1)} %get-tuple-element.35), channel_id=1, source_target_pairs={{0,16},{4,20},{8,24},{12,28},{16,0},{20,4},{24,8},{28,12},{1,17},{... | collective-permute-start | bytes 393224 | tf_op jit(solution)/shard_map/ppermute | solution.py:238
  16.7 11.9 %collective-permute-start.11 = (bf16[256,256]{1,0:T(8,128)(2,1)}, bf16[256,256]{1,0:T(8,128)(2,1)}, u32[]{:S(2)}, u32[]{:S(2)}) collective-permute-start(bf16[256,256]{1,0:T(8,128)(2,1)} %get-tuple-element.34), channel_id=1, source_target_pairs={{0,20},{4,16},{8,28},{12,24},{16,4},{20,0},{24,12},{28,8},{1,21},{... | collective-permute-start | bytes 393224 | tf_op jit(solution)/shard_map/ppermute | solution.py:238
  16.8 12.8 %collective-permute-start.12 = (bf16[256,256]{1,0:T(8,128)(2,1)}, bf16[256,256]{1,0:T(8,128)(2,1)S(1)}, u32[]{:S(2)}, u32[]{:S(2)}) collective-permute-start(bf16[256,256]{1,0:T(8,128)(2,1)} %get-tuple-element.33), channel_id=1, source_target_pairs={{0,24},{4,28},{8,16},{12,20},{16,8},{20,12},{24,0},{28,4},{1,25},{... | collective-permute-start | bytes 393224 | tf_op jit(solution)/shard_map/ppermute | solution.py:238
  20.3 9.3 %collective-permute-start.13 = (bf16[256,256]{1,0:T(8,128)(2,1)S(1)}, bf16[256,256]{1,0:T(8,128)(2,1)S(1)}, u32[]{:S(2)}, u32[]{:S(2)}) collective-permute-start(bf16[256,256]{1,0:T(8,128)(2,1)S(1)} %get-tuple-element.32), channel_id=1, source_target_pairs={{0,28},{4,24},{8,20},{12,16},{16,12},{20,8},{24,4},{28,0},{1,29},{... | collective-permute-start | bytes 393224 | tf_op jit(solution)/shard_map/ppermute | solution.py:238
  30.7 254.6 %all-gather.8.cloned.1.call-start = ((), (), s32[]{:S(2)}) async-start(), calls=%async_computation.1 | async-start | bytes 10485760 | tf_op jit(solution)/shard_map/all_gather | solution.py:278
  30.7 87.3 %collective-permute-start.1 = (bf16[1024,256]{1,0:T(8,128)(2,1)S(1)}, bf16[1024,256]{1,0:T(8,128)(2,1)S(1)}, u32[]{:S(2)}, u32[]{:S(2)}) collective-permute-start(bf16[1024,256]{1,0:T(8,128)(2,1)S(1)} %copy-done.2), channel_id=1, source_target_pairs={{0,8},{4,12},{8,0},{12,4},{16,24},{20,28},{24,16},{28,20},{1,9},{5... | collective-permute-start | bytes 1572872 | tf_op jit(solution)/shard_map/ppermute | solution.py:238
  32.3 86.1 %collective-permute-start.3 = (bf16[1024,256]{1,0:T(8,128)(2,1)S(1)}, bf16[1024,256]{1,0:T(8,128)(2,1)S(1)}, u32[]{:S(2)}, u32[]{:S(2)}) collective-permute-start(bf16[1024,256]{1,0:T(8,128)(2,1)S(1)} %copy-done.2), channel_id=1, source_target_pairs={{0,16},{4,20},{8,24},{12,28},{16,0},{20,4},{24,8},{28,12},{1,17},{... | collective-permute-start | bytes 1572872 | tf_op jit(solution)/shard_map/ppermute | solution.py:238
  34.1 84.5 %collective-permute-start.5 = (bf16[1024,256]{1,0:T(8,128)(2,1)S(1)}, bf16[1024,256]{1,0:T(8,128)(2,1)}, u32[]{:S(2)}, u32[]{:S(2)}) collective-permute-start(bf16[1024,256]{1,0:T(8,128)(2,1)S(1)} %copy-done.2), channel_id=1, source_target_pairs={{0,24},{4,28},{8,16},{12,20},{16,8},{20,12},{24,0},{28,4},{1,25},{... | collective-permute-start | bytes 1572872 | tf_op jit(solution)/shard_map/ppermute | solution.py:238
  44.4 10.0 %collective-permute-start.25 = (bf16[2,64,1024]{2,1,0:T(8,128)(2,1)}, bf16[2,64,1024]{2,1,0:T(8,128)(2,1)}, u32[]{:S(2)}, u32[]{:S(2)}) collective-permute-start(bf16[2,64,1024]{2,1,0:T(8,128)(2,1)} %bitcast.224), channel_id=1, source_target_pairs={{0,4},{4,0},{8,12},{12,8},{16,20},{20,16},{24,28},{28,24},{1,5},{5... | collective-permute-start | bytes 786440 | tf_op jit(solution)/shard_map/ppermute | solution.py:238
  45.2 17.3 %collective-permute-start.26 = (bf16[2,64,1024]{2,1,0:T(8,128)(2,1)}, bf16[2,64,1024]{2,1,0:T(8,128)(2,1)}, u32[]{:S(2)}, u32[]{:S(2)}) collective-permute-start(bf16[2,64,1024]{2,1,0:T(8,128)(2,1)} %bitcast.223), channel_id=1, source_target_pairs={{0,8},{4,12},{8,0},{12,4},{16,24},{20,28},{24,16},{28,20},{1,9},{5... | collective-permute-start | bytes 786440 | tf_op jit(solution)/shard_map/ppermute | solution.py:238
  54.4 12.9 %collective-permute-start.27 = (bf16[2,64,1024]{2,1,0:T(8,128)(2,1)}, bf16[2,64,1024]{2,1,0:T(8,128)(2,1)S(1)}, u32[]{:S(2)}, u32[]{:S(2)}) collective-permute-start(bf16[2,64,1024]{2,1,0:T(8,128)(2,1)} %bitcast.272), channel_id=1, source_target_pairs={{0,12},{4,8},{8,4},{12,0},{16,28},{20,24},{24,20},{28,16},{1,13},{... | collective-permute-start | bytes 786440 | tf_op jit(solution)/shard_map/ppermute | solution.py:238
  62.5 7.9 %collective-permute-start.28 = (bf16[2,64,1024]{2,1,0:T(8,128)(2,1)}, bf16[2,64,1024]{2,1,0:T(8,128)(2,1)S(1)}, u32[]{:S(2)}, u32[]{:S(2)}) collective-permute-start(bf16[2,64,1024]{2,1,0:T(8,128)(2,1)} %bitcast.271), channel_id=1, source_target_pairs={{0,16},{4,20},{8,24},{12,28},{16,0},{20,4},{24,8},{28,12},{1,17},{... | collective-permute-start | bytes 786440 | tf_op jit(solution)/shard_map/ppermute | solution.py:238
  67.4 13.9 %collective-permute-start.29 = (bf16[2,64,1024]{2,1,0:T(8,128)(2,1)S(1)}, bf16[2,64,1024]{2,1,0:T(8,128)(2,1)S(1)}, u32[]{:S(2)}, u32[]{:S(2)}) collective-permute-start(bf16[2,64,1024]{2,1,0:T(8,128)(2,1)S(1)} %bitcast.270), channel_id=1, source_target_pairs={{0,20},{4,16},{8,28},{12,24},{16,4},{20,0},{24,12},{28,8},{1,21},{... | collective-permute-start | bytes 786440 | tf_op jit(solution)/shard_map/ppermute | solution.py:238
  70.4 14.3 %collective-permute-start.30 = (bf16[2,64,1024]{2,1,0:T(8,128)(2,1)S(1)}, bf16[2,64,1024]{2,1,0:T(8,128)(2,1)S(1)}, u32[]{:S(2)}, u32[]{:S(2)}) collective-permute-start(bf16[2,64,1024]{2,1,0:T(8,128)(2,1)S(1)} %bitcast.269), channel_id=1, source_target_pairs={{0,24},{4,28},{8,16},{12,20},{16,8},{20,12},{24,0},{28,4},{1,25},{... | collective-permute-start | bytes 786440 | tf_op jit(solution)/shard_map/ppermute | solution.py:238
  81.2 8.8 %collective-permute-start.31 = (bf16[2,64,1024]{2,1,0:T(8,128)(2,1)S(1)}, bf16[2,64,1024]{2,1,0:T(8,128)(2,1)S(1)}, u32[]{:S(2)}, u32[]{:S(2)}) collective-permute-start(bf16[2,64,1024]{2,1,0:T(8,128)(2,1)S(1)} %bitcast.268), channel_id=1, source_target_pairs={{0,28},{4,24},{8,20},{12,16},{16,12},{20,8},{24,4},{28,0},{1,29},{... | collective-permute-start | bytes 786440 | tf_op jit(solution)/shard_map/ppermute | solution.py:238
  84.7 46.5 %collective-permute-start = (bf16[1024,256]{1,0:T(8,128)(2,1)S(1)}, bf16[1024,256]{1,0:T(8,128)(2,1)S(1)}, u32[]{:S(2)}, u32[]{:S(2)}) collective-permute-start(bf16[1024,256]{1,0:T(8,128)(2,1)S(1)} %copy-done.2), channel_id=1, source_target_pairs={{0,4},{4,0},{8,12},{12,8},{16,20},{20,16},{24,28},{28,24},{1,5},{5... | collective-permute-start | bytes 1572872 | tf_op jit(solution)/shard_map/ppermute | solution.py:238
  94.4 13.3 %slice-start = ((f32[9,2048]{1,0:T(8,128)}), f32[5,2048]{1,0:T(8,128)S(1)}, s32[]{:S(2)}) async-start(f32[9,2048]{1,0:T(8,128)} %param.17), calls=%async_computation.3 | async-start | bytes 131072 | tf_op jit(solution)/shard_map/slice | solution.py:293
  97.7 18.0 %copy-start.16 = (s32[32]{0:T(128)S(1)}, s32[32]{0:T(128)}, u32[]{:S(2)}) copy-start(s32[32]{0:T(128)} %param.12) | copy-start | bytes 388
  97.7 362.9 %all-gather.10.cloned.1.call-start = ((), (), s32[]{:S(2)}) async-start(), calls=%async_computation.2 | async-start | bytes 7077888 | tf_op jit(solution)/shard_map/all_gather | solution.py:288
  118.1 13.2 %collective-permute-start.2 = (bf16[1024,256]{1,0:T(8,128)(2,1)S(1)}, bf16[1024,256]{1,0:T(8,128)(2,1)S(1)}, u32[]{:S(2)}, u32[]{:S(2)}) collective-permute-start(bf16[1024,256]{1,0:T(8,128)(2,1)S(1)} %collective-permute-done.1.refs_2_), channel_id=1, source_target_pairs={{0,4},{4,0},{8,12},{12,8},{16,20},{20,16},{24,28},{28,24},{1,5},{5... | collective-permute-start | bytes 1572872 | tf_op jit(solution)/shard_map/ppermute | solution.py:238
  118.4 13.6 %collective-permute-start.4 = (bf16[1024,256]{1,0:T(8,128)(2,1)S(1)}, bf16[1024,256]{1,0:T(8,128)(2,1)S(1)}, u32[]{:S(2)}, u32[]{:S(2)}) collective-permute-start(bf16[1024,256]{1,0:T(8,128)(2,1)S(1)} %collective-permute-done.3.refs_4_), channel_id=1, source_target_pairs={{0,4},{4,0},{8,12},{12,8},{16,20},{20,16},{24,28},{28,24},{1,5},{5... | collective-permute-start | bytes 1572872 | tf_op jit(solution)/shard_map/ppermute | solution.py:238
  118.6 13.5 %collective-permute-start.6 = (bf16[1024,256]{1,0:T(8,128)(2,1)}, bf16[1024,256]{1,0:T(8,128)(2,1)}, u32[]{:S(2)}, u32[]{:S(2)}) collective-permute-start(bf16[1024,256]{1,0:T(8,128)(2,1)} %collective-permute-done.5.refs_6_), channel_id=1, source_target_pairs={{0,4},{4,0},{8,12},{12,8},{16,20},{20,16},{24,28},{28,24},{1,5},{5... | collective-permute-start | bytes 1572872 | tf_op jit(solution)/shard_map/ppermute | solution.py:238
  185.2 16.7 %collective-permute-start.14 = (bf16[4,128,2048]{2,1,0:T(8,128)(2,1)}, bf16[4,128,2048]{2,1,0:T(8,128)(2,1)}, u32[]{:S(2)}, u32[]{:S(2)}) collective-permute-start(bf16[4,128,2048]{2,1,0:T(8,128)(2,1)} %slice.93), channel_id=1, source_target_pairs={{0,4},{4,0},{8,12},{12,8},{16,20},{20,16},{24,28},{28,24},{1,5},{5... | collective-permute-start | bytes 6291464 | tf_op jit(solution)/shard_map/ppermute | solution.py:238
  185.4 12.4 %copy-start.13 = (f32[9,2048]{1,0:T(8,128)S(1)}, f32[9,2048]{1,0:T(8,128)}, u32[]{:S(2)}) copy-start(f32[9,2048]{1,0:T(8,128)} %param.17) | copy-start | bytes 221188
  196.2 44.1 %collective-permute-start.47 = (bf16[3,64,512]{2,1,0:T(8,128)(2,1)}, bf16[3,64,512]{2,1,0:T(8,128)(2,1)}, u32[]{:S(2)}, u32[]{:S(2)}) collective-permute-start(bf16[3,64,512]{2,1,0:T(8,128)(2,1)} %bitcast.227), channel_id=1, source_target_pairs={{0,1},{1,0},{2,3},{3,2},{4,5},{5,4},{6,7},{7,6},{8,9},{9,8},{10,11... | collective-permute-start | bytes 589832 | tf_op jit(solution)/shard_map/ppermute | solution.py:284
  206.1 15.1 %collective-permute-start.15 = (bf16[128,2048]{1,0:T(8,128)(2,1)}, bf16[128,2048]{1,0:T(8,128)(2,1)}, u32[]{:S(2)}, u32[]{:S(2)}) collective-permute-start(bf16[128,2048]{1,0:T(8,128)(2,1)} %get-tuple-element.21), channel_id=1, source_target_pairs={{0,8},{4,12},{8,0},{12,4},{16,24},{20,28},{24,16},{28,20},{1,9},{5... | collective-permute-start | bytes 1572872 | tf_op jit(solution)/shard_map/ppermute | solution.py:238
  207.0 25.1 %collective-permute-start.16 = (bf16[128,2048]{1,0:T(8,128)(2,1)}, bf16[128,2048]{1,0:T(8,128)(2,1)}, u32[]{:S(2)}, u32[]{:S(2)}) collective-permute-start(bf16[128,2048]{1,0:T(8,128)(2,1)} %get-tuple-element.23), channel_id=1, source_target_pairs={{0,16},{4,20},{8,24},{12,28},{16,0},{20,4},{24,8},{28,12},{1,17},{... | collective-permute-start | bytes 1572872 | tf_op jit(solution)/shard_map/ppermute | solution.py:238
  207.9 24.2 %collective-permute-start.17 = (bf16[128,2048]{1,0:T(8,128)(2,1)}, bf16[128,2048]{1,0:T(8,128)(2,1)}, u32[]{:S(2)}, u32[]{:S(2)}) collective-permute-start(bf16[128,2048]{1,0:T(8,128)(2,1)} %get-tuple-element.22), channel_id=1, source_target_pairs={{0,24},{4,28},{8,16},{12,20},{16,8},{20,12},{24,0},{28,4},{1,25},{... | collective-permute-start | bytes 1572872 | tf_op jit(solution)/shard_map/ppermute | solution.py:238
  221.0 16.2 %copy-start.9 = (bf16[3,64,1,512]{3,2,1,0:T(2,128)(2,1)S(1)}, bf16[3,64,1,512]{3,2,1,0:T(2,128)(2,1)}, u32[]{:S(2)}) copy-start(bf16[3,64,1,512]{3,2,1,0:T(2,128)(2,1)} %get-tuple-element.41) | copy-start | bytes 589828
  234.3 6.9 %copy-start.7 = (bf16[3,64,1,512]{3,2,1,0:T(2,128)(2,1)S(1)}, bf16[3,64,1,512]{3,2,1,0:T(2,128)(2,1)}, u32[]{:S(2)}) copy-start(bf16[3,64,1,512]{3,2,1,0:T(2,128)(2,1)} %get-tuple-element.39) | copy-start | bytes 589828
  236.0 30.4 %collective-permute-start.19 = (bf16[128,2048]{1,0:T(8,128)(2,1)S(1)}, bf16[128,2048]{1,0:T(8,128)(2,1)}, u32[]{:S(2)}, u32[]{:S(2)}) collective-permute-start(bf16[128,2048]{1,0:T(8,128)(2,1)S(1)} %get-tuple-element.14), channel_id=1, source_target_pairs={{0,8},{4,12},{8,0},{12,4},{16,24},{20,28},{24,16},{28,20},{1,9},{5... | collective-permute-start | bytes 1572872 | tf_op jit(solution)/shard_map/ppermute | solution.py:238
  237.2 26.2 %collective-permute-start.48 = (bf16[3,64,512]{2,1,0:T(8,128)(2,1)S(1)}, bf16[3,64,512]{2,1,0:T(8,128)(2,1)S(1)}, u32[]{:S(2)}, u32[]{:S(2)}) collective-permute-start(bf16[3,64,512]{2,1,0:T(8,128)(2,1)S(1)} %bitcast.278), channel_id=1, source_target_pairs={{0,2},{1,3},{2,0},{3,1},{4,6},{5,7},{6,4},{7,5},{8,10},{9,11},{10,... | collective-permute-start | bytes 589832 | tf_op jit(solution)/shard_map/ppermute | solution.py:284
  239.8 23.6 %collective-permute-start.49 = (bf16[3,64,512]{2,1,0:T(8,128)(2,1)S(1)}, bf16[3,64,512]{2,1,0:T(8,128)(2,1)S(1)}, u32[]{:S(2)}, u32[]{:S(2)}) collective-permute-start(bf16[3,64,512]{2,1,0:T(8,128)(2,1)S(1)} %bitcast.279), channel_id=1, source_target_pairs={{0,3},{1,2},{2,1},{3,0},{4,7},{5,6},{6,5},{7,4},{8,11},{9,10},{10,... | collective-permute-start | bytes 589832 | tf_op jit(solution)/shard_map/ppermute | solution.py:284
  240.3 27.9 %collective-permute-start.18 = (bf16[128,2048]{1,0:T(8,128)(2,1)S(1)}, bf16[128,2048]{1,0:T(8,128)(2,1)}, u32[]{:S(2)}, u32[]{:S(2)}) collective-permute-start(bf16[128,2048]{1,0:T(8,128)(2,1)S(1)} %get-tuple-element.14), channel_id=1, source_target_pairs={{0,4},{4,0},{8,12},{12,8},{16,20},{20,16},{24,28},{28,24},{1,5},{5... | collective-permute-start | bytes 1572872 | tf_op jit(solution)/shard_map/ppermute | solution.py:238
  240.3 27.3 %collective-permute-start.21 = (bf16[128,2048]{1,0:T(8,128)(2,1)S(1)}, bf16[128,2048]{1,0:T(8,128)(2,1)}, u32[]{:S(2)}, u32[]{:S(2)}) collective-permute-start(bf16[128,2048]{1,0:T(8,128)(2,1)S(1)} %get-tuple-element.14), channel_id=1, source_target_pairs={{0,16},{4,20},{8,24},{12,28},{16,0},{20,4},{24,8},{28,12},{1,17},{... | collective-permute-start | bytes 1572872 | tf_op jit(solution)/shard_map/ppermute | solution.py:238
  265.0 12.9 %collective-permute-start.23 = (bf16[128,2048]{1,0:T(8,128)(2,1)S(1)}, bf16[128,2048]{1,0:T(8,128)(2,1)}, u32[]{:S(2)}, u32[]{:S(2)}) collective-permute-start(bf16[128,2048]{1,0:T(8,128)(2,1)S(1)} %get-tuple-element.14), channel_id=1, source_target_pairs={{0,24},{4,28},{8,16},{12,20},{16,8},{20,12},{24,0},{28,4},{1,25},{... | collective-permute-start | bytes 1572872 | tf_op jit(solution)/shard_map/ppermute | solution.py:238
  266.4 11.5 %collective-permute-start.20 = (bf16[128,2048]{1,0:T(8,128)(2,1)}, bf16[128,2048]{1,0:T(8,128)(2,1)}, u32[]{:S(2)}, u32[]{:S(2)}) collective-permute-start(bf16[128,2048]{1,0:T(8,128)(2,1)} %collective-permute-done.19), channel_id=1, source_target_pairs={{0,4},{4,0},{8,12},{12,8},{16,20},{20,16},{24,28},{28,24},{1,5},{5... | collective-permute-start | bytes 1572872 | tf_op jit(solution)/shard_map/ppermute | solution.py:238
  267.6 14.1 %collective-permute-start.22 = (bf16[128,2048]{1,0:T(8,128)(2,1)}, bf16[128,2048]{1,0:T(8,128)(2,1)S(1)}, u32[]{:S(2)}, u32[]{:S(2)}) collective-permute-start(bf16[128,2048]{1,0:T(8,128)(2,1)} %collective-permute-done.21), channel_id=1, source_target_pairs={{0,4},{4,0},{8,12},{12,8},{16,20},{20,16},{24,28},{28,24},{1,5},{5... | collective-permute-start | bytes 1572872 | tf_op jit(solution)/shard_map/ppermute | solution.py:238
  277.9 6.5 %collective-permute-start.24 = (bf16[128,2048]{1,0:T(8,128)(2,1)}, bf16[128,2048]{1,0:T(8,128)(2,1)S(1)}, u32[]{:S(2)}, u32[]{:S(2)}) collective-permute-start(bf16[128,2048]{1,0:T(8,128)(2,1)} %collective-permute-done.23), channel_id=1, source_target_pairs={{0,4},{4,0},{8,12},{12,8},{16,20},{20,16},{24,28},{28,24},{1,5},{5... | collective-permute-start | bytes 1572872 | tf_op jit(solution)/shard_map/ppermute | solution.py:238
  311.0 4.8 %collective-permute-start.32 = (bf16[4,128,2048]{2,1,0:T(8,128)(2,1)S(1)}, bf16[4,128,2048]{2,1,0:T(8,128)(2,1)}, u32[]{:S(2)}, u32[]{:S(2)}) collective-permute-start(bf16[4,128,2048]{2,1,0:T(8,128)(2,1)S(1)} %slice.105), channel_id=1, source_target_pairs={{0,4},{4,0},{8,12},{12,8},{16,20},{20,16},{24,28},{28,24},{1,5},{5... | collective-permute-start | bytes 6291464 | tf_op jit(solution)/shard_map/ppermute | solution.py:238
  311.8 25.0 %collective-permute-start.50 = (bf16[4,4,64,64]{3,2,1,0:T(8,128)(2,1)S(1)}, bf16[4,4,64,64]{3,2,1,0:T(8,128)(2,1)S(1)}, u32[]{:S(2)}, u32[]{:S(2)}) collective-permute-start(bf16[4,4,64,64]{3,2,1,0:T(8,128)(2,1)S(1)} %get-tuple-element.43), channel_id=1, source_target_pairs={{0,0},{1,8},{2,16},{3,24},{4,4},{5,12},{6,20},{7,28},{8,1},{9,9},{... | collective-permute-start | bytes 393224 | tf_op jit(solution)/shard_map/ppermute | solution.py:310
  312.7 24.1 %collective-permute-start.51 = (bf16[4,4,64,64]{3,2,1,0:T(8,128)(2,1)S(1)}, bf16[4,4,64,64]{3,2,1,0:T(8,128)(2,1)S(1)}, u32[]{:S(2)}, u32[]{:S(2)}) collective-permute-start(bf16[4,4,64,64]{3,2,1,0:T(8,128)(2,1)S(1)} %get-tuple-element.44), channel_id=1, source_target_pairs={{0,4},{1,12},{2,20},{3,28},{4,0},{5,8},{6,16},{7,24},{8,5},{9,13},... | collective-permute-start | bytes 393224 | tf_op jit(solution)/shard_map/ppermute | solution.py:310
  318.9 17.8 %copy-start.14 = (f32[9,2048]{1,0:T(8,128)S(1)}, f32[9,2048]{1,0:T(8,128)}, u32[]{:S(2)}) copy-start(f32[9,2048]{1,0:T(8,128)} %param.17) | copy-start | bytes 221188
  320.2 38.9 %collective-permute-start.33 = (bf16[128,2048]{1,0:T(8,128)(2,1)}, bf16[128,2048]{1,0:T(8,128)(2,1)}, u32[]{:S(2)}, u32[]{:S(2)}) collective-permute-start(bf16[128,2048]{1,0:T(8,128)(2,1)} %get-tuple-element.18), channel_id=1, source_target_pairs={{0,8},{4,12},{8,0},{12,4},{16,24},{20,28},{24,16},{28,20},{1,9},{5... | collective-permute-start | bytes 1572872 | tf_op jit(solution)/shard_map/ppermute | solution.py:238
  335.3 29.0 %collective-permute-start.34 = (bf16[128,2048]{1,0:T(8,128)(2,1)}, bf16[128,2048]{1,0:T(8,128)(2,1)}, u32[]{:S(2)}, u32[]{:S(2)}) collective-permute-start(bf16[128,2048]{1,0:T(8,128)(2,1)} %get-tuple-element.20), channel_id=1, source_target_pairs={{0,16},{4,20},{8,24},{12,28},{16,0},{20,4},{24,8},{28,12},{1,17},{... | collective-permute-start | bytes 1572872 | tf_op jit(solution)/shard_map/ppermute | solution.py:238
  335.3 34.1 %collective-permute-start.35 = (bf16[128,2048]{1,0:T(8,128)(2,1)}, bf16[128,2048]{1,0:T(8,128)(2,1)}, u32[]{:S(2)}, u32[]{:S(2)}) collective-permute-start(bf16[128,2048]{1,0:T(8,128)(2,1)} %get-tuple-element.19), channel_id=1, source_target_pairs={{0,24},{4,28},{8,16},{12,20},{16,8},{20,12},{24,0},{28,4},{1,25},{... | collective-permute-start | bytes 1572872 | tf_op jit(solution)/shard_map/ppermute | solution.py:238
  371.7 82.4 %collective-permute-start.43 = (bf16[128,2048]{1,0:T(8,128)(2,1)S(1)}, bf16[128,2048]{1,0:T(8,128)(2,1)S(1)}, u32[]{:S(2)}, u32[]{:S(2)}) collective-permute-start(bf16[128,2048]{1,0:T(8,128)(2,1)S(1)} %fusion.3), channel_id=1, source_target_pairs={{0,0},{1,8},{2,16},{3,24},{4,4},{5,12},{6,20},{7,28},{8,1},{9,9},{... | collective-permute-start | bytes 1572872 | tf_op jit(solution)/shard_map/ppermute | solution.py:345
  372.4 81.7 %collective-permute-start.44 = (bf16[128,2048]{1,0:T(8,128)(2,1)S(1)}, bf16[128,2048]{1,0:T(8,128)(2,1)S(1)}, u32[]{:S(2)}, u32[]{:S(2)}) collective-permute-start(bf16[128,2048]{1,0:T(8,128)(2,1)S(1)} %fusion.3), channel_id=1, source_target_pairs={{0,1},{1,9},{2,17},{3,25},{4,5},{5,13},{6,21},{7,29},{8,0},{9,8},{... | collective-permute-start | bytes 1572872 | tf_op jit(solution)/shard_map/ppermute | solution.py:345
  372.5 81.7 %collective-permute-start.45 = (bf16[128,2048]{1,0:T(8,128)(2,1)S(1)}, bf16[128,2048]{1,0:T(8,128)(2,1)S(1)}, u32[]{:S(2)}, u32[]{:S(2)}) collective-permute-start(bf16[128,2048]{1,0:T(8,128)(2,1)S(1)} %fusion.3), channel_id=1, source_target_pairs={{0,2},{1,10},{2,18},{3,26},{4,6},{5,14},{6,22},{7,30},{8,3},{9,11}... | collective-permute-start | bytes 1572872 | tf_op jit(solution)/shard_map/ppermute | solution.py:345
  398.0 56.2 %collective-permute-start.46 = (bf16[128,2048]{1,0:T(8,128)(2,1)S(1)}, bf16[128,2048]{1,0:T(8,128)(2,1)}, u32[]{:S(2)}, u32[]{:S(2)}) collective-permute-start(bf16[128,2048]{1,0:T(8,128)(2,1)S(1)} %fusion.3), channel_id=1, source_target_pairs={{0,3},{1,11},{2,19},{3,27},{4,7},{5,15},{6,23},{7,31},{8,2},{9,10}... | collective-permute-start | bytes 1572872 | tf_op jit(solution)/shard_map/ppermute | solution.py:345
  399.2 1.3 collective-permute-start.36
  400.6 4.3 collective-permute-start.37
  404.8 3.9 collective-permute-start.38
  408.8 20.0 %collective-permute-start.39 = (bf16[128,256]{1,0:T(8,128)(2,1)S(1)}, bf16[128,256]{1,0:T(8,128)(2,1)S(1)}, u32[]{:S(2)}, u32[]{:S(2)}) collective-permute-start(bf16[128,256]{1,0:T(8,128)(2,1)S(1)} %bitcast.289), channel_id=1, source_target_pairs={{0,16},{4,20},{8,24},{12,28},{16,0},{20,4},{24,8},{28,12},{1,17},{... | collective-permute-start | bytes 196616 | tf_op jit(solution)/shard_map/ppermute | solution.py:238
  428.8 4.4 collective-permute-start.40
  433.2 14.4 %collective-permute-start.41 = (bf16[128,256]{1,0:T(8,128)(2,1)S(1)}, bf16[128,256]{1,0:T(8,128)(2,1)S(1)}, u32[]{:S(2)}, u32[]{:S(2)}) collective-permute-start(bf16[128,256]{1,0:T(8,128)(2,1)S(1)} %bitcast.287), channel_id=1, source_target_pairs={{0,24},{4,28},{8,16},{12,20},{16,8},{20,12},{24,0},{28,4},{1,25},{... | collective-permute-start | bytes 196616 | tf_op jit(solution)/shard_map/ppermute | solution.py:238
  447.6 5.1 %collective-permute-start.42 = (bf16[128,256]{1,0:T(8,128)(2,1)S(1)}, bf16[128,256]{1,0:T(8,128)(2,1)S(1)}, u32[]{:S(2)}, u32[]{:S(2)}) collective-permute-start(bf16[128,256]{1,0:T(8,128)(2,1)S(1)} %bitcast.286), channel_id=1, source_target_pairs={{0,28},{4,24},{8,20},{12,16},{16,12},{20,8},{24,4},{28,0},{1,29},{... | collective-permute-start | bytes 196616 | tf_op jit(solution)/shard_map/ppermute | solution.py:238
  460.6 7.7 %copy-start.1 = (bf16[2,96,2048]{2,1,0:T(8,128)(2,1)S(1)}, bf16[2,96,2048]{2,1,0:T(8,128)(2,1)}, u32[]{:S(2)}) copy-start(bf16[2,96,2048]{2,1,0:T(8,128)(2,1)} %param.16) | copy-start | bytes 2359300
  (9 other events, 16.8 us)
Sparse Core Ops, SparseCore 0:
  30.8 82.4 all-gather.5
  114.8 164.9 all-gather.7
  281.7 51.1 all-gather.9

commit v2 on v1

v2 whole, which is shorter than its diff:
```python
import functools

import jax
import jax.numpy as jnp
from jax import lax
from jax.experimental import pallas as pl
from jax.experimental.pallas import tpu as pltpu
from jax.sharding import PartitionSpec as P

LMAX = 128
HEAD = 64
F32 = jnp.float32
BF16 = jnp.bfloat16


def bdot(a, b, ca=1, cb=0):
    return lax.dot_general(
        a.astype(BF16), b.astype(BF16), (((ca,), (cb,)), ((), ())), preferred_element_type=F32
    )


def halves(x):
    top = x.astype(BF16)
    return top, (x - top.astype(F32)).astype(BF16)


def dot3(a, b, ca=1, cb=0):
    ah, al = halves(a)
    bh, bl = halves(b)
    return bdot(ah, bh, ca, cb) + (bdot(ah, bl, ca, cb) + bdot(al, bh, ca, cb))


def head_sums(x, same):
    top, low = halves(x)
    return bdot(top, same) + bdot(low, same)


def time_kernel(nb, nc, per, place_ref, lens, *refs):
    xg = refs[:nb]
    norms, shift, ld, lu, co = refs[nb : nb + 5]
    wt = refs[nb + 5 : nb + 5 + nc]
    even, odd, own, state_ref, mixes, w, sems = refs[-7:]
    rows = per * LMAX
    fw = xg[0].shape[1]
    width = nb * fw
    hc = w.shape[-1]
    chunk = even.shape[1]
    row, col = place_ref[0], place_ref[1]

    @pl.when(pl.program_id(0) == 0)
    def _():
        copies = [
            pltpu.make_async_copy(wt[k].at[:, m], w.at[m, :, col ^ k], sems.at[m, k])
            for m in range(4)
            for k in range(nc)
        ]
        for copy in copies:
            copy.start()
        for copy in copies:
            copy.wait()

    weight = [w[m].reshape(width, hc) for m in range(4)]
    blocks = [x[...].astype(F32) for x in xg]
    total = sum(jnp.sum(b, axis=1, keepdims=True) for b in blocks)
    square = sum(jnp.sum(b * b, axis=1, keepdims=True) for b in blocks)
    center = total / width
    scale = lax.rsqrt(square / width - center * center + 1e-05)
    first_row = lax.broadcasted_iota(jnp.int32, (rows, fw), 0) % LMAX == 0
    for i in range(nb):
        at = row ^ i
        lanes = pl.ds(pl.multiple_of(at * fw, fw), fw)
        z = (xg[i][...].astype(F32) - center) * scale * norms[at, 0:1] + norms[at, 1:2]
        z = z.astype(BF16).astype(F32)
        step = jnp.where(first_row, 0.0, pltpu.roll(z, 1, 0)) - z
        for j in range(5):
            mixes[j, :, lanes] = (z + step * shift[at, j : j + 1]).astype(BF16)
    r = bdot(mixes[0], weight[0])
    k = bdot(mixes[1], weight[1])
    v = bdot(mixes[2], weight[2])
    dl = bdot(mixes[3], ld[0])
    al = bdot(mixes[4], ld[1])
    logd = -0.606531 * jax.nn.sigmoid(co[0:1] + bdot(jnp.tanh(dl), lu[0]))
    rate = jax.nn.sigmoid(co[1:2] + bdot(al, lu[1]))
    lane_a = lax.broadcasted_iota(jnp.int32, (hc, hc), 0) // HEAD
    lane_b = lax.broadcasted_iota(jnp.int32, (hc, hc), 1) // HEAD
    same = (lane_a == lane_b).astype(BF16)
    kappa = k * co[2:3]
    kappa = kappa * lax.rsqrt(head_sums(kappa * kappa, same) + 1e-05)
    t_of = lax.broadcasted_iota(jnp.int32, (LMAX, LMAX), 0)
    u_of = lax.broadcasted_iota(jnp.int32, (LMAX, LMAX), 1)
    upto = u_of <= t_of
    before = u_of < t_of
    lower = upto.astype(BF16)
    low_lane = u_of < HEAD
    side = jnp.concatenate([low_lane, low_lane], axis=0)
    levels = [((t_of >> n) == (u_of >> n) + 1) & (((t_of >> n) & 1) == 1) for n in range(7)]
    eye = (t_of == u_of).astype(F32)
    place = lax.broadcasted_iota(jnp.int32, (LMAX, hc), 0)
    chains = []
    keep = []
    for p in range(per):
        at = slice(p * LMAX, (p + 1) * LMAX)
        live = (place < lens[pl.program_id(0) * per + p]).astype(F32)
        rp, kp, vp = r[at], k[at] * live, v[at] * live
        dp = logd[at] * live
        kh = kappa[at] * live
        wr = kh * rate[at]
        d1 = dp.astype(BF16)
        d2, d3 = halves(dp - d1.astype(F32))
        cum = bdot(lower, d1) + (bdot(lower, d2) + bdot(lower, d3))
        last = cum[LMAX - 1 : LMAX]
        mid = 0.5 * last
        grow = jnp.exp(mid - cum)
        tail = jnp.exp(last - mid)
        pull = -kh * jnp.exp(cum - dp - mid)
        read = rp * jnp.exp(cum - mid)
        wb = wr * grow
        kb = kp * grow
        keep.append((live, head_sums(rp * kp * co[3:4], same) * vp))
        for q in range(hc // 128):
            ln = slice(q * 128, (q + 1) * 128)
            right = jnp.concatenate([wb[:, ln], kb[:, ln]], axis=0)
            left = jnp.concatenate([pull[:, ln], read[:, ln]], axis=0)
            pair = []
            for h in range(2):
                g = bdot(jnp.where(side == (h == 0), left, 0.0), right, 1, 1)
                pair.append(
                    (
                        jnp.where(before, g[:LMAX, :LMAX], 0.0),
                        jnp.where(before, g[:LMAX, LMAX:], 0.0),
                        jnp.where(upto, g[LMAX:, :LMAX], 0.0),
                        jnp.where(upto, g[LMAX:, LMAX:], 0.0),
                    )
                )
            chains.append((p, q, pair, vp[:, ln], wb[:, ln] * tail[:, ln], kb[:, ln] * tail[:, ln]))
    strict = [c[2][h][0] for c in chains for h in range(2)]
    inverse = [eye + jnp.where(levels[0], a, 0.0) for a in strict]
    for n in range(1, 7):
        inner = [dot3(jnp.where(levels[n], a, 0.0), t) for a, t in zip(strict, inverse)]
        inverse = [t + dot3(t, m) for t, m in zip(inverse, inner)]
    outs = {}
    for i, (p, q, pair, vq, wt, kt) in enumerate(chains):
        us, ys = [], []
        for h in range(2):
            _, b, rw, rk = pair[h]
            u = dot3(inverse[2 * i + h], bdot(b, vq))
            us.append(u)
            ys.append(bdot(jnp.concatenate([rw, rk], axis=1), jnp.concatenate([u, vq], axis=0)))
        u = jnp.where(low_lane, us[0], us[1])
        outs[p, q] = jnp.where(low_lane, ys[0], ys[1])
        final = bdot(jnp.concatenate([u, vq], axis=0), jnp.concatenate([wt, kt], axis=0), 0, 0)
        state_ref[p, 2 * q] = final[:HEAD, :HEAD].astype(BF16)
        state_ref[p, 2 * q + 1] = final[HEAD:, HEAD:].astype(BF16)
    atts = []
    for p in range(per):
        live, extra = keep[p]
        y = jnp.concatenate([outs[p, q] for q in range(hc // 128)], axis=1)
        y = (y + extra) * live
        y = y - head_sums(y, same) / HEAD
        spread = head_sums(y * y, same) / HEAD
        atts.append((y * lax.rsqrt(spread + 0.00064) * co[4:5] + co[5:6]).astype(BF16))
    partial = bdot(jnp.concatenate(atts, axis=0), weight[3], 1, 1).astype(BF16)
    pieces = rows // chunk
    for t in range(pieces):
        n = pl.program_id(0) * pieces + t
        to = row ^ ((n % (nb // 2)) * 2 + n // (nb // 2))
        here = slice(t * chunk, (t + 1) * chunk)

        @pl.when(to == 0)
        def _():
            for i in range(nb):
                own[:, pl.ds(pl.multiple_of((row ^ i) * fw, fw), fw)] = xg[i][here]

        @pl.when(to % 2 == 0)
        def _():
            even[to // 2] = partial[here]

        @pl.when(to % 2 == 1)
        def _():
            odd[to // 2] = partial[here]


def time_mix(place, lens, xg, norms, shift, ld, lu, co, wt, extra, per):
    nb, nc = len(xg), len(wt)
    tokens, fw = xg[0].shape
    prompts = tokens // LMAX
    _, _, deep, hc = wt[0].shape
    width, chunk = nb * fw, tokens // nb

    def full(a):
        return pl.BlockSpec(a.shape, lambda i: (0,) * a.ndim)

    whole = pl.BlockSpec((nb // 2, chunk, width), lambda i: (0, 0, 0))
    rest = (norms, shift, ld, lu, co)
    return pl.pallas_call(
        functools.partial(time_kernel, nb, nc, per),
        grid=(prompts // per,),
        in_specs=[pl.BlockSpec(memory_space=pltpu.SMEM)] * 2
        + [pl.BlockSpec((per * LMAX, fw), lambda i: (i, 0))] * nb
        + [full(a) for a in rest]
        + [pl.BlockSpec(memory_space=pl.ANY)] * (nc + len(extra)),
        out_specs=[
            whole,
            whole,
            pl.BlockSpec((chunk, width), lambda i: (0, 0)),
            pl.BlockSpec((per, hc // HEAD, HEAD, HEAD), lambda i: (i, 0, 0, 0)),
        ],
        out_shape=[
            jax.ShapeDtypeStruct((nb // 2, chunk, width), BF16),
            jax.ShapeDtypeStruct((nb // 2, chunk, width), BF16),
            jax.ShapeDtypeStruct((chunk, width), BF16),
            jax.ShapeDtypeStruct((prompts, hc // HEAD, HEAD, HEAD), BF16),
        ],
        scratch_shapes=[
            pltpu.VMEM((5, per * LMAX, width), BF16),
            pltpu.VMEM((4, nb, nc, deep, hc), BF16),
            pltpu.SemaphoreType.DMA((4, nc)),
        ],
        compiler_params=pltpu.CompilerParams(vmem_limit_bytes=50 * 2**20),
        cost_estimate=pl.CostEstimate(flops=40 * 10**9, bytes_accessed=2**24, transcendentals=0),
    )(place, lens, *xg, *rest, *wt, *extra)


def shifted_mix(z, weight):
    first_row = lax.broadcasted_iota(jnp.int32, z.shape, 0) % LMAX == 0
    return (z + (jnp.where(first_row, 0.0, pltpu.roll(z, 1, 0)) - z) * weight).astype(BF16)


def settle_kernel(count, *refs):
    pieces = refs[:count]
    base, gains, out, normal, blend = refs[count:]
    total = base[...].astype(F32)
    attn = pieces[0][...].astype(F32)
    for piece in pieces[1:]:
        attn = attn + piece[...].astype(F32)
    total = (total + attn).astype(BF16)
    out[...] = total
    z = total.astype(F32)
    width = z.shape[1]
    center = jnp.sum(z, axis=1, keepdims=True) / width
    second = jnp.sum(z * z, axis=1, keepdims=True) / width
    z = (z - center) * lax.rsqrt(second - center * center + 1e-05) * gains[0:1] + gains[1:2]
    z = z.astype(BF16)
    normal[...] = z
    blend[...] = shifted_mix(z.astype(F32), gains[2:3])


def settle(pieces, base, gains):
    spec = pl.BlockSpec(memory_space=pltpu.VMEM)
    return pl.pallas_call(
        functools.partial(settle_kernel, len(pieces)),
        in_specs=[spec] * (len(pieces) + 2),
        out_specs=[spec] * 3,
        out_shape=[jax.ShapeDtypeStruct(base.shape, BF16)] * 3,
        compiler_params=pltpu.CompilerParams(vmem_limit_bytes=24 * 2**20),
        cost_estimate=pl.CostEstimate(flops=10**8, bytes_accessed=2**22, transcendentals=0),
    )(*pieces, base, gains)


def mlp_kernel(nc, chunk, *refs):
    xa, xb, late = refs[:3]
    pa, pb, w, sems = refs[-4:]
    width = xa.shape[1]
    copies = [
        [pltpu.make_async_copy(late.at[c, :, m], w.at[m, :, c], sems.at[m, c]) for c in range(nc)] for m in range(2)
    ]
    for copy in copies[0] + copies[1]:
        copy.start()
    x = jnp.concatenate([xa[...], xb[...]], axis=0)
    for copy in copies[0]:
        copy.wait()
    pre = bdot(x, w[0].reshape(width, -1))
    act = jnp.square(jnp.maximum(pre, 0.0)).astype(BF16)
    for copy in copies[1]:
        copy.wait()
    out = bdot(act, w[1].reshape(width, -1), 1, 1).astype(BF16)
    pa[...] = out[:chunk]
    pb[...] = out[chunk:]


def mlp_products(xa, xb, late, extra):
    nc, nb, _, deep, ff = late.shape
    chunk = xa.shape[0]
    spec = pl.BlockSpec(memory_space=pltpu.VMEM)
    apart = pl.BlockSpec(memory_space=pl.ANY)
    return pl.pallas_call(
        functools.partial(mlp_kernel, nc, chunk),
        in_specs=[spec, spec, apart] + [apart] * len(extra),
        out_specs=[spec, spec],
        out_shape=[jax.ShapeDtypeStruct(xa.shape, BF16)] * 2,
        scratch_shapes=[pltpu.VMEM((2, nb, nc, deep, ff), BF16), pltpu.SemaphoreType.DMA((2, nc))],
        compiler_params=pltpu.CompilerParams(vmem_limit_bytes=40 * 2**20),
        cost_estimate=pl.CostEstimate(flops=4 * 10**9, bytes_accessed=2**23, transcendentals=0),
    )(xa, xb, late, *extra)


def next_kernel(nb, nc, place_ref, *refs):
    xs = refs[:nc]
    gate = refs[nc]
    given = refs[nc + 1 : nc + 1 + nb]
    out, x, w, sems = refs[-4:]
    row, col = place_ref[0], place_ref[1]
    copies = [
        pltpu.make_async_copy(given[i].at[k], w.at[:, row ^ i, col ^ k], sems.at[i, k])
        for i in range(nb)
        for k in range(nc)
    ]
    for copy in copies:
        copy.start()
    chunk, width = xs[0].shape
    for k in range(nc):
        x[pl.ds(pl.multiple_of((col ^ k) * chunk, chunk), chunk), :] = xs[k][...]
    z = x[...].astype(F32)
    mixed = [shifted_mix(z, gate[m : m + 1]) for m in range(3)]
    for copy in copies:
        copy.wait()
    for m in range(3):
        out[m] = bdot(mixed[m], w[m].reshape(width, -1)).astype(BF16)


def next_products(place, xs, gate, given):
    nb, nc = len(given), len(xs)
    chunk, width = xs[0].shape
    _, _, deep, cols = given[0].shape
    spec = pl.BlockSpec(memory_space=pltpu.VMEM)
    return pl.pallas_call(
        functools.partial(next_kernel, nb, nc),
        in_specs=[pl.BlockSpec(memory_space=pltpu.SMEM)]
        + [spec] * (nc + 1)
        + [pl.BlockSpec(memory_space=pl.ANY)] * nb,
        out_specs=spec,
        out_shape=jax.ShapeDtypeStruct((3, nc * chunk, cols), BF16),
        scratch_shapes=[
            pltpu.VMEM((nc * chunk, width), BF16),
            pltpu.VMEM((3, nb, nc, deep, cols), BF16),
            pltpu.SemaphoreType.DMA((nb, nc)),
        ],
        compiler_params=pltpu.CompilerParams(vmem_limit_bytes=50 * 2**20),
        cost_estimate=pl.CostEstimate(flops=6 * 10**9, bytes_accessed=2**24, transcendentals=0),
    )(place, *xs, gate, *given)


def per_device(
    hidden,
    lengths,
    square_matrix_shards,
    channel_mix_shards,
    lowrank_down,
    lowrank_up,
    token_shift_weights,
    attention_coefficients,
    norm_parameters,
):
    n_row = lax.axis_size("row")
    n_col = lax.axis_size("col")
    row = lax.axis_index("row")
    col = lax.axis_index("col")
    chips = n_row // 2
    tokens, fw = hidden.shape
    width = token_shift_weights.shape[1]
    chunk = tokens // n_row
    deep = square_matrix_shards.shape[1]
    hc = width // n_row
    place = jnp.stack([row, col]).astype(jnp.int32)

    def to_row(x, k):
        return lax.ppermute(x, "row", [(i, i ^ k) for i in range(n_row)])

    def to_col(x, k):
        return lax.ppermute(x, "col", [(i, i ^ k) for i in range(n_col)])

    def chunk_of(r):
        return (r % 2) * chips + r // 2

    def row_of(n):
        return (n % chips) * 2 + n // chips

    def gather_row(x):
        mine = [x] + [to_row(x, 2 * k) for k in range(1, chips)]
        return [piece for m in mine for piece in (m, to_row(m, 1))]

    xg = gather_row(hidden)
    norms = lax.all_gather(norm_parameters, "row", axis=0, tiled=False)
    square_low = square_matrix_shards.astype(BF16)
    early = square_low[0:4].reshape(4, deep, n_row, hc).transpose(2, 0, 1, 3)
    early = lax.all_to_all(early, "row", 0, 0, tiled=True)
    early = [early] + [to_col(early, k) for k in range(1, n_col)]
    ff = channel_mix_shards.shape[2] // n_row
    late = channel_mix_shards.astype(BF16).reshape(2, deep, n_row, ff).transpose(2, 0, 1, 3)
    late_row = lax.all_to_all(late.reshape(n_row, 2 * deep, ff), "row", 0, 0, tiled=True)
    late = lax.all_gather(late_row.reshape(n_row * 2 * deep, ff), "col", axis=0, tiled=True)
    late = late.reshape(n_col, n_row, 2, deep, ff)
    cols = width // n_col
    last = square_low[4:7].reshape(3, deep, n_col, cols).transpose(2, 0, 1, 3)
    sent = [lax.dynamic_index_in_dim(last, col ^ k, 0, keepdims=False) for k in range(n_col)]
    last = jnp.stack([sent[0]] + [to_col(sent[k], k) for k in range(1, n_col)])
    last = gather_row(last)

    prompts = tokens // LMAX
    lens = lax.dynamic_slice_in_dim(lengths, col * prompts, prompts, 0)
    shift = token_shift_weights.reshape(-1, n_row, fw).transpose(1, 0, 2)
    up = lax.dynamic_slice_in_dim(lowrank_up, row * hc, hc, 2)
    co = lax.dynamic_slice_in_dim(attention_coefficients, row * hc, hc, 1)
    even, odd, own, states = time_mix(
        place, lens, xg, norms, shift, lowrank_down, up, co, early, (late_row,), 2
    )

    half = prompts // 2
    share = n_row // n_col
    states = states.reshape(2, half, states.shape[1], HEAD, HEAD)
    moved = []
    for j in range(2):
        pairs = []
        for r in range(n_row):
            for c in range(n_col):
                h = (r % 2) ^ j
                pairs.append((r * n_col + c, (2 * c + h) * n_col + r // share))
        piece = lax.dynamic_index_in_dim(states, (row % 2) ^ j, 0, keepdims=False)
        moved.append(lax.ppermute(piece, ("row", "col"), pairs))
    moved = jnp.take(jnp.stack(moved), (row % 2) ^ jnp.arange(2), axis=0)
    final_state = moved.transpose(1, 0, 2, 3, 4).reshape(half, -1, HEAD * HEAD).astype(F32)

    other = to_row(odd, 1)
    near = [(even[k].astype(F32) + other[k].astype(F32)).astype(BF16) for k in range(chips)]
    pieces = [near[0]] + [to_row(near[k], 2 * k) for k in range(1, chips)]
    gains = norms.transpose(1, 0, 2).reshape(-1, width)
    mid, second, channel_in = settle(
        pieces, own, jnp.concatenate([gains[2:4], token_shift_weights[5:6]], axis=0)
    )
    if chunk % LMAX:
        pairs = [(row_of(n), row_of(n + 1)) for n in range(n_row - 1)]
        edge = lax.ppermute(second[-1:], "row", pairs).astype(F32)
        edge = jnp.where(chunk_of(row) * chunk % LMAX == 0, 0.0, edge)
        wide = second.astype(F32)
        moved_on = jnp.concatenate([edge, wide[:-1]], axis=0)
        channel_in = (wide + (moved_on - wide) * token_shift_weights[5]).astype(BF16)
    rows_in = gather_row(channel_in)
    pieces = [None] * chips
    for k in reversed(range(chips)):
        mine, theirs = mlp_products(rows_in[2 * k], rows_in[2 * k + 1], late, last if k == chips - 1 else ())
        total = (mine.astype(F32) + to_row(theirs, 1).astype(F32)).astype(BF16)
        pieces[k] = to_row(total, 2 * k) if k else total
    out_own, third, _ = settle(
        pieces, mid, jnp.concatenate([gains[4:6], token_shift_weights[5:6]], axis=0)
    )

    arrived = []
    for j in range(n_col):
        pairs = []
        for r in range(n_row):
            for c in range(n_col):
                pairs.append((r * n_col + c, (2 * c + r % 2) * n_col + ((r // 2) ^ j)))
        arrived.append(lax.ppermute(third, ("row", "col"), pairs))
    out_blocks = lax.all_to_all(out_own.reshape(chunk, n_row, fw).transpose(1, 0, 2), "row", 0, 0, tiled=True)
    out_hidden = jnp.concatenate([out_blocks[row_of(n)] for n in range(n_row)], axis=0)
    next_rkv = next_products(place, arrived, token_shift_weights[6:9], last)
    return (out_hidden, next_rkv, final_state)


def solution(mesh):
    return jax.shard_map(
        per_device,
        mesh=mesh,
        in_specs=(
            P("col", "row"),
            P(),
            P(None, ("row", "col"), None),
            P(None, ("row", "col"), None),
            P(),
            P(),
            P(),
            P(),
            P(None, "row"),
        ),
        out_specs=(P("col", "row"), P(None, "row", "col"), P("row", "col", None)),
        check_vma=False,
    )
```

time: 484 us -> 584 us (1.21)
  the two profiles are of different devices: /device:TPU:0 before, /device:TPU:12 now
where the time goes in v2:
time: 584 us; the launch traced here: 580 us
  waiting for transfers between devices  343 us (59%)
  Pallas kernels  87.9 us (15%)
  starting transfers between devices  54.5 us (9%)
  blocking collectives  39 us (7%)
  local copies, waits for them, and re-layouts  30.1 us (5%)
  between operations  14.8 us (3%)
  other arithmetic  11.1 us (2%)
    ppermute x6, waiting for transfers between devices, to_col(): return lax.ppermute(x, 'col', [(i, i ^ k) for i in range(n_col)])  176 us
    ppermute x32, waiting for transfers between devices, to_row(): return lax.ppermute(x, 'row', [(i, i ^ k) for i in range(n_row)])  130 us
    pallas_call x1, Pallas kernels, time_mix(): pl.pallas_call(functools.partial(time_kernel, nb, nc, per), grid=(prompts...  52.6 us
    ppermute x4, waiting for transfers between devices, per_device(): arrived.append(lax.ppermute(third, ('row', 'col'), pairs))  37.3 us
    all_to_all x1, blocking collectives, per_device(): lax.all_to_all(late.reshape(n_row, 2 * deep, ff), 'row', 0, 0, tiled=True)  29.3 us
    ppermute x32, starting transfers between devices, to_row(): return lax.ppermute(x, 'row', [(i, i ^ k) for i in range(n_row)])  19.6 us
    pallas_call x4, Pallas kernels, mlp_products(): pl.pallas_call(functools.partial(mlp_kernel, nc, chunk), in_specs=[spec,...  19.4 us
    unnamed x59, local copies, waits for them, and re-layouts  17.4 us
  transfers between devices with their start and end apart: 47, of which 18 were waited for; matrix products, arithmetic and copies ran while one was open for 5% of the time, Pallas kernels for 13%

profile of v2, /device:TPU:12, one launch (start us, length us, event | category | flops | bytes accessed | tf_op | source)
XLA Modules:
  0.0 580.3 jit_solution(13455311015855024802)
XLA Ops:
  7.2 2.5 convert_element_type.107
  9.9 29.3 %all_to_all.15.refs_17_ = bf16[8,128,1024]{2,1,0:T(8,128)(2,1)} all-to-all(bf16[8,128,1024]{2,1,0:T(8,128)(2,1)S(1)} %bitcast.113), channel_id=1, replica_groups=mesh['row'=8,'col'=4] {'row'}, dimensions={0} | all-to-all | bytes 4194304 | tf_op jit(solution)/shard_map/all_to_all | solution.py:390
  39.2 2.3 convert_element_type.106
  41.6 1.1 copy-done.16
  42.7 1.1 copy.65
  43.8 5.8 all-to-all-start
  49.6 1.5 collective-permute-start.1
  51.6 1.5 collective-permute-start.5
  53.1 22.2 %collective-permute-done.1.refs_2_ = bf16[1024,256]{1,0:T(8,128)(2,1)S(1)} collective-permute-done((bf16[1024,256]{1,0:T(8,128)(2,1)S(1)}, bf16[1024,256]{1,0:T(8,128)(2,1)S(1)}, u32[]{:S(2)}, u32[]{:S(2)}) %collective-permute-start.1) | collective-permute-done | bytes 524320 | tf_op jit(solution)/shard_map/ppermute | solution.py:367
  75.8 2.6 collective-permute-start.8
  78.8 7.3 %collective-permute-done.5.refs_6_ = bf16[1024,256]{1,0:T(8,128)(2,1)} collective-permute-done((bf16[1024,256]{1,0:T(8,128)(2,1)S(1)}, bf16[1024,256]{1,0:T(8,128)(2,1)}, u32[]{:S(2)}, u32[]{:S(2)}) %collective-permute-start.5) | collective-permute-done | bytes 524320 | tf_op jit(solution)/shard_map/ppermute | solution.py:367
  86.8 2.2 copy.41.refs_10_
  89.1 9.7 %all-gather.1.refs_8_ = f32[8,6,256]{2,1,0:T(8,128)S(1)} all-gather(f32[1,6,256]{2,1,0:T(8,128)S(1)} %bitcast.126), channel_id=2, replica_groups=mesh['row'=8,'col'=4] {'row'}, dimensions={0}, use_global_device_ids=true | all-gather | bytes 55296 | tf_op jit(solution)/shard_map/all_gather | solution.py:383
  99.6 67.2 %collective-permute-done.7.refs_14_ = bf16[8,4,64,256]{3,2,1,0:T(8,128)(2,1)} collective-permute-done((bf16[8,4,64,256]{3,2,1,0:T(8,128)(2,1)}, bf16[8,4,64,256]{3,2,1,0:T(8,128)(2,1)}, u32[]{:S(2)}, u32[]{:S(2)}) %collective-permute-start.7) | collective-permute-done | bytes 1048608 | tf_op jit(solution)/shard_map/ppermute | solution.py:370
  166.8 3.5 collective-permute-done.8.refs_15_
  170.2 96.3 %collective-permute-done.9.refs_16_ = bf16[8,4,64,256]{3,2,1,0:T(8,128)(2,1)} collective-permute-done((bf16[8,4,64,256]{3,2,1,0:T(8,128)(2,1)}, bf16[8,4,64,256]{3,2,1,0:T(8,128)(2,1)}, u32[]{:S(2)}, u32[]{:S(2)}) %collective-permute-start.9) | collective-permute-done | bytes 1048608 | tf_op jit(solution)/shard_map/ppermute | solution.py:370
  266.6 1.0 copy-done.13
  267.6 52.6 %shard_map.112 = (bf16[4,128,2048]{2,1,0:T(8,128)(2,1)}, bf16[4,128,2048]{2,1,0:T(8,128)(2,1)}, bf16[128,2048]{1,0:T(8,128)(2,1)S(1)}, bf16[8,4,64,64]{3,2,1,0:T(8,128)(2,1)S(1)}) custom-call(s32[2]{0:T(128)S(1)} %pad_add_fusion.place_ref, s32[8]{0:T(128)S(1)} %dynamic_slice.23.lens, bf16[1024,256]{1,0:T(8,128)(2,1)S(1)} %copy-done.11, ...), custom_call_target="tpu_custom_call" | custom-call | flops 40000000000 | bytes 16777216 | tf_op jit(solution)/shard_map/pallas_call | solution.py:195
  320.3 4.4 collective-permute-done.10
  324.7 3.2 fusion.3
  327.9 1.6 collective-permute-start.11
  330.1 1.6 constant_dynamic-slice_fusion.3
  332.3 3.2 collective-permute-start.26
  336.1 7.7 %collective-permute-done.28 = bf16[3,64,512]{2,1,0:T(8,128)(2,1)S(1)} collective-permute-done((bf16[3,64,512]{2,1,0:T(8,128)(2,1)S(1)}, bf16[3,64,512]{2,1,0:T(8,128)(2,1)S(1)}, u32[]{:S(2)}, u32[]{:S(2)}) %collective-permute-start.28) | collective-permute-done | bytes 196640 | tf_op jit(solution)/shard_map/ppermute | solution.py:370
  343.8 1.2 collective-permute-done.27
  345.2 1.1 collective-permute-start.30
  346.9 1.9 collective-permute-start.13
  349.7 1.1 collective-permute-start.34
  350.8 26.1 %collective-permute-done.13.refs_3_ = bf16[128,2048]{1,0:T(8,128)(2,1)S(1)} collective-permute-done((bf16[128,2048]{1,0:T(8,128)(2,1)S(1)}, bf16[128,2048]{1,0:T(8,128)(2,1)S(1)}, u32[]{:S(2)}, u32[]{:S(2)}) %collective-permute-start.13) | collective-permute-done | bytes 524320 | tf_op jit(solution)/shard_map/ppermute | solution.py:367
  377.0 2.9 shard_map.113
  380.7 1.1 collective-permute-start.16
  381.8 1.5 collective-permute-start.20
  383.3 11.5 %collective-permute-done.32.refs_7_.refs_9_ = bf16[4,3,64,512]{3,2,1,0:T(8,128)(2,1)S(1)} collective-permute-done((bf16[4,3,64,512]{3,2,1,0:T(8,128)(2,1)S(1)}, bf16[4,3,64,512]{3,2,1,0:T(8,128)(2,1)S(1)}, u32[]{:S(2)}, u32[]{:S(2)}) %collective-permute-start.32) | collective-permute-done | bytes 786464 | tf_op jit(solution)/shard_map/ppermute | solution.py:367
  394.7 0.9 copy-done.5
  395.6 9.4 %collective-permute-done.16.refs_0_ = bf16[128,2048]{1,0:T(8,128)(2,1)S(1)} collective-permute-done((bf16[128,2048]{1,0:T(8,128)(2,1)}, bf16[128,2048]{1,0:T(8,128)(2,1)S(1)}, u32[]{:S(2)}, u32[]{:S(2)}) %collective-permute-start.16) | collective-permute-done | bytes 524320 | tf_op jit(solution)/shard_map/ppermute | solution.py:367
  405.0 0.9 slice.96.refs_4_
  406.6 10.0 %collective-permute-done.20.refs_0_ = bf16[128,2048]{1,0:T(8,128)(2,1)} collective-permute-done((bf16[128,2048]{1,0:T(8,128)(2,1)}, bf16[128,2048]{1,0:T(8,128)(2,1)}, u32[]{:S(2)}, u32[]{:S(2)}) %collective-permute-start.20) | collective-permute-done | bytes 524320 | tf_op jit(solution)/shard_map/ppermute | solution.py:367
  417.2 3.4 copy-done.2
  420.6 4.6 shard_map.114
  425.3 4.3 shard_map.115
  430.1 4.7 shard_map.116
  435.4 5.8 %shard_map.117 = (bf16[128,2048]{1,0:T(8,128)(2,1)S(1)}, bf16[128,2048]{1,0:T(8,128)(2,1)S(1)}) custom-call(bf16[128,2048]{1,0:T(8,128)(2,1)} %collective-permute-done.24.refs_0_, bf16[128,2048]{1,0:T(8,128)(2,1)S(1)} %collective-permute-done.25.refs_1_, bf16[4,8,2,64,1024]{4,3,2,1,0:T(8,128)(2,1)} %bitcast.103, ...), custom_call_target="tpu_custom_call" | custom-call | flops 4000000000 | bytes 8388608 | tf_op jit(solution)/shard_map/pallas_call | solution.py:286
  441.5 1.0 collective-permute-start.19
  443.6 1.9 collective-permute-start.37
  445.5 1.6 collective-permute-start.43
  447.1 3.4 collective-permute-start.42
  450.7 5.6 collective-permute-done.19.refs_1_
  456.3 1.5 collective-permute-done.23.refs_2_
  457.9 31.4 %collective-permute-done.37.refs_3_ = bf16[128,2048]{1,0:T(8,128)(2,1)S(1)} collective-permute-done((bf16[128,2048]{1,0:T(8,128)(2,1)S(1)}, bf16[128,2048]{1,0:T(8,128)(2,1)S(1)}, u32[]{:S(2)}, u32[]{:S(2)}) %collective-permute-start.37) | collective-permute-done | bytes 524320 | tf_op jit(solution)/shard_map/ppermute | solution.py:367
  489.3 1.8 shard_map.118
  491.9 4.1 all-to-all-start.2
  496.0 1.1 pad_maximum_fusion.1
  497.2 1.4 gather_fusion
  498.6 1.2 convert_bitcast_fusion
  499.8 1.1 copy.47
  500.9 2.4 reshape.92
  503.2 4.9 collective-permute-start.38
  508.1 3.0 collective-permute-start.39
  511.2 4.9 collective-permute-start.41
  522.8 21.8 %collective-permute-done.38.refs_0_ = bf16[128,2048]{1,0:T(8,128)(2,1)S(1)} collective-permute-done((bf16[128,2048]{1,0:T(8,128)(2,1)S(1)}, bf16[128,2048]{1,0:T(8,128)(2,1)S(1)}, u32[]{:S(2)}, u32[]{:S(2)}) %collective-permute-start.38) | collective-permute-done | bytes 524320 | tf_op jit(solution)/shard_map/ppermute | solution.py:453
  545.4 11.9 %collective-permute-done.39.refs_1_ = bf16[128,2048]{1,0:T(8,128)(2,1)} collective-permute-done((bf16[128,2048]{1,0:T(8,128)(2,1)S(1)}, bf16[128,2048]{1,0:T(8,128)(2,1)}, u32[]{:S(2)}, u32[]{:S(2)}) %collective-permute-start.39) | collective-permute-done | bytes 524320 | tf_op jit(solution)/shard_map/ppermute | solution.py:453
  557.3 3.6 collective-permute-done.41.refs_3_
  560.9 1.0 copy-done.15
  561.9 11.2 %shard_map.119 = bf16[3,512,512]{2,1,0:T(8,128)(2,1)} custom-call(s32[2]{0:T(128)S(1)} %pad_add_fusion.place_ref, bf16[128,2048]{1,0:T(8,128)(2,1)S(1)} %copy-done.15, bf16[128,2048]{1,0:T(8,128)(2,1)} %collective-permute-done.39.refs_1_, bf16[128,2048]{1,0:T(8,128)(2,1)} %collective-permute-done.40.refs_2_, ...), custom_call_target="tpu_custom_call" | custom-call | flops 6000000000 | bytes 16777216 | tf_op jit(solution)/shard_map/pallas_call | solution.py:326
  (136 shorter events, 19.8 us)
Async XLA Ops:
  7.2 92.4 %copy-start = (bf16[2,96,2048]{2,1,0:T(8,128)(2,1)S(1)}, bf16[2,96,2048]{2,1,0:T(8,128)(2,1)}, u32[]{:S(2)}) copy-start(bf16[2,96,2048]{2,1,0:T(8,128)(2,1)} %param.14) | copy-start | bytes 2359300
  7.2 410.0 %all-gather.4.cloned.1.call-start = ((), (), s32[]{:S(2)}) async-start(), calls=%async_computation.3 | async-start | bytes 10485760 | tf_op jit(solution)/shard_map/all_gather | solution.py:391
  42.7 6.9 %copy-start.11 = (bf16[1024,256]{1,0:T(8,128)(2,1)S(1)}, bf16[1024,256]{1,0:T(8,128)(2,1)}, u32[]{:S(2)}) copy-start(bf16[1024,256]{1,0:T(8,128)(2,1)} %refs_0_.1) | copy-start | bytes 1572868
  42.7 43.9 %copy-start.19 = (f32[9,2048]{1,0:T(8,128)S(1)}, f32[9,2048]{1,0:T(8,128)}, u32[]{:S(2)}) copy-start(f32[9,2048]{1,0:T(8,128)} %param.15) | copy-start | bytes 221188
  43.8 45.2 %copy-start.22 = (s32[32]{0:T(128)S(1)}, s32[32]{0:T(128)}, u32[]{:S(2)}) copy-start(s32[32]{0:T(128)} %param.10) | copy-start | bytes 388
  43.8 45.2 %copy-start.20 = (f32[6,256]{1,0:T(8,128)S(1)}, f32[6,256]{1,0:T(8,128)}, u32[]{:S(2)}) copy-start(f32[6,256]{1,0:T(8,128)} %param.17) | copy-start | bytes 18436
  43.8 31.5 %all-to-all-start = ((bf16[8,4,64,256]{3,2,1,0:T(8,128)(2,1)}), bf16[8,4,64,256]{3,2,1,0:T(8,128)(2,1)}, u32[]{:S(2)}, u32[]{:S(2)}) async-start(bf16[8,4,64,256]{3,2,1,0:T(8,128)(2,1)} %bitcast.95), calls=%async_computation | async-start | bytes 2097152 | tf_op jit(solution)/shard_map/all_to_all | solution.py:386
  49.6 25.7 %collective-permute-start.1 = (bf16[1024,256]{1,0:T(8,128)(2,1)S(1)}, bf16[1024,256]{1,0:T(8,128)(2,1)S(1)}, u32[]{:S(2)}, u32[]{:S(2)}) collective-permute-start(bf16[1024,256]{1,0:T(8,128)(2,1)S(1)} %copy-done.11), channel_id=1, source_target_pairs={{0,8},{4,12},{8,0},{12,4},{16,24},{20,28},{24,16},{28,20},{1,9},{5... | collective-permute-start | bytes 1572872 | tf_op jit(solution)/shard_map/ppermute | solution.py:367
  51.1 24.7 %collective-permute-start = (bf16[1024,256]{1,0:T(8,128)(2,1)S(1)}, bf16[1024,256]{1,0:T(8,128)(2,1)S(1)}, u32[]{:S(2)}, u32[]{:S(2)}) collective-permute-start(bf16[1024,256]{1,0:T(8,128)(2,1)S(1)} %copy-done.11), channel_id=1, source_target_pairs={{0,4},{4,0},{8,12},{12,8},{16,20},{20,16},{24,28},{28,24},{1,5},{5... | collective-permute-start | bytes 1572872 | tf_op jit(solution)/shard_map/ppermute | solution.py:367
  51.1 27.3 %collective-permute-start.3 = (bf16[1024,256]{1,0:T(8,128)(2,1)S(1)}, bf16[1024,256]{1,0:T(8,128)(2,1)S(1)}, u32[]{:S(2)}, u32[]{:S(2)}) collective-permute-start(bf16[1024,256]{1,0:T(8,128)(2,1)S(1)} %copy-done.11), channel_id=1, source_target_pairs={{0,16},{4,20},{8,24},{12,28},{16,0},{20,4},{24,8},{28,12},{1,17},{... | collective-permute-start | bytes 1572872 | tf_op jit(solution)/shard_map/ppermute | solution.py:367
  51.6 34.5 %collective-permute-start.5 = (bf16[1024,256]{1,0:T(8,128)(2,1)S(1)}, bf16[1024,256]{1,0:T(8,128)(2,1)}, u32[]{:S(2)}, u32[]{:S(2)}) collective-permute-start(bf16[1024,256]{1,0:T(8,128)(2,1)S(1)} %copy-done.11), channel_id=1, source_target_pairs={{0,24},{4,28},{8,16},{12,20},{16,8},{20,12},{24,0},{28,4},{1,25},{... | collective-permute-start | bytes 1572872 | tf_op jit(solution)/shard_map/ppermute | solution.py:367
  75.3 10.8 %collective-permute-start.2 = (bf16[1024,256]{1,0:T(8,128)(2,1)S(1)}, bf16[1024,256]{1,0:T(8,128)(2,1)}, u32[]{:S(2)}, u32[]{:S(2)}) collective-permute-start(bf16[1024,256]{1,0:T(8,128)(2,1)S(1)} %collective-permute-done.1.refs_2_), channel_id=1, source_target_pairs={{0,4},{4,0},{8,12},{12,8},{16,20},{20,16},{24,28},{28,24},{1,5},{5... | collective-permute-start | bytes 1572872 | tf_op jit(solution)/shard_map/ppermute | solution.py:367
  75.3 91.5 %collective-permute-start.7 = (bf16[8,4,64,256]{3,2,1,0:T(8,128)(2,1)}, bf16[8,4,64,256]{3,2,1,0:T(8,128)(2,1)}, u32[]{:S(2)}, u32[]{:S(2)}) collective-permute-start(bf16[8,4,64,256]{3,2,1,0:T(8,128)(2,1)} %all-to-all-done.refs_13_), channel_id=1, source_target_pairs={{0,1},{1,0},{2,3},{3,2},{4,5},{5,4},{6,7},{7,6},{8,9},{9,8},{10,11... | collective-permute-start | bytes 3145736 | tf_op jit(solution)/shard_map/ppermute | solution.py:370
  75.8 94.5 %collective-permute-start.8 = (bf16[8,4,64,256]{3,2,1,0:T(8,128)(2,1)}, bf16[8,4,64,256]{3,2,1,0:T(8,128)(2,1)}, u32[]{:S(2)}, u32[]{:S(2)}) collective-permute-start(bf16[8,4,64,256]{3,2,1,0:T(8,128)(2,1)} %all-to-all-done.refs_13_), channel_id=1, source_target_pairs={{0,2},{1,3},{2,0},{3,1},{4,6},{5,7},{6,4},{7,5},{8,10},{9,11},{10,... | collective-permute-start | bytes 3145736 | tf_op jit(solution)/shard_map/ppermute | solution.py:370
  78.4 188.2 %copy-start.12 = (bf16[1024,256]{1,0:T(8,128)(2,1)}, bf16[1024,256]{1,0:T(8,128)(2,1)S(1)}, u32[]{:S(2)}) copy-start(bf16[1024,256]{1,0:T(8,128)(2,1)S(1)} %collective-permute-done.3.refs_4_) | copy-start | bytes 1572868
  78.4 188.2 %collective-permute-start.9 = (bf16[8,4,64,256]{3,2,1,0:T(8,128)(2,1)}, bf16[8,4,64,256]{3,2,1,0:T(8,128)(2,1)}, u32[]{:S(2)}, u32[]{:S(2)}) collective-permute-start(bf16[8,4,64,256]{3,2,1,0:T(8,128)(2,1)} %all-to-all-done.refs_13_), channel_id=1, source_target_pairs={{0,3},{1,2},{2,1},{3,0},{4,7},{5,6},{6,5},{7,4},{8,11},{9,10},{10,... | collective-permute-start | bytes 3145736 | tf_op jit(solution)/shard_map/ppermute | solution.py:370
  86.1 13.4 %collective-permute-start.4 = (bf16[1024,256]{1,0:T(8,128)(2,1)S(1)}, bf16[1024,256]{1,0:T(8,128)(2,1)}, u32[]{:S(2)}, u32[]{:S(2)}) collective-permute-start(bf16[1024,256]{1,0:T(8,128)(2,1)S(1)} %collective-permute-done.3.refs_4_), channel_id=1, source_target_pairs={{0,4},{4,0},{8,12},{12,8},{16,20},{20,16},{24,28},{28,24},{1,5},{5... | collective-permute-start | bytes 1572872 | tf_op jit(solution)/shard_map/ppermute | solution.py:367
  86.2 13.4 %collective-permute-start.6 = (bf16[1024,256]{1,0:T(8,128)(2,1)}, bf16[1024,256]{1,0:T(8,128)(2,1)}, u32[]{:S(2)}, u32[]{:S(2)}) collective-permute-start(bf16[1024,256]{1,0:T(8,128)(2,1)} %collective-permute-done.5.refs_6_), channel_id=1, source_target_pairs={{0,4},{4,0},{8,12},{12,8},{16,20},{20,16},{24,28},{28,24},{1,5},{5... | collective-permute-start | bytes 1572872 | tf_op jit(solution)/shard_map/ppermute | solution.py:367
  320.2 7.7 %copy-start.7 = (bf16[8,4,64,64]{3,2,1,0:T(8,128)(2,1)}, bf16[8,4,64,64]{3,2,1,0:T(8,128)(2,1)S(1)}, u32[]{:S(2)}) copy-start(bf16[8,4,64,64]{3,2,1,0:T(8,128)(2,1)S(1)} %get-tuple-element.34) | copy-start | bytes 786436
  320.3 4.4 collective-permute-start.10
  327.9 19.0 %collective-permute-start.11 = (bf16[128,2048]{1,0:T(8,128)(2,1)}, bf16[128,2048]{1,0:T(8,128)(2,1)}, u32[]{:S(2)}, u32[]{:S(2)}) collective-permute-start(bf16[128,2048]{1,0:T(8,128)(2,1)} %get-tuple-element.37), channel_id=1, source_target_pairs={{0,8},{4,12},{8,0},{12,4},{16,24},{20,28},{24,16},{28,20},{1,9},{5... | collective-permute-start | bytes 1572872 | tf_op jit(solution)/shard_map/ppermute | solution.py:367
  330.1 5.4 copy-start.18
  331.7 15.2 %copy-start.17 = (bf16[128,2048]{1,0:T(8,128)(2,1)S(1)}, bf16[128,2048]{1,0:T(8,128)(2,1)}, u32[]{:S(2)}) copy-start(bf16[128,2048]{1,0:T(8,128)(2,1)} %get-tuple-element.35) | copy-start | bytes 1572868
  331.8 12.1 %collective-permute-start.28 = (bf16[3,64,512]{2,1,0:T(8,128)(2,1)S(1)}, bf16[3,64,512]{2,1,0:T(8,128)(2,1)S(1)}, u32[]{:S(2)}, u32[]{:S(2)}) collective-permute-start(bf16[3,64,512]{2,1,0:T(8,128)(2,1)S(1)} %bitcast.121), channel_id=1, source_target_pairs={{0,3},{1,2},{2,1},{3,0},{4,7},{5,6},{6,5},{7,4},{8,11},{9,10},{10,... | collective-permute-start | bytes 589832 | tf_op jit(solution)/shard_map/ppermute | solution.py:370
  332.2 12.9 %collective-permute-start.27 = (bf16[3,64,512]{2,1,0:T(8,128)(2,1)S(1)}, bf16[3,64,512]{2,1,0:T(8,128)(2,1)S(1)}, u32[]{:S(2)}, u32[]{:S(2)}) collective-permute-start(bf16[3,64,512]{2,1,0:T(8,128)(2,1)S(1)} %bitcast.122), channel_id=1, source_target_pairs={{0,2},{1,3},{2,0},{3,1},{4,6},{5,7},{6,4},{7,5},{8,10},{9,11},{10,... | collective-permute-start | bytes 589832 | tf_op jit(solution)/shard_map/ppermute | solution.py:370
  332.3 12.7 %collective-permute-start.26 = (bf16[3,64,512]{2,1,0:T(8,128)(2,1)S(1)}, bf16[3,64,512]{2,1,0:T(8,128)(2,1)S(1)}, u32[]{:S(2)}, u32[]{:S(2)}) collective-permute-start(bf16[3,64,512]{2,1,0:T(8,128)(2,1)S(1)} %bitcast.123), channel_id=1, source_target_pairs={{0,1},{1,0},{2,3},{3,2},{4,5},{5,4},{6,7},{7,6},{8,9},{9,8},{10,11... | collective-permute-start | bytes 589832 | tf_op jit(solution)/shard_map/ppermute | solution.py:370
  335.5 14.2 %collective-permute-start.12 = (bf16[128,2048]{1,0:T(8,128)(2,1)S(1)}, bf16[128,2048]{1,0:T(8,128)(2,1)S(1)}, u32[]{:S(2)}, u32[]{:S(2)}) collective-permute-start(bf16[128,2048]{1,0:T(8,128)(2,1)S(1)} %copy-done.18), channel_id=1, source_target_pairs={{0,16},{4,20},{8,24},{12,28},{16,0},{20,4},{24,8},{28,12},{1,17},{... | collective-permute-start | bytes 1572872 | tf_op jit(solution)/shard_map/ppermute | solution.py:367
  345.2 36.6 %collective-permute-start.29 = (bf16[4,3,64,512]{3,2,1,0:T(8,128)(2,1)S(1)}, bf16[4,3,64,512]{3,2,1,0:T(8,128)(2,1)S(1)}, u32[]{:S(2)}, u32[]{:S(2)}) collective-permute-start(bf16[4,3,64,512]{3,2,1,0:T(8,128)(2,1)S(1)} %pad_maximum_fusion.refs_3_.refs_5_), channel_id=1, source_target_pairs={{0,4},{4,0},{8,12},{12,8},{16,20},{20,16},{24,28},{28,24},{1,5},{5... | collective-permute-start | bytes 2359304 | tf_op jit(solution)/shard_map/ppermute | solution.py:367
  345.2 36.5 %collective-permute-start.30 = (bf16[4,3,64,512]{3,2,1,0:T(8,128)(2,1)S(1)}, bf16[4,3,64,512]{3,2,1,0:T(8,128)(2,1)S(1)}, u32[]{:S(2)}, u32[]{:S(2)}) collective-permute-start(bf16[4,3,64,512]{3,2,1,0:T(8,128)(2,1)S(1)} %pad_maximum_fusion.refs_3_.refs_5_), channel_id=1, source_target_pairs={{0,8},{4,12},{8,0},{12,4},{16,24},{20,28},{24,16},{28,20},{1,9},{5... | collective-permute-start | bytes 2359304 | tf_op jit(solution)/shard_map/ppermute | solution.py:367
  346.4 48.4 %collective-permute-start.32 = (bf16[4,3,64,512]{3,2,1,0:T(8,128)(2,1)S(1)}, bf16[4,3,64,512]{3,2,1,0:T(8,128)(2,1)S(1)}, u32[]{:S(2)}, u32[]{:S(2)}) collective-permute-start(bf16[4,3,64,512]{3,2,1,0:T(8,128)(2,1)S(1)} %pad_maximum_fusion.refs_3_.refs_5_), channel_id=1, source_target_pairs={{0,16},{4,20},{8,24},{12,28},{16,0},{20,4},{24,8},{28,12},{1,17},{... | collective-permute-start | bytes 2359304 | tf_op jit(solution)/shard_map/ppermute | solution.py:367
  346.9 30.0 %collective-permute-start.13 = (bf16[128,2048]{1,0:T(8,128)(2,1)S(1)}, bf16[128,2048]{1,0:T(8,128)(2,1)S(1)}, u32[]{:S(2)}, u32[]{:S(2)}) collective-permute-start(bf16[128,2048]{1,0:T(8,128)(2,1)S(1)} %copy-done.17), channel_id=1, source_target_pairs={{0,24},{4,28},{8,16},{12,20},{16,8},{20,12},{24,0},{28,4},{1,25},{... | collective-permute-start | bytes 1572872 | tf_op jit(solution)/shard_map/ppermute | solution.py:367
  349.7 56.3 %collective-permute-start.34 = (bf16[4,3,64,512]{3,2,1,0:T(8,128)(2,1)S(1)}, bf16[4,3,64,512]{3,2,1,0:T(8,128)(2,1)}, u32[]{:S(2)}, u32[]{:S(2)}) collective-permute-start(bf16[4,3,64,512]{3,2,1,0:T(8,128)(2,1)S(1)} %pad_maximum_fusion.refs_3_.refs_5_), channel_id=1, source_target_pairs={{0,24},{4,28},{8,16},{12,20},{16,8},{20,12},{24,0},{28,4},{1,25},{... | collective-permute-start | bytes 2359304 | tf_op jit(solution)/shard_map/ppermute | solution.py:367
  380.7 24.3 %collective-permute-start.16 = (bf16[128,2048]{1,0:T(8,128)(2,1)}, bf16[128,2048]{1,0:T(8,128)(2,1)S(1)}, u32[]{:S(2)}, u32[]{:S(2)}) collective-permute-start(bf16[128,2048]{1,0:T(8,128)(2,1)} %get-tuple-element.22.refs_0_), channel_id=1, source_target_pairs={{0,8},{4,12},{8,0},{12,4},{16,24},{20,28},{24,16},{28,20},{1,9},{5... | collective-permute-start | bytes 1572872 | tf_op jit(solution)/shard_map/ppermute | solution.py:367
  381.8 24.8 %collective-permute-start.14 = (bf16[128,2048]{1,0:T(8,128)(2,1)}, bf16[128,2048]{1,0:T(8,128)(2,1)}, u32[]{:S(2)}, u32[]{:S(2)}) collective-permute-start(bf16[128,2048]{1,0:T(8,128)(2,1)} %get-tuple-element.22.refs_0_), channel_id=1, source_target_pairs={{0,4},{4,0},{8,12},{12,8},{16,20},{20,16},{24,28},{28,24},{1,5},{5... | collective-permute-start | bytes 1572872 | tf_op jit(solution)/shard_map/ppermute | solution.py:367
  381.8 53.6 %copy-start.4 = (bf16[4,3,64,512]{3,2,1,0:T(8,128)(2,1)}, bf16[4,3,64,512]{3,2,1,0:T(8,128)(2,1)S(1)}, u32[]{:S(2)}) copy-start(bf16[4,3,64,512]{3,2,1,0:T(8,128)(2,1)S(1)} %collective-permute-done.30.refs_5_.refs_7_) | copy-start | bytes 2359300
  381.8 34.9 %collective-permute-start.20 = (bf16[128,2048]{1,0:T(8,128)(2,1)}, bf16[128,2048]{1,0:T(8,128)(2,1)}, u32[]{:S(2)}, u32[]{:S(2)}) collective-permute-start(bf16[128,2048]{1,0:T(8,128)(2,1)} %get-tuple-element.22.refs_0_), channel_id=1, source_target_pairs={{0,16},{4,20},{8,24},{12,28},{16,0},{20,4},{24,8},{28,12},{1,17},{... | collective-permute-start | bytes 1572872 | tf_op jit(solution)/shard_map/ppermute | solution.py:367
  395.6 21.1 %collective-permute-start.24 = (bf16[128,2048]{1,0:T(8,128)(2,1)}, bf16[128,2048]{1,0:T(8,128)(2,1)}, u32[]{:S(2)}, u32[]{:S(2)}) collective-permute-start(bf16[128,2048]{1,0:T(8,128)(2,1)} %get-tuple-element.22.refs_0_), channel_id=1, source_target_pairs={{0,24},{4,28},{8,16},{12,20},{16,8},{20,12},{24,0},{28,4},{1,25},{... | collective-permute-start | bytes 1572872 | tf_op jit(solution)/shard_map/ppermute | solution.py:367
  405.0 20.2 %collective-permute-start.17 = (bf16[128,2048]{1,0:T(8,128)(2,1)S(1)}, bf16[128,2048]{1,0:T(8,128)(2,1)}, u32[]{:S(2)}, u32[]{:S(2)}) collective-permute-start(bf16[128,2048]{1,0:T(8,128)(2,1)S(1)} %collective-permute-done.16.refs_0_), channel_id=1, source_target_pairs={{0,4},{4,0},{8,12},{12,8},{16,20},{20,16},{24,28},{28,24},{1,5},{5... | collective-permute-start | bytes 1572872 | tf_op jit(solution)/shard_map/ppermute | solution.py:367
  406.0 28.8 %collective-permute-start.31 = (bf16[4,3,64,512]{3,2,1,0:T(8,128)(2,1)S(1)}, bf16[4,3,64,512]{3,2,1,0:T(8,128)(2,1)}, u32[]{:S(2)}, u32[]{:S(2)}) collective-permute-start(bf16[4,3,64,512]{3,2,1,0:T(8,128)(2,1)S(1)} %collective-permute-done.30.refs_5_.refs_7_), channel_id=1, source_target_pairs={{0,4},{4,0},{8,12},{12,8},{16,20},{20,16},{24,28},{28,24},{1,5},{5... | collective-permute-start | bytes 2359304 | tf_op jit(solution)/shard_map/ppermute | solution.py:367
  406.6 28.4 %collective-permute-start.33 = (bf16[4,3,64,512]{3,2,1,0:T(8,128)(2,1)}, bf16[4,3,64,512]{3,2,1,0:T(8,128)(2,1)}, u32[]{:S(2)}, u32[]{:S(2)}) collective-permute-start(bf16[4,3,64,512]{3,2,1,0:T(8,128)(2,1)} %copy-done.5), channel_id=1, source_target_pairs={{0,4},{4,0},{8,12},{12,8},{16,20},{20,16},{24,28},{28,24},{1,5},{5... | collective-permute-start | bytes 2359304 | tf_op jit(solution)/shard_map/ppermute | solution.py:367
  416.7 18.7 %collective-permute-start.35 = (bf16[4,3,64,512]{3,2,1,0:T(8,128)(2,1)}, bf16[4,3,64,512]{3,2,1,0:T(8,128)(2,1)}, u32[]{:S(2)}, u32[]{:S(2)}) collective-permute-start(bf16[4,3,64,512]{3,2,1,0:T(8,128)(2,1)} %collective-permute-done.34.refs_9_.refs_11_), channel_id=1, source_target_pairs={{0,4},{4,0},{8,12},{12,8},{16,20},{20,16},{24,28},{28,24},{1,5},{5... | collective-permute-start | bytes 2359304 | tf_op jit(solution)/shard_map/ppermute | solution.py:367
  416.7 12.9 %collective-permute-start.21 = (bf16[128,2048]{1,0:T(8,128)(2,1)}, bf16[128,2048]{1,0:T(8,128)(2,1)}, u32[]{:S(2)}, u32[]{:S(2)}) collective-permute-start(bf16[128,2048]{1,0:T(8,128)(2,1)} %collective-permute-done.20.refs_0_), channel_id=1, source_target_pairs={{0,4},{4,0},{8,12},{12,8},{16,20},{20,16},{24,28},{28,24},{1,5},{5... | collective-permute-start | bytes 1572872 | tf_op jit(solution)/shard_map/ppermute | solution.py:367
  417.2 3.4 copy-start.2
  420.6 4.7 copy-start.3
  425.2 10.2 %collective-permute-start.25 = (bf16[128,2048]{1,0:T(8,128)(2,1)}, bf16[128,2048]{1,0:T(8,128)(2,1)S(1)}, u32[]{:S(2)}, u32[]{:S(2)}) collective-permute-start(bf16[128,2048]{1,0:T(8,128)(2,1)} %collective-permute-done.24.refs_0_), channel_id=1, source_target_pairs={{0,4},{4,0},{8,12},{12,8},{16,20},{20,16},{24,28},{28,24},{1,5},{5... | collective-permute-start | bytes 1572872 | tf_op jit(solution)/shard_map/ppermute | solution.py:367
  429.6 5.8 %copy-start.6 = (bf16[4,3,64,512]{3,2,1,0:T(8,128)(2,1)S(1)}, bf16[4,3,64,512]{3,2,1,0:T(8,128)(2,1)}, u32[]{:S(2)}) copy-start(bf16[4,3,64,512]{3,2,1,0:T(8,128)(2,1)} %copy-done.5) | copy-start | bytes 2359300
  429.6 11.8 %collective-permute-start.18 = (bf16[128,2048]{1,0:T(8,128)(2,1)S(1)}, bf16[128,2048]{1,0:T(8,128)(2,1)S(1)}, u32[]{:S(2)}, u32[]{:S(2)}) collective-permute-start(bf16[128,2048]{1,0:T(8,128)(2,1)S(1)} %get-tuple-element.26), channel_id=1, source_target_pairs={{0,4},{4,0},{8,12},{12,8},{16,20},{20,16},{24,28},{28,24},{1,5},{5... | collective-permute-start | bytes 1572872 | tf_op jit(solution)/shard_map/ppermute | solution.py:367
  434.8 12.3 %collective-permute-start.15 = (bf16[128,2048]{1,0:T(8,128)(2,1)S(1)}, bf16[128,2048]{1,0:T(8,128)(2,1)S(1)}, u32[]{:S(2)}, u32[]{:S(2)}) collective-permute-start(bf16[128,2048]{1,0:T(8,128)(2,1)S(1)} %get-tuple-element.24), channel_id=1, source_target_pairs={{0,4},{4,0},{8,12},{12,8},{16,20},{20,16},{24,28},{28,24},{1,5},{5... | collective-permute-start | bytes 1572872 | tf_op jit(solution)/shard_map/ppermute | solution.py:367
  435.0 7.6 %collective-permute-start.22 = (bf16[128,2048]{1,0:T(8,128)(2,1)S(1)}, bf16[128,2048]{1,0:T(8,128)(2,1)S(1)}, u32[]{:S(2)}, u32[]{:S(2)}) collective-permute-start(bf16[128,2048]{1,0:T(8,128)(2,1)S(1)} %get-tuple-element.28), channel_id=1, source_target_pairs={{0,4},{4,0},{8,12},{12,8},{16,20},{20,16},{24,28},{28,24},{1,5},{5... | collective-permute-start | bytes 1572872 | tf_op jit(solution)/shard_map/ppermute | solution.py:367
  441.2 2.3 collective-permute-start.36
  441.4 4.1 copy-start.8
  441.5 14.8 %collective-permute-start.19 = (bf16[128,2048]{1,0:T(8,128)(2,1)S(1)}, bf16[128,2048]{1,0:T(8,128)(2,1)S(1)}, u32[]{:S(2)}, u32[]{:S(2)}) collective-permute-start(bf16[128,2048]{1,0:T(8,128)(2,1)S(1)} %add_convert_fusion.2), channel_id=1, source_target_pairs={{0,8},{4,12},{8,0},{12,4},{16,24},{20,28},{24,16},{28,20},{1,9},{5... | collective-permute-start | bytes 1572872 | tf_op jit(solution)/shard_map/ppermute | solution.py:367
  442.7 15.2 %collective-permute-start.23 = (bf16[128,2048]{1,0:T(8,128)(2,1)S(1)}, bf16[128,2048]{1,0:T(8,128)(2,1)S(1)}, u32[]{:S(2)}, u32[]{:S(2)}) collective-permute-start(bf16[128,2048]{1,0:T(8,128)(2,1)S(1)} %add_convert_fusion.1), channel_id=1, source_target_pairs={{0,16},{4,20},{8,24},{12,28},{16,0},{20,4},{24,8},{28,12},{1,17},{... | collective-permute-start | bytes 1572872 | tf_op jit(solution)/shard_map/ppermute | solution.py:367
  443.5 45.8 %copy-start.10 = (bf16[128,2048]{1,0:T(8,128)(2,1)S(1)}, bf16[128,2048]{1,0:T(8,128)(2,1)}, u32[]{:S(2)}) copy-start(bf16[128,2048]{1,0:T(8,128)(2,1)} %copy-done.9) | copy-start | bytes 1572868
  443.6 45.6 %collective-permute-start.37 = (bf16[128,2048]{1,0:T(8,128)(2,1)S(1)}, bf16[128,2048]{1,0:T(8,128)(2,1)S(1)}, u32[]{:S(2)}, u32[]{:S(2)}) collective-permute-start(bf16[128,2048]{1,0:T(8,128)(2,1)S(1)} %add_convert_fusion), channel_id=1, source_target_pairs={{0,24},{4,28},{8,16},{12,20},{16,8},{20,12},{24,0},{28,4},{1,25},{... | collective-permute-start | bytes 1572872 | tf_op jit(solution)/shard_map/ppermute | solution.py:367
  445.5 50.5 %collective-permute-start.43 = (bf16[4,4,64,64]{3,2,1,0:T(8,128)(2,1)S(1)}, bf16[4,4,64,64]{3,2,1,0:T(8,128)(2,1)}, u32[]{:S(2)}, u32[]{:S(2)}) collective-permute-start(bf16[4,4,64,64]{3,2,1,0:T(8,128)(2,1)S(1)} %get-tuple-element.44), channel_id=1, source_target_pairs={{0,4},{1,12},{2,20},{3,28},{4,0},{5,8},{6,16},{7,24},{8,5},{9,13},... | collective-permute-start | bytes 393224 | tf_op jit(solution)/shard_map/ppermute | solution.py:419
  447.1 48.9 %collective-permute-start.42 = (bf16[4,4,64,64]{3,2,1,0:T(8,128)(2,1)S(1)}, bf16[4,4,64,64]{3,2,1,0:T(8,128)(2,1)}, u32[]{:S(2)}, u32[]{:S(2)}) collective-permute-start(bf16[4,4,64,64]{3,2,1,0:T(8,128)(2,1)S(1)} %get-tuple-element.43), channel_id=1, source_target_pairs={{0,0},{1,8},{2,16},{3,24},{4,4},{5,12},{6,20},{7,28},{8,1},{9,9},{... | collective-permute-start | bytes 393224 | tf_op jit(solution)/shard_map/ppermute | solution.py:419
  491.9 24.1 %all-to-all-start.2 = ((bf16[8,128,256]{2,1,0:T(8,128)(2,1)}), bf16[8,128,256]{2,1,0:T(8,128)(2,1)}, u32[]{:S(2)}, u32[]{:S(2)}) async-start(bf16[8,128,256]{2,1,0:T(8,128)(2,1)} %bitcast.97), calls=%async_computation.2 | async-start | bytes 1048576 | tf_op jit(solution)/shard_map/all_to_all | solution.py:454
  503.2 41.4 %collective-permute-start.38 = (bf16[128,2048]{1,0:T(8,128)(2,1)S(1)}, bf16[128,2048]{1,0:T(8,128)(2,1)S(1)}, u32[]{:S(2)}, u32[]{:S(2)}) collective-permute-start(bf16[128,2048]{1,0:T(8,128)(2,1)S(1)} %get-tuple-element.33), channel_id=1, source_target_pairs={{0,0},{1,8},{2,16},{3,24},{4,4},{5,12},{6,20},{7,28},{8,1},{9,9},{... | collective-permute-start | bytes 1572872 | tf_op jit(solution)/shard_map/ppermute | solution.py:453
  508.1 49.2 %collective-permute-start.39 = (bf16[128,2048]{1,0:T(8,128)(2,1)S(1)}, bf16[128,2048]{1,0:T(8,128)(2,1)}, u32[]{:S(2)}, u32[]{:S(2)}) collective-permute-start(bf16[128,2048]{1,0:T(8,128)(2,1)S(1)} %get-tuple-element.33), channel_id=1, source_target_pairs={{0,1},{1,9},{2,17},{3,25},{4,5},{5,13},{6,21},{7,29},{8,0},{9,8},{... | collective-permute-start | bytes 1572872 | tf_op jit(solution)/shard_map/ppermute | solution.py:453
  511.2 46.1 %collective-permute-start.40 = (bf16[128,2048]{1,0:T(8,128)(2,1)S(1)}, bf16[128,2048]{1,0:T(8,128)(2,1)}, u32[]{:S(2)}, u32[]{:S(2)}) collective-permute-start(bf16[128,2048]{1,0:T(8,128)(2,1)S(1)} %get-tuple-element.33), channel_id=1, source_target_pairs={{0,2},{1,10},{2,18},{3,26},{4,6},{5,14},{6,22},{7,30},{8,3},{9,11}... | collective-permute-start | bytes 1572872 | tf_op jit(solution)/shard_map/ppermute | solution.py:453
  511.2 49.7 %collective-permute-start.41 = (bf16[128,2048]{1,0:T(8,128)(2,1)S(1)}, bf16[128,2048]{1,0:T(8,128)(2,1)}, u32[]{:S(2)}, u32[]{:S(2)}) collective-permute-start(bf16[128,2048]{1,0:T(8,128)(2,1)S(1)} %get-tuple-element.33), channel_id=1, source_target_pairs={{0,3},{1,11},{2,19},{3,27},{4,7},{5,15},{6,23},{7,31},{8,2},{9,10}... | collective-permute-start | bytes 1572872 | tf_op jit(solution)/shard_map/ppermute | solution.py:453
  522.8 50.4 %copy-start.21 = (bf16[1024,256]{1,0:T(8,128)(2,1)}, bf16[1024,256]{1,0:T(8,128)(2,1)S(1)}, u32[]{:S(2)}) copy-start(bf16[1024,256]{1,0:T(8,128)(2,1)S(1)} %fusion.4) | copy-start | bytes 1572868
  561.9 11.2 %copy-start.1 = (bf16[2,96,2048]{2,1,0:T(8,128)(2,1)S(1)}, bf16[2,96,2048]{2,1,0:T(8,128)(2,1)}, u32[]{:S(2)}) copy-start(bf16[2,96,2048]{2,1,0:T(8,128)(2,1)} %param.14) | copy-start | bytes 2359300
  (7 other events, 7.3 us)
Sparse Core Ops, SparseCore 0:
  39.3 235.2 all-gather.3

commit v3 on v2

--- a/solution.py
+++ b/solution.py
@@ -35,13 +35,11 @@
     return bdot(top, same) + bdot(low, same)
 
 
-def time_kernel(nb, nc, per, place_ref, lens, *refs):
-    xg = refs[:nb]
-    norms, shift, ld, lu, co = refs[nb : nb + 5]
-    wt = refs[nb + 5 : nb + 5 + nc]
+def time_kernel(nc, per, place_ref, lens, xg, norms, shift, ld, lu, co, *refs):
+    wt = refs[:nc]
     even, odd, own, state_ref, mixes, w, sems = refs[-7:]
     rows = per * LMAX
-    fw = xg[0].shape[1]
+    nb, _, fw = xg.shape
     width = nb * fw
     hc = w.shape[-1]
     chunk = even.shape[1]
@@ -50,7 +48,7 @@
     @pl.when(pl.program_id(0) == 0)
     def _():
         copies = [
-            pltpu.make_async_copy(wt[k].at[:, m], w.at[m, :, col ^ k], sems.at[m, k])
+            pltpu.make_async_copy(wt[k].at[:, m], w.at[m, :, (col + nc - k) % nc], sems.at[m, k])
             for m in range(4)
             for k in range(nc)
         ]
@@ -60,20 +58,18 @@
             copy.wait()
 
     weight = [w[m].reshape(width, hc) for m in range(4)]
-    blocks = [x[...].astype(F32) for x in xg]
+    blocks = [xg[i].astype(F32) for i in range(nb)]
     total = sum(jnp.sum(b, axis=1, keepdims=True) for b in blocks)
     square = sum(jnp.sum(b * b, axis=1, keepdims=True) for b in blocks)
     center = total / width
     scale = lax.rsqrt(square / width - center * center + 1e-05)
     first_row = lax.broadcasted_iota(jnp.int32, (rows, fw), 0) % LMAX == 0
     for i in range(nb):
-        at = row ^ i
-        lanes = pl.ds(pl.multiple_of(at * fw, fw), fw)
-        z = (xg[i][...].astype(F32) - center) * scale * norms[at, 0:1] + norms[at, 1:2]
+        z = (xg[i].astype(F32) - center) * scale * norms[i, 0:1] + norms[i, 1:2]
         z = z.astype(BF16).astype(F32)
         step = jnp.where(first_row, 0.0, pltpu.roll(z, 1, 0)) - z
         for j in range(5):
-            mixes[j, :, lanes] = (z + step * shift[at, j : j + 1]).astype(BF16)
+            mixes[j, :, i * fw : (i + 1) * fw] = (z + step * shift[i, j : j + 1]).astype(BF16)
     r = bdot(mixes[0], weight[0])
     k = bdot(mixes[1], weight[1])
     v = bdot(mixes[2], weight[2])
@@ -169,7 +165,7 @@
         @pl.when(to == 0)
         def _():
             for i in range(nb):
-                own[:, pl.ds(pl.multiple_of((row ^ i) * fw, fw), fw)] = xg[i][here]
+                own[:, i * fw : (i + 1) * fw] = xg[i, here]
 
         @pl.when(to % 2 == 0)
         def _():
@@ -181,10 +177,11 @@
 
 
 def time_mix(place, lens, xg, norms, shift, ld, lu, co, wt, extra, per):
-    nb, nc = len(xg), len(wt)
-    tokens, fw = xg[0].shape
-    prompts = tokens // LMAX
+    nb, _, fw = xg.shape
+    nc = len(wt)
     _, _, deep, hc = wt[0].shape
+    prompts = lens.shape[0]
+    tokens = prompts * LMAX
     width, chunk = nb * fw, tokens // nb
 
     def full(a):
@@ -193,10 +190,10 @@
     whole = pl.BlockSpec((nb // 2, chunk, width), lambda i: (0, 0, 0))
     rest = (norms, shift, ld, lu, co)
     return pl.pallas_call(
-        functools.partial(time_kernel, nb, nc, per),
+        functools.partial(time_kernel, nc, per),
         grid=(prompts // per,),
         in_specs=[pl.BlockSpec(memory_space=pltpu.SMEM)] * 2
-        + [pl.BlockSpec((per * LMAX, fw), lambda i: (i, 0))] * nb
+        + [pl.BlockSpec((nb, per * LMAX, fw), lambda i: (0, i, 0))]
         + [full(a) for a in rest]
         + [pl.BlockSpec(memory_space=pl.ANY)] * (nc + len(extra)),
         out_specs=[
@@ -218,7 +215,7 @@
         ],
         compiler_params=pltpu.CompilerParams(vmem_limit_bytes=50 * 2**20),
         cost_estimate=pl.CostEstimate(flops=40 * 10**9, bytes_accessed=2**24, transcendentals=0),
-    )(place, lens, *xg, *rest, *wt, *extra)
+    )(place, lens, xg, *rest, *wt, *extra)
 
 
 def shifted_mix(z, weight):
@@ -226,17 +223,32 @@
     return (z + (jnp.where(first_row, 0.0, pltpu.roll(z, 1, 0)) - z) * weight).astype(BF16)
 
 
-def settle_kernel(count, *refs):
-    pieces = refs[:count]
-    base, gains, out, normal, blend = refs[count:]
-    total = base[...].astype(F32)
-    attn = pieces[0][...].astype(F32)
-    for piece in pieces[1:]:
-        attn = attn + piece[...].astype(F32)
-    total = (total + attn).astype(BF16)
+def settle_kernel(count, groups, quarters, place_ref, *refs):
+    pieces = refs[: count * groups]
+    base, gains, out, normal, blend = refs[count * groups : count * groups + 5]
+    sums = []
+    for g in range(groups):
+        total = pieces[g * count][...].astype(F32)
+        for piece in pieces[g * count + 1 : (g + 1) * count]:
+            total = total + piece[...].astype(F32)
+        sums.append(total)
+    width = base.shape[1]
+    if quarters == 1:
+        added = sums[0]
+    else:
+        share = width // quarters
+        sums = jnp.concatenate(sums, axis=1)
+        sums = [sums[:, i : i + share] for i in range(0, width, share)]
+        held = refs[-1]
+        for q in range(quarters):
+            held[(place_ref[1] + quarters - q) % quarters] = sums[q]
+        deep = sums[0].shape[1] // (2 * count)
+        added = jnp.concatenate(
+            [held[q, :, r * deep : (r + 1) * deep] for r in range(2 * count) for q in range(quarters)], axis=1
+        )
+    total = (base[...].astype(F32) + added).astype(BF16)
     out[...] = total
     z = total.astype(F32)
-    width = z.shape[1]
     center = jnp.sum(z, axis=1, keepdims=True) / width
     second = jnp.sum(z * z, axis=1, keepdims=True) / width
     z = (z - center) * lax.rsqrt(second - center * center + 1e-05) * gains[0:1] + gains[1:2]
@@ -245,64 +257,117 @@
     blend[...] = shifted_mix(z.astype(F32), gains[2:3])
 
 
-def settle(pieces, base, gains):
+def settle(place, pieces, base, gains, quarters):
+    groups, count = len(pieces), len(pieces[0])
+    flat = [piece for group in pieces for piece in group]
+    spec = pl.BlockSpec(memory_space=pltpu.VMEM)
+    held = [pltpu.VMEM((quarters, base.shape[0], base.shape[1] // quarters), F32)] if quarters > 1 else []
+    return pl.pallas_call(
+        functools.partial(settle_kernel, count, groups, quarters),
+        in_specs=[pl.BlockSpec(memory_space=pltpu.SMEM)] + [spec] * (len(flat) + 2),
+        out_specs=[spec] * 3,
+        out_shape=[jax.ShapeDtypeStruct(base.shape, BF16)] * 3,
+        scratch_shapes=held,
+        compiler_params=pltpu.CompilerParams(vmem_limit_bytes=24 * 2**20),
+        cost_estimate=pl.CostEstimate(flops=10**6, bytes_accessed=2**12, transcendentals=0),
+    )(place, *flat, base, gains)
+
+
+def after_kernel(*refs):
+    pass
+
+
+def after(x, *earlier):
+    apart = pl.BlockSpec(memory_space=pl.ANY)
+    return pl.pallas_call(
+        after_kernel,
+        in_specs=[apart] * (1 + len(earlier)),
+        out_specs=apart,
+        out_shape=jax.ShapeDtypeStruct(x.shape, x.dtype),
+        input_output_aliases={0: 0},
+    )(x, *earlier)
+
+
+def key_kernel(nb, nc, place_ref, *refs):
+    xs, shards = refs[:nb], refs[nb : nb + nc]
+    act, x, w, sems = refs[-4:]
+    col = place_ref[1]
+    chunk, width = xs[0].shape
+    moves = [pltpu.make_async_copy(xs[i], x.at[i], sems.at[nc + i]) for i in range(nb)]
+    copies = [
+        pltpu.make_async_copy(shards[k], w.at[:, (col + nc - k) % nc], sems.at[k]) for k in range(nc)
+    ]
+    for copy in copies + moves:
+        copy.start()
+    for copy in copies:
+        copy.wait()
+    weight = w[...].reshape(width, -1)
+    for i in range(0, nb, 2):
+        moves[i].wait()
+        moves[i + 1].wait()
+        pre = bdot(x[i : i + 2].reshape(2 * chunk, width), weight)
+        act[i * chunk : (i + 2) * chunk, :] = jnp.square(jnp.maximum(pre, 0.0)).astype(BF16)
+
+
+def key_products(place, xs, shards, extra):
+    nb, nc = len(xs), len(shards)
+    _, deep, ff = shards[0].shape
+    chunk, width = xs[0].shape
+    apart = pl.BlockSpec(memory_space=pl.ANY)
+    return pl.pallas_call(
+        functools.partial(key_kernel, nb, nc),
+        in_specs=[pl.BlockSpec(memory_space=pltpu.SMEM)] + [apart] * (nb + nc + len(extra)),
+        out_specs=pl.BlockSpec(memory_space=pltpu.VMEM),
+        out_shape=jax.ShapeDtypeStruct((nb * chunk, ff), BF16),
+        scratch_shapes=[
+            pltpu.VMEM((nb, chunk, width), BF16),
+            pltpu.VMEM((nb, nc, deep, ff), BF16),
+            pltpu.SemaphoreType.DMA((nc + nb,)),
+        ],
+        compiler_params=pltpu.CompilerParams(vmem_limit_bytes=40 * 2**20),
+        cost_estimate=pl.CostEstimate(flops=10**6, bytes_accessed=2**12, transcendentals=0),
+    )(place, *xs, *shards, *extra)
+
+
+def value_kernel(count, act, *refs):
+    shards, (even, odd) = refs[:count], refs[-2:]
+    nb = 2 * even.shape[0]
+    chunk = even.shape[1]
+    start = 0
+    for q in range(count):
+        weight = shards[q][...].reshape(-1, shards[q].shape[-1])
+        at = slice(start, start + weight.shape[0])
+        start += weight.shape[0]
+        for k in range(nb // 2):
+            out = bdot(act[2 * k * chunk : (2 * k + 2) * chunk, :], weight, 1, 1).astype(BF16)
+            even[k, :, at] = out[:chunk]
+            odd[k, :, at] = out[chunk:]
+
+
+def value_products(nb, act, shards):
+    deep = shards[0].shape[1]
+    chunk = act.shape[0] // nb
+    width = sum(x.shape[0] for x in shards) * deep
+
     spec = pl.BlockSpec(memory_space=pltpu.VMEM)
     return pl.pallas_call(
-        functools.partial(settle_kernel, len(pieces)),
-        in_specs=[spec] * (len(pieces) + 2),
-        out_specs=[spec] * 3,
-        out_shape=[jax.ShapeDtypeStruct(base.shape, BF16)] * 3,
-        compiler_params=pltpu.CompilerParams(vmem_limit_bytes=24 * 2**20),
-        cost_estimate=pl.CostEstimate(flops=10**8, bytes_accessed=2**22, transcendentals=0),
-    )(*pieces, base, gains)
-
-
-def mlp_kernel(nc, chunk, *refs):
-    xa, xb, late = refs[:3]
-    pa, pb, w, sems = refs[-4:]
-    width = xa.shape[1]
+        functools.partial(value_kernel, len(shards)),
+        in_specs=[spec] * (1 + len(shards)),
+        out_specs=[spec] * 2,
+        out_shape=[jax.ShapeDtypeStruct((nb // 2, chunk, width), BF16)] * 2,
+        compiler_params=pltpu.CompilerParams(vmem_limit_bytes=40 * 2**20),
+        cost_estimate=pl.CostEstimate(flops=10**6, bytes_accessed=2**12, transcendentals=0),
+    )(act, *shards)
+
+
+def next_kernel(nc, place_ref, *refs):
+    xs = refs[:nc]
+    gate, given = refs[nc : nc + 2]
+    out, x, w, sems = refs[-4:]
+    col = place_ref[1]
     copies = [
-        [pltpu.make_async_copy(late.at[c, :, m], w.at[m, :, c], sems.at[m, c]) for c in range(nc)] for m in range(2)
-    ]
-    for copy in copies[0] + copies[1]:
-        copy.start()
-    x = jnp.concatenate([xa[...], xb[...]], axis=0)
-    for copy in copies[0]:
-        copy.wait()
-    pre = bdot(x, w[0].reshape(width, -1))
-    act = jnp.square(jnp.maximum(pre, 0.0)).astype(BF16)
-    for copy in copies[1]:
-        copy.wait()
-    out = bdot(act, w[1].reshape(width, -1), 1, 1).astype(BF16)
-    pa[...] = out[:chunk]
-    pb[...] = out[chunk:]
-
-
-def mlp_products(xa, xb, late, extra):
-    nc, nb, _, deep, ff = late.shape
-    chunk = xa.shape[0]
-    spec = pl.BlockSpec(memory_space=pltpu.VMEM)
-    apart = pl.BlockSpec(memory_space=pl.ANY)
-    return pl.pallas_call(
-        functools.partial(mlp_kernel, nc, chunk),
-        in_specs=[spec, spec, apart] + [apart] * len(extra),
-        out_specs=[spec, spec],
-        out_shape=[jax.ShapeDtypeStruct(xa.shape, BF16)] * 2,
-        scratch_shapes=[pltpu.VMEM((2, nb, nc, deep, ff), BF16), pltpu.SemaphoreType.DMA((2, nc))],
-        compiler_params=pltpu.CompilerParams(vmem_limit_bytes=40 * 2**20),
-        cost_estimate=pl.CostEstimate(flops=4 * 10**9, bytes_accessed=2**23, transcendentals=0),
-    )(xa, xb, late, *extra)
-
-
-def next_kernel(nb, nc, place_ref, *refs):
-    xs = refs[:nc]
-    gate = refs[nc]
-    given = refs[nc + 1 : nc + 1 + nb]
-    out, x, w, sems = refs[-4:]
-    row, col = place_ref[0], place_ref[1]
-    copies = [
-        pltpu.make_async_copy(given[i].at[k], w.at[:, row ^ i, col ^ k], sems.at[i, k])
-        for i in range(nb)
+        pltpu.make_async_copy(given.at[:, k, m], w.at[m, :, col ^ k], sems.at[m, k])
+        for m in range(3)
         for k in range(nc)
     ]
     for copy in copies:
@@ -311,33 +376,35 @@
     for k in range(nc):
         x[pl.ds(pl.multiple_of((col ^ k) * chunk, chunk), chunk), :] = xs[k][...]
     z = x[...].astype(F32)
-    mixed = [shifted_mix(z, gate[m : m + 1]) for m in range(3)]
+    mixed = shifted_mix(z, gate[0:1])
     for copy in copies:
         copy.wait()
     for m in range(3):
-        out[m] = bdot(mixed[m], w[m].reshape(width, -1)).astype(BF16)
+        out[m] = bdot(mixed, w[m].reshape(width, -1)).astype(BF16)
+        if m < 2:
+            mixed = shifted_mix(z, gate[m + 1 : m + 2])
 
 
 def next_products(place, xs, gate, given):
-    nb, nc = len(given), len(xs)
+    nc = len(xs)
     chunk, width = xs[0].shape
-    _, _, deep, cols = given[0].shape
+    nb, _, _, deep, cols = given.shape
     spec = pl.BlockSpec(memory_space=pltpu.VMEM)
     return pl.pallas_call(
-        functools.partial(next_kernel, nb, nc),
+        functools.partial(next_kernel, nc),
         in_specs=[pl.BlockSpec(memory_space=pltpu.SMEM)]
         + [spec] * (nc + 1)
-        + [pl.BlockSpec(memory_space=pl.ANY)] * nb,
+        + [pl.BlockSpec(memory_space=pl.ANY)],
         out_specs=spec,
         out_shape=jax.ShapeDtypeStruct((3, nc * chunk, cols), BF16),
         scratch_shapes=[
             pltpu.VMEM((nc * chunk, width), BF16),
             pltpu.VMEM((3, nb, nc, deep, cols), BF16),
-            pltpu.SemaphoreType.DMA((nb, nc)),
+            pltpu.SemaphoreType.DMA((3, nc)),
         ],
         compiler_params=pltpu.CompilerParams(vmem_limit_bytes=50 * 2**20),
-        cost_estimate=pl.CostEstimate(flops=6 * 10**9, bytes_accessed=2**24, transcendentals=0),
-    )(place, *xs, gate, *given)
+        cost_estimate=pl.CostEstimate(flops=10**6, bytes_accessed=2**12, transcendentals=0),
+    )(place, *xs, gate, given)
 
 
 def per_device(
@@ -379,22 +446,41 @@
         mine = [x] + [to_row(x, 2 * k) for k in range(1, chips)]
         return [piece for m in mine for piece in (m, to_row(m, 1))]
 
-    xg = gather_row(hidden)
-    norms = lax.all_gather(norm_parameters, "row", axis=0, tiled=False)
-    square_low = square_matrix_shards.astype(BF16)
-    early = square_low[0:4].reshape(4, deep, n_row, hc).transpose(2, 0, 1, 3)
-    early = lax.all_to_all(early, "row", 0, 0, tiled=True)
-    early = [early] + [to_col(early, k) for k in range(1, n_col)]
+    def ring(x):
+        return lax.ppermute(x, "col", [(i, (i + 1) % n_col) for i in range(n_col)])
+
+    def relay(x):
+        return lax.all_to_all(x, "row", 0, 0, tiled=True)
+
+    moving = square_matrix_shards[0:4].astype(BF16).reshape(4, deep, n_row, hc).transpose(2, 0, 1, 3)
+    early = [relay(moving)]
+    cols = width // n_col
+    sent = [
+        lax.dynamic_slice_in_dim(square_matrix_shards[4:7], (col ^ k) * cols, cols, 2).astype(BF16)
+        for k in range(n_col)
+    ]
+    last = jnp.stack([sent[0]] + [to_col(sent[k], k) for k in range(1, n_col)])
+    early[0] = after(early[0], last)
+    for k in range(1, n_col):
+        early.append(ring(early[-1]))
+    top = lax.reduce_precision(norm_parameters, 8, 7)
+    middle = lax.reduce_precision(norm_parameters - top, 8, 7)
+    terms = jnp.concatenate([top, middle, norm_parameters - top - middle], axis=0).astype(BF16)
+    terms = jnp.pad(terms, ((0, -terms.shape[0] % 16), (0, 0)))
+    xg = lax.all_gather(after(jnp.concatenate([hidden, terms], axis=0), early[0]), "row", axis=0, tiled=True)
+    xg = xg.reshape(n_row, -1, fw)
+    count = norm_parameters.shape[0]
+    norms = xg[:, tokens : tokens + 3 * count].astype(F32)
+    norms = norms[:, :count] + norms[:, count : 2 * count] + norms[:, 2 * count :]
+    last = last.reshape(n_col * 3 * deep, cols)
+    last = lax.all_gather(last, "row", axis=0, tiled=True).reshape(n_row, n_col, 3, deep, cols)
     ff = channel_mix_shards.shape[2] // n_row
     late = channel_mix_shards.astype(BF16).reshape(2, deep, n_row, ff).transpose(2, 0, 1, 3)
-    late_row = lax.all_to_all(late.reshape(n_row, 2 * deep, ff), "row", 0, 0, tiled=True)
-    late = lax.all_gather(late_row.reshape(n_row * 2 * deep, ff), "col", axis=0, tiled=True)
-    late = late.reshape(n_col, n_row, 2, deep, ff)
-    cols = width // n_col
-    last = square_low[4:7].reshape(3, deep, n_col, cols).transpose(2, 0, 1, 3)
-    sent = [lax.dynamic_index_in_dim(last, col ^ k, 0, keepdims=False) for k in range(n_col)]
-    last = jnp.stack([sent[0]] + [to_col(sent[k], k) for k in range(1, n_col)])
-    last = gather_row(last)
+    late = relay(after(late, early[0]))
+    keys = [after(late[:, 0], early[-1])]
+    values = [after(late[:, 1], early[-1])]
+    keys.append(ring(keys[0]))
+    values.append(ring(values[0]))
 
     prompts = tokens // LMAX
     lens = lax.dynamic_slice_in_dim(lengths, col * prompts, prompts, 0)
@@ -402,12 +488,45 @@
     up = lax.dynamic_slice_in_dim(lowrank_up, row * hc, hc, 2)
     co = lax.dynamic_slice_in_dim(attention_coefficients, row * hc, hc, 1)
     even, odd, own, states = time_mix(
-        place, lens, xg, norms, shift, lowrank_down, up, co, early, (late_row,), 2
+        place, lens, xg, norms, shift, lowrank_down, up, co, early, (keys[0], values[0]), 2
     )
 
+    keys[1], values[1] = after(keys[1], odd), after(values[1], odd)
+    for k in range(2, n_col - 1):
+        keys.append(ring(keys[-1]))
+        values.append(ring(values[-1]))
+    other = to_row(after(odd, keys[1], values[1]), 1)
+    near = [(even[k].astype(F32) + other[k].astype(F32)).astype(BF16) for k in range(chips)]
+    pieces = [near[0]] + [to_row(near[k], 2 * k) for k in range(1, chips)]
+    gains = norms.transpose(1, 0, 2).reshape(-1, width)
+    mid, second, channel_in = settle(
+        place, [pieces], own, jnp.concatenate([gains[2:4], token_shift_weights[5:6]], axis=0), 1
+    )
+    if chunk % LMAX:
+        pairs = [(row_of(n), row_of(n + 1)) for n in range(n_row - 1)]
+        edge = lax.ppermute(second[-1:], "row", pairs).astype(F32)
+        edge = jnp.where(chunk_of(row) * chunk % LMAX == 0, 0.0, edge)
+        wide = second.astype(F32)
+        moved_on = jnp.concatenate([edge, wide[:-1]], axis=0)
+        channel_in = (wide + (moved_on - wide) * token_shift_weights[5]).astype(BF16)
+    keys[-1], values[-1] = after(keys[-1], mid), after(values[-1], mid)
+    keys.append(ring(keys[-1]))
+    values.append(ring(values[-1]))
+    rows_in = [channel_in] + [to_row(channel_in, 2 * k) for k in range(1, chips)]
+    rows_in = [piece for x in rows_in for piece in (x, to_row(x, 1))]
+    act = key_products(place, rows_in, keys, (last,))
+    pieces = []
+    for group in (values[:-1], values[-1:]):
+        even, odd = value_products(n_row, act, group)
+        other = to_row(odd, 1)
+        near = [(even[k].astype(F32) + other[k].astype(F32)).astype(BF16) for k in range(chips)]
+        pieces.append([near[0]] + [to_row(near[k], 2 * k) for k in range(1, chips)])
+    out_own, third, _ = settle(
+        place, pieces, mid, jnp.concatenate([gains[4:6], token_shift_weights[5:6]], axis=0), n_col
+    )
     half = prompts // 2
     share = n_row // n_col
-    states = states.reshape(2, half, states.shape[1], HEAD, HEAD)
+    states = after(states, out_own).reshape(2, half, states.shape[1], HEAD, HEAD)
     moved = []
     for j in range(2):
         pairs = []
@@ -417,32 +536,8 @@
                 pairs.append((r * n_col + c, (2 * c + h) * n_col + r // share))
         piece = lax.dynamic_index_in_dim(states, (row % 2) ^ j, 0, keepdims=False)
         moved.append(lax.ppermute(piece, ("row", "col"), pairs))
-    moved = jnp.take(jnp.stack(moved), (row % 2) ^ jnp.arange(2), axis=0)
-    final_state = moved.transpose(1, 0, 2, 3, 4).reshape(half, -1, HEAD * HEAD).astype(F32)
-
-    other = to_row(odd, 1)
-    near = [(even[k].astype(F32) + other[k].astype(F32)).astype(BF16) for k in range(chips)]
-    pieces = [near[0]] + [to_row(near[k], 2 * k) for k in range(1, chips)]
-    gains = norms.transpose(1, 0, 2).reshape(-1, width)
-    mid, second, channel_in = settle(
-        pieces, own, jnp.concatenate([gains[2:4], token_shift_weights[5:6]], axis=0)
-    )
-    if chunk % LMAX:
-        pairs = [(row_of(n), row_of(n + 1)) for n in range(n_row - 1)]
-        edge = lax.ppermute(second[-1:], "row", pairs).astype(F32)
-        edge = jnp.where(chunk_of(row) * chunk % LMAX == 0, 0.0, edge)
-        wide = second.astype(F32)
-        moved_on = jnp.concatenate([edge, wide[:-1]], axis=0)
-        channel_in = (wide + (moved_on - wide) * token_shift_weights[5]).astype(BF16)
-    rows_in = gather_row(channel_in)
-    pieces = [None] * chips
-    for k in reversed(range(chips)):
-        mine, theirs = mlp_products(rows_in[2 * k], rows_in[2 * k + 1], late, last if k == chips - 1 else ())
-        total = (mine.astype(F32) + to_row(theirs, 1).astype(F32)).astype(BF16)
-        pieces[k] = to_row(total, 2 * k) if k else total
-    out_own, third, _ = settle(
-        pieces, mid, jnp.concatenate([gains[4:6], token_shift_weights[5:6]], axis=0)
-    )
+    settled = jnp.take(jnp.stack(moved), (row % 2) ^ jnp.arange(2), axis=0)
+    final_state = settled.transpose(1, 0, 2, 3, 4).reshape(half, -1, HEAD * HEAD).astype(F32)
 
     arrived = []
     for j in range(n_col):
@@ -451,8 +546,8 @@
             for c in range(n_col):
                 pairs.append((r * n_col + c, (2 * c + r % 2) * n_col + ((r // 2) ^ j)))
         arrived.append(lax.ppermute(third, ("row", "col"), pairs))
-    out_blocks = lax.all_to_all(out_own.reshape(chunk, n_row, fw).transpose(1, 0, 2), "row", 0, 0, tiled=True)
-    out_hidden = jnp.concatenate([out_blocks[row_of(n)] for n in range(n_row)], axis=0)
+    blocks = relay(out_own.reshape(chunk, n_row, fw).transpose(1, 0, 2))
+    out_hidden = blocks.reshape(chips, 2, chunk, fw).transpose(1, 0, 2, 3).reshape(tokens, fw)
     next_rkv = next_products(place, arrived, token_shift_weights[6:9], last)
     return (out_hidden, next_rkv, final_state)
 

time: 584 us -> 414 us (0.71)
  waiting for transfers between devices: 343 us -> 218 us
  blocking collectives: 39 us -> 0 us
  Pallas kernels: 87.9 us -> 70 us
  starting transfers between devices: 54.5 us -> 65.7 us
    ppermute x6 -> x3, waiting for transfers between devices: 176 us -> 13.8 us  [to_col(): return lax.ppermute(x, 'col', [(i, i ^ k) for i in range(n_col)])]
    ppermute x0 -> x9, waiting for transfers between devices: none -> 95.8 us  [ring(): return lax.ppermute(x, 'col', [(i, (i + 1) % n_col) for i in range(n_col)])]
    ppermute x32 -> x19, waiting for transfers between devices: 130 us -> 57 us  [to_row(): return lax.ppermute(x, 'row', [(i, i ^ k) for i in range(n_row)])]
    ppermute x2, waiting for transfers between devices: 0.01 us -> 51.5 us  [per_device(): moved.append(lax.ppermute(piece, ('row', 'col'), pairs))]
    ppermute x4, waiting for transfers between devices: 37.3 us -> 0.01 us  [per_device(): arrived.append(lax.ppermute(third, ('row', 'col'), pairs))]
    all_to_all x1 -> x0, blocking collectives: 29.3 us -> none  [per_device(): lax.all_to_all(late.reshape(n_row, 2 * deep, ff), 'row', 0, 0, tiled=True)]
    pallas_call x8 -> x18, Pallas kernels: 87.9 us -> 70 us  [the longest x1 43.2 us: time_mix(): pl.pallas_call(functools.partial(time_kernel, nc, per), grid=(prompts //...]
    ppermute x0 -> x9, starting transfers between devices: none -> 14.1 us  [ring(): return lax.ppermute(x, 'col', [(i, (i + 1) % n_col) for i in range(n_col)])]
  transfers between devices with their start and end apart: 47 -> 42, of which waited for: 18 -> 15; matrix products, arithmetic and copies ran while one was open for 5% -> 7% of each run, Pallas kernels for 13% -> 11%
where the time goes in v3:
time: 414 us; the launch traced here: 412 us
  waiting for transfers between devices  218 us (53%)
  Pallas kernels  70 us (17%)
  starting transfers between devices  65.7 us (16%)
  local copies, waits for them, and re-layouts  32.1 us (8%)
  between operations  14.5 us (4%)
  other arithmetic  12 us (3%)
    ppermute x9, waiting for transfers between devices, ring(): return lax.ppermute(x, 'col', [(i, (i + 1) % n_col) for i in range(n_col)])  95.8 us
    ppermute x19, waiting for transfers between devices, to_row(): return lax.ppermute(x, 'row', [(i, i ^ k) for i in range(n_row)])  57 us
    ppermute x2, waiting for transfers between devices, per_device(): moved.append(lax.ppermute(piece, ('row', 'col'), pairs))  51.5 us
    pallas_call x1, Pallas kernels, time_mix(): pl.pallas_call(functools.partial(time_kernel, nc, per), grid=(prompts //...  43.2 us
    ppermute x19, starting transfers between devices, to_row(): return lax.ppermute(x, 'row', [(i, i ^ k) for i in range(n_row)])  15.3 us
    ppermute x9, starting transfers between devices, ring(): return lax.ppermute(x, 'col', [(i, (i + 1) % n_col) for i in range(n_col)])  14.1 us
    ppermute x3, waiting for transfers between devices, to_col(): return lax.ppermute(x, 'col', [(i, i ^ k) for i in range(n_col)])  13.8 us
    unnamed x52, local copies, waits for them, and re-layouts  13.4 us
  transfers between devices with their start and end apart: 42, of which 15 were waited for; matrix products, arithmetic and copies ran while one was open for 7% of the time, Pallas kernels for 11%

profile of v3, /device:TPU:12, one launch (start us, length us, event | category | flops | bytes accessed | tf_op | source)
XLA Modules:
  0.0 412.5 jit_solution(1740844998341602489)
XLA Ops:
  7.2 1.8 slice.214
  9.0 1.1 copy.59
  10.1 4.2 %all-to-all-start = ((bf16[8,4,64,256]{3,2,1,0:T(8,128)(2,1)}), bf16[8,4,64,256]{3,2,1,0:T(8,128)(2,1)S(1)}, u32[]{:S(2)}, u32[]{:S(2)}) async-start(bf16[8,4,64,256]{3,2,1,0:T(8,128)(2,1)} %bitcast.86), calls=%async_computation | async-start | bytes 2097152 | tf_op jit(solution)/shard_map/all_to_all | solution.py:453
  14.4 1.6 slice.120
  16.1 1.6 collective-permute-start.2
  17.7 1.2 collective-permute-start.1
  18.9 1.2 collective-permute-start
  21.0 11.2 %collective-permute-done.2 = bf16[3,64,512]{2,1,0:T(8,128)(2,1)S(1)} collective-permute-done((bf16[3,64,512]{2,1,0:T(8,128)(2,1)S(1)}, bf16[3,64,512]{2,1,0:T(8,128)(2,1)S(1)}, u32[]{:S(2)}, u32[]{:S(2)}) %collective-permute-start.2) | collective-permute-done | bytes 196640 | tf_op jit(solution)/shard_map/ppermute | solution.py:437
  32.3 2.5 collective-permute-done.1
  36.9 1.1 copy-done.3
  38.5 2.4 convert_element_type.201
  41.0 1.6 copy.58
  42.6 4.7 %all-to-all-start.1 = ((bf16[8,2,64,1024]{3,2,1,0:T(8,128)(2,1)}), bf16[8,2,64,1024]{3,2,1,0:T(8,128)(2,1)}, u32[]{:S(2)}, u32[]{:S(2)}) async-start(bf16[8,2,64,1024]{3,2,1,0:T(8,128)(2,1)} %shard_map.114), calls=%async_computation.1 | async-start | bytes 4194304 | tf_op jit(solution)/shard_map/all_to_all | solution.py:453
  47.3 15.8 %collective-permute-done.3.refs_1_ = bf16[8,4,64,256]{3,2,1,0:T(8,128)(2,1)} collective-permute-done((bf16[8,4,64,256]{3,2,1,0:T(8,128)(2,1)S(1)}, bf16[8,4,64,256]{3,2,1,0:T(8,128)(2,1)}, u32[]{:S(2)}, u32[]{:S(2)}) %collective-permute-start.3) | collective-permute-done | bytes 1048608 | tf_op jit(solution)/shard_map/ppermute | solution.py:450
  63.9 24.8 %collective-permute-done.4.refs_2_ = bf16[8,4,64,256]{3,2,1,0:T(8,128)(2,1)} collective-permute-done((bf16[8,4,64,256]{3,2,1,0:T(8,128)(2,1)}, bf16[8,4,64,256]{3,2,1,0:T(8,128)(2,1)}, u32[]{:S(2)}, u32[]{:S(2)}) %collective-permute-start.4) | collective-permute-done | bytes 1048608 | tf_op jit(solution)/shard_map/ppermute | solution.py:450
  88.9 1.3 copy.44.ld
  91.0 3.2 slice_bitcast_fusion
  94.2 19.1 %collective-permute-done.5.refs_1_.refs_3_ = bf16[8,4,64,256]{3,2,1,0:T(8,128)(2,1)S(1)} collective-permute-done((bf16[8,4,64,256]{3,2,1,0:T(8,128)(2,1)}, bf16[8,4,64,256]{3,2,1,0:T(8,128)(2,1)S(1)}, u32[]{:S(2)}, u32[]{:S(2)}) %collective-permute-start.5) | collective-permute-done | bytes 1048608 | tf_op jit(solution)/shard_map/ppermute | solution.py:450
  114.3 2.3 collective-permute-start.7
  117.5 1.5 copy-done.16
  119.1 43.2 %shard_map.117 = (bf16[4,128,2048]{2,1,0:T(8,128)(2,1)}, bf16[4,128,2048]{2,1,0:T(8,128)(2,1)}, bf16[128,2048]{1,0:T(8,128)(2,1)S(1)}, bf16[8,4,64,64]{3,2,1,0:T(8,128)(2,1)S(1)}) custom-call(s32[2]{0:T(128)S(1)} %pad_add_fusion.place_ref, s32[8]{0:T(128)S(1)} %dynamic_slice.28.lens, bf16[8,1056,256]{2,1,0:T(8,128)(2,1)} %bitcast.111, ...), custom_call_target="tpu_custom_call" | custom-call | flops 40000000000 | bytes 16777216 | tf_op jit(solution)/shard_map/pallas_call | solution.py:192
  164.1 1.1 copy-done.8
  165.2 3.9 collective-permute-start.19
  169.2 2.3 fusion.3
  171.5 1.5 collective-permute-start.9
  173.6 1.5 collective-permute-start.11
  175.2 11.3 %collective-permute-done.9.refs_1_ = bf16[128,2048]{1,0:T(8,128)(2,1)S(1)} collective-permute-done((bf16[128,2048]{1,0:T(8,128)(2,1)S(1)}, bf16[128,2048]{1,0:T(8,128)(2,1)S(1)}, u32[]{:S(2)}, u32[]{:S(2)}) %collective-permute-start.9) | collective-permute-done | bytes 524320 | tf_op jit(solution)/shard_map/ppermute | solution.py:434
  186.5 10.8 %collective-permute-done.10.refs_2_ = bf16[128,2048]{1,0:T(8,128)(2,1)S(1)} collective-permute-done((bf16[128,2048]{1,0:T(8,128)(2,1)S(1)}, bf16[128,2048]{1,0:T(8,128)(2,1)S(1)}, u32[]{:S(2)}, u32[]{:S(2)}) %collective-permute-start.10) | collective-permute-done | bytes 524320 | tf_op jit(solution)/shard_map/ppermute | solution.py:434
  197.2 2.3 shard_map.121
  201.8 3.9 collective-permute-start.20
  205.7 1.6 collective-permute-start.15
  207.3 1.3 collective-permute-start.17
  208.7 6.7 %collective-permute-done.21.refs_0_ = bf16[8,64,1024]{2,1,0:T(8,128)(2,1)} collective-permute-done((bf16[8,64,1024]{2,1,0:T(8,128)(2,1)}, bf16[8,64,1024]{2,1,0:T(8,128)(2,1)}, u32[]{:S(2)}, u32[]{:S(2)}) %collective-permute-start.21) | collective-permute-done | bytes 1048608 | tf_op jit(solution)/shard_map/ppermute | solution.py:450
  215.8 13.6 %collective-permute-done.15.refs_4_ = bf16[128,2048]{1,0:T(8,128)(2,1)} collective-permute-done((bf16[128,2048]{1,0:T(8,128)(2,1)S(1)}, bf16[128,2048]{1,0:T(8,128)(2,1)}, u32[]{:S(2)}, u32[]{:S(2)}) %collective-permute-start.15) | collective-permute-done | bytes 524320 | tf_op jit(solution)/shard_map/ppermute | solution.py:434
  229.9 6.2 %collective-permute-done.20.refs_11_ = bf16[8,64,1024]{2,1,0:T(8,128)(2,1)} collective-permute-done((bf16[8,64,1024]{2,1,0:T(8,128)(2,1)}, bf16[8,64,1024]{2,1,0:T(8,128)(2,1)}, u32[]{:S(2)}, u32[]{:S(2)}) %collective-permute-start.20) | collective-permute-done | bytes 1048608 | tf_op jit(solution)/shard_map/ppermute | solution.py:450
  236.2 1.2 copy-done.12
  237.4 7.4 %shard_map.123.act = bf16[1024,1024]{1,0:T(8,128)(2,1)S(1)} custom-call(s32[2]{0:T(128)S(1)} %pad_add_fusion.place_ref, bf16[128,2048]{1,0:T(8,128)(2,1)S(1)} %get-tuple-element.18.refs_0_, bf16[128,2048]{1,0:T(8,128)(2,1)} %collective-permute-done.12.refs_1_, bf16[128,2048]{1,0:T(8,128)(2,1)S(1)} %collective-permute-done.13.refs_2_, ...), custom_call_target="tpu_custom_call" | custom-call | flops 1000000 | bytes 4096 | tf_op jit(solution)/shard_map/pallas_call | solution.py:317
  244.8 5.0 %shard_map.125 = (bf16[4,128,1536]{2,1,0:T(8,128)(2,1)S(1)}, bf16[4,128,1536]{2,1,0:T(8,128)(2,1)S(1)}) custom-call(bf16[1024,1024]{1,0:T(8,128)(2,1)S(1)} %shard_map.123.act, bf16[8,64,1024]{2,1,0:T(8,128)(2,1)S(1)} %copy-done.5, bf16[8,64,1024]{2,1,0:T(8,128)(2,1)} %shard_map.119.refs_2_.refs_1_, bf16[8,64,1024]{2,1,0:T(8,128)(2,1)} %shard_map.124.refs_2_), custom_call_target="tpu_custom_call" | custom-call | flops 1000000 | bytes 4096 | tf_op jit(solution)/shard_map/pallas_call | solution.py:353
  249.9 2.8 collective-permute-start.26
  252.7 23.1 %collective-permute-done.26.refs_0_ = bf16[8,64,1024]{2,1,0:T(8,128)(2,1)S(1)} collective-permute-done((bf16[8,64,1024]{2,1,0:T(8,128)(2,1)}, bf16[8,64,1024]{2,1,0:T(8,128)(2,1)S(1)}, u32[]{:S(2)}, u32[]{:S(2)}) %collective-permute-start.26) | collective-permute-done | bytes 1048608 | tf_op jit(solution)/shard_map/ppermute | solution.py:450
  275.8 1.3 shard_map.126
  277.2 1.2 fusion.7
  278.4 1.5 collective-permute-start.23
  280.4 1.4 collective-permute-start.25
  282.7 1.5 collective-permute-start.28
  284.8 16.6 %collective-permute-done.28.refs_5_ = bf16[128,512]{1,0:T(8,128)(2,1)S(1)} collective-permute-done((bf16[128,512]{1,0:T(8,128)(2,1)S(1)}, bf16[128,512]{1,0:T(8,128)(2,1)S(1)}, u32[]{:S(2)}, u32[]{:S(2)}) %collective-permute-start.28) | collective-permute-done | bytes 131104 | tf_op jit(solution)/shard_map/ppermute | solution.py:434
  301.4 1.5 collective-permute-start.30
  302.9 4.7 %collective-permute-done.30.refs_7_ = bf16[128,512]{1,0:T(8,128)(2,1)S(1)} collective-permute-done((bf16[128,512]{1,0:T(8,128)(2,1)}, bf16[128,512]{1,0:T(8,128)(2,1)S(1)}, u32[]{:S(2)}, u32[]{:S(2)}) %collective-permute-start.30) | collective-permute-done | bytes 131104 | tf_op jit(solution)/shard_map/ppermute | solution.py:434
  307.6 2.9 shard_map.127
  311.3 1.1 dynamic-slice_bitcast_fusion.1
  312.4 1.8 collective-permute-start.36
  314.2 3.5 collective-permute-start.31
  317.7 2.0 collective-permute-start.32
  320.3 6.4 %collective-permute-start.34 = (bf16[128,2048]{1,0:T(8,128)(2,1)}, bf16[128,2048]{1,0:T(8,128)(2,1)S(1)}, u32[]{:S(2)}, u32[]{:S(2)}) collective-permute-start(bf16[128,2048]{1,0:T(8,128)(2,1)} %get-tuple-element.25), channel_id=1, source_target_pairs={{0,3},{1,11},{2,19},{3,27},{4,7},{5,15},{6,23},{7,31},{8,2},{9,10}... | collective-permute-start | bytes 1572872 | tf_op jit(solution)/shard_map/ppermute | solution.py:548
  326.7 24.1 %collective-permute-done.36 = bf16[4,4,64,64]{3,2,1,0:T(8,128)(2,1)S(1)} collective-permute-done((bf16[4,4,64,64]{3,2,1,0:T(8,128)(2,1)S(1)}, bf16[4,4,64,64]{3,2,1,0:T(8,128)(2,1)S(1)}, u32[]{:S(2)}, u32[]{:S(2)}) %collective-permute-start.36) | collective-permute-done | bytes 131104 | tf_op jit(solution)/shard_map/ppermute | solution.py:538
  350.8 5.4 %collective-permute-start.35 = (bf16[4,4,64,64]{3,2,1,0:T(8,128)(2,1)S(1)}, bf16[4,4,64,64]{3,2,1,0:T(8,128)(2,1)S(1)}, u32[]{:S(2)}, u32[]{:S(2)}) collective-permute-start(bf16[4,4,64,64]{3,2,1,0:T(8,128)(2,1)S(1)} %get-tuple-element.45), channel_id=1, source_target_pairs={{0,0},{1,8},{2,16},{3,24},{4,4},{5,12},{6,20},{7,28},{8,1},{9,9},{... | collective-permute-start | bytes 393224 | tf_op jit(solution)/shard_map/ppermute | solution.py:538
  358.0 3.4 all-to-all-start.2
  361.5 27.4 %collective-permute-done.35 = bf16[4,4,64,64]{3,2,1,0:T(8,128)(2,1)S(1)} collective-permute-done((bf16[4,4,64,64]{3,2,1,0:T(8,128)(2,1)S(1)}, bf16[4,4,64,64]{3,2,1,0:T(8,128)(2,1)S(1)}, u32[]{:S(2)}, u32[]{:S(2)}) %collective-permute-start.35) | collective-permute-done | bytes 131104 | tf_op jit(solution)/shard_map/ppermute | solution.py:538
  389.6 1.1 pad_maximum_fusion.2
  390.7 1.4 gather_fusion
  392.1 1.2 convert_bitcast_fusion
  393.3 1.1 copy.47
  394.4 2.4 reshape.121
  397.6 8.0 %shard_map.128 = bf16[3,512,512]{2,1,0:T(8,128)(2,1)} custom-call(s32[2]{0:T(128)S(1)} %pad_add_fusion.place_ref, bf16[128,2048]{1,0:T(8,128)(2,1)S(1)} %collective-permute-done.31.refs_0_, bf16[128,2048]{1,0:T(8,128)(2,1)S(1)} %collective-permute-done.32.refs_1_, bf16[128,2048]{1,0:T(8,128)(2,1)S(1)} %collective-permute-done.33.refs_2_, ...), custom_call_target="tpu_custom_call" | custom-call | flops 1000000 | bytes 4096 | tf_op jit(solution)/shard_map/pallas_call | solution.py:393
  (130 shorter events, 20.0 us)
Async XLA Ops:
  7.2 83.8 %copy-start = (bf16[2,96,2048]{2,1,0:T(8,128)(2,1)S(1)}, bf16[2,96,2048]{2,1,0:T(8,128)(2,1)}, u32[]{:S(2)}) copy-start(bf16[2,96,2048]{2,1,0:T(8,128)(2,1)} %param.14) | copy-start | bytes 2359300
  10.1 25.8 %all-to-all-start = ((bf16[8,4,64,256]{3,2,1,0:T(8,128)(2,1)}), bf16[8,4,64,256]{3,2,1,0:T(8,128)(2,1)S(1)}, u32[]{:S(2)}, u32[]{:S(2)}) async-start(bf16[8,4,64,256]{3,2,1,0:T(8,128)(2,1)} %bitcast.86), calls=%async_computation | async-start | bytes 2097152 | tf_op jit(solution)/shard_map/all_to_all | solution.py:453
  14.3 5.9 %copy-start.23 = (f32[6,256]{1,0:T(8,128)S(1)}, f32[6,256]{1,0:T(8,128)}, u32[]{:S(2)}) copy-start(f32[6,256]{1,0:T(8,128)} %param.17) | copy-start | bytes 18436
  14.3 5.9 %copy-start.19 = (bf16[1024,256]{1,0:T(8,128)(2,1)S(1)}, bf16[1024,256]{1,0:T(8,128)(2,1)}, u32[]{:S(2)}) copy-start(bf16[1024,256]{1,0:T(8,128)(2,1)} %param.9) | copy-start | bytes 1572868
  14.3 102.3 %all-gather.3.cloned.1.call-start = ((), (), s32[]{:S(2)}) async-start(), calls=%async_computation.3 | async-start | bytes 4866048 | tf_op jit(solution)/shard_map/all_gather | solution.py:470
  16.1 16.2 %collective-permute-start.2 = (bf16[3,64,512]{2,1,0:T(8,128)(2,1)S(1)}, bf16[3,64,512]{2,1,0:T(8,128)(2,1)S(1)}, u32[]{:S(2)}, u32[]{:S(2)}) collective-permute-start(bf16[3,64,512]{2,1,0:T(8,128)(2,1)S(1)} %get-tuple-element.42), channel_id=1, source_target_pairs={{0,3},{1,2},{2,1},{3,0},{4,7},{5,6},{6,5},{7,4},{8,11},{9,10},{10,... | collective-permute-start | bytes 589832 | tf_op jit(solution)/shard_map/ppermute | solution.py:437
  17.7 17.1 %collective-permute-start.1 = (bf16[3,64,512]{2,1,0:T(8,128)(2,1)S(1)}, bf16[3,64,512]{2,1,0:T(8,128)(2,1)S(1)}, u32[]{:S(2)}, u32[]{:S(2)}) collective-permute-start(bf16[3,64,512]{2,1,0:T(8,128)(2,1)S(1)} %get-tuple-element.43), channel_id=1, source_target_pairs={{0,2},{1,3},{2,0},{3,1},{4,6},{5,7},{6,4},{7,5},{8,10},{9,11},{10,... | collective-permute-start | bytes 589832 | tf_op jit(solution)/shard_map/ppermute | solution.py:437
  18.9 15.9 %collective-permute-start = (bf16[3,64,512]{2,1,0:T(8,128)(2,1)S(1)}, bf16[3,64,512]{2,1,0:T(8,128)(2,1)S(1)}, u32[]{:S(2)}, u32[]{:S(2)}) collective-permute-start(bf16[3,64,512]{2,1,0:T(8,128)(2,1)S(1)} %get-tuple-element.44), channel_id=1, source_target_pairs={{0,1},{1,0},{2,3},{3,2},{4,5},{5,4},{6,7},{7,6},{8,9},{9,8},{10,11... | collective-permute-start | bytes 589832 | tf_op jit(solution)/shard_map/ppermute | solution.py:437
  35.8 1.0 copy-start.2
  36.8 1.2 copy-start.3
  36.8 193.1 %all-gather.5.cloned.1.call-start = ((), (), s32[]{:S(2)}) async-start(), calls=%async_computation.4 | async-start | bytes 7077888 | tf_op jit(solution)/shard_map/all_gather | solution.py:476
  38.0 25.1 %collective-permute-start.3 = (bf16[8,4,64,256]{3,2,1,0:T(8,128)(2,1)S(1)}, bf16[8,4,64,256]{3,2,1,0:T(8,128)(2,1)}, u32[]{:S(2)}, u32[]{:S(2)}) collective-permute-start(bf16[8,4,64,256]{3,2,1,0:T(8,128)(2,1)S(1)} %copy-done.3), channel_id=1, source_target_pairs={{0,1},{1,2},{2,3},{3,0},{4,5},{5,6},{6,7},{7,4},{8,9},{9,10},{10,1... | collective-permute-start | bytes 3145736 | tf_op jit(solution)/shard_map/ppermute | solution.py:450
  42.6 46.2 %copy-start.22 = (f32[9,2048]{1,0:T(8,128)S(1)}, f32[9,2048]{1,0:T(8,128)}, u32[]{:S(2)}) copy-start(f32[9,2048]{1,0:T(8,128)} %param.15) | copy-start | bytes 221188
  42.6 46.3 %copy-start.18 = (bf16[2,2048,96]{1,2,0:T(8,128)(2,1)S(1)}, bf16[2,2048,96]{1,2,0:T(8,128)(2,1)}, u32[]{:S(2)}) copy-start(bf16[2,2048,96]{1,2,0:T(8,128)(2,1)} %param.13) | copy-start | bytes 2359300
  42.6 48.5 %all-to-all-start.1 = ((bf16[8,2,64,1024]{3,2,1,0:T(8,128)(2,1)}), bf16[8,2,64,1024]{3,2,1,0:T(8,128)(2,1)}, u32[]{:S(2)}, u32[]{:S(2)}) async-start(bf16[8,2,64,1024]{3,2,1,0:T(8,128)(2,1)} %shard_map.114), calls=%async_computation.1 | async-start | bytes 4194304 | tf_op jit(solution)/shard_map/all_to_all | solution.py:453
  47.3 42.8 %copy-start.24 = (s32[32]{0:T(128)S(1)}, s32[32]{0:T(128)}, u32[]{:S(2)}) copy-start(s32[32]{0:T(128)} %param.10) | copy-start | bytes 388
  63.2 25.6 %collective-permute-start.4 = (bf16[8,4,64,256]{3,2,1,0:T(8,128)(2,1)}, bf16[8,4,64,256]{3,2,1,0:T(8,128)(2,1)}, u32[]{:S(2)}, u32[]{:S(2)}) collective-permute-start(bf16[8,4,64,256]{3,2,1,0:T(8,128)(2,1)} %collective-permute-done.3.refs_1_), channel_id=1, source_target_pairs={{0,1},{1,2},{2,3},{3,0},{4,5},{5,6},{6,7},{7,4},{8,9},{9,10},{10,1... | collective-permute-start | bytes 3145736 | tf_op jit(solution)/shard_map/ppermute | solution.py:450
  88.7 24.5 %collective-permute-start.5 = (bf16[8,4,64,256]{3,2,1,0:T(8,128)(2,1)}, bf16[8,4,64,256]{3,2,1,0:T(8,128)(2,1)S(1)}, u32[]{:S(2)}, u32[]{:S(2)}) collective-permute-start(bf16[8,4,64,256]{3,2,1,0:T(8,128)(2,1)} %collective-permute-done.4.refs_2_), channel_id=1, source_target_pairs={{0,1},{1,2},{2,3},{3,0},{4,5},{5,6},{6,7},{7,4},{8,9},{9,10},{10,1... | collective-permute-start | bytes 3145736 | tf_op jit(solution)/shard_map/ppermute | solution.py:450
  113.3 1.0 copy-start.17
  114.3 3.2 copy-start.4
  114.3 48.8 %collective-permute-start.6 = (bf16[8,64,1024]{2,1,0:T(8,128)(2,1)}, bf16[8,64,1024]{2,1,0:T(8,128)(2,1)S(1)}, u32[]{:S(2)}, u32[]{:S(2)}) collective-permute-start(bf16[8,64,1024]{2,1,0:T(8,128)(2,1)} %shard_map.115.refs_4_.refs_8_), channel_id=1, source_target_pairs={{0,1},{1,2},{2,3},{3,0},{4,5},{5,6},{6,7},{7,4},{8,9},{9,10},{10,1... | collective-permute-start | bytes 3145736 | tf_op jit(solution)/shard_map/ppermute | solution.py:450
  114.3 49.7 %collective-permute-start.7 = (bf16[8,64,1024]{2,1,0:T(8,128)(2,1)}, bf16[8,64,1024]{2,1,0:T(8,128)(2,1)}, u32[]{:S(2)}, u32[]{:S(2)}) collective-permute-start(bf16[8,64,1024]{2,1,0:T(8,128)(2,1)} %shard_map.116.refs_5_.refs_0_), channel_id=1, source_target_pairs={{0,1},{1,2},{2,3},{3,0},{4,5},{5,6},{6,7},{7,4},{8,9},{9,10},{10,1... | collective-permute-start | bytes 3145736 | tf_op jit(solution)/shard_map/ppermute | solution.py:450
  117.5 1.5 copy-start.16
  162.2 0.8 copy-start.13
  163.0 1.0 copy-start.7
  164.0 1.2 copy-start.8
  164.0 5.2 %collective-permute-start.8 = (bf16[4,128,2048]{2,1,0:T(8,128)(2,1)}, bf16[4,128,2048]{2,1,0:T(8,128)(2,1)S(1)}, u32[]{:S(2)}, u32[]{:S(2)}) collective-permute-start(bf16[4,128,2048]{2,1,0:T(8,128)(2,1)} %shard_map.120), channel_id=1, source_target_pairs={{0,4},{4,0},{8,12},{12,8},{16,20},{20,16},{24,28},{28,24},{1,5},{5... | collective-permute-start | bytes 6291464 | tf_op jit(solution)/shard_map/ppermute | solution.py:434
  165.2 35.6 %collective-permute-start.19 = (bf16[8,64,1024]{2,1,0:T(8,128)(2,1)S(1)}, bf16[8,64,1024]{2,1,0:T(8,128)(2,1)S(1)}, u32[]{:S(2)}, u32[]{:S(2)}) collective-permute-start(bf16[8,64,1024]{2,1,0:T(8,128)(2,1)S(1)} %copy-done.8), channel_id=1, source_target_pairs={{0,1},{1,2},{2,3},{3,0},{4,5},{5,6},{6,7},{7,4},{8,9},{9,10},{10,1... | collective-permute-start | bytes 3145736 | tf_op jit(solution)/shard_map/ppermute | solution.py:450
  169.1 46.2 %collective-permute-start.21 = (bf16[8,64,1024]{2,1,0:T(8,128)(2,1)}, bf16[8,64,1024]{2,1,0:T(8,128)(2,1)}, u32[]{:S(2)}, u32[]{:S(2)}) collective-permute-start(bf16[8,64,1024]{2,1,0:T(8,128)(2,1)} %shard_map.119.refs_2_.refs_1_), channel_id=1, source_target_pairs={{0,1},{1,2},{2,3},{3,0},{4,5},{5,6},{6,7},{7,4},{8,9},{9,10},{10,1... | collective-permute-start | bytes 3145736 | tf_op jit(solution)/shard_map/ppermute | solution.py:450
  171.5 14.9 %collective-permute-start.9 = (bf16[128,2048]{1,0:T(8,128)(2,1)S(1)}, bf16[128,2048]{1,0:T(8,128)(2,1)S(1)}, u32[]{:S(2)}, u32[]{:S(2)}) collective-permute-start(bf16[128,2048]{1,0:T(8,128)(2,1)S(1)} %get-tuple-element.29), channel_id=1, source_target_pairs={{0,8},{4,12},{8,0},{12,4},{16,24},{20,28},{24,16},{28,20},{1,9},{5... | collective-permute-start | bytes 1572872 | tf_op jit(solution)/shard_map/ppermute | solution.py:434
  173.1 24.2 %collective-permute-start.10 = (bf16[128,2048]{1,0:T(8,128)(2,1)S(1)}, bf16[128,2048]{1,0:T(8,128)(2,1)S(1)}, u32[]{:S(2)}, u32[]{:S(2)}) collective-permute-start(bf16[128,2048]{1,0:T(8,128)(2,1)S(1)} %get-tuple-element.28), channel_id=1, source_target_pairs={{0,16},{4,20},{8,24},{12,28},{16,0},{20,4},{24,8},{28,12},{1,17},{... | collective-permute-start | bytes 1572872 | tf_op jit(solution)/shard_map/ppermute | solution.py:434
  173.6 23.6 %collective-permute-start.11 = (bf16[128,2048]{1,0:T(8,128)(2,1)S(1)}, bf16[128,2048]{1,0:T(8,128)(2,1)S(1)}, u32[]{:S(2)}, u32[]{:S(2)}) collective-permute-start(bf16[128,2048]{1,0:T(8,128)(2,1)S(1)} %get-tuple-element.27), channel_id=1, source_target_pairs={{0,24},{4,28},{8,16},{12,20},{16,8},{20,12},{24,0},{28,4},{1,25},{... | collective-permute-start | bytes 1572872 | tf_op jit(solution)/shard_map/ppermute | solution.py:434
  200.3 15.0 %collective-permute-start.13 = (bf16[128,2048]{1,0:T(8,128)(2,1)S(1)}, bf16[128,2048]{1,0:T(8,128)(2,1)S(1)}, u32[]{:S(2)}, u32[]{:S(2)}) collective-permute-start(bf16[128,2048]{1,0:T(8,128)(2,1)S(1)} %get-tuple-element.18.refs_0_), channel_id=1, source_target_pairs={{0,8},{4,12},{8,0},{12,4},{16,24},{20,28},{24,16},{28,20},{1,9},{5... | collective-permute-start | bytes 1572872 | tf_op jit(solution)/shard_map/ppermute | solution.py:434
  200.9 1.0 copy-start.11
  201.8 34.4 %copy-start.6 = (bf16[8,64,1024]{2,1,0:T(8,128)(2,1)S(1)}, bf16[8,64,1024]{2,1,0:T(8,128)(2,1)}, u32[]{:S(2)}) copy-start(bf16[8,64,1024]{2,1,0:T(8,128)(2,1)} %shard_map.115.refs_4_.refs_8_) | copy-start | bytes 3145732
  201.8 34.3 %collective-permute-start.20 = (bf16[8,64,1024]{2,1,0:T(8,128)(2,1)}, bf16[8,64,1024]{2,1,0:T(8,128)(2,1)}, u32[]{:S(2)}, u32[]{:S(2)}) collective-permute-start(bf16[8,64,1024]{2,1,0:T(8,128)(2,1)} %shard_map.122.refs_10_), channel_id=1, source_target_pairs={{0,1},{1,2},{2,3},{3,0},{4,5},{5,6},{6,7},{7,4},{8,9},{9,10},{10,1... | collective-permute-start | bytes 3145736 | tf_op jit(solution)/shard_map/ppermute | solution.py:450
  205.7 23.7 %collective-permute-start.15 = (bf16[128,2048]{1,0:T(8,128)(2,1)S(1)}, bf16[128,2048]{1,0:T(8,128)(2,1)}, u32[]{:S(2)}, u32[]{:S(2)}) collective-permute-start(bf16[128,2048]{1,0:T(8,128)(2,1)S(1)} %get-tuple-element.18.refs_0_), channel_id=1, source_target_pairs={{0,16},{4,20},{8,24},{12,28},{16,0},{20,4},{24,8},{28,12},{1,17},{... | collective-permute-start | bytes 1572872 | tf_op jit(solution)/shard_map/ppermute | solution.py:434
  207.3 22.1 %collective-permute-start.17 = (bf16[128,2048]{1,0:T(8,128)(2,1)S(1)}, bf16[128,2048]{1,0:T(8,128)(2,1)}, u32[]{:S(2)}, u32[]{:S(2)}) collective-permute-start(bf16[128,2048]{1,0:T(8,128)(2,1)S(1)} %get-tuple-element.18.refs_0_), channel_id=1, source_target_pairs={{0,24},{4,28},{8,16},{12,20},{16,8},{20,12},{24,0},{28,4},{1,25},{... | collective-permute-start | bytes 1572872 | tf_op jit(solution)/shard_map/ppermute | solution.py:434
  215.3 14.6 %collective-permute-start.12 = (bf16[128,2048]{1,0:T(8,128)(2,1)S(1)}, bf16[128,2048]{1,0:T(8,128)(2,1)}, u32[]{:S(2)}, u32[]{:S(2)}) collective-permute-start(bf16[128,2048]{1,0:T(8,128)(2,1)S(1)} %get-tuple-element.18.refs_0_), channel_id=1, source_target_pairs={{0,4},{4,0},{8,12},{12,8},{16,20},{20,16},{24,28},{28,24},{1,5},{5... | collective-permute-start | bytes 1572872 | tf_op jit(solution)/shard_map/ppermute | solution.py:434
  215.3 20.9 %collective-permute-start.14 = (bf16[128,2048]{1,0:T(8,128)(2,1)S(1)}, bf16[128,2048]{1,0:T(8,128)(2,1)}, u32[]{:S(2)}, u32[]{:S(2)}) collective-permute-start(bf16[128,2048]{1,0:T(8,128)(2,1)S(1)} %collective-permute-done.13.refs_2_), channel_id=1, source_target_pairs={{0,4},{4,0},{8,12},{12,8},{16,20},{20,16},{24,28},{28,24},{1,5},{5... | collective-permute-start | bytes 1572872 | tf_op jit(solution)/shard_map/ppermute | solution.py:434
  229.4 6.8 %collective-permute-start.16 = (bf16[128,2048]{1,0:T(8,128)(2,1)}, bf16[128,2048]{1,0:T(8,128)(2,1)}, u32[]{:S(2)}, u32[]{:S(2)}) collective-permute-start(bf16[128,2048]{1,0:T(8,128)(2,1)} %collective-permute-done.15.refs_4_), channel_id=1, source_target_pairs={{0,4},{4,0},{8,12},{12,8},{16,20},{20,16},{24,28},{28,24},{1,5},{5... | collective-permute-start | bytes 1572872 | tf_op jit(solution)/shard_map/ppermute | solution.py:434
  229.4 6.8 %collective-permute-start.18 = (bf16[128,2048]{1,0:T(8,128)(2,1)}, bf16[128,2048]{1,0:T(8,128)(2,1)}, u32[]{:S(2)}, u32[]{:S(2)}) collective-permute-start(bf16[128,2048]{1,0:T(8,128)(2,1)} %collective-permute-done.17.refs_6_), channel_id=1, source_target_pairs={{0,4},{4,0},{8,12},{12,8},{16,20},{20,16},{24,28},{28,24},{1,5},{5... | collective-permute-start | bytes 1572872 | tf_op jit(solution)/shard_map/ppermute | solution.py:434
  236.2 1.2 copy-start.12
  237.4 7.4 %copy-start.5 = (bf16[8,64,1024]{2,1,0:T(8,128)(2,1)S(1)}, bf16[8,64,1024]{2,1,0:T(8,128)(2,1)}, u32[]{:S(2)}) copy-start(bf16[8,64,1024]{2,1,0:T(8,128)(2,1)} %shard_map.116.refs_5_.refs_0_) | copy-start | bytes 3145732
  249.8 27.3 %collective-permute-start.22 = (bf16[4,128,1536]{2,1,0:T(8,128)(2,1)S(1)}, bf16[4,128,1536]{2,1,0:T(8,128)(2,1)S(1)}, u32[]{:S(2)}, u32[]{:S(2)}) collective-permute-start(bf16[4,128,1536]{2,1,0:T(8,128)(2,1)S(1)} %get-tuple-element.21), channel_id=1, source_target_pairs={{0,4},{4,0},{8,12},{12,8},{16,20},{20,16},{24,28},{28,24},{1,5},{5... | collective-permute-start | bytes 4718600 | tf_op jit(solution)/shard_map/ppermute | solution.py:434
  249.9 25.9 %collective-permute-start.26 = (bf16[8,64,1024]{2,1,0:T(8,128)(2,1)}, bf16[8,64,1024]{2,1,0:T(8,128)(2,1)S(1)}, u32[]{:S(2)}, u32[]{:S(2)}) collective-permute-start(bf16[8,64,1024]{2,1,0:T(8,128)(2,1)} %shard_map.124.refs_2_), channel_id=1, source_target_pairs={{0,1},{1,2},{2,3},{3,0},{4,5},{5,6},{6,7},{7,4},{8,9},{9,10},{10,1... | collective-permute-start | bytes 3145736 | tf_op jit(solution)/shard_map/ppermute | solution.py:450
  277.1 4.8 %collective-permute-start.27 = (bf16[4,128,512]{2,1,0:T(8,128)(2,1)S(1)}, bf16[4,128,512]{2,1,0:T(8,128)(2,1)S(1)}, u32[]{:S(2)}, u32[]{:S(2)}) collective-permute-start(bf16[4,128,512]{2,1,0:T(8,128)(2,1)S(1)} %get-tuple-element.23), channel_id=1, source_target_pairs={{0,4},{4,0},{8,12},{12,8},{16,20},{20,16},{24,28},{28,24},{1,5},{5... | collective-permute-start | bytes 1572872 | tf_op jit(solution)/shard_map/ppermute | solution.py:434
  277.2 30.4 %copy-start.10 = (bf16[128,2048]{1,0:T(8,128)(2,1)S(1)}, bf16[128,2048]{1,0:T(8,128)(2,1)}, u32[]{:S(2)}) copy-start(bf16[128,2048]{1,0:T(8,128)(2,1)} %copy-done.9) | copy-start | bytes 1572868
  278.4 29.2 %collective-permute-start.23 = (bf16[128,1536]{1,0:T(8,128)(2,1)}, bf16[128,1536]{1,0:T(8,128)(2,1)S(1)}, u32[]{:S(2)}, u32[]{:S(2)}) collective-permute-start(bf16[128,1536]{1,0:T(8,128)(2,1)} %get-tuple-element.33), channel_id=1, source_target_pairs={{0,8},{4,12},{8,0},{12,4},{16,24},{20,28},{24,16},{28,20},{1,9},{5... | collective-permute-start | bytes 1179656 | tf_op jit(solution)/shard_map/ppermute | solution.py:434
  279.9 27.7 %collective-permute-start.24 = (bf16[128,1536]{1,0:T(8,128)(2,1)S(1)}, bf16[128,1536]{1,0:T(8,128)(2,1)S(1)}, u32[]{:S(2)}, u32[]{:S(2)}) collective-permute-start(bf16[128,1536]{1,0:T(8,128)(2,1)S(1)} %get-tuple-element.32), channel_id=1, source_target_pairs={{0,16},{4,20},{8,24},{12,28},{16,0},{20,4},{24,8},{28,12},{1,17},{... | collective-permute-start | bytes 1179656 | tf_op jit(solution)/shard_map/ppermute | solution.py:434
  280.4 27.1 %collective-permute-start.25 = (bf16[128,1536]{1,0:T(8,128)(2,1)S(1)}, bf16[128,1536]{1,0:T(8,128)(2,1)S(1)}, u32[]{:S(2)}, u32[]{:S(2)}) collective-permute-start(bf16[128,1536]{1,0:T(8,128)(2,1)S(1)} %get-tuple-element.31), channel_id=1, source_target_pairs={{0,24},{4,28},{8,16},{12,20},{16,8},{20,12},{24,0},{28,4},{1,25},{... | collective-permute-start | bytes 1179656 | tf_op jit(solution)/shard_map/ppermute | solution.py:434
  282.7 18.7 %collective-permute-start.28 = (bf16[128,512]{1,0:T(8,128)(2,1)S(1)}, bf16[128,512]{1,0:T(8,128)(2,1)S(1)}, u32[]{:S(2)}, u32[]{:S(2)}) collective-permute-start(bf16[128,512]{1,0:T(8,128)(2,1)S(1)} %get-tuple-element.39), channel_id=1, source_target_pairs={{0,8},{4,12},{8,0},{12,4},{16,24},{20,28},{24,16},{28,20},{1,9},{5... | collective-permute-start | bytes 393224 | tf_op jit(solution)/shard_map/ppermute | solution.py:434
  284.2 18.7 %collective-permute-start.29 = (bf16[128,512]{1,0:T(8,128)(2,1)}, bf16[128,512]{1,0:T(8,128)(2,1)S(1)}, u32[]{:S(2)}, u32[]{:S(2)}) collective-permute-start(bf16[128,512]{1,0:T(8,128)(2,1)} %get-tuple-element.38), channel_id=1, source_target_pairs={{0,16},{4,20},{8,24},{12,28},{16,0},{20,4},{24,8},{28,12},{1,17},{... | collective-permute-start | bytes 393224 | tf_op jit(solution)/shard_map/ppermute | solution.py:434
  301.4 6.2 %collective-permute-start.30 = (bf16[128,512]{1,0:T(8,128)(2,1)}, bf16[128,512]{1,0:T(8,128)(2,1)S(1)}, u32[]{:S(2)}, u32[]{:S(2)}) collective-permute-start(bf16[128,512]{1,0:T(8,128)(2,1)} %get-tuple-element.37), channel_id=1, source_target_pairs={{0,24},{4,28},{8,16},{12,20},{16,8},{20,12},{24,0},{28,4},{1,25},{... | collective-permute-start | bytes 393224 | tf_op jit(solution)/shard_map/ppermute | solution.py:434
  311.3 45.9 %copy-start.15 = (bf16[128,2048]{1,0:T(8,128)(2,1)S(1)}, bf16[128,2048]{1,0:T(8,128)(2,1)}, u32[]{:S(2)}) copy-start(bf16[128,2048]{1,0:T(8,128)(2,1)} %copy-done.14) | copy-start | bytes 1572868
  312.4 38.4 %collective-permute-start.36 = (bf16[4,4,64,64]{3,2,1,0:T(8,128)(2,1)S(1)}, bf16[4,4,64,64]{3,2,1,0:T(8,128)(2,1)S(1)}, u32[]{:S(2)}, u32[]{:S(2)}) collective-permute-start(bf16[4,4,64,64]{3,2,1,0:T(8,128)(2,1)S(1)} %get-tuple-element.46), channel_id=1, source_target_pairs={{0,4},{1,12},{2,20},{3,28},{4,0},{5,8},{6,16},{7,24},{8,5},{9,13},... | collective-permute-start | bytes 393224 | tf_op jit(solution)/shard_map/ppermute | solution.py:538
  314.2 83.4 %collective-permute-start.31 = (bf16[128,2048]{1,0:T(8,128)(2,1)}, bf16[128,2048]{1,0:T(8,128)(2,1)S(1)}, u32[]{:S(2)}, u32[]{:S(2)}) collective-permute-start(bf16[128,2048]{1,0:T(8,128)(2,1)} %get-tuple-element.25), channel_id=1, source_target_pairs={{0,0},{1,8},{2,16},{3,24},{4,4},{5,12},{6,20},{7,28},{8,1},{9,9},{... | collective-permute-start | bytes 1572872 | tf_op jit(solution)/shard_map/ppermute | solution.py:548
  317.7 79.9 %collective-permute-start.32 = (bf16[128,2048]{1,0:T(8,128)(2,1)}, bf16[128,2048]{1,0:T(8,128)(2,1)S(1)}, u32[]{:S(2)}, u32[]{:S(2)}) collective-permute-start(bf16[128,2048]{1,0:T(8,128)(2,1)} %get-tuple-element.25), channel_id=1, source_target_pairs={{0,1},{1,9},{2,17},{3,25},{4,5},{5,13},{6,21},{7,29},{8,0},{9,8},{... | collective-permute-start | bytes 1572872 | tf_op jit(solution)/shard_map/ppermute | solution.py:548
  319.7 77.9 %collective-permute-start.33 = (bf16[128,2048]{1,0:T(8,128)(2,1)}, bf16[128,2048]{1,0:T(8,128)(2,1)S(1)}, u32[]{:S(2)}, u32[]{:S(2)}) collective-permute-start(bf16[128,2048]{1,0:T(8,128)(2,1)} %get-tuple-element.25), channel_id=1, source_target_pairs={{0,2},{1,10},{2,18},{3,26},{4,6},{5,14},{6,22},{7,30},{8,3},{9,11}... | collective-permute-start | bytes 1572872 | tf_op jit(solution)/shard_map/ppermute | solution.py:548
  320.3 77.4 %collective-permute-start.34 = (bf16[128,2048]{1,0:T(8,128)(2,1)}, bf16[128,2048]{1,0:T(8,128)(2,1)S(1)}, u32[]{:S(2)}, u32[]{:S(2)}) collective-permute-start(bf16[128,2048]{1,0:T(8,128)(2,1)} %get-tuple-element.25), channel_id=1, source_target_pairs={{0,3},{1,11},{2,19},{3,27},{4,7},{5,15},{6,23},{7,31},{8,2},{9,10}... | collective-permute-start | bytes 1572872 | tf_op jit(solution)/shard_map/ppermute | solution.py:548
  350.8 38.0 %copy-start.20 = (bf16[4,4,64,64]{3,2,1,0:T(8,128)(2,1)}, bf16[4,4,64,64]{3,2,1,0:T(8,128)(2,1)S(1)}, u32[]{:S(2)}) copy-start(bf16[4,4,64,64]{3,2,1,0:T(8,128)(2,1)S(1)} %collective-permute-done.36) | copy-start | bytes 393220
  350.8 38.0 %collective-permute-start.35 = (bf16[4,4,64,64]{3,2,1,0:T(8,128)(2,1)S(1)}, bf16[4,4,64,64]{3,2,1,0:T(8,128)(2,1)S(1)}, u32[]{:S(2)}, u32[]{:S(2)}) collective-permute-start(bf16[4,4,64,64]{3,2,1,0:T(8,128)(2,1)S(1)} %get-tuple-element.45), channel_id=1, source_target_pairs={{0,0},{1,8},{2,16},{3,24},{4,4},{5,12},{6,20},{7,28},{8,1},{9,9},{... | collective-permute-start | bytes 393224 | tf_op jit(solution)/shard_map/ppermute | solution.py:538
  358.0 38.7 %all-to-all-start.2 = ((bf16[8,128,256]{2,1,0:T(8,128)(2,1)}), bf16[8,128,256]{2,1,0:T(8,128)(2,1)S(1)}, u32[]{:S(2)}, u32[]{:S(2)}) async-start(bf16[8,128,256]{2,1,0:T(8,128)(2,1)} %bitcast.88), calls=%async_computation.2 | async-start | bytes 1048576 | tf_op jit(solution)/shard_map/all_to_all | solution.py:453
  397.6 8.0 %copy-start.1 = (bf16[2,96,2048]{2,1,0:T(8,128)(2,1)S(1)}, bf16[2,96,2048]{2,1,0:T(8,128)(2,1)}, u32[]{:S(2)}) copy-start(bf16[2,96,2048]{2,1,0:T(8,128)(2,1)} %param.14) | copy-start | bytes 2359300
  (3 other events, 2.3 us)
Sparse Core Ops, SparseCore 0:
  37.0 54.1 all-gather.2
  93.0 45.4 all-gather.4

commit v4 on v3

--- a/solution.py
+++ b/solution.py
@@ -240,8 +240,9 @@
         sums = jnp.concatenate(sums, axis=1)
         sums = [sums[:, i : i + share] for i in range(0, width, share)]
         held = refs[-1]
+        order = list(range(quarters - 2)) + [quarters - 1, quarters - 2]
         for q in range(quarters):
-            held[(place_ref[1] + quarters - q) % quarters] = sums[q]
+            held[(place_ref[1] + quarters - order[q]) % quarters] = sums[q]
         deep = sums[0].shape[1] // (2 * count)
         added = jnp.concatenate(
             [held[q, :, r * deep : (r + 1) * deep] for r in range(2 * count) for q in range(quarters)], axis=1
@@ -330,34 +331,33 @@
 
 
 def value_kernel(count, act, *refs):
-    shards, (even, odd) = refs[:count], refs[-2:]
-    nb = 2 * even.shape[0]
-    chunk = even.shape[1]
+    shards, (even, low, high) = refs[:count], refs[-3:]
+    chips, chunk, _ = even.shape
     start = 0
     for q in range(count):
         weight = shards[q][...].reshape(-1, shards[q].shape[-1])
         at = slice(start, start + weight.shape[0])
         start += weight.shape[0]
-        for k in range(nb // 2):
+        for k in range(chips):
             out = bdot(act[2 * k * chunk : (2 * k + 2) * chunk, :], weight, 1, 1).astype(BF16)
             even[k, :, at] = out[:chunk]
-            odd[k, :, at] = out[chunk:]
-
-
-def value_products(nb, act, shards):
+            odd = low if k < chips // 2 else high
+            odd[k % (chips // 2), :, at] = out[chunk:]
+
+
+def value_products(nb, act, shards, extra):
     deep = shards[0].shape[1]
     chunk = act.shape[0] // nb
     width = sum(x.shape[0] for x in shards) * deep
-
     spec = pl.BlockSpec(memory_space=pltpu.VMEM)
     return pl.pallas_call(
         functools.partial(value_kernel, len(shards)),
-        in_specs=[spec] * (1 + len(shards)),
-        out_specs=[spec] * 2,
-        out_shape=[jax.ShapeDtypeStruct((nb // 2, chunk, width), BF16)] * 2,
+        in_specs=[spec] * (1 + len(shards)) + [pl.BlockSpec(memory_space=pl.ANY)] * len(extra),
+        out_specs=[spec] * 3,
+        out_shape=[jax.ShapeDtypeStruct((n, chunk, width), BF16) for n in (nb // 2, nb // 4, nb // 4)],
         compiler_params=pltpu.CompilerParams(vmem_limit_bytes=40 * 2**20),
         cost_estimate=pl.CostEstimate(flops=10**6, bytes_accessed=2**12, transcendentals=0),
-    )(act, *shards)
+    )(act, *shards, *extra)
 
 
 def next_kernel(nc, place_ref, *refs):
@@ -374,7 +374,8 @@
         copy.start()
     chunk, width = xs[0].shape
     for k in range(nc):
-        x[pl.ds(pl.multiple_of((col ^ k) * chunk, chunk), chunk), :] = xs[k][...]
+        at = col ^ k ^ (place_ref[0] % 2 * (nc // 2))
+        x[pl.ds(pl.multiple_of(at * chunk, chunk), chunk), :] = xs[k][...]
     z = x[...].astype(F32)
     mixed = shifted_mix(z, gate[0:1])
     for copy in copies:
@@ -448,6 +449,9 @@
 
     def ring(x):
         return lax.ppermute(x, "col", [(i, (i + 1) % n_col) for i in range(n_col)])
+
+    def back(x):
+        return lax.ppermute(x, "col", [(i, (i - 1) % n_col) for i in range(n_col)])
 
     def relay(x):
         return lax.all_to_all(x, "row", 0, 0, tiled=True)
@@ -477,10 +481,9 @@
     ff = channel_mix_shards.shape[2] // n_row
     late = channel_mix_shards.astype(BF16).reshape(2, deep, n_row, ff).transpose(2, 0, 1, 3)
     late = relay(after(late, early[0]))
-    keys = [after(late[:, 0], early[-1])]
-    values = [after(late[:, 1], early[-1])]
-    keys.append(ring(keys[0]))
-    values.append(ring(values[0]))
+    key, value = after(late[:, 0], early[-1]), after(late[:, 1], early[-1])
+    keys = [key, ring(key)]
+    key_last = back(key)
 
     prompts = tokens // LMAX
     lens = lax.dynamic_slice_in_dim(lengths, col * prompts, prompts, 0)
@@ -488,15 +491,18 @@
     up = lax.dynamic_slice_in_dim(lowrank_up, row * hc, hc, 2)
     co = lax.dynamic_slice_in_dim(attention_coefficients, row * hc, hc, 1)
     even, odd, own, states = time_mix(
-        place, lens, xg, norms, shift, lowrank_down, up, co, early, (keys[0], values[0]), 2
+        place, lens, xg, norms, shift, lowrank_down, up, co, early, (key,), 2
     )
 
-    keys[1], values[1] = after(keys[1], odd), after(values[1], odd)
+    keys[1] = after(keys[1], odd)
     for k in range(2, n_col - 1):
         keys.append(ring(keys[-1]))
-        values.append(ring(values[-1]))
-    other = to_row(after(odd, keys[1], values[1]), 1)
+    keys.append(key_last)
+    other = to_row(after(odd, keys[1], key_last), 1)
     near = [(even[k].astype(F32) + other[k].astype(F32)).astype(BF16) for k in range(chips)]
+    value = after(value, near[0])
+    values = [value, ring(value)]
+    value_last = back(value)
     pieces = [near[0]] + [to_row(near[k], 2 * k) for k in range(1, chips)]
     gains = norms.transpose(1, 0, 2).reshape(-1, width)
     mid, second, channel_in = settle(
@@ -509,16 +515,17 @@
         wide = second.astype(F32)
         moved_on = jnp.concatenate([edge, wide[:-1]], axis=0)
         channel_in = (wide + (moved_on - wide) * token_shift_weights[5]).astype(BF16)
-    keys[-1], values[-1] = after(keys[-1], mid), after(values[-1], mid)
-    keys.append(ring(keys[-1]))
-    values.append(ring(values[-1]))
+    values[1] = after(values[1], mid)
+    for k in range(2, n_col - 1):
+        values.append(ring(values[-1]))
+    values.insert(n_col - 2, value_last)
     rows_in = [channel_in] + [to_row(channel_in, 2 * k) for k in range(1, chips)]
     rows_in = [piece for x in rows_in for piece in (x, to_row(x, 1))]
     act = key_products(place, rows_in, keys, (last,))
     pieces = []
     for group in (values[:-1], values[-1:]):
-        even, odd = value_products(n_row, act, group)
-        other = to_row(odd, 1)
+        even, low, high = value_products(n_row, act, group, pieces[0][1:] if pieces else ())
+        other = [half[k] for half in (to_row(low, 1), to_row(high, 1)) for k in range(chips // 2)]
         near = [(even[k].astype(F32) + other[k].astype(F32)).astype(BF16) for k in range(chips)]
         pieces.append([near[0]] + [to_row(near[k], 2 * k) for k in range(1, chips)])
     out_own, third, _ = settle(
@@ -526,7 +533,7 @@
     )
     half = prompts // 2
     share = n_row // n_col
-    states = after(states, out_own).reshape(2, half, states.shape[1], HEAD, HEAD)
+    states = after(states, values[-1]).reshape(2, half, states.shape[1], HEAD, HEAD)
     moved = []
     for j in range(2):
         pairs = []
@@ -544,7 +551,7 @@
         pairs = []
         for r in range(n_row):
             for c in range(n_col):
-                pairs.append((r * n_col + c, (2 * c + r % 2) * n_col + ((r // 2) ^ j)))
+                pairs.append((r * n_col + c, (2 * c + r % 2) * n_col + ((r // 2) ^ j ^ (r % 2 * (n_col // 2)))))
         arrived.append(lax.ppermute(third, ("row", "col"), pairs))
     blocks = relay(out_own.reshape(chunk, n_row, fw).transpose(1, 0, 2))
     out_hidden = blocks.reshape(chips, 2, chunk, fw).transpose(1, 0, 2, 3).reshape(tokens, fw)

time: 414 us -> 384 us (0.928)
  waiting for transfers between devices: 218 us -> 188 us
  starting transfers between devices: 65.7 us -> 60.9 us
    ppermute x2, waiting for transfers between devices: 51.5 us -> 0.01 us  [per_device(): moved.append(lax.ppermute(piece, ('row', 'col'), pairs))]
    ppermute x19 -> x21, waiting for transfers between devices: 57 us -> 71.2 us  [to_row(): return lax.ppermute(x, 'row', [(i, i ^ k) for i in range(n_row)])]
    ppermute x9 -> x7, waiting for transfers between devices: 95.8 us -> 82.6 us  [ring(): return lax.ppermute(x, 'col', [(i, (i + 1) % n_col) for i in range(n_col)])]
    ppermute x9 -> x7, starting transfers between devices: 14.1 us -> 1.43 us  [ring(): return lax.ppermute(x, 'col', [(i, (i + 1) % n_col) for i in range(n_col)])]
    ppermute x4, waiting for transfers between devices: 0.01 us -> 12 us  [per_device(): arrived.append(lax.ppermute(third, ('row', 'col'), pairs))]
    all_to_all x3, starting transfers between devices: 12.4 us -> 23.2 us  [relay(): return lax.all_to_all(x, 'row', 0, 0, tiled=True)]
    ppermute x4, starting transfers between devices: 12.5 us -> 3.94 us  [per_device(): arrived.append(lax.ppermute(third, ('row', 'col'), pairs))]
    all_to_all x3, waiting for transfers between devices: 0.01 us -> 8.02 us  [relay(): return lax.all_to_all(x, 'row', 0, 0, tiled=True)]
  transfers between devices with their start and end apart: 42 -> 44, of which waited for: 15 -> 21; matrix products, arithmetic and copies ran while one was open for 7% -> 8% of each run, Pallas kernels for 11% -> 15%
where the time goes in v4:
time: 384 us; the launch traced here: 381 us
  waiting for transfers between devices  188 us (49%)
  Pallas kernels  71.6 us (19%)
  starting transfers between devices  60.9 us (16%)
  local copies, waits for them, and re-layouts  34.3 us (9%)
  between operations  14.5 us (4%)
  other arithmetic  11.7 us (3%)
    ppermute x7, waiting for transfers between devices, ring(): return lax.ppermute(x, 'col', [(i, (i + 1) % n_col) for i in range(n_col)])  82.6 us
    ppermute x21, waiting for transfers between devices, to_row(): return lax.ppermute(x, 'row', [(i, i ^ k) for i in range(n_row)])  71.2 us
    pallas_call x1, Pallas kernels, time_mix(): pl.pallas_call(functools.partial(time_kernel, nc, per), grid=(prompts //...  43.1 us
    all_to_all x3, starting transfers between devices, relay(): return lax.all_to_all(x, 'row', 0, 0, tiled=True)  23.2 us
    unnamed x68, local copies, waits for them, and re-layouts  15.7 us
    ppermute x21, starting transfers between devices, to_row(): return lax.ppermute(x, 'row', [(i, i ^ k) for i in range(n_row)])  15.7 us
    ppermute x3, waiting for transfers between devices, to_col(): return lax.ppermute(x, 'col', [(i, i ^ k) for i in range(n_col)])  13.8 us
    ppermute x4, waiting for transfers between devices, per_device(): arrived.append(lax.ppermute(third, ('row', 'col'), pairs))  12 us
  transfers between devices with their start and end apart: 44, of which 21 were waited for; matrix products, arithmetic and copies ran while one was open for 8% of the time, Pallas kernels for 15%

profile of v4, /device:TPU:12, one launch (start us, length us, event | category | flops | bytes accessed | tf_op | source)
XLA Modules:
  0.0 380.6 jit_solution(5672408766890949541)
XLA Ops:
  7.2 1.8 slice.214
  9.0 1.1 copy.58
  10.1 4.2 %all-to-all-start = ((bf16[8,4,64,256]{3,2,1,0:T(8,128)(2,1)}), bf16[8,4,64,256]{3,2,1,0:T(8,128)(2,1)S(1)}, u32[]{:S(2)}, u32[]{:S(2)}) async-start(bf16[8,4,64,256]{3,2,1,0:T(8,128)(2,1)} %bitcast.86), calls=%async_computation | async-start | bytes 2097152 | tf_op jit(solution)/shard_map/all_to_all | solution.py:457
  14.4 1.6 slice.120
  16.1 1.6 collective-permute-start.2
  17.7 1.2 collective-permute-start.1
  18.9 1.2 collective-permute-start
  21.0 11.2 %collective-permute-done.2 = bf16[3,64,512]{2,1,0:T(8,128)(2,1)S(1)} collective-permute-done((bf16[3,64,512]{2,1,0:T(8,128)(2,1)S(1)}, bf16[3,64,512]{2,1,0:T(8,128)(2,1)S(1)}, u32[]{:S(2)}, u32[]{:S(2)}) %collective-permute-start.2) | collective-permute-done | bytes 196640 | tf_op jit(solution)/shard_map/ppermute | solution.py:438
  32.3 2.5 collective-permute-done.1
  36.8 1.1 copy-done.4
  38.5 2.4 convert_element_type.201
  40.9 1.6 copy.57
  42.5 4.7 %all-to-all-start.1 = ((bf16[8,2,64,1024]{3,2,1,0:T(8,128)(2,1)}), bf16[8,2,64,1024]{3,2,1,0:T(8,128)(2,1)}, u32[]{:S(2)}, u32[]{:S(2)}) async-start(bf16[8,2,64,1024]{3,2,1,0:T(8,128)(2,1)} %shard_map.114), calls=%async_computation.1 | async-start | bytes 4194304 | tf_op jit(solution)/shard_map/all_to_all | solution.py:457
  47.2 15.9 %collective-permute-done.3.refs_1_ = bf16[8,4,64,256]{3,2,1,0:T(8,128)(2,1)} collective-permute-done((bf16[8,4,64,256]{3,2,1,0:T(8,128)(2,1)S(1)}, bf16[8,4,64,256]{3,2,1,0:T(8,128)(2,1)}, u32[]{:S(2)}, u32[]{:S(2)}) %collective-permute-start.3) | collective-permute-done | bytes 1048608 | tf_op jit(solution)/shard_map/ppermute | solution.py:451
  63.8 24.8 %collective-permute-done.4.refs_2_ = bf16[8,4,64,256]{3,2,1,0:T(8,128)(2,1)} collective-permute-done((bf16[8,4,64,256]{3,2,1,0:T(8,128)(2,1)}, bf16[8,4,64,256]{3,2,1,0:T(8,128)(2,1)}, u32[]{:S(2)}, u32[]{:S(2)}) %collective-permute-start.4) | collective-permute-done | bytes 1048608 | tf_op jit(solution)/shard_map/ppermute | solution.py:451
  88.8 1.3 copy.42.ld
  91.0 3.1 slice_bitcast_fusion
  94.1 19.1 %collective-permute-done.5.refs_1_.refs_3_ = bf16[8,4,64,256]{3,2,1,0:T(8,128)(2,1)S(1)} collective-permute-done((bf16[8,4,64,256]{3,2,1,0:T(8,128)(2,1)}, bf16[8,4,64,256]{3,2,1,0:T(8,128)(2,1)S(1)}, u32[]{:S(2)}, u32[]{:S(2)}) %collective-permute-start.5) | collective-permute-done | bytes 1048608 | tf_op jit(solution)/shard_map/ppermute | solution.py:451
  114.2 3.6 collective-permute-start.7
  119.5 1.2 copy-done.14
  120.7 43.1 %shard_map.116 = (bf16[4,128,2048]{2,1,0:T(8,128)(2,1)}, bf16[4,128,2048]{2,1,0:T(8,128)(2,1)}, bf16[128,2048]{1,0:T(8,128)(2,1)S(1)}, bf16[8,4,64,64]{3,2,1,0:T(8,128)(2,1)S(1)}) custom-call(s32[2]{0:T(128)S(1)} %pad_add_fusion.place_ref, s32[8]{0:T(128)S(1)} %dynamic_slice.28.lens, bf16[8,1056,256]{2,1,0:T(8,128)(2,1)} %bitcast.110, ...), custom_call_target="tpu_custom_call" | custom-call | flops 40000000000 | bytes 16777216 | tf_op jit(solution)/shard_map/pallas_call | solution.py:192
  165.8 4.2 %collective-permute-done.8 = bf16[4,128,2048]{2,1,0:T(8,128)(2,1)} collective-permute-done((bf16[4,128,2048]{2,1,0:T(8,128)(2,1)}, bf16[4,128,2048]{2,1,0:T(8,128)(2,1)}, u32[]{:S(2)}, u32[]{:S(2)}) %collective-permute-start.8) | collective-permute-done | bytes 2097184 | tf_op jit(solution)/shard_map/ppermute | solution.py:435
  170.1 3.4 fusion.3
  173.5 1.5 collective-permute-start.9
  175.6 1.4 collective-permute-start.11
  177.1 11.4 %collective-permute-done.9.refs_1_ = bf16[128,2048]{1,0:T(8,128)(2,1)S(1)} collective-permute-done((bf16[128,2048]{1,0:T(8,128)(2,1)}, bf16[128,2048]{1,0:T(8,128)(2,1)S(1)}, u32[]{:S(2)}, u32[]{:S(2)}) %collective-permute-start.9) | collective-permute-done | bytes 524320 | tf_op jit(solution)/shard_map/ppermute | solution.py:435
  189.4 10.8 %collective-permute-done.10.refs_2_ = bf16[128,2048]{1,0:T(8,128)(2,1)S(1)} collective-permute-done((bf16[128,2048]{1,0:T(8,128)(2,1)}, bf16[128,2048]{1,0:T(8,128)(2,1)S(1)}, u32[]{:S(2)}, u32[]{:S(2)}) %collective-permute-start.10) | collective-permute-done | bytes 524320 | tf_op jit(solution)/shard_map/ppermute | solution.py:435
  200.9 1.0 copy-done.20
  202.0 1.0 copy-done.22
  203.0 3.1 shard_map.119
  207.4 1.5 collective-permute-start.15
  209.0 1.4 collective-permute-start.17
  210.4 3.9 %collective-permute-start.21 = (bf16[8,64,1024]{2,1,0:T(8,128)(2,1)S(1)}, bf16[8,64,1024]{2,1,0:T(8,128)(2,1)}, u32[]{:S(2)}, u32[]{:S(2)}) collective-permute-start(bf16[8,64,1024]{2,1,0:T(8,128)(2,1)S(1)} %copy-done.2), channel_id=1, source_target_pairs={{0,3},{1,0},{2,1},{3,2},{4,7},{5,4},{6,5},{7,6},{8,11},{9,8},{10,9... | collective-permute-start | bytes 3145736 | tf_op jit(solution)/shard_map/ppermute | solution.py:454
  214.3 2.2 collective-permute-done.20.refs_0_
  216.4 5.5 %collective-permute-done.13.refs_2_ = bf16[128,2048]{1,0:T(8,128)(2,1)S(1)} collective-permute-done((bf16[128,2048]{1,0:T(8,128)(2,1)}, bf16[128,2048]{1,0:T(8,128)(2,1)S(1)}, u32[]{:S(2)}, u32[]{:S(2)}) %collective-permute-start.13) | collective-permute-done | bytes 524320 | tf_op jit(solution)/shard_map/ppermute | solution.py:435
  222.0 8.9 %collective-permute-done.15.refs_4_ = bf16[128,2048]{1,0:T(8,128)(2,1)S(1)} collective-permute-done((bf16[128,2048]{1,0:T(8,128)(2,1)}, bf16[128,2048]{1,0:T(8,128)(2,1)S(1)}, u32[]{:S(2)}, u32[]{:S(2)}) %collective-permute-start.15) | collective-permute-done | bytes 524320 | tf_op jit(solution)/shard_map/ppermute | solution.py:435
  231.4 1.5 collective-permute-done.16.refs_5_
  233.9 1.2 copy-done.9
  236.1 7.6 %shard_map.120.act = bf16[1024,1024]{1,0:T(8,128)(2,1)S(1)} custom-call(s32[2]{0:T(128)S(1)} %pad_add_fusion.place_ref, bf16[128,2048]{1,0:T(8,128)(2,1)} %get-tuple-element.20.refs_0_, bf16[128,2048]{1,0:T(8,128)(2,1)} %collective-permute-done.12.refs_1_, bf16[128,2048]{1,0:T(8,128)(2,1)S(1)} %collective-permute-done.13.refs_2_, ...), custom_call_target="tpu_custom_call" | custom-call | flops 1000000 | bytes 4096 | tf_op jit(solution)/shard_map/pallas_call | solution.py:318
  243.8 5.0 %shard_map.124 = (bf16[4,128,1536]{2,1,0:T(8,128)(2,1)S(1)}, bf16[2,128,1536]{2,1,0:T(8,128)(2,1)S(1)}, bf16[2,128,1536]{2,1,0:T(8,128)(2,1)S(1)}) custom-call(bf16[1024,1024]{1,0:T(8,128)(2,1)S(1)} %shard_map.120.act, bf16[8,64,1024]{2,1,0:T(8,128)(2,1)S(1)} %copy-done.2, bf16[8,64,1024]{2,1,0:T(8,128)(2,1)} %shard_map.123.refs_1_, ...), custom_call_target="tpu_custom_call" | custom-call | flops 1000000 | bytes 4096 | tf_op jit(solution)/shard_map/pallas_call | solution.py:353
  249.3 1.8 collective-permute-done.24
  251.1 1.1 collective-permute-done.22
  252.7 1.6 collective-permute-start.23
  254.7 1.5 collective-permute-start.26
  256.2 20.5 %collective-permute-done.27.refs_0_.refs_1_ = bf16[8,64,1024]{2,1,0:T(8,128)(2,1)S(1)} collective-permute-done((bf16[8,64,1024]{2,1,0:T(8,128)(2,1)}, bf16[8,64,1024]{2,1,0:T(8,128)(2,1)S(1)}, u32[]{:S(2)}, u32[]{:S(2)}) %collective-permute-start.27) | collective-permute-done | bytes 1048608 | tf_op jit(solution)/shard_map/ppermute | solution.py:451
  276.8 2.0 shard_map.125
  280.1 1.6 collective-permute-done.30
  281.8 1.7 collective-permute-start.29
  283.9 1.5 collective-permute-start.32
  285.4 1.1 dynamic-slice_bitcast_fusion.1
  286.5 4.8 %collective-permute-start.37 = (bf16[4,4,64,64]{3,2,1,0:T(8,128)(2,1)S(1)}, bf16[4,4,64,64]{3,2,1,0:T(8,128)(2,1)}, u32[]{:S(2)}, u32[]{:S(2)}) collective-permute-start(bf16[4,4,64,64]{3,2,1,0:T(8,128)(2,1)S(1)} %get-tuple-element.51), channel_id=1, source_target_pairs={{0,0},{1,8},{2,16},{3,24},{4,4},{5,12},{6,20},{7,28},{8,1},{9,9},{... | collective-permute-start | bytes 393224 | tf_op jit(solution)/shard_map/ppermute | solution.py:545
  292.1 22.7 %collective-permute-done.32.refs_7_ = bf16[128,512]{1,0:T(8,128)(2,1)S(1)} collective-permute-done((bf16[128,512]{1,0:T(8,128)(2,1)S(1)}, bf16[128,512]{1,0:T(8,128)(2,1)S(1)}, u32[]{:S(2)}, u32[]{:S(2)}) %collective-permute-start.32) | collective-permute-done | bytes 131104 | tf_op jit(solution)/shard_map/ppermute | solution.py:435
  314.8 2.9 shard_map.126
  317.7 1.9 collective-permute-start.33
  319.6 1.9 collective-permute-start.35
  323.4 14.3 %all-to-all-start.2 = ((bf16[8,128,256]{2,1,0:T(8,128)(2,1)}), bf16[8,128,256]{2,1,0:T(8,128)(2,1)S(1)}, u32[]{:S(2)}, u32[]{:S(2)}) async-start(bf16[8,128,256]{2,1,0:T(8,128)(2,1)} %bitcast.88), calls=%async_computation.2 | async-start | bytes 1048576 | tf_op jit(solution)/shard_map/all_to_all | solution.py:457
  337.7 1.2 pad_maximum_fusion.2
  338.9 1.4 gather_fusion
  340.3 1.2 convert_bitcast_fusion
  341.5 1.1 copy.46
  342.6 2.4 reshape.121
  344.9 8.0 %all-to-all-done.2 = bf16[8,128,256]{2,1,0:T(8,128)(2,1)S(1)} async-done(((bf16[8,128,256]{2,1,0:T(8,128)(2,1)}), bf16[8,128,256]{2,1,0:T(8,128)(2,1)S(1)}, u32[]{:S(2)}, u32[]{:S(2)}) %all-to-all-start.2) | async-done | bytes 524320 | tf_op jit(solution)/shard_map/all_to_all | solution.py:457
  353.8 12.0 %collective-permute-done.34.refs_1_ = bf16[128,2048]{1,0:T(8,128)(2,1)S(1)} collective-permute-done((bf16[128,2048]{1,0:T(8,128)(2,1)}, bf16[128,2048]{1,0:T(8,128)(2,1)S(1)}, u32[]{:S(2)}, u32[]{:S(2)}) %collective-permute-start.34) | collective-permute-done | bytes 524320 | tf_op jit(solution)/shard_map/ppermute | solution.py:555
  365.8 8.0 %shard_map.127 = bf16[3,512,512]{2,1,0:T(8,128)(2,1)} custom-call(s32[2]{0:T(128)S(1)} %pad_add_fusion.place_ref, bf16[128,2048]{1,0:T(8,128)(2,1)S(1)} %collective-permute-done.33.refs_0_, bf16[128,2048]{1,0:T(8,128)(2,1)S(1)} %collective-permute-done.34.refs_1_, bf16[128,2048]{1,0:T(8,128)(2,1)S(1)} %collective-permute-done.35.refs_2_, ...), custom_call_target="tpu_custom_call" | custom-call | flops 1000000 | bytes 4096 | tf_op jit(solution)/shard_map/pallas_call | solution.py:394
  (149 shorter events, 22.9 us)
Async XLA Ops:
  7.2 83.8 %copy-start = (bf16[2,96,2048]{2,1,0:T(8,128)(2,1)S(1)}, bf16[2,96,2048]{2,1,0:T(8,128)(2,1)}, u32[]{:S(2)}) copy-start(bf16[2,96,2048]{2,1,0:T(8,128)(2,1)} %param.14) | copy-start | bytes 2359300
  10.1 25.7 %all-to-all-start = ((bf16[8,4,64,256]{3,2,1,0:T(8,128)(2,1)}), bf16[8,4,64,256]{3,2,1,0:T(8,128)(2,1)S(1)}, u32[]{:S(2)}, u32[]{:S(2)}) async-start(bf16[8,4,64,256]{3,2,1,0:T(8,128)(2,1)} %bitcast.86), calls=%async_computation | async-start | bytes 2097152 | tf_op jit(solution)/shard_map/all_to_all | solution.py:457
  14.3 5.9 %copy-start.31 = (f32[6,256]{1,0:T(8,128)S(1)}, f32[6,256]{1,0:T(8,128)}, u32[]{:S(2)}) copy-start(f32[6,256]{1,0:T(8,128)} %param.17) | copy-start | bytes 18436
  14.3 5.9 %copy-start.28 = (bf16[1024,256]{1,0:T(8,128)(2,1)S(1)}, bf16[1024,256]{1,0:T(8,128)(2,1)}, u32[]{:S(2)}) copy-start(bf16[1024,256]{1,0:T(8,128)(2,1)} %param.9) | copy-start | bytes 1572868
  14.3 103.5 %all-gather.3.cloned.1.call-start = ((), (), s32[]{:S(2)}) async-start(), calls=%async_computation.3 | async-start | bytes 4866048 | tf_op jit(solution)/shard_map/all_gather | solution.py:474
  16.1 16.2 %collective-permute-start.2 = (bf16[3,64,512]{2,1,0:T(8,128)(2,1)S(1)}, bf16[3,64,512]{2,1,0:T(8,128)(2,1)S(1)}, u32[]{:S(2)}, u32[]{:S(2)}) collective-permute-start(bf16[3,64,512]{2,1,0:T(8,128)(2,1)S(1)} %get-tuple-element.48), channel_id=1, source_target_pairs={{0,3},{1,2},{2,1},{3,0},{4,7},{5,6},{6,5},{7,4},{8,11},{9,10},{10,... | collective-permute-start | bytes 589832 | tf_op jit(solution)/shard_map/ppermute | solution.py:438
  17.7 17.1 %collective-permute-start.1 = (bf16[3,64,512]{2,1,0:T(8,128)(2,1)S(1)}, bf16[3,64,512]{2,1,0:T(8,128)(2,1)S(1)}, u32[]{:S(2)}, u32[]{:S(2)}) collective-permute-start(bf16[3,64,512]{2,1,0:T(8,128)(2,1)S(1)} %get-tuple-element.49), channel_id=1, source_target_pairs={{0,2},{1,3},{2,0},{3,1},{4,6},{5,7},{6,4},{7,5},{8,10},{9,11},{10,... | collective-permute-start | bytes 589832 | tf_op jit(solution)/shard_map/ppermute | solution.py:438
  18.9 15.9 %collective-permute-start = (bf16[3,64,512]{2,1,0:T(8,128)(2,1)S(1)}, bf16[3,64,512]{2,1,0:T(8,128)(2,1)S(1)}, u32[]{:S(2)}, u32[]{:S(2)}) collective-permute-start(bf16[3,64,512]{2,1,0:T(8,128)(2,1)S(1)} %get-tuple-element.50), channel_id=1, source_target_pairs={{0,1},{1,0},{2,3},{3,2},{4,5},{5,4},{6,7},{7,6},{8,9},{9,8},{10,11... | collective-permute-start | bytes 589832 | tf_op jit(solution)/shard_map/ppermute | solution.py:438
  36.8 194.6 %all-gather.5.cloned.1.call-start = ((), (), s32[]{:S(2)}) async-start(), calls=%async_computation.4 | async-start | bytes 7077888 | tf_op jit(solution)/shard_map/all_gather | solution.py:480
  38.0 25.1 %collective-permute-start.3 = (bf16[8,4,64,256]{3,2,1,0:T(8,128)(2,1)S(1)}, bf16[8,4,64,256]{3,2,1,0:T(8,128)(2,1)}, u32[]{:S(2)}, u32[]{:S(2)}) collective-permute-start(bf16[8,4,64,256]{3,2,1,0:T(8,128)(2,1)S(1)} %copy-done.4), channel_id=1, source_target_pairs={{0,1},{1,2},{2,3},{3,0},{4,5},{5,6},{6,7},{7,4},{8,9},{9,10},{10,1... | collective-permute-start | bytes 3145736 | tf_op jit(solution)/shard_map/ppermute | solution.py:451
  42.5 46.2 %copy-start.30 = (f32[9,2048]{1,0:T(8,128)S(1)}, f32[9,2048]{1,0:T(8,128)}, u32[]{:S(2)}) copy-start(f32[9,2048]{1,0:T(8,128)} %param.15) | copy-start | bytes 221188
  42.5 46.3 %copy-start.27 = (bf16[2,2048,96]{1,2,0:T(8,128)(2,1)S(1)}, bf16[2,2048,96]{1,2,0:T(8,128)(2,1)}, u32[]{:S(2)}) copy-start(bf16[2,2048,96]{1,2,0:T(8,128)(2,1)} %param.13) | copy-start | bytes 2359300
  42.5 48.5 %all-to-all-start.1 = ((bf16[8,2,64,1024]{3,2,1,0:T(8,128)(2,1)}), bf16[8,2,64,1024]{3,2,1,0:T(8,128)(2,1)}, u32[]{:S(2)}, u32[]{:S(2)}) async-start(bf16[8,2,64,1024]{3,2,1,0:T(8,128)(2,1)} %shard_map.114), calls=%async_computation.1 | async-start | bytes 4194304 | tf_op jit(solution)/shard_map/all_to_all | solution.py:457
  47.2 42.9 %copy-start.32 = (s32[32]{0:T(128)S(1)}, s32[32]{0:T(128)}, u32[]{:S(2)}) copy-start(s32[32]{0:T(128)} %param.10) | copy-start | bytes 388
  63.1 25.6 %collective-permute-start.4 = (bf16[8,4,64,256]{3,2,1,0:T(8,128)(2,1)}, bf16[8,4,64,256]{3,2,1,0:T(8,128)(2,1)}, u32[]{:S(2)}, u32[]{:S(2)}) collective-permute-start(bf16[8,4,64,256]{3,2,1,0:T(8,128)(2,1)} %collective-permute-done.3.refs_1_), channel_id=1, source_target_pairs={{0,1},{1,2},{2,3},{3,0},{4,5},{5,6},{6,7},{7,4},{8,9},{9,10},{10,1... | collective-permute-start | bytes 3145736 | tf_op jit(solution)/shard_map/ppermute | solution.py:451
  88.7 24.5 %collective-permute-start.5 = (bf16[8,4,64,256]{3,2,1,0:T(8,128)(2,1)}, bf16[8,4,64,256]{3,2,1,0:T(8,128)(2,1)S(1)}, u32[]{:S(2)}, u32[]{:S(2)}) collective-permute-start(bf16[8,4,64,256]{3,2,1,0:T(8,128)(2,1)} %collective-permute-done.4.refs_2_), channel_id=1, source_target_pairs={{0,1},{1,2},{2,3},{3,0},{4,5},{5,6},{6,7},{7,4},{8,9},{9,10},{10,1... | collective-permute-start | bytes 3145736 | tf_op jit(solution)/shard_map/ppermute | solution.py:451
  94.1 25.4 %copy-start.5 = (bf16[8,4,64,256]{3,2,1,0:T(8,128)(2,1)S(1)}, bf16[8,4,64,256]{3,2,1,0:T(8,128)(2,1)}, u32[]{:S(2)}) copy-start(bf16[8,4,64,256]{3,2,1,0:T(8,128)(2,1)} %shard_map.112.refs_1_.refs_0_) | copy-start | bytes 3145732
  114.2 50.4 %collective-permute-start.6 = (bf16[8,64,1024]{2,1,0:T(8,128)(2,1)}, bf16[8,64,1024]{2,1,0:T(8,128)(2,1)}, u32[]{:S(2)}, u32[]{:S(2)}) collective-permute-start(bf16[8,64,1024]{2,1,0:T(8,128)(2,1)} %shard_map.115.refs_4_.refs_8_), channel_id=1, source_target_pairs={{0,1},{1,2},{2,3},{3,0},{4,5},{5,6},{6,7},{7,4},{8,9},{9,10},{10,1... | collective-permute-start | bytes 3145736 | tf_op jit(solution)/shard_map/ppermute | solution.py:451
  114.2 50.4 %collective-permute-start.7 = (bf16[8,64,1024]{2,1,0:T(8,128)(2,1)}, bf16[8,64,1024]{2,1,0:T(8,128)(2,1)S(1)}, u32[]{:S(2)}, u32[]{:S(2)}) collective-permute-start(bf16[8,64,1024]{2,1,0:T(8,128)(2,1)} %shard_map.115.refs_4_.refs_8_), channel_id=1, source_target_pairs={{0,3},{1,0},{2,1},{3,2},{4,7},{5,4},{6,5},{7,6},{8,11},{9,8},{10,9... | collective-permute-start | bytes 3145736 | tf_op jit(solution)/shard_map/ppermute | solution.py:454
  119.5 1.2 copy-start.14
  165.6 4.5 %copy-start.24 = (bf16[4,128,2048]{2,1,0:T(8,128)(2,1)S(1)}, bf16[4,128,2048]{2,1,0:T(8,128)(2,1)}, u32[]{:S(2)}) copy-start(bf16[4,128,2048]{2,1,0:T(8,128)(2,1)} %get-tuple-element.17) | copy-start | bytes 6291460
  165.6 4.5 %collective-permute-start.8 = (bf16[4,128,2048]{2,1,0:T(8,128)(2,1)}, bf16[4,128,2048]{2,1,0:T(8,128)(2,1)}, u32[]{:S(2)}, u32[]{:S(2)}) collective-permute-start(bf16[4,128,2048]{2,1,0:T(8,128)(2,1)} %shard_map.118), channel_id=1, source_target_pairs={{0,4},{4,0},{8,12},{12,8},{16,20},{20,16},{24,28},{28,24},{1,5},{5... | collective-permute-start | bytes 6291464 | tf_op jit(solution)/shard_map/ppermute | solution.py:435
  165.6 44.8 %collective-permute-start.19 = (bf16[8,64,1024]{2,1,0:T(8,128)(2,1)}, bf16[8,64,1024]{2,1,0:T(8,128)(2,1)}, u32[]{:S(2)}, u32[]{:S(2)}) collective-permute-start(bf16[8,64,1024]{2,1,0:T(8,128)(2,1)} %shard_map.117.refs_1_.refs_9_), channel_id=1, source_target_pairs={{0,1},{1,2},{2,3},{3,0},{4,5},{5,6},{6,7},{7,4},{8,9},{9,10},{10,1... | collective-permute-start | bytes 3145736 | tf_op jit(solution)/shard_map/ppermute | solution.py:451
  173.5 3.5 copy-start.26
  173.5 27.4 %copy-start.7 = (bf16[128,2048]{1,0:T(8,128)(2,1)S(1)}, bf16[128,2048]{1,0:T(8,128)(2,1)}, u32[]{:S(2)}) copy-start(bf16[128,2048]{1,0:T(8,128)(2,1)} %get-tuple-element.34.refs_0_.refs_1_) | copy-start | bytes 1572868
  173.5 15.0 %collective-permute-start.9 = (bf16[128,2048]{1,0:T(8,128)(2,1)}, bf16[128,2048]{1,0:T(8,128)(2,1)S(1)}, u32[]{:S(2)}, u32[]{:S(2)}) collective-permute-start(bf16[128,2048]{1,0:T(8,128)(2,1)} %get-tuple-element.33), channel_id=1, source_target_pairs={{0,8},{4,12},{8,0},{12,4},{16,24},{20,28},{24,16},{28,20},{1,9},{5... | collective-permute-start | bytes 1572872 | tf_op jit(solution)/shard_map/ppermute | solution.py:435
  175.0 25.1 %collective-permute-start.10 = (bf16[128,2048]{1,0:T(8,128)(2,1)}, bf16[128,2048]{1,0:T(8,128)(2,1)S(1)}, u32[]{:S(2)}, u32[]{:S(2)}) collective-permute-start(bf16[128,2048]{1,0:T(8,128)(2,1)} %get-tuple-element.32), channel_id=1, source_target_pairs={{0,16},{4,20},{8,24},{12,28},{16,0},{20,4},{24,8},{28,12},{1,17},{... | collective-permute-start | bytes 1572872 | tf_op jit(solution)/shard_map/ppermute | solution.py:435
  175.6 25.3 %collective-permute-start.11 = (bf16[128,2048]{1,0:T(8,128)(2,1)}, bf16[128,2048]{1,0:T(8,128)(2,1)}, u32[]{:S(2)}, u32[]{:S(2)}) collective-permute-start(bf16[128,2048]{1,0:T(8,128)(2,1)} %get-tuple-element.31), channel_id=1, source_target_pairs={{0,24},{4,28},{8,16},{12,20},{16,8},{20,12},{24,0},{28,4},{1,25},{... | collective-permute-start | bytes 1572872 | tf_op jit(solution)/shard_map/ppermute | solution.py:435
  177.0 33.4 %copy-start.2 = (bf16[8,64,1024]{2,1,0:T(8,128)(2,1)S(1)}, bf16[8,64,1024]{2,1,0:T(8,128)(2,1)}, u32[]{:S(2)}) copy-start(bf16[8,64,1024]{2,1,0:T(8,128)(2,1)} %shard_map.122.refs_0_) | copy-start | bytes 3145732
  177.0 39.4 %collective-permute-start.20 = (bf16[8,64,1024]{2,1,0:T(8,128)(2,1)}, bf16[8,64,1024]{2,1,0:T(8,128)(2,1)}, u32[]{:S(2)}, u32[]{:S(2)}) collective-permute-start(bf16[8,64,1024]{2,1,0:T(8,128)(2,1)} %shard_map.122.refs_0_), channel_id=1, source_target_pairs={{0,1},{1,2},{2,3},{3,0},{4,5},{5,6},{6,7},{7,4},{8,9},{9,10},{10,1... | collective-permute-start | bytes 3145736 | tf_op jit(solution)/shard_map/ppermute | solution.py:451
  203.0 30.9 %copy-start.6 = (bf16[8,64,1024]{2,1,0:T(8,128)(2,1)S(1)}, bf16[8,64,1024]{2,1,0:T(8,128)(2,1)}, u32[]{:S(2)}) copy-start(bf16[8,64,1024]{2,1,0:T(8,128)(2,1)} %shard_map.115.refs_4_.refs_8_) | copy-start | bytes 3145732
  206.9 15.1 %collective-permute-start.13 = (bf16[128,2048]{1,0:T(8,128)(2,1)}, bf16[128,2048]{1,0:T(8,128)(2,1)S(1)}, u32[]{:S(2)}, u32[]{:S(2)}) collective-permute-start(bf16[128,2048]{1,0:T(8,128)(2,1)} %get-tuple-element.20.refs_0_), channel_id=1, source_target_pairs={{0,8},{4,12},{8,0},{12,4},{16,24},{20,28},{24,16},{28,20},{1,9},{5... | collective-permute-start | bytes 1572872 | tf_op jit(solution)/shard_map/ppermute | solution.py:435
  207.4 23.4 %collective-permute-start.15 = (bf16[128,2048]{1,0:T(8,128)(2,1)}, bf16[128,2048]{1,0:T(8,128)(2,1)S(1)}, u32[]{:S(2)}, u32[]{:S(2)}) collective-permute-start(bf16[128,2048]{1,0:T(8,128)(2,1)} %get-tuple-element.20.refs_0_), channel_id=1, source_target_pairs={{0,16},{4,20},{8,24},{12,28},{16,0},{20,4},{24,8},{28,12},{1,17},{... | collective-permute-start | bytes 1572872 | tf_op jit(solution)/shard_map/ppermute | solution.py:435
  209.0 21.9 %collective-permute-start.17 = (bf16[128,2048]{1,0:T(8,128)(2,1)}, bf16[128,2048]{1,0:T(8,128)(2,1)}, u32[]{:S(2)}, u32[]{:S(2)}) collective-permute-start(bf16[128,2048]{1,0:T(8,128)(2,1)} %get-tuple-element.20.refs_0_), channel_id=1, source_target_pairs={{0,24},{4,28},{8,16},{12,20},{16,8},{20,12},{24,0},{28,4},{1,25},{... | collective-permute-start | bytes 1572872 | tf_op jit(solution)/shard_map/ppermute | solution.py:435
  210.4 33.4 %collective-permute-start.21 = (bf16[8,64,1024]{2,1,0:T(8,128)(2,1)S(1)}, bf16[8,64,1024]{2,1,0:T(8,128)(2,1)}, u32[]{:S(2)}, u32[]{:S(2)}) collective-permute-start(bf16[8,64,1024]{2,1,0:T(8,128)(2,1)S(1)} %copy-done.2), channel_id=1, source_target_pairs={{0,3},{1,0},{2,1},{3,2},{4,7},{5,4},{6,5},{7,6},{8,11},{9,8},{10,9... | collective-permute-start | bytes 3145736 | tf_op jit(solution)/shard_map/ppermute | solution.py:454
  216.4 14.9 %collective-permute-start.12 = (bf16[128,2048]{1,0:T(8,128)(2,1)}, bf16[128,2048]{1,0:T(8,128)(2,1)}, u32[]{:S(2)}, u32[]{:S(2)}) collective-permute-start(bf16[128,2048]{1,0:T(8,128)(2,1)} %get-tuple-element.20.refs_0_), channel_id=1, source_target_pairs={{0,4},{4,0},{8,12},{12,8},{16,20},{20,16},{24,28},{28,24},{1,5},{5... | collective-permute-start | bytes 1572872 | tf_op jit(solution)/shard_map/ppermute | solution.py:435
  222.0 9.4 %collective-permute-start.14 = (bf16[128,2048]{1,0:T(8,128)(2,1)S(1)}, bf16[128,2048]{1,0:T(8,128)(2,1)}, u32[]{:S(2)}, u32[]{:S(2)}) collective-permute-start(bf16[128,2048]{1,0:T(8,128)(2,1)S(1)} %collective-permute-done.13.refs_2_), channel_id=1, source_target_pairs={{0,4},{4,0},{8,12},{12,8},{16,20},{20,16},{24,28},{28,24},{1,5},{5... | collective-permute-start | bytes 1572872 | tf_op jit(solution)/shard_map/ppermute | solution.py:435
  230.9 3.0 copy-start.15
  230.9 2.0 collective-permute-start.16
  230.9 3.0 collective-permute-start.18
  233.9 1.2 copy-start.9
  248.8 2.4 collective-permute-start.24
  249.0 3.3 collective-permute-start.22
  249.3 27.4 %collective-permute-start.27 = (bf16[8,64,1024]{2,1,0:T(8,128)(2,1)}, bf16[8,64,1024]{2,1,0:T(8,128)(2,1)S(1)}, u32[]{:S(2)}, u32[]{:S(2)}) collective-permute-start(bf16[8,64,1024]{2,1,0:T(8,128)(2,1)} %shard_map.123.refs_1_), channel_id=1, source_target_pairs={{0,1},{1,2},{2,3},{3,0},{4,5},{5,6},{6,7},{7,4},{8,9},{9,10},{10,1... | collective-permute-start | bytes 3145736 | tf_op jit(solution)/shard_map/ppermute | solution.py:451
  252.7 24.1 %collective-permute-start.23 = (bf16[128,1536]{1,0:T(8,128)(2,1)S(1)}, bf16[128,1536]{1,0:T(8,128)(2,1)S(1)}, u32[]{:S(2)}, u32[]{:S(2)}) collective-permute-start(bf16[128,1536]{1,0:T(8,128)(2,1)S(1)} %get-tuple-element.42), channel_id=1, source_target_pairs={{0,8},{4,12},{8,0},{12,4},{16,24},{20,28},{24,16},{28,20},{1,9},{5... | collective-permute-start | bytes 1179656 | tf_op jit(solution)/shard_map/ppermute | solution.py:435
  254.2 22.5 %collective-permute-start.25 = (bf16[128,1536]{1,0:T(8,128)(2,1)S(1)}, bf16[128,1536]{1,0:T(8,128)(2,1)S(1)}, u32[]{:S(2)}, u32[]{:S(2)}) collective-permute-start(bf16[128,1536]{1,0:T(8,128)(2,1)S(1)} %get-tuple-element.36), channel_id=1, source_target_pairs={{0,16},{4,20},{8,24},{12,28},{16,0},{20,4},{24,8},{28,12},{1,17},{... | collective-permute-start | bytes 1179656 | tf_op jit(solution)/shard_map/ppermute | solution.py:435
  254.7 22.1 %collective-permute-start.26 = (bf16[128,1536]{1,0:T(8,128)(2,1)S(1)}, bf16[128,1536]{1,0:T(8,128)(2,1)S(1)}, u32[]{:S(2)}, u32[]{:S(2)}) collective-permute-start(bf16[128,1536]{1,0:T(8,128)(2,1)S(1)} %get-tuple-element.35), channel_id=1, source_target_pairs={{0,24},{4,28},{8,16},{12,20},{16,8},{20,12},{24,0},{28,4},{1,25},{... | collective-permute-start | bytes 1179656 | tf_op jit(solution)/shard_map/ppermute | solution.py:435
  276.8 2.0 copy-start.10
  279.6 2.1 copy-start.18
  279.6 2.1 collective-permute-start.30
  279.6 2.1 collective-permute-start.28
  280.1 34.7 %copy-start.13 = (bf16[128,2048]{1,0:T(8,128)(2,1)S(1)}, bf16[128,2048]{1,0:T(8,128)(2,1)}, u32[]{:S(2)}) copy-start(bf16[128,2048]{1,0:T(8,128)(2,1)} %copy-done.12) | copy-start | bytes 1572868
  281.8 9.6 %collective-permute-start.29 = (bf16[128,512]{1,0:T(8,128)(2,1)S(1)}, bf16[128,512]{1,0:T(8,128)(2,1)S(1)}, u32[]{:S(2)}, u32[]{:S(2)}) collective-permute-start(bf16[128,512]{1,0:T(8,128)(2,1)S(1)} %get-tuple-element.54), channel_id=1, source_target_pairs={{0,8},{4,12},{8,0},{12,4},{16,24},{20,28},{24,16},{28,20},{1,9},{5... | collective-permute-start | bytes 393224 | tf_op jit(solution)/shard_map/ppermute | solution.py:435
  283.5 8.6 %collective-permute-start.31 = (bf16[128,512]{1,0:T(8,128)(2,1)S(1)}, bf16[128,512]{1,0:T(8,128)(2,1)S(1)}, u32[]{:S(2)}, u32[]{:S(2)}) collective-permute-start(bf16[128,512]{1,0:T(8,128)(2,1)S(1)} %get-tuple-element.44), channel_id=1, source_target_pairs={{0,16},{4,20},{8,24},{12,28},{16,0},{20,4},{24,8},{28,12},{1,17},{... | collective-permute-start | bytes 393224 | tf_op jit(solution)/shard_map/ppermute | solution.py:435
  283.9 30.9 %collective-permute-start.32 = (bf16[128,512]{1,0:T(8,128)(2,1)S(1)}, bf16[128,512]{1,0:T(8,128)(2,1)S(1)}, u32[]{:S(2)}, u32[]{:S(2)}) collective-permute-start(bf16[128,512]{1,0:T(8,128)(2,1)S(1)} %get-tuple-element.43), channel_id=1, source_target_pairs={{0,24},{4,28},{8,16},{12,20},{16,8},{20,12},{24,0},{28,4},{1,25},{... | collective-permute-start | bytes 393224 | tf_op jit(solution)/shard_map/ppermute | solution.py:435
  286.4 35.1 %collective-permute-start.38 = (bf16[4,4,64,64]{3,2,1,0:T(8,128)(2,1)S(1)}, bf16[4,4,64,64]{3,2,1,0:T(8,128)(2,1)S(1)}, u32[]{:S(2)}, u32[]{:S(2)}) collective-permute-start(bf16[4,4,64,64]{3,2,1,0:T(8,128)(2,1)S(1)} %get-tuple-element.52), channel_id=1, source_target_pairs={{0,4},{1,12},{2,20},{3,28},{4,0},{5,8},{6,16},{7,24},{8,5},{9,13},... | collective-permute-start | bytes 393224 | tf_op jit(solution)/shard_map/ppermute | solution.py:545
  286.5 51.2 %collective-permute-start.37 = (bf16[4,4,64,64]{3,2,1,0:T(8,128)(2,1)S(1)}, bf16[4,4,64,64]{3,2,1,0:T(8,128)(2,1)}, u32[]{:S(2)}, u32[]{:S(2)}) collective-permute-start(bf16[4,4,64,64]{3,2,1,0:T(8,128)(2,1)S(1)} %get-tuple-element.51), channel_id=1, source_target_pairs={{0,0},{1,8},{2,16},{3,24},{4,4},{5,12},{6,20},{7,28},{8,1},{9,9},{... | collective-permute-start | bytes 393224 | tf_op jit(solution)/shard_map/ppermute | solution.py:545
  317.7 36.1 %collective-permute-start.33 = (bf16[128,2048]{1,0:T(8,128)(2,1)}, bf16[128,2048]{1,0:T(8,128)(2,1)S(1)}, u32[]{:S(2)}, u32[]{:S(2)}) collective-permute-start(bf16[128,2048]{1,0:T(8,128)(2,1)} %get-tuple-element.29), channel_id=1, source_target_pairs={{0,0},{1,8},{2,16},{3,24},{4,6},{5,14},{6,22},{7,30},{8,1},{9,9},{... | collective-permute-start | bytes 1572872 | tf_op jit(solution)/shard_map/ppermute | solution.py:555
  319.6 46.2 %collective-permute-start.34 = (bf16[128,2048]{1,0:T(8,128)(2,1)}, bf16[128,2048]{1,0:T(8,128)(2,1)S(1)}, u32[]{:S(2)}, u32[]{:S(2)}) collective-permute-start(bf16[128,2048]{1,0:T(8,128)(2,1)} %get-tuple-element.29), channel_id=1, source_target_pairs={{0,1},{1,9},{2,17},{3,25},{4,7},{5,15},{6,23},{7,31},{8,0},{9,8},{... | collective-permute-start | bytes 1572872 | tf_op jit(solution)/shard_map/ppermute | solution.py:555
  319.6 46.2 %collective-permute-start.35 = (bf16[128,2048]{1,0:T(8,128)(2,1)}, bf16[128,2048]{1,0:T(8,128)(2,1)S(1)}, u32[]{:S(2)}, u32[]{:S(2)}) collective-permute-start(bf16[128,2048]{1,0:T(8,128)(2,1)} %get-tuple-element.29), channel_id=1, source_target_pairs={{0,2},{1,10},{2,18},{3,26},{4,4},{5,12},{6,20},{7,28},{8,3},{9,11}... | collective-permute-start | bytes 1572872 | tf_op jit(solution)/shard_map/ppermute | solution.py:555
  321.6 16.2 %copy-start.29 = (bf16[4,4,64,64]{3,2,1,0:T(8,128)(2,1)}, bf16[4,4,64,64]{3,2,1,0:T(8,128)(2,1)S(1)}, u32[]{:S(2)}) copy-start(bf16[4,4,64,64]{3,2,1,0:T(8,128)(2,1)S(1)} %collective-permute-done.38) | copy-start | bytes 393220
  321.6 44.2 %collective-permute-start.36 = (bf16[128,2048]{1,0:T(8,128)(2,1)}, bf16[128,2048]{1,0:T(8,128)(2,1)S(1)}, u32[]{:S(2)}, u32[]{:S(2)}) collective-permute-start(bf16[128,2048]{1,0:T(8,128)(2,1)} %get-tuple-element.29), channel_id=1, source_target_pairs={{0,3},{1,11},{2,19},{3,27},{4,5},{5,13},{6,21},{7,29},{8,2},{9,10}... | collective-permute-start | bytes 1572872 | tf_op jit(solution)/shard_map/ppermute | solution.py:555
  323.4 29.5 %all-to-all-start.2 = ((bf16[8,128,256]{2,1,0:T(8,128)(2,1)}), bf16[8,128,256]{2,1,0:T(8,128)(2,1)S(1)}, u32[]{:S(2)}, u32[]{:S(2)}) async-start(bf16[8,128,256]{2,1,0:T(8,128)(2,1)} %bitcast.88), calls=%async_computation.2 | async-start | bytes 1048576 | tf_op jit(solution)/shard_map/all_to_all | solution.py:457
  365.8 8.0 %copy-start.1 = (bf16[2,96,2048]{2,1,0:T(8,128)(2,1)S(1)}, bf16[2,96,2048]{2,1,0:T(8,128)(2,1)}, u32[]{:S(2)}) copy-start(bf16[2,96,2048]{2,1,0:T(8,128)(2,1)} %param.14) | copy-start | bytes 2359300
  (13 other events, 12.0 us)
Sparse Core Ops, SparseCore 0:
  36.9 54.1 all-gather.2
  93.0 45.4 all-gather.4

commit v5 on v4

--- a/solution.py
+++ b/solution.py
@@ -325,7 +325,7 @@
             pltpu.VMEM((nb, nc, deep, ff), BF16),
             pltpu.SemaphoreType.DMA((nc + nb,)),
         ],
-        compiler_params=pltpu.CompilerParams(vmem_limit_bytes=40 * 2**20),
+        compiler_params=pltpu.CompilerParams(vmem_limit_bytes=58 * 2**20),
         cost_estimate=pl.CostEstimate(flops=10**6, bytes_accessed=2**12, transcendentals=0),
     )(place, *xs, *shards, *extra)
 
@@ -406,6 +406,26 @@
         compiler_params=pltpu.CompilerParams(vmem_limit_bytes=50 * 2**20),
         cost_estimate=pl.CostEstimate(flops=10**6, bytes_accessed=2**12, transcendentals=0),
     )(place, *xs, gate, given)
+
+
+def state_kernel(place_ref, a, b, out):
+    even = place_ref[0] % 2 == 0
+    a, b = a[...].astype(F32), b[...].astype(F32)
+    x = jnp.concatenate([jnp.where(even, a, b), jnp.where(even, b, a)], axis=1)
+    for v in range(0, HEAD, 2):
+        out[:, :, v * HEAD : (v + 2) * HEAD] = jnp.concatenate([x[:, :, v, :], x[:, :, v + 1, :]], axis=2)
+
+
+def state_rows(place, a, b):
+    spec = pl.BlockSpec(memory_space=pltpu.VMEM)
+    return pl.pallas_call(
+        state_kernel,
+        in_specs=[pl.BlockSpec(memory_space=pltpu.SMEM), spec, spec],
+        out_specs=spec,
+        out_shape=jax.ShapeDtypeStruct((a.shape[0], 2 * a.shape[1], HEAD * HEAD), F32),
+        compiler_params=pltpu.CompilerParams(vmem_limit_bytes=24 * 2**20),
+        cost_estimate=pl.CostEstimate(flops=10**6, bytes_accessed=2**12, transcendentals=0),
+    )(place, a, b)
 
 
 def per_device(
@@ -531,9 +551,18 @@
     out_own, third, _ = settle(
         place, pieces, mid, jnp.concatenate([gains[4:6], token_shift_weights[5:6]], axis=0), n_col
     )
+    arrived = []
+    for j in range(n_col):
+        pairs = []
+        for r in range(n_row):
+            for c in range(n_col):
+                pairs.append((r * n_col + c, (2 * c + r % 2) * n_col + ((r // 2) ^ j ^ (r % 2 * (n_col // 2)))))
+        arrived.append(lax.ppermute(third, ("row", "col"), pairs))
+    blocks = relay(out_own.reshape(chunk, n_row, fw).transpose(1, 0, 2))
+    out_hidden = blocks.reshape(chips, 2, chunk, fw).transpose(1, 0, 2, 3).reshape(tokens, fw)
     half = prompts // 2
     share = n_row // n_col
-    states = after(states, values[-1]).reshape(2, half, states.shape[1], HEAD, HEAD)
+    states = after(states, arrived[-1]).reshape(2, half, states.shape[1], HEAD, HEAD)
     moved = []
     for j in range(2):
         pairs = []
@@ -543,18 +572,7 @@
                 pairs.append((r * n_col + c, (2 * c + h) * n_col + r // share))
         piece = lax.dynamic_index_in_dim(states, (row % 2) ^ j, 0, keepdims=False)
         moved.append(lax.ppermute(piece, ("row", "col"), pairs))
-    settled = jnp.take(jnp.stack(moved), (row % 2) ^ jnp.arange(2), axis=0)
-    final_state = settled.transpose(1, 0, 2, 3, 4).reshape(half, -1, HEAD * HEAD).astype(F32)
-
-    arrived = []
-    for j in range(n_col):
-        pairs = []
-        for r in range(n_row):
-            for c in range(n_col):
-                pairs.append((r * n_col + c, (2 * c + r % 2) * n_col + ((r // 2) ^ j ^ (r % 2 * (n_col // 2)))))
-        arrived.append(lax.ppermute(third, ("row", "col"), pairs))
-    blocks = relay(out_own.reshape(chunk, n_row, fw).transpose(1, 0, 2))
-    out_hidden = blocks.reshape(chips, 2, chunk, fw).transpose(1, 0, 2, 3).reshape(tokens, fw)
+    final_state = state_rows(place, *moved)
     next_rkv = next_products(place, arrived, token_shift_weights[6:9], last)
     return (out_hidden, next_rkv, final_state)
 

time: 384 us -> 376 us (0.979)
  local copies, waits for them, and re-layouts: 34.3 us -> 23.2 us
  starting transfers between devices: 60.9 us -> 69.5 us
  waiting for transfers between devices: 188 us -> 180 us
    ppermute x21, waiting for transfers between devices: 71.2 us -> 52.5 us  [to_row(): return lax.ppermute(x, 'row', [(i, i ^ k) for i in range(n_row)])]
    ppermute x4, waiting for transfers between devices: 12 us -> 23 us  [per_device(): arrived.append(lax.ppermute(third, ('row', 'col'), pairs))]
    ppermute x2, starting transfers between devices: 4.89 us -> 15 us  [per_device(): moved.append(lax.ppermute(piece, ('row', 'col'), pairs))]
    all_to_all x3, starting transfers between devices: 23.2 us -> 13.2 us  [relay(): return lax.all_to_all(x, 'row', 0, 0, tiled=True)]
    unnamed x68 -> x56, local copies, waits for them, and re-layouts: 15.7 us -> 7.52 us
    ppermute x4, starting transfers between devices: 3.94 us -> 12 us  [per_device(): arrived.append(lax.ppermute(third, ('row', 'col'), pairs))]
    all_to_all x3, waiting for transfers between devices: 8.02 us -> 0.01 us  [relay(): return lax.all_to_all(x, 'row', 0, 0, tiled=True)]
    ppermute x2, waiting for transfers between devices: 0.01 us -> 5.36 us  [per_device(): moved.append(lax.ppermute(piece, ('row', 'col'), pairs))]
  transfers between devices with their start and end apart: 44 -> 44, of which waited for: 21 -> 24; matrix products, arithmetic and copies ran while one was open for 8% -> 6% of each run, Pallas kernels for 15% -> 17%
where the time goes in v5:
time: 376 us; the launch traced here: 372 us
  waiting for transfers between devices  180 us (48%)
  Pallas kernels  74.7 us (20%)
  starting transfers between devices  69.5 us (18%)
  local copies, waits for them, and re-layouts  23.2 us (6%)
  between operations  14.5 us (4%)
  other arithmetic  9.21 us (2%)
    ppermute x7, waiting for transfers between devices, ring(): return lax.ppermute(x, 'col', [(i, (i + 1) % n_col) for i in range(n_col)])  85.7 us
    ppermute x21, waiting for transfers between devices, to_row(): return lax.ppermute(x, 'row', [(i, i ^ k) for i in range(n_row)])  52.5 us
    pallas_call x1, Pallas kernels, time_mix(): pl.pallas_call(functools.partial(time_kernel, nc, per), grid=(prompts //...  43.1 us
    ppermute x4, waiting for transfers between devices, per_device(): arrived.append(lax.ppermute(third, ('row', 'col'), pairs))  23 us
    ppermute x21, starting transfers between devices, to_row(): return lax.ppermute(x, 'row', [(i, i ^ k) for i in range(n_row)])  15.8 us
    ppermute x2, starting transfers between devices, per_device(): moved.append(lax.ppermute(piece, ('row', 'col'), pairs))  15 us
    ppermute x3, waiting for transfers between devices, to_col(): return lax.ppermute(x, 'col', [(i, i ^ k) for i in range(n_col)])  13.8 us
    all_to_all x3, starting transfers between devices, relay(): return lax.all_to_all(x, 'row', 0, 0, tiled=True)  13.2 us
  transfers between devices with their start and end apart: 44, of which 24 were waited for; matrix products, arithmetic and copies ran while one was open for 6% of the time, Pallas kernels for 17%

profile of v5, /device:TPU:12, one launch (start us, length us, event | category | flops | bytes accessed | tf_op | source)
XLA Modules:
  0.0 371.6 jit_solution(1443060060982197371)
XLA Ops:
  7.2 1.8 slice.212
  9.0 1.1 copy.50
  10.1 4.2 %all-to-all-start = ((bf16[8,4,64,256]{3,2,1,0:T(8,128)(2,1)}), bf16[8,4,64,256]{3,2,1,0:T(8,128)(2,1)S(1)}, u32[]{:S(2)}, u32[]{:S(2)}) async-start(bf16[8,4,64,256]{3,2,1,0:T(8,128)(2,1)} %bitcast.78), calls=%async_computation | async-start | bytes 2097152 | tf_op jit(solution)/shard_map/all_to_all | solution.py:477
  14.4 1.6 slice.120
  16.1 1.6 collective-permute-start.2
  17.7 1.2 collective-permute-start.1
  18.9 1.2 collective-permute-start
  21.1 11.2 %collective-permute-done.2 = bf16[3,64,512]{2,1,0:T(8,128)(2,1)S(1)} collective-permute-done((bf16[3,64,512]{2,1,0:T(8,128)(2,1)S(1)}, bf16[3,64,512]{2,1,0:T(8,128)(2,1)S(1)}, u32[]{:S(2)}, u32[]{:S(2)}) %collective-permute-start.2) | collective-permute-done | bytes 196640 | tf_op jit(solution)/shard_map/ppermute | solution.py:458
  32.3 2.5 collective-permute-done.1
  34.8 1.0 pad_maximum_fusion.refs_1_
  36.8 1.1 copy-done.5
  38.5 2.4 convert_element_type.192
  40.9 1.6 copy.49
  42.5 4.7 %all-to-all-start.1 = ((bf16[8,2,64,1024]{3,2,1,0:T(8,128)(2,1)}), bf16[8,2,64,1024]{3,2,1,0:T(8,128)(2,1)}, u32[]{:S(2)}, u32[]{:S(2)}) async-start(bf16[8,2,64,1024]{3,2,1,0:T(8,128)(2,1)} %shard_map.114), calls=%async_computation.1 | async-start | bytes 4194304 | tf_op jit(solution)/shard_map/all_to_all | solution.py:477
  47.2 15.9 %collective-permute-done.3.refs_1_ = bf16[8,4,64,256]{3,2,1,0:T(8,128)(2,1)} collective-permute-done((bf16[8,4,64,256]{3,2,1,0:T(8,128)(2,1)S(1)}, bf16[8,4,64,256]{3,2,1,0:T(8,128)(2,1)}, u32[]{:S(2)}, u32[]{:S(2)}) %collective-permute-start.3) | collective-permute-done | bytes 1048608 | tf_op jit(solution)/shard_map/ppermute | solution.py:471
  63.8 24.8 %collective-permute-done.4.refs_2_ = bf16[8,4,64,256]{3,2,1,0:T(8,128)(2,1)} collective-permute-done((bf16[8,4,64,256]{3,2,1,0:T(8,128)(2,1)}, bf16[8,4,64,256]{3,2,1,0:T(8,128)(2,1)}, u32[]{:S(2)}, u32[]{:S(2)}) %collective-permute-start.4) | collective-permute-done | bytes 1048608 | tf_op jit(solution)/shard_map/ppermute | solution.py:471
  90.4 3.1 slice_bitcast_fusion
  93.5 19.8 %collective-permute-done.5.refs_1_.refs_3_ = bf16[8,4,64,256]{3,2,1,0:T(8,128)(2,1)} collective-permute-done((bf16[8,4,64,256]{3,2,1,0:T(8,128)(2,1)}, bf16[8,4,64,256]{3,2,1,0:T(8,128)(2,1)}, u32[]{:S(2)}, u32[]{:S(2)}) %collective-permute-start.5) | collective-permute-done | bytes 1048608 | tf_op jit(solution)/shard_map/ppermute | solution.py:471
  113.3 3.7 collective-permute-start.7
  118.6 43.1 %shard_map.116 = (bf16[4,128,2048]{2,1,0:T(8,128)(2,1)}, bf16[4,128,2048]{2,1,0:T(8,128)(2,1)}, bf16[128,2048]{1,0:T(8,128)(2,1)S(1)}, bf16[8,4,64,64]{3,2,1,0:T(8,128)(2,1)S(1)}) custom-call(s32[2]{0:T(128)S(1)} %pad_add_fusion.place_ref, s32[8]{0:T(128)S(1)} %dynamic_slice.28.lens, bf16[8,1056,256]{2,1,0:T(8,128)(2,1)} %bitcast.100, ...), custom_call_target="tpu_custom_call" | custom-call | flops 40000000000 | bytes 16777216 | tf_op jit(solution)/shard_map/pallas_call | solution.py:192
  162.9 4.2 %collective-permute-done.8 = bf16[4,128,2048]{2,1,0:T(8,128)(2,1)} collective-permute-done((bf16[4,128,2048]{2,1,0:T(8,128)(2,1)}, bf16[4,128,2048]{2,1,0:T(8,128)(2,1)}, u32[]{:S(2)}, u32[]{:S(2)}) %collective-permute-start.8) | collective-permute-done | bytes 2097184 | tf_op jit(solution)/shard_map/ppermute | solution.py:455
  167.1 3.4 fusion.3
  170.5 1.5 collective-permute-start.9
  172.5 1.5 collective-permute-start.11
  174.0 11.5 %collective-permute-done.9.refs_1_ = bf16[128,2048]{1,0:T(8,128)(2,1)} collective-permute-done((bf16[128,2048]{1,0:T(8,128)(2,1)}, bf16[128,2048]{1,0:T(8,128)(2,1)}, u32[]{:S(2)}, u32[]{:S(2)}) %collective-permute-start.9) | collective-permute-done | bytes 524320 | tf_op jit(solution)/shard_map/ppermute | solution.py:455
  185.5 11.6 %collective-permute-done.10.refs_2_ = bf16[128,2048]{1,0:T(8,128)(2,1)} collective-permute-done((bf16[128,2048]{1,0:T(8,128)(2,1)}, bf16[128,2048]{1,0:T(8,128)(2,1)}, u32[]{:S(2)}, u32[]{:S(2)}) %collective-permute-start.10) | collective-permute-done | bytes 524320 | tf_op jit(solution)/shard_map/ppermute | solution.py:455
  197.2 3.3 shard_map.119
  201.8 1.6 collective-permute-start.15
  203.4 1.3 collective-permute-start.17
  204.8 3.9 %collective-permute-start.21 = (bf16[8,64,1024]{2,1,0:T(8,128)(2,1)S(1)}, bf16[8,64,1024]{2,1,0:T(8,128)(2,1)}, u32[]{:S(2)}, u32[]{:S(2)}) collective-permute-start(bf16[8,64,1024]{2,1,0:T(8,128)(2,1)S(1)} %copy-done.3), channel_id=1, source_target_pairs={{0,3},{1,0},{2,1},{3,2},{4,7},{5,4},{6,5},{7,6},{8,11},{9,8},{10,9... | collective-permute-start | bytes 3145736 | tf_op jit(solution)/shard_map/ppermute | solution.py:474
  208.7 4.8 %collective-permute-done.20.refs_0_ = bf16[8,64,1024]{2,1,0:T(8,128)(2,1)S(1)} collective-permute-done((bf16[8,64,1024]{2,1,0:T(8,128)(2,1)}, bf16[8,64,1024]{2,1,0:T(8,128)(2,1)S(1)}, u32[]{:S(2)}, u32[]{:S(2)}) %collective-permute-start.20) | collective-permute-done | bytes 1048608 | tf_op jit(solution)/shard_map/ppermute | solution.py:471
  213.4 2.9 collective-permute-done.13.refs_2_
  216.3 9.5 %collective-permute-done.15.refs_4_ = bf16[128,2048]{1,0:T(8,128)(2,1)S(1)} collective-permute-done((bf16[128,2048]{1,0:T(8,128)(2,1)}, bf16[128,2048]{1,0:T(8,128)(2,1)S(1)}, u32[]{:S(2)}, u32[]{:S(2)}) %collective-permute-start.15) | collective-permute-done | bytes 524320 | tf_op jit(solution)/shard_map/ppermute | solution.py:455
  226.4 1.5 collective-permute-done.16.refs_5_
  228.9 9.8 %shard_map.120.act = bf16[1024,1024]{1,0:T(8,128)(2,1)} custom-call(s32[2]{0:T(128)} %copy-done.15, bf16[128,2048]{1,0:T(8,128)(2,1)} %get-tuple-element.20.refs_0_, bf16[128,2048]{1,0:T(8,128)(2,1)} %collective-permute-done.12.refs_1_, bf16[128,2048]{1,0:T(8,128)(2,1)} %copy-done.21, bf16[128,2048]{1,0:T(8,128)(2,1)} %collective-permute-done.14.refs_3_, ...), custom_call_target="tpu_custom_call" | custom-call | flops 1000000 | bytes 4096 | tf_op jit(solution)/shard_map/pallas_call | solution.py:318
  238.7 1.6 copy-done.2
  240.3 4.7 %shard_map.124 = (bf16[4,128,1536]{2,1,0:T(8,128)(2,1)S(1)}, bf16[2,128,1536]{2,1,0:T(8,128)(2,1)S(1)}, bf16[2,128,1536]{2,1,0:T(8,128)(2,1)S(1)}) custom-call(bf16[1024,1024]{1,0:T(8,128)(2,1)S(1)} %copy-done.2, bf16[8,64,1024]{2,1,0:T(8,128)(2,1)S(1)} %copy-done.3, bf16[8,64,1024]{2,1,0:T(8,128)(2,1)S(1)} %copy-done.9, ...), custom_call_target="tpu_custom_call" | custom-call | flops 1000000 | bytes 4096 | tf_op jit(solution)/shard_map/pallas_call | solution.py:353
  245.8 1.6 collective-permute-done.24
  247.3 1.1 collective-permute-done.22
  248.9 1.6 collective-permute-start.23
  251.0 1.5 collective-permute-start.26
  252.4 20.4 %collective-permute-done.27.refs_0_ = bf16[8,64,1024]{2,1,0:T(8,128)(2,1)S(1)} collective-permute-done((bf16[8,64,1024]{2,1,0:T(8,128)(2,1)S(1)}, bf16[8,64,1024]{2,1,0:T(8,128)(2,1)S(1)}, u32[]{:S(2)}, u32[]{:S(2)}) %collective-permute-start.27) | collective-permute-done | bytes 1048608 | tf_op jit(solution)/shard_map/ppermute | solution.py:471
  272.9 1.3 shard_map.125
  274.7 1.0 collective-permute-done.30
  276.3 1.7 collective-permute-start.29
  278.4 1.4 collective-permute-start.32
  279.8 2.2 collective-permute-done.29.refs_5_
  282.1 4.0 %collective-permute-done.31.refs_6_ = bf16[128,512]{1,0:T(8,128)(2,1)S(1)} collective-permute-done((bf16[128,512]{1,0:T(8,128)(2,1)S(1)}, bf16[128,512]{1,0:T(8,128)(2,1)S(1)}, u32[]{:S(2)}, u32[]{:S(2)}) %collective-permute-start.31) | collective-permute-done | bytes 131104 | tf_op jit(solution)/shard_map/ppermute | solution.py:455
  286.0 2.8 shard_map.126
  288.9 1.4 collective-permute-start.36
  290.3 1.9 collective-permute-start.33
  292.2 6.8 %collective-permute-start.34 = (bf16[128,2048]{1,0:T(8,128)(2,1)}, bf16[128,2048]{1,0:T(8,128)(2,1)S(1)}, u32[]{:S(2)}, u32[]{:S(2)}) collective-permute-start(bf16[128,2048]{1,0:T(8,128)(2,1)} %get-tuple-element.29), channel_id=1, source_target_pairs={{0,1},{1,9},{2,17},{3,25},{4,7},{5,15},{6,23},{7,31},{8,0},{9,8},{... | collective-permute-start | bytes 1572872 | tf_op jit(solution)/shard_map/ppermute | solution.py:560
  299.0 1.9 collective-permute-start.35
  301.8 4.2 %all-to-all-start.2 = ((bf16[8,128,256]{2,1,0:T(8,128)(2,1)}), bf16[8,128,256]{2,1,0:T(8,128)(2,1)}, u32[]{:S(2)}, u32[]{:S(2)}) async-start(bf16[8,128,256]{2,1,0:T(8,128)(2,1)} %bitcast.80), calls=%async_computation.2 | async-start | bytes 1048576 | tf_op jit(solution)/shard_map/all_to_all | solution.py:477
  306.0 19.5 %collective-permute-done.36.refs_3_.refs_1_ = bf16[128,2048]{1,0:T(8,128)(2,1)S(1)} collective-permute-done((bf16[128,2048]{1,0:T(8,128)(2,1)}, bf16[128,2048]{1,0:T(8,128)(2,1)S(1)}, u32[]{:S(2)}, u32[]{:S(2)}) %collective-permute-start.36) | collective-permute-done | bytes 524320 | tf_op jit(solution)/shard_map/ppermute | solution.py:560
  326.3 2.0 dynamic-slice_bitcast_fusion
  328.2 1.9 collective-permute-start.37
  330.2 13.1 %collective-permute-start.38 = (bf16[4,4,64,64]{3,2,1,0:T(8,128)(2,1)}, bf16[4,4,64,64]{3,2,1,0:T(8,128)(2,1)S(1)}, u32[]{:S(2)}, u32[]{:S(2)}) collective-permute-start(bf16[4,4,64,64]{3,2,1,0:T(8,128)(2,1)} %get-tuple-element.51), channel_id=1, source_target_pairs={{0,4},{1,12},{2,20},{3,28},{4,0},{5,8},{6,16},{7,24},{8,5},{9,13},... | collective-permute-start | bytes 393224 | tf_op jit(solution)/shard_map/ppermute | solution.py:574
  344.2 1.9 copy.38
  346.1 3.5 collective-permute-done.34.refs_1_
  349.6 8.0 %shard_map.127 = bf16[3,512,512]{2,1,0:T(8,128)(2,1)} custom-call(s32[2]{0:T(128)S(1)} %copy-done.16, bf16[128,2048]{1,0:T(8,128)(2,1)S(1)} %collective-permute-done.33.refs_0_, bf16[128,2048]{1,0:T(8,128)(2,1)S(1)} %collective-permute-done.34.refs_1_, bf16[128,2048]{1,0:T(8,128)(2,1)S(1)} %collective-permute-done.35.refs_2_, ...), custom_call_target="tpu_custom_call" | custom-call | flops 1000000 | bytes 4096 | tf_op jit(solution)/shard_map/pallas_call | solution.py:394
  357.6 2.1 collective-permute-done.37.a
  359.7 3.3 collective-permute-done.38.b
  363.0 1.8 shard_map.129
  (130 shorter events, 16.8 us)
Async XLA Ops:
  7.2 83.2 %copy-start = (bf16[2,96,2048]{2,1,0:T(8,128)(2,1)S(1)}, bf16[2,96,2048]{2,1,0:T(8,128)(2,1)}, u32[]{:S(2)}) copy-start(bf16[2,96,2048]{2,1,0:T(8,128)(2,1)} %param.14) | copy-start | bytes 2359300
  10.1 25.7 %all-to-all-start = ((bf16[8,4,64,256]{3,2,1,0:T(8,128)(2,1)}), bf16[8,4,64,256]{3,2,1,0:T(8,128)(2,1)S(1)}, u32[]{:S(2)}, u32[]{:S(2)}) async-start(bf16[8,4,64,256]{3,2,1,0:T(8,128)(2,1)} %bitcast.78), calls=%async_computation | async-start | bytes 2097152 | tf_op jit(solution)/shard_map/all_to_all | solution.py:477
  14.3 5.9 %copy-start.25 = (f32[6,256]{1,0:T(8,128)S(1)}, f32[6,256]{1,0:T(8,128)}, u32[]{:S(2)}) copy-start(f32[6,256]{1,0:T(8,128)} %param.17) | copy-start | bytes 18436
  14.3 5.9 %copy-start.23 = (bf16[1024,256]{1,0:T(8,128)(2,1)S(1)}, bf16[1024,256]{1,0:T(8,128)(2,1)}, u32[]{:S(2)}) copy-start(bf16[1024,256]{1,0:T(8,128)(2,1)} %param.9) | copy-start | bytes 1572868
  14.3 102.7 %all-gather.3.cloned.1.call-start = ((), (), s32[]{:S(2)}) async-start(), calls=%async_computation.3 | async-start | bytes 4866048 | tf_op jit(solution)/shard_map/all_gather | solution.py:494
  16.1 16.2 %collective-permute-start.2 = (bf16[3,64,512]{2,1,0:T(8,128)(2,1)S(1)}, bf16[3,64,512]{2,1,0:T(8,128)(2,1)S(1)}, u32[]{:S(2)}, u32[]{:S(2)}) collective-permute-start(bf16[3,64,512]{2,1,0:T(8,128)(2,1)S(1)} %get-tuple-element.48), channel_id=1, source_target_pairs={{0,3},{1,2},{2,1},{3,0},{4,7},{5,6},{6,5},{7,4},{8,11},{9,10},{10,... | collective-permute-start | bytes 589832 | tf_op jit(solution)/shard_map/ppermute | solution.py:458
  17.7 17.1 %collective-permute-start.1 = (bf16[3,64,512]{2,1,0:T(8,128)(2,1)S(1)}, bf16[3,64,512]{2,1,0:T(8,128)(2,1)S(1)}, u32[]{:S(2)}, u32[]{:S(2)}) collective-permute-start(bf16[3,64,512]{2,1,0:T(8,128)(2,1)S(1)} %get-tuple-element.49), channel_id=1, source_target_pairs={{0,2},{1,3},{2,0},{3,1},{4,6},{5,7},{6,4},{7,5},{8,10},{9,11},{10,... | collective-permute-start | bytes 589832 | tf_op jit(solution)/shard_map/ppermute | solution.py:458
  18.9 15.9 %collective-permute-start = (bf16[3,64,512]{2,1,0:T(8,128)(2,1)S(1)}, bf16[3,64,512]{2,1,0:T(8,128)(2,1)S(1)}, u32[]{:S(2)}, u32[]{:S(2)}) collective-permute-start(bf16[3,64,512]{2,1,0:T(8,128)(2,1)S(1)} %get-tuple-element.50), channel_id=1, source_target_pairs={{0,1},{1,0},{2,3},{3,2},{4,5},{5,4},{6,7},{7,6},{8,9},{9,8},{10,11... | collective-permute-start | bytes 589832 | tf_op jit(solution)/shard_map/ppermute | solution.py:458
  36.8 189.6 %all-gather.5.cloned.1.call-start = ((), (), s32[]{:S(2)}) async-start(), calls=%async_computation.4 | async-start | bytes 7077888 | tf_op jit(solution)/shard_map/all_gather | solution.py:500
  38.0 25.1 %collective-permute-start.3 = (bf16[8,4,64,256]{3,2,1,0:T(8,128)(2,1)S(1)}, bf16[8,4,64,256]{3,2,1,0:T(8,128)(2,1)}, u32[]{:S(2)}, u32[]{:S(2)}) collective-permute-start(bf16[8,4,64,256]{3,2,1,0:T(8,128)(2,1)S(1)} %copy-done.5), channel_id=1, source_target_pairs={{0,1},{1,2},{2,3},{3,0},{4,5},{5,6},{6,7},{7,4},{8,9},{9,10},{10,1... | collective-permute-start | bytes 3145736 | tf_op jit(solution)/shard_map/ppermute | solution.py:471
  42.5 46.2 %copy-start.24 = (f32[9,2048]{1,0:T(8,128)S(1)}, f32[9,2048]{1,0:T(8,128)}, u32[]{:S(2)}) copy-start(f32[9,2048]{1,0:T(8,128)} %param.15) | copy-start | bytes 221188
  42.5 46.3 %copy-start.20 = (bf16[2,2048,96]{1,2,0:T(8,128)(2,1)S(1)}, bf16[2,2048,96]{1,2,0:T(8,128)(2,1)}, u32[]{:S(2)}) copy-start(bf16[2,2048,96]{1,2,0:T(8,128)(2,1)} %param.13) | copy-start | bytes 2359300
  42.5 47.9 %all-to-all-start.1 = ((bf16[8,2,64,1024]{3,2,1,0:T(8,128)(2,1)}), bf16[8,2,64,1024]{3,2,1,0:T(8,128)(2,1)}, u32[]{:S(2)}, u32[]{:S(2)}) async-start(bf16[8,2,64,1024]{3,2,1,0:T(8,128)(2,1)} %shard_map.114), calls=%async_computation.1 | async-start | bytes 4194304 | tf_op jit(solution)/shard_map/all_to_all | solution.py:477
  47.2 42.3 %copy-start.26 = (s32[32]{0:T(128)S(1)}, s32[32]{0:T(128)}, u32[]{:S(2)}) copy-start(s32[32]{0:T(128)} %param.10) | copy-start | bytes 388
  63.1 25.6 %collective-permute-start.4 = (bf16[8,4,64,256]{3,2,1,0:T(8,128)(2,1)}, bf16[8,4,64,256]{3,2,1,0:T(8,128)(2,1)}, u32[]{:S(2)}, u32[]{:S(2)}) collective-permute-start(bf16[8,4,64,256]{3,2,1,0:T(8,128)(2,1)} %collective-permute-done.3.refs_1_), channel_id=1, source_target_pairs={{0,1},{1,2},{2,3},{3,0},{4,5},{5,6},{6,7},{7,4},{8,9},{9,10},{10,1... | collective-permute-start | bytes 3145736 | tf_op jit(solution)/shard_map/ppermute | solution.py:471
  88.7 24.7 %collective-permute-start.5 = (bf16[8,4,64,256]{3,2,1,0:T(8,128)(2,1)}, bf16[8,4,64,256]{3,2,1,0:T(8,128)(2,1)}, u32[]{:S(2)}, u32[]{:S(2)}) collective-permute-start(bf16[8,4,64,256]{3,2,1,0:T(8,128)(2,1)} %collective-permute-done.4.refs_2_), channel_id=1, source_target_pairs={{0,1},{1,2},{2,3},{3,0},{4,5},{5,6},{6,7},{7,4},{8,9},{9,10},{10,1... | collective-permute-start | bytes 3145736 | tf_op jit(solution)/shard_map/ppermute | solution.py:471
  89.7 107.5 %copy-start.15 = (s32[2]{0:T(128)}, s32[2]{0:T(128)S(1)}, u32[]{:S(2)}) copy-start(s32[2]{0:T(128)S(1)} %pad_add_fusion.place_ref) | copy-start | bytes 28
  93.5 25.1 %copy-start.6 = (bf16[8,4,64,256]{3,2,1,0:T(8,128)(2,1)S(1)}, bf16[8,4,64,256]{3,2,1,0:T(8,128)(2,1)}, u32[]{:S(2)}) copy-start(bf16[8,4,64,256]{3,2,1,0:T(8,128)(2,1)} %shard_map.112.refs_1_.refs_0_) | copy-start | bytes 3145732
  113.3 49.2 %collective-permute-start.6 = (bf16[8,64,1024]{2,1,0:T(8,128)(2,1)}, bf16[8,64,1024]{2,1,0:T(8,128)(2,1)}, u32[]{:S(2)}, u32[]{:S(2)}) collective-permute-start(bf16[8,64,1024]{2,1,0:T(8,128)(2,1)} %shard_map.115.refs_4_.refs_8_), channel_id=1, source_target_pairs={{0,1},{1,2},{2,3},{3,0},{4,5},{5,6},{6,7},{7,4},{8,9},{9,10},{10,1... | collective-permute-start | bytes 3145736 | tf_op jit(solution)/shard_map/ppermute | solution.py:471
  113.3 49.2 %collective-permute-start.7 = (bf16[8,64,1024]{2,1,0:T(8,128)(2,1)}, bf16[8,64,1024]{2,1,0:T(8,128)(2,1)}, u32[]{:S(2)}, u32[]{:S(2)}) collective-permute-start(bf16[8,64,1024]{2,1,0:T(8,128)(2,1)} %shard_map.115.refs_4_.refs_8_), channel_id=1, source_target_pairs={{0,3},{1,0},{2,1},{3,2},{4,7},{5,4},{6,5},{7,6},{8,11},{9,8},{10,9... | collective-permute-start | bytes 3145736 | tf_op jit(solution)/shard_map/ppermute | solution.py:474
  162.5 4.6 %copy-start.17 = (bf16[4,128,2048]{2,1,0:T(8,128)(2,1)S(1)}, bf16[4,128,2048]{2,1,0:T(8,128)(2,1)}, u32[]{:S(2)}) copy-start(bf16[4,128,2048]{2,1,0:T(8,128)(2,1)} %get-tuple-element.17) | copy-start | bytes 6291460
  162.5 4.6 %collective-permute-start.8 = (bf16[4,128,2048]{2,1,0:T(8,128)(2,1)}, bf16[4,128,2048]{2,1,0:T(8,128)(2,1)}, u32[]{:S(2)}, u32[]{:S(2)}) collective-permute-start(bf16[4,128,2048]{2,1,0:T(8,128)(2,1)} %shard_map.118), channel_id=1, source_target_pairs={{0,4},{4,0},{8,12},{12,8},{16,20},{20,16},{24,28},{28,24},{1,5},{5... | collective-permute-start | bytes 6291464 | tf_op jit(solution)/shard_map/ppermute | solution.py:455
  162.6 42.1 %collective-permute-start.19 = (bf16[8,64,1024]{2,1,0:T(8,128)(2,1)}, bf16[8,64,1024]{2,1,0:T(8,128)(2,1)}, u32[]{:S(2)}, u32[]{:S(2)}) collective-permute-start(bf16[8,64,1024]{2,1,0:T(8,128)(2,1)} %shard_map.117.refs_1_.refs_9_), channel_id=1, source_target_pairs={{0,1},{1,2},{2,3},{3,0},{4,5},{5,6},{6,7},{7,4},{8,9},{9,10},{10,1... | collective-permute-start | bytes 3145736 | tf_op jit(solution)/shard_map/ppermute | solution.py:471
  170.5 3.5 copy-start.19
  170.5 26.7 %copy-start.7 = (bf16[128,2048]{1,0:T(8,128)(2,1)S(1)}, bf16[128,2048]{1,0:T(8,128)(2,1)}, u32[]{:S(2)}) copy-start(bf16[128,2048]{1,0:T(8,128)(2,1)} %get-tuple-element.34.refs_0_.refs_1_) | copy-start | bytes 1572868
  170.5 15.1 %collective-permute-start.9 = (bf16[128,2048]{1,0:T(8,128)(2,1)}, bf16[128,2048]{1,0:T(8,128)(2,1)}, u32[]{:S(2)}, u32[]{:S(2)}) collective-permute-start(bf16[128,2048]{1,0:T(8,128)(2,1)} %get-tuple-element.33), channel_id=1, source_target_pairs={{0,8},{4,12},{8,0},{12,4},{16,24},{20,28},{24,16},{28,20},{1,9},{5... | collective-permute-start | bytes 1572872 | tf_op jit(solution)/shard_map/ppermute | solution.py:455
  171.9 25.2 %collective-permute-start.10 = (bf16[128,2048]{1,0:T(8,128)(2,1)}, bf16[128,2048]{1,0:T(8,128)(2,1)}, u32[]{:S(2)}, u32[]{:S(2)}) collective-permute-start(bf16[128,2048]{1,0:T(8,128)(2,1)} %get-tuple-element.32), channel_id=1, source_target_pairs={{0,16},{4,20},{8,24},{12,28},{16,0},{20,4},{24,8},{28,12},{1,17},{... | collective-permute-start | bytes 1572872 | tf_op jit(solution)/shard_map/ppermute | solution.py:455
  172.5 24.7 %collective-permute-start.11 = (bf16[128,2048]{1,0:T(8,128)(2,1)}, bf16[128,2048]{1,0:T(8,128)(2,1)}, u32[]{:S(2)}, u32[]{:S(2)}) collective-permute-start(bf16[128,2048]{1,0:T(8,128)(2,1)} %get-tuple-element.31), channel_id=1, source_target_pairs={{0,24},{4,28},{8,16},{12,20},{16,8},{20,12},{24,0},{28,4},{1,25},{... | collective-permute-start | bytes 1572872 | tf_op jit(solution)/shard_map/ppermute | solution.py:455
  174.0 30.8 %copy-start.3 = (bf16[8,64,1024]{2,1,0:T(8,128)(2,1)S(1)}, bf16[8,64,1024]{2,1,0:T(8,128)(2,1)}, u32[]{:S(2)}) copy-start(bf16[8,64,1024]{2,1,0:T(8,128)(2,1)} %shard_map.122.refs_0_) | copy-start | bytes 3145732
  174.0 39.5 %collective-permute-start.20 = (bf16[8,64,1024]{2,1,0:T(8,128)(2,1)}, bf16[8,64,1024]{2,1,0:T(8,128)(2,1)S(1)}, u32[]{:S(2)}, u32[]{:S(2)}) collective-permute-start(bf16[8,64,1024]{2,1,0:T(8,128)(2,1)} %shard_map.122.refs_0_), channel_id=1, source_target_pairs={{0,1},{1,2},{2,3},{3,0},{4,5},{5,6},{6,7},{7,4},{8,9},{9,10},{10,1... | collective-permute-start | bytes 3145736 | tf_op jit(solution)/shard_map/ppermute | solution.py:471
  201.3 15.1 %collective-permute-start.13 = (bf16[128,2048]{1,0:T(8,128)(2,1)}, bf16[128,2048]{1,0:T(8,128)(2,1)S(1)}, u32[]{:S(2)}, u32[]{:S(2)}) collective-permute-start(bf16[128,2048]{1,0:T(8,128)(2,1)} %get-tuple-element.20.refs_0_), channel_id=1, source_target_pairs={{0,8},{4,12},{8,0},{12,4},{16,24},{20,28},{24,16},{28,20},{1,9},{5... | collective-permute-start | bytes 1572872 | tf_op jit(solution)/shard_map/ppermute | solution.py:455
  201.8 24.1 %collective-permute-start.15 = (bf16[128,2048]{1,0:T(8,128)(2,1)}, bf16[128,2048]{1,0:T(8,128)(2,1)S(1)}, u32[]{:S(2)}, u32[]{:S(2)}) collective-permute-start(bf16[128,2048]{1,0:T(8,128)(2,1)} %get-tuple-element.20.refs_0_), channel_id=1, source_target_pairs={{0,16},{4,20},{8,24},{12,28},{16,0},{20,4},{24,8},{28,12},{1,17},{... | collective-permute-start | bytes 1572872 | tf_op jit(solution)/shard_map/ppermute | solution.py:455
  203.4 22.5 %collective-permute-start.17 = (bf16[128,2048]{1,0:T(8,128)(2,1)}, bf16[128,2048]{1,0:T(8,128)(2,1)}, u32[]{:S(2)}, u32[]{:S(2)}) collective-permute-start(bf16[128,2048]{1,0:T(8,128)(2,1)} %get-tuple-element.20.refs_0_), channel_id=1, source_target_pairs={{0,24},{4,28},{8,16},{12,20},{16,8},{20,12},{24,0},{28,4},{1,25},{... | collective-permute-start | bytes 1572872 | tf_op jit(solution)/shard_map/ppermute | solution.py:455
  204.8 33.9 %collective-permute-start.21 = (bf16[8,64,1024]{2,1,0:T(8,128)(2,1)S(1)}, bf16[8,64,1024]{2,1,0:T(8,128)(2,1)}, u32[]{:S(2)}, u32[]{:S(2)}) collective-permute-start(bf16[8,64,1024]{2,1,0:T(8,128)(2,1)S(1)} %copy-done.3), channel_id=1, source_target_pairs={{0,3},{1,0},{2,1},{3,2},{4,7},{5,4},{6,5},{7,6},{8,11},{9,8},{10,9... | collective-permute-start | bytes 3145736 | tf_op jit(solution)/shard_map/ppermute | solution.py:474
  213.4 13.0 %copy-start.8 = (bf16[8,64,1024]{2,1,0:T(8,128)(2,1)}, bf16[8,64,1024]{2,1,0:T(8,128)(2,1)S(1)}, u32[]{:S(2)}) copy-start(bf16[8,64,1024]{2,1,0:T(8,128)(2,1)S(1)} %collective-permute-done.20.refs_0_) | copy-start | bytes 3145732
  213.4 13.0 %collective-permute-start.12 = (bf16[128,2048]{1,0:T(8,128)(2,1)}, bf16[128,2048]{1,0:T(8,128)(2,1)}, u32[]{:S(2)}, u32[]{:S(2)}) collective-permute-start(bf16[128,2048]{1,0:T(8,128)(2,1)} %get-tuple-element.20.refs_0_), channel_id=1, source_target_pairs={{0,4},{4,0},{8,12},{12,8},{16,20},{20,16},{24,28},{28,24},{1,5},{5... | collective-permute-start | bytes 1572872 | tf_op jit(solution)/shard_map/ppermute | solution.py:455
  216.3 12.6 %copy-start.21 = (bf16[128,2048]{1,0:T(8,128)(2,1)}, bf16[128,2048]{1,0:T(8,128)(2,1)S(1)}, u32[]{:S(2)}) copy-start(bf16[128,2048]{1,0:T(8,128)(2,1)S(1)} %collective-permute-done.13.refs_2_) | copy-start | bytes 1572868
  216.3 10.1 %collective-permute-start.14 = (bf16[128,2048]{1,0:T(8,128)(2,1)S(1)}, bf16[128,2048]{1,0:T(8,128)(2,1)}, u32[]{:S(2)}, u32[]{:S(2)}) collective-permute-start(bf16[128,2048]{1,0:T(8,128)(2,1)S(1)} %collective-permute-done.13.refs_2_), channel_id=1, source_target_pairs={{0,4},{4,0},{8,12},{12,8},{16,20},{20,16},{24,28},{28,24},{1,5},{5... | collective-permute-start | bytes 1572872 | tf_op jit(solution)/shard_map/ppermute | solution.py:455
  225.9 3.0 copy-start.22
  225.9 2.0 collective-permute-start.16
  225.9 3.0 collective-permute-start.18
  228.9 9.8 %copy-start.9 = (bf16[8,64,1024]{2,1,0:T(8,128)(2,1)S(1)}, bf16[8,64,1024]{2,1,0:T(8,128)(2,1)}, u32[]{:S(2)}) copy-start(bf16[8,64,1024]{2,1,0:T(8,128)(2,1)} %shard_map.123.refs_1_) | copy-start | bytes 3145732
  245.0 2.4 collective-permute-start.24
  245.2 3.3 collective-permute-start.22
  245.6 27.3 %collective-permute-start.27 = (bf16[8,64,1024]{2,1,0:T(8,128)(2,1)S(1)}, bf16[8,64,1024]{2,1,0:T(8,128)(2,1)S(1)}, u32[]{:S(2)}, u32[]{:S(2)}) collective-permute-start(bf16[8,64,1024]{2,1,0:T(8,128)(2,1)S(1)} %copy-done.9), channel_id=1, source_target_pairs={{0,1},{1,2},{2,3},{3,0},{4,5},{5,6},{6,7},{7,4},{8,9},{9,10},{10,1... | collective-permute-start | bytes 3145736 | tf_op jit(solution)/shard_map/ppermute | solution.py:471
  248.9 24.0 %collective-permute-start.23 = (bf16[128,1536]{1,0:T(8,128)(2,1)S(1)}, bf16[128,1536]{1,0:T(8,128)(2,1)S(1)}, u32[]{:S(2)}, u32[]{:S(2)}) collective-permute-start(bf16[128,1536]{1,0:T(8,128)(2,1)S(1)} %get-tuple-element.42), channel_id=1, source_target_pairs={{0,8},{4,12},{8,0},{12,4},{16,24},{20,28},{24,16},{28,20},{1,9},{5... | collective-permute-start | bytes 1179656 | tf_op jit(solution)/shard_map/ppermute | solution.py:455
  250.5 22.3 %collective-permute-start.25 = (bf16[128,1536]{1,0:T(8,128)(2,1)S(1)}, bf16[128,1536]{1,0:T(8,128)(2,1)S(1)}, u32[]{:S(2)}, u32[]{:S(2)}) collective-permute-start(bf16[128,1536]{1,0:T(8,128)(2,1)S(1)} %get-tuple-element.36), channel_id=1, source_target_pairs={{0,16},{4,20},{8,24},{12,28},{16,0},{20,4},{24,8},{28,12},{1,17},{... | collective-permute-start | bytes 1179656 | tf_op jit(solution)/shard_map/ppermute | solution.py:455
  251.0 35.1 %copy-start.14 = (bf16[128,2048]{1,0:T(8,128)(2,1)S(1)}, bf16[128,2048]{1,0:T(8,128)(2,1)}, u32[]{:S(2)}) copy-start(bf16[128,2048]{1,0:T(8,128)(2,1)} %copy-done.13) | copy-start | bytes 1572868
  251.0 35.1 %copy-start.16 = (s32[2]{0:T(128)S(1)}, s32[2]{0:T(128)}, u32[]{:S(2)}) copy-start(s32[2]{0:T(128)} %copy-done.15) | copy-start | bytes 28
  251.0 21.9 %collective-permute-start.26 = (bf16[128,1536]{1,0:T(8,128)(2,1)S(1)}, bf16[128,1536]{1,0:T(8,128)(2,1)S(1)}, u32[]{:S(2)}, u32[]{:S(2)}) collective-permute-start(bf16[128,1536]{1,0:T(8,128)(2,1)S(1)} %get-tuple-element.35), channel_id=1, source_target_pairs={{0,24},{4,28},{8,16},{12,20},{16,8},{20,12},{24,0},{28,4},{1,25},{... | collective-permute-start | bytes 1179656 | tf_op jit(solution)/shard_map/ppermute | solution.py:455
  274.1 1.6 collective-permute-start.30
  274.2 1.9 collective-permute-start.28
  276.3 5.8 %collective-permute-start.29 = (bf16[128,512]{1,0:T(8,128)(2,1)S(1)}, bf16[128,512]{1,0:T(8,128)(2,1)S(1)}, u32[]{:S(2)}, u32[]{:S(2)}) collective-permute-start(bf16[128,512]{1,0:T(8,128)(2,1)S(1)} %get-tuple-element.54), channel_id=1, source_target_pairs={{0,8},{4,12},{8,0},{12,4},{16,24},{20,28},{24,16},{28,20},{1,9},{5... | collective-permute-start | bytes 393224 | tf_op jit(solution)/shard_map/ppermute | solution.py:455
  278.0 8.1 %collective-permute-start.31 = (bf16[128,512]{1,0:T(8,128)(2,1)S(1)}, bf16[128,512]{1,0:T(8,128)(2,1)S(1)}, u32[]{:S(2)}, u32[]{:S(2)}) collective-permute-start(bf16[128,512]{1,0:T(8,128)(2,1)S(1)} %get-tuple-element.44), channel_id=1, source_target_pairs={{0,16},{4,20},{8,24},{12,28},{16,0},{20,4},{24,8},{28,12},{1,17},{... | collective-permute-start | bytes 393224 | tf_op jit(solution)/shard_map/ppermute | solution.py:455
  278.4 7.6 %collective-permute-start.32 = (bf16[128,512]{1,0:T(8,128)(2,1)S(1)}, bf16[128,512]{1,0:T(8,128)(2,1)S(1)}, u32[]{:S(2)}, u32[]{:S(2)}) collective-permute-start(bf16[128,512]{1,0:T(8,128)(2,1)S(1)} %get-tuple-element.43), channel_id=1, source_target_pairs={{0,24},{4,28},{8,16},{12,20},{16,8},{20,12},{24,0},{28,4},{1,25},{... | collective-permute-start | bytes 393224 | tf_op jit(solution)/shard_map/ppermute | solution.py:455
  288.9 36.6 %collective-permute-start.36 = (bf16[128,2048]{1,0:T(8,128)(2,1)}, bf16[128,2048]{1,0:T(8,128)(2,1)S(1)}, u32[]{:S(2)}, u32[]{:S(2)}) collective-permute-start(bf16[128,2048]{1,0:T(8,128)(2,1)} %get-tuple-element.29), channel_id=1, source_target_pairs={{0,3},{1,11},{2,19},{3,27},{4,5},{5,13},{6,21},{7,29},{8,2},{9,10}... | collective-permute-start | bytes 1572872 | tf_op jit(solution)/shard_map/ppermute | solution.py:560
  290.3 55.8 %collective-permute-start.33 = (bf16[128,2048]{1,0:T(8,128)(2,1)}, bf16[128,2048]{1,0:T(8,128)(2,1)S(1)}, u32[]{:S(2)}, u32[]{:S(2)}) collective-permute-start(bf16[128,2048]{1,0:T(8,128)(2,1)} %get-tuple-element.29), channel_id=1, source_target_pairs={{0,0},{1,8},{2,16},{3,24},{4,6},{5,14},{6,22},{7,30},{8,1},{9,9},{... | collective-permute-start | bytes 1572872 | tf_op jit(solution)/shard_map/ppermute | solution.py:560
  292.2 57.4 %collective-permute-start.34 = (bf16[128,2048]{1,0:T(8,128)(2,1)}, bf16[128,2048]{1,0:T(8,128)(2,1)S(1)}, u32[]{:S(2)}, u32[]{:S(2)}) collective-permute-start(bf16[128,2048]{1,0:T(8,128)(2,1)} %get-tuple-element.29), channel_id=1, source_target_pairs={{0,1},{1,9},{2,17},{3,25},{4,7},{5,15},{6,23},{7,31},{8,0},{9,8},{... | collective-permute-start | bytes 1572872 | tf_op jit(solution)/shard_map/ppermute | solution.py:560
  299.0 50.6 %collective-permute-start.35 = (bf16[128,2048]{1,0:T(8,128)(2,1)}, bf16[128,2048]{1,0:T(8,128)(2,1)S(1)}, u32[]{:S(2)}, u32[]{:S(2)}) collective-permute-start(bf16[128,2048]{1,0:T(8,128)(2,1)} %get-tuple-element.29), channel_id=1, source_target_pairs={{0,2},{1,10},{2,18},{3,26},{4,4},{5,12},{6,20},{7,28},{8,3},{9,11}... | collective-permute-start | bytes 1572872 | tf_op jit(solution)/shard_map/ppermute | solution.py:560
  301.8 42.4 %all-to-all-start.2 = ((bf16[8,128,256]{2,1,0:T(8,128)(2,1)}), bf16[8,128,256]{2,1,0:T(8,128)(2,1)}, u32[]{:S(2)}, u32[]{:S(2)}) async-start(bf16[8,128,256]{2,1,0:T(8,128)(2,1)} %bitcast.80), calls=%async_computation.2 | async-start | bytes 1048576 | tf_op jit(solution)/shard_map/all_to_all | solution.py:477
  326.3 23.4 %copy-start.12 = (bf16[128,2048]{1,0:T(8,128)(2,1)S(1)}, bf16[128,2048]{1,0:T(8,128)(2,1)}, u32[]{:S(2)}) copy-start(bf16[128,2048]{1,0:T(8,128)(2,1)} %copy-done.11) | copy-start | bytes 1572868
  328.2 31.4 %collective-permute-start.37 = (bf16[4,4,64,64]{3,2,1,0:T(8,128)(2,1)}, bf16[4,4,64,64]{3,2,1,0:T(8,128)(2,1)S(1)}, u32[]{:S(2)}, u32[]{:S(2)}) collective-permute-start(bf16[4,4,64,64]{3,2,1,0:T(8,128)(2,1)} %get-tuple-element.52), channel_id=1, source_target_pairs={{0,0},{1,8},{2,16},{3,24},{4,4},{5,12},{6,20},{7,28},{8,1},{9,9},{... | collective-permute-start | bytes 393224 | tf_op jit(solution)/shard_map/ppermute | solution.py:574
  330.2 32.8 %collective-permute-start.38 = (bf16[4,4,64,64]{3,2,1,0:T(8,128)(2,1)}, bf16[4,4,64,64]{3,2,1,0:T(8,128)(2,1)S(1)}, u32[]{:S(2)}, u32[]{:S(2)}) collective-permute-start(bf16[4,4,64,64]{3,2,1,0:T(8,128)(2,1)} %get-tuple-element.51), channel_id=1, source_target_pairs={{0,4},{1,12},{2,20},{3,28},{4,0},{5,8},{6,16},{7,24},{8,5},{9,13},... | collective-permute-start | bytes 393224 | tf_op jit(solution)/shard_map/ppermute | solution.py:574
  349.6 15.2 %copy-start.1 = (bf16[2,96,2048]{2,1,0:T(8,128)(2,1)S(1)}, bf16[2,96,2048]{2,1,0:T(8,128)(2,1)}, u32[]{:S(2)}) copy-start(bf16[2,96,2048]{2,1,0:T(8,128)(2,1)} %param.14) | copy-start | bytes 2359300
  (7 other events, 6.8 us)
Sparse Core Ops, SparseCore 0:
  36.9 54.1 all-gather.2
  93.0 45.4 all-gather.4

commit v6 on v5

--- a/solution.py
+++ b/solution.py
@@ -325,7 +325,7 @@
             pltpu.VMEM((nb, nc, deep, ff), BF16),
             pltpu.SemaphoreType.DMA((nc + nb,)),
         ],
-        compiler_params=pltpu.CompilerParams(vmem_limit_bytes=58 * 2**20),
+        compiler_params=pltpu.CompilerParams(vmem_limit_bytes=40 * 2**20),
         cost_estimate=pl.CostEstimate(flops=10**6, bytes_accessed=2**12, transcendentals=0),
     )(place, *xs, *shards, *extra)
 
@@ -562,7 +562,7 @@
     out_hidden = blocks.reshape(chips, 2, chunk, fw).transpose(1, 0, 2, 3).reshape(tokens, fw)
     half = prompts // 2
     share = n_row // n_col
-    states = after(states, arrived[-1]).reshape(2, half, states.shape[1], HEAD, HEAD)
+    states = after(states, arrived[2]).reshape(2, half, states.shape[1], HEAD, HEAD)
     moved = []
     for j in range(2):
         pairs = []

time: 376 us -> 379 us (level)
  waiting for transfers between devices: 180 us -> 193 us
  starting transfers between devices: 69.5 us -> 56.6 us
  local copies, waits for them, and re-layouts: 23.2 us -> 31.4 us
    ppermute x4, waiting for transfers between devices: 23 us -> 42.3 us  [per_device(): arrived.append(lax.ppermute(third, ('row', 'col'), pairs))]
    ppermute x2, starting transfers between devices: 15 us -> 3.08 us  [per_device(): moved.append(lax.ppermute(piece, ('row', 'col'), pairs))]
    unnamed x56 -> x64, local copies, waits for them, and re-layouts: 7.52 us -> 15.7 us
    ppermute x2, waiting for transfers between devices: 5.36 us -> 0.01 us  [per_device(): moved.append(lax.ppermute(piece, ('row', 'col'), pairs))]
  transfers between devices with their start and end apart: 44 -> 44, of which waited for: 24 -> 22; matrix products, arithmetic and copies ran while one was open for 6% -> 6% of each run, Pallas kernels for 17% -> 16%
where the time goes in v6:
time: 379 us; the launch traced here: 377 us
  waiting for transfers between devices  193 us (51%)
  Pallas kernels  72.7 us (19%)
  starting transfers between devices  56.6 us (15%)
  local copies, waits for them, and re-layouts  31.4 us (8%)
  between operations  14.4 us (4%)
  other arithmetic  9.35 us (2%)
    ppermute x7, waiting for transfers between devices, ring(): return lax.ppermute(x, 'col', [(i, (i + 1) % n_col) for i in range(n_col)])  82.6 us
    ppermute x21, waiting for transfers between devices, to_row(): return lax.ppermute(x, 'row', [(i, i ^ k) for i in range(n_row)])  53.8 us
    pallas_call x1, Pallas kernels, time_mix(): pl.pallas_call(functools.partial(time_kernel, nc, per), grid=(prompts //...  43.1 us
    ppermute x4, waiting for transfers between devices, per_device(): arrived.append(lax.ppermute(third, ('row', 'col'), pairs))  42.3 us
    ppermute x21, starting transfers between devices, to_row(): return lax.ppermute(x, 'row', [(i, i ^ k) for i in range(n_row)])  15.7 us
    unnamed x64, local copies, waits for them, and re-layouts  15.7 us
    all_to_all x3, starting transfers between devices, relay(): return lax.all_to_all(x, 'row', 0, 0, tiled=True)  15.6 us
    ppermute x3, waiting for transfers between devices, to_col(): return lax.ppermute(x, 'col', [(i, i ^ k) for i in range(n_col)])  13.8 us
  transfers between devices with their start and end apart: 44, of which 22 were waited for; matrix products, arithmetic and copies ran while one was open for 6% of the time, Pallas kernels for 16%

profile of v6, /device:TPU:12, one launch (start us, length us, event | category | flops | bytes accessed | tf_op | source)
XLA Modules:
  0.0 377.0 jit_solution(16112809782649764406)
XLA Ops:
  7.2 1.8 slice.212
  9.0 1.1 copy.50
  10.1 4.2 %all-to-all-start = ((bf16[8,4,64,256]{3,2,1,0:T(8,128)(2,1)}), bf16[8,4,64,256]{3,2,1,0:T(8,128)(2,1)S(1)}, u32[]{:S(2)}, u32[]{:S(2)}) async-start(bf16[8,4,64,256]{3,2,1,0:T(8,128)(2,1)} %bitcast.78), calls=%async_computation | async-start | bytes 2097152 | tf_op jit(solution)/shard_map/all_to_all | solution.py:477
  14.4 1.6 slice.120
  16.1 1.6 collective-permute-start.2
  17.7 1.2 collective-permute-start.1
  18.9 1.2 collective-permute-start
  21.0 11.2 %collective-permute-done.2 = bf16[3,64,512]{2,1,0:T(8,128)(2,1)S(1)} collective-permute-done((bf16[3,64,512]{2,1,0:T(8,128)(2,1)S(1)}, bf16[3,64,512]{2,1,0:T(8,128)(2,1)S(1)}, u32[]{:S(2)}, u32[]{:S(2)}) %collective-permute-start.2) | collective-permute-done | bytes 196640 | tf_op jit(solution)/shard_map/ppermute | solution.py:458
  32.3 2.5 collective-permute-done.1
  34.8 1.0 pad_maximum_fusion.refs_1_
  36.8 1.1 copy-done.4
  38.5 2.4 convert_element_type.192
  40.9 1.6 copy.49
  42.5 4.7 %all-to-all-start.1 = ((bf16[8,2,64,1024]{3,2,1,0:T(8,128)(2,1)}), bf16[8,2,64,1024]{3,2,1,0:T(8,128)(2,1)}, u32[]{:S(2)}, u32[]{:S(2)}) async-start(bf16[8,2,64,1024]{3,2,1,0:T(8,128)(2,1)} %shard_map.114), calls=%async_computation.1 | async-start | bytes 4194304 | tf_op jit(solution)/shard_map/all_to_all | solution.py:477
  47.2 15.9 %collective-permute-done.3.refs_1_ = bf16[8,4,64,256]{3,2,1,0:T(8,128)(2,1)} collective-permute-done((bf16[8,4,64,256]{3,2,1,0:T(8,128)(2,1)S(1)}, bf16[8,4,64,256]{3,2,1,0:T(8,128)(2,1)}, u32[]{:S(2)}, u32[]{:S(2)}) %collective-permute-start.3) | collective-permute-done | bytes 1048608 | tf_op jit(solution)/shard_map/ppermute | solution.py:471
  63.8 24.8 %collective-permute-done.4.refs_2_ = bf16[8,4,64,256]{3,2,1,0:T(8,128)(2,1)} collective-permute-done((bf16[8,4,64,256]{3,2,1,0:T(8,128)(2,1)}, bf16[8,4,64,256]{3,2,1,0:T(8,128)(2,1)}, u32[]{:S(2)}, u32[]{:S(2)}) %collective-permute-start.4) | collective-permute-done | bytes 1048608 | tf_op jit(solution)/shard_map/ppermute | solution.py:471
  88.8 1.3 copy.35.ld
  91.0 3.1 slice_bitcast_fusion
  94.1 19.1 %collective-permute-done.5.refs_1_.refs_3_ = bf16[8,4,64,256]{3,2,1,0:T(8,128)(2,1)S(1)} collective-permute-done((bf16[8,4,64,256]{3,2,1,0:T(8,128)(2,1)}, bf16[8,4,64,256]{3,2,1,0:T(8,128)(2,1)S(1)}, u32[]{:S(2)}, u32[]{:S(2)}) %collective-permute-start.5) | collective-permute-done | bytes 1048608 | tf_op jit(solution)/shard_map/ppermute | solution.py:471
  114.2 3.6 collective-permute-start.7
  119.5 1.2 copy-done.15
  120.7 43.1 %shard_map.116 = (bf16[4,128,2048]{2,1,0:T(8,128)(2,1)}, bf16[4,128,2048]{2,1,0:T(8,128)(2,1)}, bf16[128,2048]{1,0:T(8,128)(2,1)S(1)}, bf16[8,4,64,64]{3,2,1,0:T(8,128)(2,1)S(1)}) custom-call(s32[2]{0:T(128)S(1)} %pad_add_fusion.place_ref, s32[8]{0:T(128)S(1)} %dynamic_slice.28.lens, bf16[8,1056,256]{2,1,0:T(8,128)(2,1)} %bitcast.100, ...), custom_call_target="tpu_custom_call" | custom-call | flops 40000000000 | bytes 16777216 | tf_op jit(solution)/shard_map/pallas_call | solution.py:192
  165.8 4.2 %collective-permute-done.8 = bf16[4,128,2048]{2,1,0:T(8,128)(2,1)} collective-permute-done((bf16[4,128,2048]{2,1,0:T(8,128)(2,1)}, bf16[4,128,2048]{2,1,0:T(8,128)(2,1)}, u32[]{:S(2)}, u32[]{:S(2)}) %collective-permute-start.8) | collective-permute-done | bytes 2097184 | tf_op jit(solution)/shard_map/ppermute | solution.py:455
  170.1 3.4 fusion.3
  173.5 1.5 collective-permute-start.9
  175.6 1.4 collective-permute-start.11
  177.1 11.4 %collective-permute-done.9.refs_1_ = bf16[128,2048]{1,0:T(8,128)(2,1)S(1)} collective-permute-done((bf16[128,2048]{1,0:T(8,128)(2,1)}, bf16[128,2048]{1,0:T(8,128)(2,1)S(1)}, u32[]{:S(2)}, u32[]{:S(2)}) %collective-permute-start.9) | collective-permute-done | bytes 524320 | tf_op jit(solution)/shard_map/ppermute | solution.py:455
  189.3 10.8 %collective-permute-done.10.refs_2_ = bf16[128,2048]{1,0:T(8,128)(2,1)S(1)} collective-permute-done((bf16[128,2048]{1,0:T(8,128)(2,1)}, bf16[128,2048]{1,0:T(8,128)(2,1)S(1)}, u32[]{:S(2)}, u32[]{:S(2)}) %collective-permute-start.10) | collective-permute-done | bytes 524320 | tf_op jit(solution)/shard_map/ppermute | solution.py:455
  200.9 1.0 copy-done.19
  202.0 1.0 copy-done.21
  203.0 3.1 shard_map.119
  207.4 1.5 collective-permute-start.15
  209.0 1.4 collective-permute-start.17
  210.4 3.9 %collective-permute-start.21 = (bf16[8,64,1024]{2,1,0:T(8,128)(2,1)S(1)}, bf16[8,64,1024]{2,1,0:T(8,128)(2,1)}, u32[]{:S(2)}, u32[]{:S(2)}) collective-permute-start(bf16[8,64,1024]{2,1,0:T(8,128)(2,1)S(1)} %copy-done.2), channel_id=1, source_target_pairs={{0,3},{1,0},{2,1},{3,2},{4,7},{5,4},{6,5},{7,6},{8,11},{9,8},{10,9... | collective-permute-start | bytes 3145736 | tf_op jit(solution)/shard_map/ppermute | solution.py:474
  214.2 2.2 collective-permute-done.20.refs_0_
  216.4 5.5 %collective-permute-done.13.refs_2_ = bf16[128,2048]{1,0:T(8,128)(2,1)S(1)} collective-permute-done((bf16[128,2048]{1,0:T(8,128)(2,1)}, bf16[128,2048]{1,0:T(8,128)(2,1)S(1)}, u32[]{:S(2)}, u32[]{:S(2)}) %collective-permute-start.13) | collective-permute-done | bytes 524320 | tf_op jit(solution)/shard_map/ppermute | solution.py:455
  222.0 8.9 %collective-permute-done.15.refs_4_ = bf16[128,2048]{1,0:T(8,128)(2,1)S(1)} collective-permute-done((bf16[128,2048]{1,0:T(8,128)(2,1)}, bf16[128,2048]{1,0:T(8,128)(2,1)S(1)}, u32[]{:S(2)}, u32[]{:S(2)}) %collective-permute-start.15) | collective-permute-done | bytes 524320 | tf_op jit(solution)/shard_map/ppermute | solution.py:455
  231.4 1.5 collective-permute-done.16.refs_5_
  233.9 1.2 copy-done.9
  235.1 1.0 copy-done.17
  236.1 7.6 %shard_map.120.act = bf16[1024,1024]{1,0:T(8,128)(2,1)S(1)} custom-call(s32[2]{0:T(128)S(1)} %pad_add_fusion.place_ref, bf16[128,2048]{1,0:T(8,128)(2,1)} %get-tuple-element.20.refs_0_, bf16[128,2048]{1,0:T(8,128)(2,1)} %collective-permute-done.12.refs_1_, bf16[128,2048]{1,0:T(8,128)(2,1)S(1)} %collective-permute-done.13.refs_2_, ...), custom_call_target="tpu_custom_call" | custom-call | flops 1000000 | bytes 4096 | tf_op jit(solution)/shard_map/pallas_call | solution.py:318
  243.7 5.0 %shard_map.124 = (bf16[4,128,1536]{2,1,0:T(8,128)(2,1)S(1)}, bf16[2,128,1536]{2,1,0:T(8,128)(2,1)S(1)}, bf16[2,128,1536]{2,1,0:T(8,128)(2,1)S(1)}) custom-call(bf16[1024,1024]{1,0:T(8,128)(2,1)S(1)} %shard_map.120.act, bf16[8,64,1024]{2,1,0:T(8,128)(2,1)S(1)} %copy-done.2, bf16[8,64,1024]{2,1,0:T(8,128)(2,1)} %shard_map.123.refs_1_, ...), custom_call_target="tpu_custom_call" | custom-call | flops 1000000 | bytes 4096 | tf_op jit(solution)/shard_map/pallas_call | solution.py:353
  249.3 1.8 collective-permute-done.24
  251.1 1.1 collective-permute-done.22
  252.6 1.6 collective-permute-start.23
  254.7 1.5 collective-permute-start.26
  256.2 20.5 %collective-permute-done.27.refs_0_ = bf16[8,64,1024]{2,1,0:T(8,128)(2,1)S(1)} collective-permute-done((bf16[8,64,1024]{2,1,0:T(8,128)(2,1)}, bf16[8,64,1024]{2,1,0:T(8,128)(2,1)S(1)}, u32[]{:S(2)}, u32[]{:S(2)}) %collective-permute-start.27) | collective-permute-done | bytes 1048608 | tf_op jit(solution)/shard_map/ppermute | solution.py:471
  276.8 1.3 shard_map.125
  278.6 1.0 collective-permute-done.30
  280.2 1.7 collective-permute-start.29
  282.3 1.5 collective-permute-start.32
  283.7 2.3 collective-permute-done.29.refs_5_
  286.0 3.9 %collective-permute-done.31.refs_6_ = bf16[128,512]{1,0:T(8,128)(2,1)S(1)} collective-permute-done((bf16[128,512]{1,0:T(8,128)(2,1)S(1)}, bf16[128,512]{1,0:T(8,128)(2,1)S(1)}, u32[]{:S(2)}, u32[]{:S(2)}) %collective-permute-start.31) | collective-permute-done | bytes 131104 | tf_op jit(solution)/shard_map/ppermute | solution.py:455
  289.9 2.9 shard_map.126
  292.8 6.3 %collective-permute-start.35 = (bf16[128,2048]{1,0:T(8,128)(2,1)}, bf16[128,2048]{1,0:T(8,128)(2,1)S(1)}, u32[]{:S(2)}, u32[]{:S(2)}) collective-permute-start(bf16[128,2048]{1,0:T(8,128)(2,1)} %get-tuple-element.29), channel_id=1, source_target_pairs={{0,2},{1,10},{2,18},{3,26},{4,4},{5,12},{6,20},{7,28},{8,3},{9,11}... | collective-permute-start | bytes 1572872 | tf_op jit(solution)/shard_map/ppermute | solution.py:560
  299.1 1.9 collective-permute-start.33
  302.7 6.6 %all-to-all-start.2 = ((bf16[8,128,256]{2,1,0:T(8,128)(2,1)}), bf16[8,128,256]{2,1,0:T(8,128)(2,1)}, u32[]{:S(2)}, u32[]{:S(2)}) async-start(bf16[8,128,256]{2,1,0:T(8,128)(2,1)} %bitcast.80), calls=%async_computation.2 | async-start | bytes 1048576 | tf_op jit(solution)/shard_map/all_to_all | solution.py:477
  309.3 23.6 %collective-permute-done.35.refs_2_.refs_1_ = bf16[128,2048]{1,0:T(8,128)(2,1)S(1)} collective-permute-done((bf16[128,2048]{1,0:T(8,128)(2,1)}, bf16[128,2048]{1,0:T(8,128)(2,1)S(1)}, u32[]{:S(2)}, u32[]{:S(2)}) %collective-permute-start.35) | collective-permute-done | bytes 524320 | tf_op jit(solution)/shard_map/ppermute | solution.py:560
  333.7 2.0 dynamic-slice_bitcast_fusion
  335.7 2.3 collective-permute-start.37
  339.7 1.9 copy.38
  341.5 18.8 %collective-permute-done.34.refs_1_ = bf16[128,2048]{1,0:T(8,128)(2,1)S(1)} collective-permute-done((bf16[128,2048]{1,0:T(8,128)(2,1)}, bf16[128,2048]{1,0:T(8,128)(2,1)S(1)}, u32[]{:S(2)}, u32[]{:S(2)}) %collective-permute-start.34) | collective-permute-done | bytes 524320 | tf_op jit(solution)/shard_map/ppermute | solution.py:560
  360.3 8.0 %shard_map.127 = bf16[3,512,512]{2,1,0:T(8,128)(2,1)} custom-call(s32[2]{0:T(128)S(1)} %pad_add_fusion.place_ref, bf16[128,2048]{1,0:T(8,128)(2,1)S(1)} %collective-permute-done.33.refs_0_, bf16[128,2048]{1,0:T(8,128)(2,1)S(1)} %collective-permute-done.34.refs_1_, bf16[128,2048]{1,0:T(8,128)(2,1)S(1)} %copy-done.12, ...), custom_call_target="tpu_custom_call" | custom-call | flops 1000000 | bytes 4096 | tf_op jit(solution)/shard_map/pallas_call | solution.py:394
  368.3 1.8 shard_map.129
  (138 shorter events, 21.1 us)
Async XLA Ops:
  7.2 83.8 %copy-start = (bf16[2,96,2048]{2,1,0:T(8,128)(2,1)S(1)}, bf16[2,96,2048]{2,1,0:T(8,128)(2,1)}, u32[]{:S(2)}) copy-start(bf16[2,96,2048]{2,1,0:T(8,128)(2,1)} %param.14) | copy-start | bytes 2359300
  10.1 25.7 %all-to-all-start = ((bf16[8,4,64,256]{3,2,1,0:T(8,128)(2,1)}), bf16[8,4,64,256]{3,2,1,0:T(8,128)(2,1)S(1)}, u32[]{:S(2)}, u32[]{:S(2)}) async-start(bf16[8,4,64,256]{3,2,1,0:T(8,128)(2,1)} %bitcast.78), calls=%async_computation | async-start | bytes 2097152 | tf_op jit(solution)/shard_map/all_to_all | solution.py:477
  14.3 5.9 %copy-start.29 = (f32[6,256]{1,0:T(8,128)S(1)}, f32[6,256]{1,0:T(8,128)}, u32[]{:S(2)}) copy-start(f32[6,256]{1,0:T(8,128)} %param.17) | copy-start | bytes 18436
  14.3 5.9 %copy-start.27 = (bf16[1024,256]{1,0:T(8,128)(2,1)S(1)}, bf16[1024,256]{1,0:T(8,128)(2,1)}, u32[]{:S(2)}) copy-start(bf16[1024,256]{1,0:T(8,128)(2,1)} %param.9) | copy-start | bytes 1572868
  14.3 103.5 %all-gather.3.cloned.1.call-start = ((), (), s32[]{:S(2)}) async-start(), calls=%async_computation.3 | async-start | bytes 4866048 | tf_op jit(solution)/shard_map/all_gather | solution.py:494
  16.1 16.2 %collective-permute-start.2 = (bf16[3,64,512]{2,1,0:T(8,128)(2,1)S(1)}, bf16[3,64,512]{2,1,0:T(8,128)(2,1)S(1)}, u32[]{:S(2)}, u32[]{:S(2)}) collective-permute-start(bf16[3,64,512]{2,1,0:T(8,128)(2,1)S(1)} %get-tuple-element.48), channel_id=1, source_target_pairs={{0,3},{1,2},{2,1},{3,0},{4,7},{5,6},{6,5},{7,4},{8,11},{9,10},{10,... | collective-permute-start | bytes 589832 | tf_op jit(solution)/shard_map/ppermute | solution.py:458
  17.7 17.1 %collective-permute-start.1 = (bf16[3,64,512]{2,1,0:T(8,128)(2,1)S(1)}, bf16[3,64,512]{2,1,0:T(8,128)(2,1)S(1)}, u32[]{:S(2)}, u32[]{:S(2)}) collective-permute-start(bf16[3,64,512]{2,1,0:T(8,128)(2,1)S(1)} %get-tuple-element.49), channel_id=1, source_target_pairs={{0,2},{1,3},{2,0},{3,1},{4,6},{5,7},{6,4},{7,5},{8,10},{9,11},{10,... | collective-permute-start | bytes 589832 | tf_op jit(solution)/shard_map/ppermute | solution.py:458
  18.9 15.9 %collective-permute-start = (bf16[3,64,512]{2,1,0:T(8,128)(2,1)S(1)}, bf16[3,64,512]{2,1,0:T(8,128)(2,1)S(1)}, u32[]{:S(2)}, u32[]{:S(2)}) collective-permute-start(bf16[3,64,512]{2,1,0:T(8,128)(2,1)S(1)} %get-tuple-element.50), channel_id=1, source_target_pairs={{0,1},{1,0},{2,3},{3,2},{4,5},{5,4},{6,7},{7,6},{8,9},{9,8},{10,11... | collective-permute-start | bytes 589832 | tf_op jit(solution)/shard_map/ppermute | solution.py:458
  36.8 1.2 copy-start.4
  36.8 194.6 %all-gather.5.cloned.1.call-start = ((), (), s32[]{:S(2)}) async-start(), calls=%async_computation.4 | async-start | bytes 7077888 | tf_op jit(solution)/shard_map/all_gather | solution.py:500
  38.0 25.1 %collective-permute-start.3 = (bf16[8,4,64,256]{3,2,1,0:T(8,128)(2,1)S(1)}, bf16[8,4,64,256]{3,2,1,0:T(8,128)(2,1)}, u32[]{:S(2)}, u32[]{:S(2)}) collective-permute-start(bf16[8,4,64,256]{3,2,1,0:T(8,128)(2,1)S(1)} %copy-done.4), channel_id=1, source_target_pairs={{0,1},{1,2},{2,3},{3,0},{4,5},{5,6},{6,7},{7,4},{8,9},{9,10},{10,1... | collective-permute-start | bytes 3145736 | tf_op jit(solution)/shard_map/ppermute | solution.py:471
  42.5 46.2 %copy-start.28 = (f32[9,2048]{1,0:T(8,128)S(1)}, f32[9,2048]{1,0:T(8,128)}, u32[]{:S(2)}) copy-start(f32[9,2048]{1,0:T(8,128)} %param.15) | copy-start | bytes 221188
  42.5 46.3 %copy-start.26 = (bf16[2,2048,96]{1,2,0:T(8,128)(2,1)S(1)}, bf16[2,2048,96]{1,2,0:T(8,128)(2,1)}, u32[]{:S(2)}) copy-start(bf16[2,2048,96]{1,2,0:T(8,128)(2,1)} %param.13) | copy-start | bytes 2359300
  42.5 48.5 %all-to-all-start.1 = ((bf16[8,2,64,1024]{3,2,1,0:T(8,128)(2,1)}), bf16[8,2,64,1024]{3,2,1,0:T(8,128)(2,1)}, u32[]{:S(2)}, u32[]{:S(2)}) async-start(bf16[8,2,64,1024]{3,2,1,0:T(8,128)(2,1)} %shard_map.114), calls=%async_computation.1 | async-start | bytes 4194304 | tf_op jit(solution)/shard_map/all_to_all | solution.py:477
  47.2 42.9 %copy-start.30 = (s32[32]{0:T(128)S(1)}, s32[32]{0:T(128)}, u32[]{:S(2)}) copy-start(s32[32]{0:T(128)} %param.10) | copy-start | bytes 388
  63.1 25.6 %collective-permute-start.4 = (bf16[8,4,64,256]{3,2,1,0:T(8,128)(2,1)}, bf16[8,4,64,256]{3,2,1,0:T(8,128)(2,1)}, u32[]{:S(2)}, u32[]{:S(2)}) collective-permute-start(bf16[8,4,64,256]{3,2,1,0:T(8,128)(2,1)} %collective-permute-done.3.refs_1_), channel_id=1, source_target_pairs={{0,1},{1,2},{2,3},{3,0},{4,5},{5,6},{6,7},{7,4},{8,9},{9,10},{10,1... | collective-permute-start | bytes 3145736 | tf_op jit(solution)/shard_map/ppermute | solution.py:471
  88.7 24.5 %collective-permute-start.5 = (bf16[8,4,64,256]{3,2,1,0:T(8,128)(2,1)}, bf16[8,4,64,256]{3,2,1,0:T(8,128)(2,1)S(1)}, u32[]{:S(2)}, u32[]{:S(2)}) collective-permute-start(bf16[8,4,64,256]{3,2,1,0:T(8,128)(2,1)} %collective-permute-done.4.refs_2_), channel_id=1, source_target_pairs={{0,1},{1,2},{2,3},{3,0},{4,5},{5,6},{6,7},{7,4},{8,9},{9,10},{10,1... | collective-permute-start | bytes 3145736 | tf_op jit(solution)/shard_map/ppermute | solution.py:471
  94.1 25.4 %copy-start.5 = (bf16[8,4,64,256]{3,2,1,0:T(8,128)(2,1)S(1)}, bf16[8,4,64,256]{3,2,1,0:T(8,128)(2,1)}, u32[]{:S(2)}) copy-start(bf16[8,4,64,256]{3,2,1,0:T(8,128)(2,1)} %shard_map.112.refs_1_.refs_0_) | copy-start | bytes 3145732
  114.2 50.4 %collective-permute-start.6 = (bf16[8,64,1024]{2,1,0:T(8,128)(2,1)}, bf16[8,64,1024]{2,1,0:T(8,128)(2,1)}, u32[]{:S(2)}, u32[]{:S(2)}) collective-permute-start(bf16[8,64,1024]{2,1,0:T(8,128)(2,1)} %shard_map.115.refs_4_.refs_8_), channel_id=1, source_target_pairs={{0,1},{1,2},{2,3},{3,0},{4,5},{5,6},{6,7},{7,4},{8,9},{9,10},{10,1... | collective-permute-start | bytes 3145736 | tf_op jit(solution)/shard_map/ppermute | solution.py:471
  114.2 50.4 %collective-permute-start.7 = (bf16[8,64,1024]{2,1,0:T(8,128)(2,1)}, bf16[8,64,1024]{2,1,0:T(8,128)(2,1)S(1)}, u32[]{:S(2)}, u32[]{:S(2)}) collective-permute-start(bf16[8,64,1024]{2,1,0:T(8,128)(2,1)} %shard_map.115.refs_4_.refs_8_), channel_id=1, source_target_pairs={{0,3},{1,0},{2,1},{3,2},{4,7},{5,4},{6,5},{7,6},{8,11},{9,8},{10,9... | collective-permute-start | bytes 3145736 | tf_op jit(solution)/shard_map/ppermute | solution.py:474
  119.5 1.2 copy-start.15
  165.6 4.5 %copy-start.23 = (bf16[4,128,2048]{2,1,0:T(8,128)(2,1)S(1)}, bf16[4,128,2048]{2,1,0:T(8,128)(2,1)}, u32[]{:S(2)}) copy-start(bf16[4,128,2048]{2,1,0:T(8,128)(2,1)} %get-tuple-element.17) | copy-start | bytes 6291460
  165.6 4.5 %collective-permute-start.8 = (bf16[4,128,2048]{2,1,0:T(8,128)(2,1)}, bf16[4,128,2048]{2,1,0:T(8,128)(2,1)}, u32[]{:S(2)}, u32[]{:S(2)}) collective-permute-start(bf16[4,128,2048]{2,1,0:T(8,128)(2,1)} %shard_map.118), channel_id=1, source_target_pairs={{0,4},{4,0},{8,12},{12,8},{16,20},{20,16},{24,28},{28,24},{1,5},{5... | collective-permute-start | bytes 6291464 | tf_op jit(solution)/shard_map/ppermute | solution.py:455
  165.6 44.8 %collective-permute-start.19 = (bf16[8,64,1024]{2,1,0:T(8,128)(2,1)}, bf16[8,64,1024]{2,1,0:T(8,128)(2,1)}, u32[]{:S(2)}, u32[]{:S(2)}) collective-permute-start(bf16[8,64,1024]{2,1,0:T(8,128)(2,1)} %shard_map.117.refs_1_.refs_9_), channel_id=1, source_target_pairs={{0,1},{1,2},{2,3},{3,0},{4,5},{5,6},{6,7},{7,4},{8,9},{9,10},{10,1... | collective-permute-start | bytes 3145736 | tf_op jit(solution)/shard_map/ppermute | solution.py:471
  173.5 3.5 copy-start.25
  173.5 27.4 %copy-start.7 = (bf16[128,2048]{1,0:T(8,128)(2,1)S(1)}, bf16[128,2048]{1,0:T(8,128)(2,1)}, u32[]{:S(2)}) copy-start(bf16[128,2048]{1,0:T(8,128)(2,1)} %get-tuple-element.34.refs_0_.refs_1_) | copy-start | bytes 1572868
  173.5 15.0 %collective-permute-start.9 = (bf16[128,2048]{1,0:T(8,128)(2,1)}, bf16[128,2048]{1,0:T(8,128)(2,1)S(1)}, u32[]{:S(2)}, u32[]{:S(2)}) collective-permute-start(bf16[128,2048]{1,0:T(8,128)(2,1)} %get-tuple-element.33), channel_id=1, source_target_pairs={{0,8},{4,12},{8,0},{12,4},{16,24},{20,28},{24,16},{28,20},{1,9},{5... | collective-permute-start | bytes 1572872 | tf_op jit(solution)/shard_map/ppermute | solution.py:455
  175.0 25.1 %collective-permute-start.10 = (bf16[128,2048]{1,0:T(8,128)(2,1)}, bf16[128,2048]{1,0:T(8,128)(2,1)S(1)}, u32[]{:S(2)}, u32[]{:S(2)}) collective-permute-start(bf16[128,2048]{1,0:T(8,128)(2,1)} %get-tuple-element.32), channel_id=1, source_target_pairs={{0,16},{4,20},{8,24},{12,28},{16,0},{20,4},{24,8},{28,12},{1,17},{... | collective-permute-start | bytes 1572872 | tf_op jit(solution)/shard_map/ppermute | solution.py:455
  175.6 25.3 %collective-permute-start.11 = (bf16[128,2048]{1,0:T(8,128)(2,1)}, bf16[128,2048]{1,0:T(8,128)(2,1)}, u32[]{:S(2)}, u32[]{:S(2)}) collective-permute-start(bf16[128,2048]{1,0:T(8,128)(2,1)} %get-tuple-element.31), channel_id=1, source_target_pairs={{0,24},{4,28},{8,16},{12,20},{16,8},{20,12},{24,0},{28,4},{1,25},{... | collective-permute-start | bytes 1572872 | tf_op jit(solution)/shard_map/ppermute | solution.py:455
  177.0 33.4 %copy-start.2 = (bf16[8,64,1024]{2,1,0:T(8,128)(2,1)S(1)}, bf16[8,64,1024]{2,1,0:T(8,128)(2,1)}, u32[]{:S(2)}) copy-start(bf16[8,64,1024]{2,1,0:T(8,128)(2,1)} %shard_map.122.refs_0_) | copy-start | bytes 3145732
  177.0 39.4 %collective-permute-start.20 = (bf16[8,64,1024]{2,1,0:T(8,128)(2,1)}, bf16[8,64,1024]{2,1,0:T(8,128)(2,1)}, u32[]{:S(2)}, u32[]{:S(2)}) collective-permute-start(bf16[8,64,1024]{2,1,0:T(8,128)(2,1)} %shard_map.122.refs_0_), channel_id=1, source_target_pairs={{0,1},{1,2},{2,3},{3,0},{4,5},{5,6},{6,7},{7,4},{8,9},{9,10},{10,1... | collective-permute-start | bytes 3145736 | tf_op jit(solution)/shard_map/ppermute | solution.py:471
  200.9 1.0 copy-start.19
  203.0 30.8 %copy-start.6 = (bf16[8,64,1024]{2,1,0:T(8,128)(2,1)S(1)}, bf16[8,64,1024]{2,1,0:T(8,128)(2,1)}, u32[]{:S(2)}) copy-start(bf16[8,64,1024]{2,1,0:T(8,128)(2,1)} %shard_map.115.refs_4_.refs_8_) | copy-start | bytes 3145732
  206.9 15.1 %collective-permute-start.13 = (bf16[128,2048]{1,0:T(8,128)(2,1)}, bf16[128,2048]{1,0:T(8,128)(2,1)S(1)}, u32[]{:S(2)}, u32[]{:S(2)}) collective-permute-start(bf16[128,2048]{1,0:T(8,128)(2,1)} %get-tuple-element.20.refs_0_), channel_id=1, source_target_pairs={{0,8},{4,12},{8,0},{12,4},{16,24},{20,28},{24,16},{28,20},{1,9},{5... | collective-permute-start | bytes 1572872 | tf_op jit(solution)/shard_map/ppermute | solution.py:455
  207.4 23.4 %collective-permute-start.15 = (bf16[128,2048]{1,0:T(8,128)(2,1)}, bf16[128,2048]{1,0:T(8,128)(2,1)S(1)}, u32[]{:S(2)}, u32[]{:S(2)}) collective-permute-start(bf16[128,2048]{1,0:T(8,128)(2,1)} %get-tuple-element.20.refs_0_), channel_id=1, source_target_pairs={{0,16},{4,20},{8,24},{12,28},{16,0},{20,4},{24,8},{28,12},{1,17},{... | collective-permute-start | bytes 1572872 | tf_op jit(solution)/shard_map/ppermute | solution.py:455
  209.0 21.9 %collective-permute-start.17 = (bf16[128,2048]{1,0:T(8,128)(2,1)}, bf16[128,2048]{1,0:T(8,128)(2,1)}, u32[]{:S(2)}, u32[]{:S(2)}) collective-permute-start(bf16[128,2048]{1,0:T(8,128)(2,1)} %get-tuple-element.20.refs_0_), channel_id=1, source_target_pairs={{0,24},{4,28},{8,16},{12,20},{16,8},{20,12},{24,0},{28,4},{1,25},{... | collective-permute-start | bytes 1572872 | tf_op jit(solution)/shard_map/ppermute | solution.py:455
  210.4 33.3 %collective-permute-start.21 = (bf16[8,64,1024]{2,1,0:T(8,128)(2,1)S(1)}, bf16[8,64,1024]{2,1,0:T(8,128)(2,1)}, u32[]{:S(2)}, u32[]{:S(2)}) collective-permute-start(bf16[8,64,1024]{2,1,0:T(8,128)(2,1)S(1)} %copy-done.2), channel_id=1, source_target_pairs={{0,3},{1,0},{2,1},{3,2},{4,7},{5,4},{6,5},{7,6},{8,11},{9,8},{10,9... | collective-permute-start | bytes 3145736 | tf_op jit(solution)/shard_map/ppermute | solution.py:474
  216.4 14.9 %collective-permute-start.12 = (bf16[128,2048]{1,0:T(8,128)(2,1)}, bf16[128,2048]{1,0:T(8,128)(2,1)}, u32[]{:S(2)}, u32[]{:S(2)}) collective-permute-start(bf16[128,2048]{1,0:T(8,128)(2,1)} %get-tuple-element.20.refs_0_), channel_id=1, source_target_pairs={{0,4},{4,0},{8,12},{12,8},{16,20},{20,16},{24,28},{28,24},{1,5},{5... | collective-permute-start | bytes 1572872 | tf_op jit(solution)/shard_map/ppermute | solution.py:455
  222.0 9.4 %collective-permute-start.14 = (bf16[128,2048]{1,0:T(8,128)(2,1)S(1)}, bf16[128,2048]{1,0:T(8,128)(2,1)}, u32[]{:S(2)}, u32[]{:S(2)}) collective-permute-start(bf16[128,2048]{1,0:T(8,128)(2,1)S(1)} %collective-permute-done.13.refs_2_), channel_id=1, source_target_pairs={{0,4},{4,0},{8,12},{12,8},{16,20},{20,16},{24,28},{28,24},{1,5},{5... | collective-permute-start | bytes 1572872 | tf_op jit(solution)/shard_map/ppermute | solution.py:455
  230.8 3.0 copy-start.16
  230.8 2.0 collective-permute-start.16
  230.9 3.0 collective-permute-start.18
  233.9 1.2 copy-start.9
  248.7 2.4 collective-permute-start.24
  248.9 3.3 collective-permute-start.22
  249.3 27.4 %collective-permute-start.27 = (bf16[8,64,1024]{2,1,0:T(8,128)(2,1)}, bf16[8,64,1024]{2,1,0:T(8,128)(2,1)S(1)}, u32[]{:S(2)}, u32[]{:S(2)}) collective-permute-start(bf16[8,64,1024]{2,1,0:T(8,128)(2,1)} %shard_map.123.refs_1_), channel_id=1, source_target_pairs={{0,1},{1,2},{2,3},{3,0},{4,5},{5,6},{6,7},{7,4},{8,9},{9,10},{10,1... | collective-permute-start | bytes 3145736 | tf_op jit(solution)/shard_map/ppermute | solution.py:471
  252.6 24.1 %collective-permute-start.23 = (bf16[128,1536]{1,0:T(8,128)(2,1)S(1)}, bf16[128,1536]{1,0:T(8,128)(2,1)S(1)}, u32[]{:S(2)}, u32[]{:S(2)}) collective-permute-start(bf16[128,1536]{1,0:T(8,128)(2,1)S(1)} %get-tuple-element.42), channel_id=1, source_target_pairs={{0,8},{4,12},{8,0},{12,4},{16,24},{20,28},{24,16},{28,20},{1,9},{5... | collective-permute-start | bytes 1179656 | tf_op jit(solution)/shard_map/ppermute | solution.py:455
  254.2 22.5 %collective-permute-start.25 = (bf16[128,1536]{1,0:T(8,128)(2,1)S(1)}, bf16[128,1536]{1,0:T(8,128)(2,1)S(1)}, u32[]{:S(2)}, u32[]{:S(2)}) collective-permute-start(bf16[128,1536]{1,0:T(8,128)(2,1)S(1)} %get-tuple-element.36), channel_id=1, source_target_pairs={{0,16},{4,20},{8,24},{12,28},{16,0},{20,4},{24,8},{28,12},{1,17},{... | collective-permute-start | bytes 1179656 | tf_op jit(solution)/shard_map/ppermute | solution.py:455
  254.7 35.2 %copy-start.14 = (bf16[128,2048]{1,0:T(8,128)(2,1)S(1)}, bf16[128,2048]{1,0:T(8,128)(2,1)}, u32[]{:S(2)}) copy-start(bf16[128,2048]{1,0:T(8,128)(2,1)} %copy-done.13) | copy-start | bytes 1572868
  254.7 22.1 %collective-permute-start.26 = (bf16[128,1536]{1,0:T(8,128)(2,1)S(1)}, bf16[128,1536]{1,0:T(8,128)(2,1)S(1)}, u32[]{:S(2)}, u32[]{:S(2)}) collective-permute-start(bf16[128,1536]{1,0:T(8,128)(2,1)S(1)} %get-tuple-element.35), channel_id=1, source_target_pairs={{0,24},{4,28},{8,16},{12,20},{16,8},{20,12},{24,0},{28,4},{1,25},{... | collective-permute-start | bytes 1179656 | tf_op jit(solution)/shard_map/ppermute | solution.py:455
  278.0 1.6 collective-permute-start.30
  278.1 1.9 collective-permute-start.28
  280.2 5.8 %collective-permute-start.29 = (bf16[128,512]{1,0:T(8,128)(2,1)S(1)}, bf16[128,512]{1,0:T(8,128)(2,1)S(1)}, u32[]{:S(2)}, u32[]{:S(2)}) collective-permute-start(bf16[128,512]{1,0:T(8,128)(2,1)S(1)} %get-tuple-element.54), channel_id=1, source_target_pairs={{0,8},{4,12},{8,0},{12,4},{16,24},{20,28},{24,16},{28,20},{1,9},{5... | collective-permute-start | bytes 393224 | tf_op jit(solution)/shard_map/ppermute | solution.py:455
  281.8 8.1 %collective-permute-start.31 = (bf16[128,512]{1,0:T(8,128)(2,1)S(1)}, bf16[128,512]{1,0:T(8,128)(2,1)S(1)}, u32[]{:S(2)}, u32[]{:S(2)}) collective-permute-start(bf16[128,512]{1,0:T(8,128)(2,1)S(1)} %get-tuple-element.44), channel_id=1, source_target_pairs={{0,16},{4,20},{8,24},{12,28},{16,0},{20,4},{24,8},{28,12},{1,17},{... | collective-permute-start | bytes 393224 | tf_op jit(solution)/shard_map/ppermute | solution.py:455
  282.3 7.6 %collective-permute-start.32 = (bf16[128,512]{1,0:T(8,128)(2,1)S(1)}, bf16[128,512]{1,0:T(8,128)(2,1)S(1)}, u32[]{:S(2)}, u32[]{:S(2)}) collective-permute-start(bf16[128,512]{1,0:T(8,128)(2,1)S(1)} %get-tuple-element.43), channel_id=1, source_target_pairs={{0,24},{4,28},{8,16},{12,20},{16,8},{20,12},{24,0},{28,4},{1,25},{... | collective-permute-start | bytes 393224 | tf_op jit(solution)/shard_map/ppermute | solution.py:455
  292.8 40.1 %collective-permute-start.35 = (bf16[128,2048]{1,0:T(8,128)(2,1)}, bf16[128,2048]{1,0:T(8,128)(2,1)S(1)}, u32[]{:S(2)}, u32[]{:S(2)}) collective-permute-start(bf16[128,2048]{1,0:T(8,128)(2,1)} %get-tuple-element.29), channel_id=1, source_target_pairs={{0,2},{1,10},{2,18},{3,26},{4,4},{5,12},{6,20},{7,28},{8,3},{9,11}... | collective-permute-start | bytes 1572872 | tf_op jit(solution)/shard_map/ppermute | solution.py:560
  299.1 42.5 %collective-permute-start.33 = (bf16[128,2048]{1,0:T(8,128)(2,1)}, bf16[128,2048]{1,0:T(8,128)(2,1)S(1)}, u32[]{:S(2)}, u32[]{:S(2)}) collective-permute-start(bf16[128,2048]{1,0:T(8,128)(2,1)} %get-tuple-element.29), channel_id=1, source_target_pairs={{0,0},{1,8},{2,16},{3,24},{4,6},{5,14},{6,22},{7,30},{8,1},{9,9},{... | collective-permute-start | bytes 1572872 | tf_op jit(solution)/shard_map/ppermute | solution.py:560
  301.0 59.3 %collective-permute-start.34 = (bf16[128,2048]{1,0:T(8,128)(2,1)}, bf16[128,2048]{1,0:T(8,128)(2,1)S(1)}, u32[]{:S(2)}, u32[]{:S(2)}) collective-permute-start(bf16[128,2048]{1,0:T(8,128)(2,1)} %get-tuple-element.29), channel_id=1, source_target_pairs={{0,1},{1,9},{2,17},{3,25},{4,7},{5,15},{6,23},{7,31},{8,0},{9,8},{... | collective-permute-start | bytes 1572872 | tf_op jit(solution)/shard_map/ppermute | solution.py:560
  301.9 58.4 %collective-permute-start.36 = (bf16[128,2048]{1,0:T(8,128)(2,1)}, bf16[128,2048]{1,0:T(8,128)(2,1)S(1)}, u32[]{:S(2)}, u32[]{:S(2)}) collective-permute-start(bf16[128,2048]{1,0:T(8,128)(2,1)} %get-tuple-element.29), channel_id=1, source_target_pairs={{0,3},{1,11},{2,19},{3,27},{4,5},{5,13},{6,21},{7,29},{8,2},{9,10}... | collective-permute-start | bytes 1572872 | tf_op jit(solution)/shard_map/ppermute | solution.py:560
  302.7 37.0 %all-to-all-start.2 = ((bf16[8,128,256]{2,1,0:T(8,128)(2,1)}), bf16[8,128,256]{2,1,0:T(8,128)(2,1)}, u32[]{:S(2)}, u32[]{:S(2)}) async-start(bf16[8,128,256]{2,1,0:T(8,128)(2,1)} %bitcast.80), calls=%async_computation.2 | async-start | bytes 1048576 | tf_op jit(solution)/shard_map/all_to_all | solution.py:477
  333.7 26.6 %copy-start.12 = (bf16[128,2048]{1,0:T(8,128)(2,1)S(1)}, bf16[128,2048]{1,0:T(8,128)(2,1)}, u32[]{:S(2)}) copy-start(bf16[128,2048]{1,0:T(8,128)(2,1)} %copy-done.11) | copy-start | bytes 1572868
  335.7 32.6 %collective-permute-start.37 = (bf16[4,4,64,64]{3,2,1,0:T(8,128)(2,1)}, bf16[4,4,64,64]{3,2,1,0:T(8,128)(2,1)S(1)}, u32[]{:S(2)}, u32[]{:S(2)}) collective-permute-start(bf16[4,4,64,64]{3,2,1,0:T(8,128)(2,1)} %get-tuple-element.52), channel_id=1, source_target_pairs={{0,0},{1,8},{2,16},{3,24},{4,4},{5,12},{6,20},{7,28},{8,1},{9,9},{... | collective-permute-start | bytes 393224 | tf_op jit(solution)/shard_map/ppermute | solution.py:574
  338.0 30.3 %collective-permute-start.38 = (bf16[4,4,64,64]{3,2,1,0:T(8,128)(2,1)}, bf16[4,4,64,64]{3,2,1,0:T(8,128)(2,1)S(1)}, u32[]{:S(2)}, u32[]{:S(2)}) collective-permute-start(bf16[4,4,64,64]{3,2,1,0:T(8,128)(2,1)} %get-tuple-element.51), channel_id=1, source_target_pairs={{0,4},{1,12},{2,20},{3,28},{4,0},{5,8},{6,16},{7,24},{8,5},{9,13},... | collective-permute-start | bytes 393224 | tf_op jit(solution)/shard_map/ppermute | solution.py:574
  360.3 9.8 %copy-start.1 = (bf16[2,96,2048]{2,1,0:T(8,128)(2,1)S(1)}, bf16[2,96,2048]{2,1,0:T(8,128)(2,1)}, u32[]{:S(2)}) copy-start(bf16[2,96,2048]{2,1,0:T(8,128)(2,1)} %param.14) | copy-start | bytes 2359300
  (11 other events, 9.7 us)
Sparse Core Ops, SparseCore 0:
  36.9 54.1 all-gather.2
  93.0 45.4 all-gather.4
